TPU v7x, 32 devices: a whole 2x2x4 slice. The times are simulated.
32 devices in a mesh: dp: 8 (over z, x), seq: 4 (over y, core).
Axes of the slice: x: 2, y: 2, z: 4, core: 2. Of those that a mesh axis runs over, the one named last changes fastest.
Arguments:
- tokens: bfloat16 [32, 512, 768], P('dp', 'seq'), may hold values from -6 to 6
- seg_lengths: int32 [32, 8], P('dp'), may hold values from 1 to 392, 512 in all within a row
- w_query: bfloat16 [768, 768], replicated, may hold values from -0.3125 to 0.3125
- b_query: bfloat16 [768], replicated, may hold values from -3 to 3
- w_key: bfloat16 [768, 768], replicated, may hold values from -0.3125 to 0.3125
- w_value: bfloat16 [768, 768], replicated, may hold values from -0.21875 to 0.21875
- b_value: bfloat16 [768], replicated, may hold values from -3 to 3
- w_out: bfloat16 [768, 768], replicated, may hold values from -0.625 to 0.625
- b_out: bfloat16 [768], replicated, may hold values from -3 to 3
- gain_attn: bfloat16 [768], replicated, may hold values from 0.25 to 1.75
- shift_attn: bfloat16 [768], replicated, may hold values from -3 to 3
- w_up: bfloat16 [768, 3072], replicated, may hold values from -0.21875 to 0.21875
- b_up: bfloat16 [3072], replicated, may hold values from -3 to 3
- w_down: bfloat16 [3072, 768], replicated, may hold values from -0.109375 to 0.109375
- b_down: bfloat16 [768], replicated, may hold values from -3 to 3
- gain_ffn: bfloat16 [768], replicated, may hold values from 0.25 to 1.75
- shift_ffn: bfloat16 [768], replicated, may hold values from -3 to 3
- grad_output: bfloat16 [32, 512, 768], P('dp', 'seq'), may hold values from -6 to 6
- grad_pooled: bfloat16 [32, 8, 768], P('dp'), may hold values from -12 to 12
Outputs:
- output: bfloat16 [32, 512, 768], P('dp', 'seq')
- pooled: float32 [32, 8, 768], P('dp')
- grad_tokens: bfloat16 [32, 512, 768], P('dp', 'seq')
- grad_w_query: float32 [768, 768], P(None, 'dp')
- grad_b_query: float32 [768], P('dp')
- grad_w_key: float32 [768, 768], P(None, 'dp')
- grad_w_value: float32 [768, 768], P(None, 'dp')
- grad_b_value: float32 [768], P('dp')
- grad_w_out: float32 [768, 768], P(None, 'dp')
- grad_b_out: float32 [768], P('dp')
- grad_gain_attn: float32 [768], P('dp')
- grad_shift_attn: float32 [768], P('dp')
- grad_w_up: float32 [768, 3072], P(None, 'dp')
- grad_b_up: float32 [3072], P('dp')
- grad_w_down: float32 [3072, 768], P(None, 'dp')
- grad_b_down: float32 [768], P('dp')
- grad_gain_ffn: float32 [768], P('dp')
- grad_shift_ffn: float32 [768], P('dp')
Inputs may be any that keep to these rules, and one draw needn't show every extreme that they name: `seg_lengths`: in every row the 8 lengths are at least 1 and sum to 512; the longest in every row equals the stated maximum.
All inputs are finite; a program needn't handle non-finite values.
Results may differ from a plain program's by a relative error of at most 0.024.
Values may be sent and summed in bfloat16 or wider, within the bound.
No kernel may reach another device: no remote copies, remote signals or barrier semaphores. Data moves between devices by JAX's collectives and lax.ppermute only.
A program may use at most 192 MiB of HBM per device.

v0:
```python
import jax
import jax.numpy as jnp
from jax import lax
from jax.sharding import PartitionSpec as P

HD = 64
SEGS = 8


epsilon = 1e-06
masked = -1e30


def dense(left, right):
    return jnp.dot(left, right, preferred_element_type=jnp.float32)


def dense_t(left, right):
    return lax.dot_general(
        left, right, (((1,), (1,)), ((), ())), preferred_element_type=jnp.float32
    )


def inner(left, right):
    return lax.dot_general(
        left, right, (((0,), (0,)), ((), ())), preferred_element_type=jnp.float32
    )


def norm_parts(value):
    centre = value - jnp.mean(value, axis=-1, keepdims=True)
    inverse = lax.rsqrt(jnp.mean(centre * centre, axis=-1, keepdims=True) + epsilon)
    return (centre * inverse, inverse)


def norm_back(grad_norm, normed, inverse):
    mean_grad = jnp.mean(grad_norm, axis=-1, keepdims=True)
    mean_cross = jnp.mean(grad_norm * normed, axis=-1, keepdims=True)
    return (grad_norm - mean_grad - normed * mean_cross) * inverse


def exact_gelu(value):
    return jax.nn.gelu(value, approximate=False)


def as_rows(vector):
    return vector.reshape(1, vector.shape[0])


def score_grads(
    query_heads, grad_heads, lse_rows, delta_rows, query_seg, key_heads, value_heads, key_seg
):
    scale_factor = HD ** (-0.5)
    scores = (
        jnp.einsum("rqhd,rkhd->rhqk", query_heads, key_heads, preferred_element_type=jnp.float32)
        * scale_factor
    )
    allowed = (query_seg[:, :, None] == key_seg[:, None, :])[:, None]
    lse_t = jnp.transpose(lse_rows, (0, 2, 1))[..., None]
    delta_t = jnp.transpose(delta_rows, (0, 2, 1))[..., None]
    probability = jnp.where(allowed, jnp.exp(scores - lse_t), 0.0)
    grad_values = jnp.einsum(
        "rhqk,rqhd->rkhd",
        probability.astype(jnp.bfloat16),
        grad_heads,
        preferred_element_type=jnp.float32,
    )
    grad_probs = jnp.einsum(
        "rqhd,rkhd->rhqk", grad_heads, value_heads, preferred_element_type=jnp.float32
    )
    grad_scores = (probability * (grad_probs - delta_t)).astype(jnp.bfloat16)
    grad_query = (
        jnp.einsum("rhqk,rkhd->rqhd", grad_scores, key_heads, preferred_element_type=jnp.float32)
        * scale_factor
    )
    grad_keys = (
        jnp.einsum("rhqk,rqhd->rkhd", grad_scores, query_heads, preferred_element_type=jnp.float32)
        * scale_factor
    )
    return (grad_query, grad_keys, grad_values)


def local(
    tokens,
    seg_lengths,
    w_query,
    b_query,
    w_key,
    w_value,
    b_value,
    w_out,
    b_out,
    gain_attn,
    shift_attn,
    w_up,
    b_up,
    w_down,
    b_down,
    gain_ffn,
    shift_ffn,
    grad_output,
    grad_pooled,
):
    seq_rank = lax.axis_index("seq")
    work_in, work_grad, work_lengths, work_pool_grad = (
        tokens,
        grad_output,
        seg_lengths,
        grad_pooled,
    )
    offset = seq_rank * tokens.shape[1]
    row_count, local_len, width = work_in.shape
    head_count = width // HD
    token_count = row_count * local_len
    seg_ends = jnp.cumsum(work_lengths, axis=1)

    def segment_of(positions):
        return jnp.sum((positions[None, :, None] >= seg_ends[:, None, :]).astype(jnp.int32), axis=2)

    query_pos = offset + jnp.arange(local_len, dtype=jnp.int32)
    query_seg = segment_of(query_pos)
    flat_in = work_in.reshape(token_count, width)
    query = (dense(flat_in, w_query) + b_query).astype(jnp.bfloat16)
    keys = dense(flat_in, w_key).astype(jnp.bfloat16).reshape(row_count, local_len, width)
    values = (
        (dense(flat_in, w_value) + b_value)
        .astype(jnp.bfloat16)
        .reshape(row_count, local_len, width)
    )
    query_heads = query.reshape(row_count, local_len, head_count, HD)
    scale_factor = HD ** (-0.5)
    run_max = jnp.full((row_count, head_count, local_len), masked, jnp.float32)
    key_piece = lax.all_gather(keys, "seq", axis=1, tiled=True)
    value_piece = lax.all_gather(values, "seq", axis=1, tiled=True)
    span_len = key_piece.shape[1]
    key_heads = key_piece.reshape(row_count, span_len, head_count, HD)
    value_heads = value_piece.reshape(row_count, span_len, head_count, HD)
    scores = (
        jnp.einsum("rqhd,rkhd->rhqk", query_heads, key_heads, preferred_element_type=jnp.float32)
        * scale_factor
    )
    key_seg = segment_of(jnp.arange(span_len, dtype=jnp.int32))
    allowed = (query_seg[:, :, None] == key_seg[:, None, :])[:, None]
    scores = jnp.where(allowed, scores, masked)
    new_max = jnp.maximum(run_max, jnp.max(scores, axis=-1))
    expwts = jnp.where(allowed, jnp.exp(scores - new_max[..., None]), 0.0)
    new_sum = jnp.sum(expwts, axis=-1)
    new_acc = jnp.einsum(
        "rhqk,rkhd->rhqd",
        expwts.astype(jnp.bfloat16),
        value_heads,
        preferred_element_type=jnp.float32,
    )
    log_sum = jnp.transpose(new_max + jnp.log(new_sum), (0, 2, 1))
    attn_out = jnp.transpose(new_acc / new_sum[..., None], (0, 2, 1, 3)).reshape(token_count, width)
    attn_low = attn_out.astype(jnp.bfloat16)
    mixed = dense(attn_low, w_out) + b_out
    normed_one, inverse_one = norm_parts(flat_in.astype(jnp.float32) + mixed)
    hidden = normed_one * gain_attn + shift_attn
    hidden_low = hidden.astype(jnp.bfloat16)
    pre_act = dense(hidden_low, w_up) + b_up
    activated, gelu_pull = jax.vjp(exact_gelu, pre_act)
    act_low = activated.astype(jnp.bfloat16)
    ffn_out = dense(act_low, w_down) + b_down
    normed_two, inverse_two = norm_parts(hidden + ffn_out)
    result = normed_two * gain_ffn + shift_ffn
    seg_onehot = (query_seg[:, :, None] == jnp.arange(SEGS, dtype=jnp.int32)[None, None, :]).astype(
        jnp.float32
    )
    pool_part = jnp.einsum(
        "rcs,rcd->rsd",
        seg_onehot,
        result.reshape(row_count, local_len, width),
        precision=lax.Precision.HIGHEST,
    )
    pool_total = lax.psum(pool_part.astype(jnp.bfloat16), "seq").astype(jnp.float32)
    length_cols = work_lengths.astype(jnp.float32)[:, :, None]
    pooled = pool_total / length_cols
    grad_result = work_grad.astype(jnp.float32).reshape(token_count, width) + jnp.einsum(
        "rcs,rsd->rcd",
        seg_onehot,
        work_pool_grad.astype(jnp.float32) / length_cols,
        precision=lax.Precision.HIGHEST,
    ).reshape(token_count, width)
    grad_gain_two = jnp.sum(grad_result * normed_two, axis=0)
    grad_shift_two = jnp.sum(grad_result, axis=0)
    grad_res_two = norm_back(grad_result * gain_ffn, normed_two, inverse_two)
    grad_ffn_low = grad_res_two.astype(jnp.bfloat16)
    grad_b_down = jnp.sum(grad_ffn_low.astype(jnp.float32), axis=0)
    grad_w_down = inner(act_low, grad_ffn_low)
    grad_pre = gelu_pull(dense_t(grad_ffn_low, w_down))[0]
    grad_pre_low = grad_pre.astype(jnp.bfloat16)
    grad_b_up = jnp.sum(grad_pre_low.astype(jnp.float32), axis=0)
    grad_w_up = inner(hidden_low, grad_pre_low)
    grad_hidden = grad_res_two + dense_t(grad_pre_low, w_up)
    grad_gain_one = jnp.sum(grad_hidden * normed_one, axis=0)
    grad_shift_one = jnp.sum(grad_hidden, axis=0)
    grad_res_one = norm_back(grad_hidden * gain_attn, normed_one, inverse_one)
    grad_mixed_low = grad_res_one.astype(jnp.bfloat16)
    grad_b_out = jnp.sum(grad_mixed_low.astype(jnp.float32), axis=0)
    grad_w_out = inner(attn_low, grad_mixed_low)
    grad_attn_low = dense_t(grad_mixed_low, w_out).astype(jnp.bfloat16)
    delta = jnp.sum(
        (grad_attn_low.astype(jnp.float32) * attn_out).reshape(
            row_count, local_len, head_count, HD
        ),
        axis=-1,
    )
    grad_attn_heads = grad_attn_low.reshape(row_count, local_len, head_count, HD)
    all_keys, all_values = (
        lax.all_gather(keys, "seq", axis=1, tiled=True),
        lax.all_gather(values, "seq", axis=1, tiled=True),
    )
    full_len = all_keys.shape[1]
    key_seg_all = segment_of(jnp.arange(full_len, dtype=jnp.int32))
    grad_query, grad_keys, grad_values = score_grads(
        query_heads,
        grad_attn_heads,
        log_sum,
        delta,
        query_seg,
        all_keys.reshape(row_count, full_len, head_count, HD),
        all_values.reshape(row_count, full_len, head_count, HD),
        key_seg_all,
    )
    grad_keys_own, grad_values_own = (
        lax.psum_scatter(
            grad_keys.reshape(row_count, full_len, width).astype(jnp.bfloat16),
            "seq",
            scatter_dimension=1,
            tiled=True,
        ).astype(jnp.float32),
        lax.psum_scatter(
            grad_values.reshape(row_count, full_len, width).astype(jnp.bfloat16),
            "seq",
            scatter_dimension=1,
            tiled=True,
        ).astype(jnp.float32),
    )
    grad_query_own = grad_query.reshape(token_count, width)
    grad_query_low = grad_query_own.astype(jnp.bfloat16)
    grad_key_low = grad_keys_own.reshape(token_count, width).astype(jnp.bfloat16)
    grad_value_low = grad_values_own.reshape(token_count, width).astype(jnp.bfloat16)
    grad_b_query = jnp.sum(grad_query_low.astype(jnp.float32), axis=0)
    grad_b_value = jnp.sum(grad_value_low.astype(jnp.float32), axis=0)
    grad_w_query = inner(flat_in, grad_query_low)
    grad_w_key = inner(flat_in, grad_key_low)
    grad_w_value = inner(flat_in, grad_value_low)
    grad_input = (
        grad_res_one
        + dense_t(grad_query_low, w_query)
        + dense_t(grad_key_low, w_key)
        + dense_t(grad_value_low, w_value)
    )
    shares = (
        lax.psum_scatter(grad_w_query, "dp", scatter_dimension=1, tiled=True),
        lax.psum_scatter(as_rows(grad_b_query), "dp", scatter_dimension=1, tiled=True),
        lax.psum_scatter(grad_w_key, "dp", scatter_dimension=1, tiled=True),
        lax.psum_scatter(grad_w_value, "dp", scatter_dimension=1, tiled=True),
        lax.psum_scatter(as_rows(grad_b_value), "dp", scatter_dimension=1, tiled=True),
        lax.psum_scatter(grad_w_out, "dp", scatter_dimension=1, tiled=True),
        lax.psum_scatter(as_rows(grad_b_out), "dp", scatter_dimension=1, tiled=True),
        lax.psum_scatter(as_rows(grad_gain_one), "dp", scatter_dimension=1, tiled=True),
        lax.psum_scatter(as_rows(grad_shift_one), "dp", scatter_dimension=1, tiled=True),
        lax.psum_scatter(grad_w_up, "dp", scatter_dimension=1, tiled=True),
        lax.psum_scatter(as_rows(grad_b_up), "dp", scatter_dimension=1, tiled=True),
        lax.psum_scatter(grad_w_down, "dp", scatter_dimension=1, tiled=True),
        lax.psum_scatter(as_rows(grad_b_down), "dp", scatter_dimension=1, tiled=True),
        lax.psum_scatter(as_rows(grad_gain_two), "dp", scatter_dimension=1, tiled=True),
        lax.psum_scatter(as_rows(grad_shift_two), "dp", scatter_dimension=1, tiled=True),
    )
    shares = (
        lax.psum(shares[0].astype(jnp.bfloat16), "seq").astype(jnp.float32),
        lax.psum(shares[1].astype(jnp.bfloat16), "seq").astype(jnp.float32),
        lax.psum(shares[2].astype(jnp.bfloat16), "seq").astype(jnp.float32),
        lax.psum(shares[3].astype(jnp.bfloat16), "seq").astype(jnp.float32),
        lax.psum(shares[4].astype(jnp.bfloat16), "seq").astype(jnp.float32),
        lax.psum(shares[5].astype(jnp.bfloat16), "seq").astype(jnp.float32),
        lax.psum(shares[6].astype(jnp.bfloat16), "seq").astype(jnp.float32),
        lax.psum(shares[7].astype(jnp.bfloat16), "seq").astype(jnp.float32),
        lax.psum(shares[8].astype(jnp.bfloat16), "seq").astype(jnp.float32),
        lax.psum(shares[9].astype(jnp.bfloat16), "seq").astype(jnp.float32),
        lax.psum(shares[10].astype(jnp.bfloat16), "seq").astype(jnp.float32),
        lax.psum(shares[11].astype(jnp.bfloat16), "seq").astype(jnp.float32),
        lax.psum(shares[12].astype(jnp.bfloat16), "seq").astype(jnp.float32),
        lax.psum(shares[13].astype(jnp.bfloat16), "seq").astype(jnp.float32),
        lax.psum(shares[14].astype(jnp.bfloat16), "seq").astype(jnp.float32),
    )
    out_low = result.astype(jnp.bfloat16).reshape(row_count, local_len, width)
    input_low = grad_input.astype(jnp.bfloat16).reshape(row_count, local_len, width)
    return (
        out_low,
        pooled,
        input_low,
        shares[0],
        shares[1].reshape(-1),
        shares[2],
        shares[3],
        shares[4].reshape(-1),
        shares[5],
        shares[6].reshape(-1),
        shares[7].reshape(-1),
        shares[8].reshape(-1),
        shares[9],
        shares[10].reshape(-1),
        shares[11],
        shares[12].reshape(-1),
        shares[13].reshape(-1),
        shares[14].reshape(-1),
    )


def solution(mesh):
    placed = (
        P("dp", "seq", None),
        P("dp", None),
        P(),
        P(),
        P(),
        P(),
        P(),
        P(),
        P(),
        P(),
        P(),
        P(),
        P(),
        P(),
        P(),
        P(),
        P(),
        P("dp", "seq", None),
        P("dp", None, None),
    )
    return jax.shard_map(
        local,
        mesh=mesh,
        in_specs=placed,
        out_specs=(
            P("dp", "seq", None),
            P("dp", None, None),
            P("dp", "seq", None),
            P(None, "dp"),
            P("dp"),
            P(None, "dp"),
            P(None, "dp"),
            P("dp"),
            P(None, "dp"),
            P("dp"),
            P("dp"),
            P("dp"),
            P(None, "dp"),
            P("dp"),
            P(None, "dp"),
            P("dp"),
            P("dp"),
            P("dp"),
        ),
        check_vma=False,
    )
```

profile of v0, /device:TPU:0, one launch (start us, length us, event | category | flops | bytes accessed | tf_op | source)
XLA Modules:
  0.0 1513.9 jit_solution(11935637868939328244)
XLA Ops:
  7.3 3.3 convolution_convert_fusion.1
  10.7 1.7 add_convert_fusion.2
  12.7 2.1 add_convert_fusion.3
  21.9 2.9 fusion.61
  26.3 15.7 %all-gather.3.cloned.1.call-done = bf16[4,512,768]{2,1,0:T(8,128)(2,1)} async-done(((bf16[4,128,768]{2,1,0:T(8,128)(2,1)}), bf16[4,512,768]{2,1,0:T(8,128)(2,1)}) %all-gather.3.cloned.1.call-update) | async-done | bytes 3145744 | tf_op jit(solution)/shard_map/all_gather | solution.py:133
  42.0 5.1 copy.77
  47.2 4.2 select_reduce_fusion
  51.5 4.1 fusion.1
  57.4 15.3 %all-gather.5.cloned.1.call-done = bf16[4,512,768]{2,1,0:T(8,128)(2,1)} async-done(((bf16[4,128,768]{2,1,0:T(8,128)(2,1)}), bf16[4,512,768]{2,1,0:T(8,128)(2,1)}) %all-gather.5.cloned.1.call-update) | async-done | bytes 3145744 | tf_op jit(solution)/shard_map/all_gather | solution.py:134
  72.7 4.7 copy.79
  77.4 7.5 bitcast_divide_fusion
  88.7 20.2 %multiply_convert_fusion.2 = (bf16[512,3072]{1,0:T(8,128)(2,1)S(1)}, f32[512,3072]{1,0:T(8,128)}, f32[512,3072]{1,0:T(8,128)}) fusion(f32[3072]{0:T(1024)S(1)} %copy-done.33, bf16[768,3072]{1,0:T(8,128)(2,1)} %param.30, f32[512,768]{1,0:T(8,128)S(1)} %get-tuple-element.55, f32[768]{0:T(1024)S(1)} %copy-done.39, f32[768]{0:T(1024)S(1)} %convert_element_type.246, ...), kind=kOutput, calls=%fused_computation.14 | convolution fusion | flops 2521694208 | bytes 22042624 | tf_op jit(solution)/shard_map/dot_general | solution.py:15
  109.0 2.8 fusion.65
  112.8 2.7 convert_reduce_fusion.1
  115.5 8.8 convert_reduce_fusion
  124.3 8.3 multiply_reduce_fusion
  132.6 1.7 copy.83
  135.1 3.0 convert_reduce_fusion.2
  138.1 2.2 convert_multiply_fusion
  140.3 3.0 copy.84
  143.3 2.7 reshape.264
  146.1 2.2 reduce_sum.204
  149.7 2.3 copy.81
  152.0 2.6 reshape.263
  154.6 8.3 multiply_convert_fusion
  162.9 3.1 multiply_convert_fusion.1
  166.5 4.7 copy.88
  172.1 9.1 fusion.18
  181.2 4.7 copy.90
  187.6 6.6 convert_reduce_fusion.4
  203.1 2.4 copy.105
  205.6 3.7 fusion.36
  210.8 3.4 convolution_bitcast_fusion.2
  214.6 3.3 convolution_bitcast_fusion.1
  218.0 31.8 %reduce-scatter.38.cloned.1.call-done = bf16[4,128,768]{2,1,0:T(8,128)(2,1)} async-done(((bf16[4,512,768]{2,1,0:T(8,128)(2,1)}), bf16[4,128,768]{2,1,0:T(8,128)(2,1)}) %reduce-scatter.38.cloned.1.call-update) | async-done | bytes 786448 | tf_op jit(solution)/shard_map/reduce_scatter | solution.py:233
  249.8 3.4 convolution_bitcast_fusion
  253.3 8.8 fusion.57
  262.2 8.6 fusion.46
  270.8 43.6 %reduce-scatter.68.cloned.1.call-done = f32[96,1]{1,0:T(8,128)} async-done(((f32[768,1]{1,0:T(8,128)}), f32[96,1]{1,0:T(8,128)}) %reduce-scatter.68.cloned.1.call-update) | async-done | bytes 400
  315.2 2.7 convolution_convert_fusion.2
  318.0 3.5 fusion.27
  321.5 57.0 %reduce-scatter.52.cloned.1.call-done = f32[96,1]{1,0:T(8,128)} async-done(((f32[768,1]{1,0:T(8,128)}), f32[96,1]{1,0:T(8,128)}) %reduce-scatter.52.cloned.1.call-update) | async-done | bytes 400
  380.7 62.0 %reduce-scatter.56.cloned.1.call-done = f32[96,1]{1,0:T(8,128)} async-done(((f32[768,1]{1,0:T(8,128)}), f32[96,1]{1,0:T(8,128)}) %reduce-scatter.56.cloned.1.call-update) | async-done | bytes 400
  445.5 61.0 %reduce-scatter.58.cloned.1.call-done = f32[96,1]{1,0:T(8,128)} async-done(((f32[768,1]{1,0:T(8,128)}), f32[96,1]{1,0:T(8,128)}) %reduce-scatter.58.cloned.1.call-update) | async-done | bytes 400
  509.2 61.0 %reduce-scatter.60.cloned.1.call-done = f32[96,1]{1,0:T(8,128)} async-done(((f32[768,1]{1,0:T(8,128)}), f32[96,1]{1,0:T(8,128)}) %reduce-scatter.60.cloned.1.call-update) | async-done | bytes 400
  572.9 60.8 %reduce-scatter.64.cloned.1.call-done = f32[96,1]{1,0:T(8,128)} async-done(((f32[768,1]{1,0:T(8,128)}), f32[96,1]{1,0:T(8,128)}) %reduce-scatter.64.cloned.1.call-update) | async-done | bytes 400
  636.5 61.0 %reduce-scatter.66.cloned.1.call-done = f32[96,1]{1,0:T(8,128)} async-done(((f32[768,1]{1,0:T(8,128)}), f32[96,1]{1,0:T(8,128)}) %reduce-scatter.66.cloned.1.call-update) | async-done | bytes 400
  700.2 64.5 %reduce-scatter.62.cloned.1.call-done = f32[384,1]{1,0:T(8,128)} async-done(((f32[3072,1]{1,0:T(8,128)}), f32[384,1]{1,0:T(8,128)}) %reduce-scatter.62.cloned.1.call-update) | async-done | bytes 1552
  765.8 70.6 %reduce-scatter.46.cloned.1.call-done = f32[768,96]{0,1:T(8,128)} async-done(((f32[768,768]{0,1:T(8,128)}), f32[768,96]{0,1:T(8,128)}) %reduce-scatter.46.cloned.1.call-update) | async-done | bytes 294928 | tf_op jit(solution)/shard_map/reduce_scatter | solution.py:261
  838.0 70.2 %reduce-scatter.40.cloned.1.call-done = f32[768,96]{0,1:T(8,128)} async-done(((f32[768,768]{0,1:T(8,128)}), f32[768,96]{0,1:T(8,128)}) %reduce-scatter.40.cloned.1.call-update) | async-done | bytes 294928 | tf_op jit(solution)/shard_map/reduce_scatter | solution.py:256
  908.2 1.6 convert_element_type.279
  911.0 3.5 fusion.66
  914.4 65.8 %reduce-scatter.42.cloned.1.call-done = f32[768,96]{0,1:T(8,128)} async-done(((f32[768,768]{0,1:T(8,128)}), f32[768,96]{0,1:T(8,128)}) %reduce-scatter.42.cloned.1.call-update) | async-done | bytes 294928 | tf_op jit(solution)/shard_map/reduce_scatter | solution.py:258
  981.9 70.3 %reduce-scatter.44.cloned.1.call-done = f32[768,96]{0,1:T(8,128)} async-done(((f32[768,768]{0,1:T(8,128)}), f32[768,96]{0,1:T(8,128)}) %reduce-scatter.44.cloned.1.call-update) | async-done | bytes 294928 | tf_op jit(solution)/shard_map/reduce_scatter | solution.py:259
  1053.7 164.7 %reduce-scatter.48.cloned.1.call-done = f32[768,384]{1,0:T(8,128)} async-done(((f32[768,3072]{1,0:T(8,128)}), f32[768,384]{1,0:T(8,128)}) %reduce-scatter.48.cloned.1.call-update) | async-done | bytes 1179664 | tf_op jit(solution)/shard_map/reduce_scatter | solution.py:265
  1218.5 2.1 convert_element_type.295
  1220.6 164.3 %reduce-scatter.50.cloned.1.call-done = f32[3072,96]{0,1:T(8,128)} async-done(((f32[3072,768]{0,1:T(8,128)}), f32[3072,96]{0,1:T(8,128)}) %reduce-scatter.50.cloned.1.call-update) | async-done | bytes 1179664 | tf_op jit(solution)/shard_map/reduce_scatter | solution.py:267
  1384.9 2.2 convert_element_type.299
  1387.1 3.9 add_convert_fusion.1
  1391.1 58.0 %reduce-scatter.54.cloned.1.call-done = f32[96,1]{1,0:T(8,128)} async-done(((f32[768,1]{1,0:T(8,128)}), f32[96,1]{1,0:T(8,128)}) %reduce-scatter.54.cloned.1.call-update) | async-done | bytes 400
  1450.0 11.9 all-reduce
  1467.3 32.0 %all-reduce.4.cloned.1.call-done = (bf16[768,96]{0,1:T(8,128)(2,1)}, bf16[768,96]{0,1:T(8,128)(2,1)}, bf16[768,96]{0,1:T(8,128)(2,1)}, bf16[768,96]{0,1:T(8,128)...) async-done(((bf16[768,96]{0,1:T(8,128)(2,1)}, bf16[768,96]{0,1:T(8,128)(2,1)}, bf16[768,96]{0,1:T(8,128)(2,1)}, bf16[768,96]{0,1:T(8,128)(2,1)}, ...) | async-done | bytes 1769488 | tf_op jit(solution)/shard_map/psum | solution.py:273
  1499.3 2.2 convert_element_type.296
  1501.5 2.2 convert_element_type.300
  (220 shorter events, 64.8 us)
Async XLA Ops:
  7.2 80.1 %copy-start = (bf16[768,768]{1,0:T(8,128)(2,1)S(1)}, bf16[768,768]{1,0:T(8,128)(2,1)}, u32[]{:S(2)}) copy-start(bf16[768,768]{1,0:T(8,128)(2,1)} %param.26) | copy-start | bytes 3538948
  7.2 3.5 copy-start.14
  7.2 3.5 copy-start.43
  7.2 3.5 copy-start.13
  7.2 34.8 %all-gather.3.cloned.1.call-start = ((), (), s32[]{:S(2)}) async-start(), calls=%async_computation.17 | async-start | bytes 3932160 | tf_op jit(solution)/shard_map/all_gather | solution.py:133
  10.6 1.9 copy-start.38
  10.6 2.1 copy-start.44
  10.6 62.1 %all-gather.5.cloned.1.call-start = ((), (), s32[]{:S(2)}) async-start(), calls=%async_computation.18 | async-start | bytes 3932160 | tf_op jit(solution)/shard_map/all_gather | solution.py:134
  12.4 202.1 %reduce-scatter.36.cloned.1.call-start = ((), (), s32[]{:S(2)}) async-start(), calls=%async_computation.19 | async-start | bytes 3932160 | tf_op jit(solution)/shard_map/reduce_scatter | solution.py:227
  12.5 9.4 copy-start.26
  12.7 2.6 copy-start.45
  14.8 1.1 copy-start.46
  15.8 93.1 %copy-start.29 = (f32[768]{0:T(1024)}, f32[768]{0:T(1024)S(1)}, u32[]{:S(2)}) copy-start(f32[768]{0:T(1024)S(1)} %convert_element_type.246) | copy-start | bytes 9220
  21.9 3.5 copy-start.24
  47.2 4.3 copy-start.11
  51.4 4.7 copy-start.1
  51.4 4.7 copy-start.22
  84.9 2.4 copy-start.15
  84.9 2.4 copy-start.42
  85.9 2.4 copy-start.3
  87.3 1.3 copy-start.33
  87.3 1.3 copy-start.39
  87.3 21.6 %slice-start = ((s8[4718592]{0:T(1024)(128)(4,1)}), s8[4194304]{0:T(1024)(128)(4,1)S(1)}, s32[]{:S(2)}) async-start(s8[4718592]{0:T(1024)(128)(4,1)} %bitcast.194), calls=%async_computation.37 | async-start | bytes 8388608
  88.3 36.0 %copy-start.6 = (f32[512,768]{1,0:T(8,128)}, f32[512,768]{1,0:T(8,128)S(1)}, u32[]{:S(2)}) copy-start(f32[512,768]{1,0:T(8,128)S(1)} %get-tuple-element.55) | copy-start | bytes 4718596
  88.7 35.7 %copy-start.34 = (f32[512]{0:T(512)}, f32[512]{0:T(512)S(1)}, u32[]{:S(2)}) copy-start(f32[512]{0:T(512)S(1)} %add_rsqrt_fusion.1) | copy-start | bytes 6148
  88.7 20.3 %copy-start.41 = (f32[768]{0:T(1024)S(1)}, f32[768]{0:T(1024)}, u32[]{:S(2)}) copy-start(f32[768]{0:T(1024)} %convert_element_type.251) | copy-start | bytes 9220
  88.7 20.3 %slice-start.1 = ((s8[4718592]{0:T(1024)(128)(4,1)}), s8[524288]{0:T(1024)(128)(4,1)S(1)}, s32[]{:S(2)}) async-start(s8[4718592]{0:T(1024)(128)(4,1)} %bitcast.194), calls=%async_computation.38 | async-start | bytes 1048576
  108.9 2.9 copy-start.8
  115.5 8.8 copy-start.4
  115.5 8.8 copy-start.30
  124.3 8.3 copy-start.47
  124.3 8.3 copy-start.5
  132.6 2.5 copy-start.35
  134.3 3.8 copy-start.7
  162.9 3.5 copy-start.2
  171.1 1.0 copy-start.23
  171.2 78.6 %reduce-scatter.38.cloned.1.call-start = ((), (), s32[]{:S(2)}) async-start(), calls=%async_computation.20 | async-start | bytes 3932160 | tf_op jit(solution)/shard_map/reduce_scatter | solution.py:233
  186.0 128.4 %reduce-scatter.68.cloned.1.call-start = ((), (), s32[]{:S(2)}) async-start(), calls=%async_computation.35 | async-start | bytes 442368
  187.6 190.9 %reduce-scatter.52.cloned.1.call-start = ((), (), s32[]{:S(2)}) async-start(), calls=%async_computation.27 | async-start | bytes 442368
  195.3 247.4 %reduce-scatter.56.cloned.1.call-start = ((), (), s32[]{:S(2)}) async-start(), calls=%async_computation.29 | async-start | bytes 442368
  197.0 309.5 %reduce-scatter.58.cloned.1.call-start = ((), (), s32[]{:S(2)}) async-start(), calls=%async_computation.30 | async-start | bytes 442368
  198.7 371.5 %reduce-scatter.60.cloned.1.call-start = ((), (), s32[]{:S(2)}) async-start(), calls=%async_computation.31 | async-start | bytes 442368
  200.4 433.4 %reduce-scatter.64.cloned.1.call-start = ((), (), s32[]{:S(2)}) async-start(), calls=%async_computation.33 | async-start | bytes 442368
  202.0 495.4 %reduce-scatter.66.cloned.1.call-start = ((), (), s32[]{:S(2)}) async-start(), calls=%async_computation.34 | async-start | bytes 442368
  203.1 561.6 %reduce-scatter.62.cloned.1.call-start = ((), (), s32[]{:S(2)}) async-start(), calls=%async_computation.32 | async-start | bytes 1769472
  205.5 630.8 %reduce-scatter.46.cloned.1.call-start = ((), (), s32[]{:S(2)}) async-start(), calls=%async_computation.24 | async-start | bytes 2654208 | tf_op jit(solution)/shard_map/reduce_scatter | solution.py:261
  209.3 698.9 %reduce-scatter.40.cloned.1.call-start = ((), (), s32[]{:S(2)}) async-start(), calls=%async_computation.21 | async-start | bytes 2654208 | tf_op jit(solution)/shard_map/reduce_scatter | solution.py:256
  210.8 3.7 copy-start.16
  214.2 766.0 %reduce-scatter.42.cloned.1.call-start = ((), (), s32[]{:S(2)}) async-start(), calls=%async_computation.22 | async-start | bytes 2654208 | tf_op jit(solution)/shard_map/reduce_scatter | solution.py:258
  217.9 35.3 %copy-start.31 = (f32[768]{0:T(1024)S(1)}, f32[768]{0:T(1024)}, u32[]{:S(2)}) copy-start(f32[768]{0:T(1024)} %copy-done.29) | copy-start | bytes 9220
  217.9 35.3 %copy-start.36 = (f32[512]{0:T(512)S(1)}, f32[512]{0:T(512)}, u32[]{:S(2)}) copy-start(f32[512]{0:T(512)} %copy-done.34) | copy-start | bytes 6148
  218.0 35.3 %copy-start.40 = (f32[768]{0:T(1024)S(1)}, f32[768]{0:T(1024)}, u32[]{:S(2)}) copy-start(f32[768]{0:T(1024)} %convert_element_type.247) | copy-start | bytes 9220
  218.0 834.1 %reduce-scatter.44.cloned.1.call-start = ((), (), s32[]{:S(2)}) async-start(), calls=%async_computation.23 | async-start | bytes 2654208 | tf_op jit(solution)/shard_map/reduce_scatter | solution.py:259
  253.2 965.3 %reduce-scatter.48.cloned.1.call-start = ((), (), s32[]{:S(2)}) async-start(), calls=%async_computation.25 | async-start | bytes 10616832 | tf_op jit(solution)/shard_map/reduce_scatter | solution.py:265
  262.1 1122.8 %reduce-scatter.50.cloned.1.call-start = ((), (), s32[]{:S(2)}) async-start(), calls=%async_computation.26 | async-start | bytes 10616832 | tf_op jit(solution)/shard_map/reduce_scatter | solution.py:267
  270.7 44.5 %copy-start.25 = (s32[4,128]{1,0:T(4,128)S(1)}, s32[4,128]{1,0:T(4,128)}, u32[]{:S(2)}) copy-start(s32[4,128]{1,0:T(4,128)} %copy-done.24) | copy-start | bytes 6148
  270.8 1178.3 %reduce-scatter.54.cloned.1.call-start = ((), (), s32[]{:S(2)}) async-start(), calls=%async_computation.28 | async-start | bytes 442368
  315.2 594.6 %copy-start.9 = (bf16[4,128,768]{2,1,0:T(8,128)(2,1)S(1)}, bf16[4,128,768]{2,1,0:T(8,128)(2,1)}, u32[]{:S(2)}) copy-start(bf16[4,128,768]{2,1,0:T(8,128)(2,1)} %reduce-scatter.38.cloned.1.call-done) | copy-start | bytes 2359300
  910.9 588.4 %all-reduce.4.cloned.1.call-start = ((), (), s32[]{:S(2)}) async-start(), calls=%async_computation.36 | async-start | bytes 3538944 | tf_op jit(solution)/shard_map/psum | solution.py:273
  1387.1 79.4 %copy-start.27 = (f32[4,8]{1,0:T(4,128)S(1)}, f32[4,8]{1,0:T(4,128)}, u32[]{:S(2)}) copy-start(f32[4,8]{1,0:T(4,128)} %copy-done.26) | copy-start | bytes 388
  1499.3 4.4 copy-start.20
  1499.3 5.1 copy-start.19
  1499.3 5.9 copy-start.18
  1499.3 6.6 copy-start.17
  (6 other events, 5.0 us)
Sparse Core Ops, SparseCore 0:
  10.8 31.2 all-gather.2
  44.2 28.5 all-gather.4
  171.3 37.9 reduce-scatter.35
  211.8 37.9 reduce-scatter.37
  252.9 61.3 reduce-scatter.67
  318.0 60.4 reduce-scatter.51
  382.3 60.3 reduce-scatter.55
  446.0 60.4 reduce-scatter.57
  509.8 60.3 reduce-scatter.59
  573.3 60.3 reduce-scatter.63
  637.0 60.4 reduce-scatter.65
  700.8 63.8 reduce-scatter.61
  768.6 67.6 reduce-scatter.45
  840.1 68.0 reduce-scatter.39
  911.9 68.2 reduce-scatter.41
  984.0 68.0 reduce-scatter.43
  1056.0 162.4 reduce-scatter.47
  1222.3 162.5 reduce-scatter.49
  1388.6 60.4 reduce-scatter.53
  1453.1 46.1 all-reduce.3
where the time goes:
time: 1520 us; the launch traced here: 1510 us
  waiting for transfers between devices  1230 us (81%)
  matrix products  137 us (9%)
  local copies, waits for them, and re-layouts  62 us (4%)
  other arithmetic  56.8 us (4%)
  between operations  15.4 us (1%)
    unnamed x29, waiting for transfers between devices  529 us
    reduce_scatter x1, waiting for transfers between devices, local(): lax.psum_scatter(grad_w_up, 'dp', scatter_dimension=1, tiled=True)  165 us
    reduce_scatter x1, waiting for transfers between devices, local(): lax.psum_scatter(grad_w_down, 'dp', scatter_dimension=1, tiled=True)  164 us
    reduce_scatter x1, waiting for transfers between devices, local(): lax.psum_scatter(grad_w_out, 'dp', scatter_dimension=1, tiled=True)  70.6 us
    reduce_scatter x1, waiting for transfers between devices, local(): lax.psum_scatter(grad_w_value, 'dp', scatter_dimension=1, tiled=True)  70.3 us
    reduce_scatter x1, waiting for transfers between devices, local(): lax.psum_scatter(grad_w_query, 'dp', scatter_dimension=1, tiled=True)  70.2 us
    reduce_scatter x1, waiting for transfers between devices, local(): lax.psum_scatter(grad_w_key, 'dp', scatter_dimension=1, tiled=True)  65.8 us
    psum x1, waiting for transfers between devices, local(): lax.psum(shares[0].astype(jnp.bfloat16), 'seq').astype(jnp.float32)  32 us
  transfers between devices with their start and end apart: 20, of which 19 were waited for; matrix products, arithmetic and copies ran while one was open for 9% of the time, Pallas kernels for 0%

commit v1 on v0

v1 whole, which is shorter than its diff:
```python
import functools

import jax
import jax.numpy as jnp
from jax import lax
from jax.experimental import pallas as pl
from jax.experimental.pallas import tpu as pltpu
from jax.sharding import PartitionSpec as P

HD = 64
SEGS = 8
BF = jnp.bfloat16
F32 = jnp.float32
EPS = 1e-06
NEG = -1e30
LANES = 128
VMEM_BYTES = 56 * 1024 * 1024

PART = 16


def nn(a, b):
    return jnp.dot(a, b, preferred_element_type=F32)


def nt(a, b):
    return lax.dot_general(a, b, (((1,), (1,)), ((), ())), preferred_element_type=F32)


def three_parts(v):
    hi = v.astype(BF)
    rest = v - hi.astype(F32)
    mid = rest.astype(BF)
    low = (rest - mid.astype(F32)).astype(BF)
    return hi, mid, low


def two_parts(v):
    hi = v.astype(BF)
    return hi, (v - hi.astype(F32)).astype(BF)


def norm(value):
    centre = value - jnp.mean(value, axis=-1, keepdims=True)
    inverse = lax.rsqrt(jnp.mean(centre * centre, axis=-1, keepdims=True) + EPS)
    return centre * inverse, inverse


def norm_back(grad, normed, inverse):
    a = jnp.mean(grad, axis=-1, keepdims=True)
    b = jnp.mean(grad * normed, axis=-1, keepdims=True)
    return (grad - a - normed * b) * inverse


def gelu_both(x):
    z = jnp.abs(x) * (0.5**0.5)
    e = jnp.exp(-z * z)
    t = 1.0 / (1.0 + 0.3275911 * z)
    poly = t * (
        0.254829592
        + t * (-0.284496736 + t * (1.421413741 + t * (-1.453152027 + t * 1.061405429)))
    )
    tail = 0.5 * poly * e
    phi = jnp.where(x >= 0, 1.0 - tail, tail)
    return x * phi, phi + x * e * 0.3989422804014327


def head_lane(h):
    lane = lax.broadcasted_iota(jnp.int32, (1, LANES), 1)
    return (lane % PART == h) & (lane >= PART) & (lane < 4 * PART)


def put_shards(res, out_ref, info, lay, cols, first=0):
    n, rs, ra, hb = lay
    for j in range(n):
        pj = info[j]
        base = j * rs
        out_ref[pj, pl.ds(first, ra), cols] = res[base : base + ra].astype(BF)
        for a in range(2 if hb else 0):
            yrow = first + ra + jnp.where(info[9] == a, 0, hb)
            at = base + ra + a * hb
            out_ref[pj, pl.ds(pl.multiple_of(yrow, 16), hb), cols] = res[at : at + hb].astype(BF)


def split_kernel(info, x_ref, g_ref, *outs):
    me = info[10]
    for r in range(4):
        outs[r][...] = x_ref[me ^ r]
        outs[4 + r][...] = g_ref[me ^ r]


def join_kernel(info, *refs):
    me = info[10]
    out = refs[-1]
    for r in range(4):
        out[me ^ r] = refs[r][...]


def attend_kernel(
    x0, x1, x2, x3, oh_ref, ka_ref, wq, bq, wk, wv, bv, wo, bo,
    x_out, q_out, k_out, v_out, att_out, n1_out, inv_out, qa_out, stat,
):
    n = x0.shape[0]
    for r, ref in enumerate((x0, x1, x2, x3)):
        x_out[r * n : (r + 1) * n] = ref[...]
    x = x_out[...]
    q_out[...] = ((nn(x, wq[...]) + bq[...]).astype(BF).astype(F32) * (HD**-0.5)).astype(BF)
    k_out[...] = nn(x, wk[...]).astype(BF)
    v_out[...] = (nn(x, wv[...]) + bv[...]).astype(BF)
    tok, width = x.shape
    stat[...] = jnp.zeros_like(stat)
    ones = jnp.ones((16, tok), BF)

    def pair(p, carry):
        sl = pl.ds(pl.multiple_of(p * LANES, LANES), LANES)
        qcat = jnp.concatenate([q_out[:, sl], oh_ref[...]], axis=1)
        kp = k_out[:, sl]
        vt = v_out[:, sl].T
        lane = lax.broadcasted_iota(jnp.int32, (1, LANES), 1)
        parts = []
        for h in range(2):
            kh = jnp.where((lane < HD) == (h == 0), kp, jnp.zeros_like(kp))
            st = nt(jnp.concatenate([kh, ka_ref[...]], axis=1), qcat)
            m = jnp.max(st, axis=0, keepdims=True)
            pb = jnp.exp(st - m).astype(BF)
            ot = nn(jnp.concatenate([vt[h * HD : (h + 1) * HD], ones], axis=0), pb)
            total = ot[HD : HD + 1]
            stat[pl.ds(2 * p + h, 1), :] = m + jnp.log(total)
            parts.append(ot[:HD] / total)
        att_out[:, sl] = jnp.concatenate(parts, axis=0).T
        return carry

    lax.fori_loop(0, width // LANES, pair, 0)
    hi, mid, low = three_parts(stat[...])
    zero = jnp.zeros((PART, tok), BF)
    qa_out[...] = jnp.concatenate([zero, hi, mid, low, zero, zero, zero, zero], axis=0).T + oh_ref[...]
    mixed = nn(att_out[...].astype(BF), wo[...]) + bo[...]
    n1, inv = norm(x.astype(F32) + mixed)
    n1_out[...] = n1
    inv_out[...] = jnp.broadcast_to(inv, inv_out.shape)


def ffn_kernel(
    lay, info, n1_ref, ga, sa, wu, bu, wd, bd, gf, sf, g0, g1, g2, g3, oh_ref, oht_ref, gpl,
    o0, o1, o2, o3, pool_out, r2_out, gp_out, vec_out, send, keep,
    hl, acc, act, gt,
):
    t = pl.program_id(0)
    tile = wu.shape[1]
    n = g0.shape[0]

    @pl.when(t == 0)
    def _():
        hl[...] = (n1_ref[...] * ga[...] + sa[...]).astype(BF)
        acc[...] = jnp.zeros_like(acc)

    for r in range(4):
        rows = pl.ds(r * n, n)
        pre = nn(hl[rows, :], wu[...]) + bu[...]
        a, d = gelu_both(pre)
        ab = a.astype(BF)
        act[rows, pl.ds(pl.multiple_of(t * tile, tile), tile)] = ab
        gp_out[rows, :] = d.astype(BF)
        acc[rows, :] += nn(ab, wd[...])

    @pl.when(t == pl.num_programs(0) - 1)
    def _():
        width = acc.shape[1]
        gain = jnp.zeros((1, width), F32)
        shift = jnp.zeros((1, width), F32)
        bias = jnp.zeros((1, width), F32)
        pool = jnp.zeros(pool_out.shape, F32)
        for r, (o, g) in enumerate(((o0, g0), (o1, g1), (o2, g2), (o3, g3))):
            rows = pl.ds(r * n, n)
            hidden = n1_ref[rows, :] * ga[...] + sa[...]
            n2, inv = norm(hidden + (acc[rows, :] + bd[...]))
            result = n2 * gf[...] + sf[...]
            o[...] = result.astype(BF)
            hi, low = two_parts(result)
            oht = oht_ref[:, r * n : (r + 1) * n]
            pool += nn(oht, hi) + nn(oht, low)
            oh = oh_ref[rows, :]
            gout = g[...].astype(F32) + nn(jnp.concatenate([oh, oh], axis=1), gpl[...])
            gain += jnp.sum(gout * n2, axis=0, keepdims=True)
            shift += jnp.sum(gout, axis=0, keepdims=True)
            gr2 = norm_back(gout * gf[...], n2, inv)
            r2_out[rows, :] = gr2
            low_g = gr2.astype(BF)
            bias += jnp.sum(low_g.astype(F32), axis=0, keepdims=True)
            gt[:, r * n : (r + 1) * n] = low_g.T
        pool_out[...] = pool
        vec_out[...] = jnp.concatenate([bias, gain, shift, jnp.zeros((5, width), F32)], axis=0)
        half = act.shape[1] // 2
        step = 256

        def piece(i, carry):
            for rc, ref in ((1, send), (0, keep)):
                at = (info[8] ^ rc) * half + i * step
                res = nn(gt[...], act[:, pl.ds(pl.multiple_of(at, step), step)])
                put_shards(res, ref, info, lay, pl.ds(pl.multiple_of(i * step, step), step))
            return carry

        lax.fori_loop(0, half // step, piece, 0)


def ffn_back_kernel(
    lay_up, lay_out, info, r2_ref, gp, wd, wu, n1_ref, inv_ref, ga, sa, wo, att,
    send, keep, bup_out, r1_out, gatt_out, gaug_out, vec_out, osend, okeep,
    gl, hlt, acc, gt,
):
    t = pl.program_id(0)
    width = acc.shape[1]
    half = width // 2

    @pl.when(t == 0)
    def _():
        gl[...] = r2_ref[...].astype(BF)
        hlt[...] = (n1_ref[...] * ga[...] + sa[...]).astype(BF).T
        acc[...] = r2_ref[...]

    gpre = (nt(gl[...], wd[...]) * gp[...].astype(F32)).astype(BF)
    bup_out[...] = jnp.broadcast_to(
        jnp.sum(gpre.astype(F32), axis=0, keepdims=True), bup_out.shape
    )
    acc[...] += nt(gpre, wu[...])
    ra, hb = lay_up
    for rc, ref in ((1, send), (0, keep)):
        at = pl.multiple_of((info[8] ^ rc) * half, half)
        res = nn(hlt[pl.ds(at, half), :], gpre).astype(BF)
        ref[0, :ra, :] = res[:ra]
        for a in range(2 if hb else 0):
            yrow = ra + jnp.where(info[9] == a, 0, hb)
            ref[0, pl.ds(pl.multiple_of(yrow, 16), hb), :] = res[ra + a * hb : ra + (a + 1) * hb]

    @pl.when(t == pl.num_programs(0) - 1)
    def _():
        n = acc.shape[0] // 4
        gain = jnp.zeros((1, width), F32)
        shift = jnp.zeros((1, width), F32)
        bias = jnp.zeros((1, width), F32)
        row = lax.broadcasted_iota(jnp.int32, (width, LANES), 0) // HD
        lane = lax.broadcasted_iota(jnp.int32, (width, LANES), 1)
        pick = ((lane % PART == row) & (lane >= PART) & (lane < 4 * PART)).astype(BF)
        lane1 = lax.broadcasted_iota(jnp.int32, (1, LANES), 1)
        for r in range(4):
            rows = pl.ds(r * n, n)
            gh = acc[rows, :]
            n1 = n1_ref[rows, :]
            gain += jnp.sum(gh * n1, axis=0, keepdims=True)
            shift += jnp.sum(gh, axis=0, keepdims=True)
            gr1 = norm_back(gh * ga[...], n1, inv_ref[rows, :1])
            r1_out[rows, :] = gr1
            gm = gr1.astype(BF)
            bias += jnp.sum(gm.astype(F32), axis=0, keepdims=True)
            gt[:, r * n : (r + 1) * n] = gm.T
            gatt = nt(gm, wo[...]).astype(BF)
            gatt_out[rows, :] = gatt
            a, b, c = three_parts(gatt.astype(F32) * att[rows, :])
            delta = nn(a, pick) + nn(b, pick) + nn(c, pick)
            a, b, c = three_parts(delta)
            gaug_out[rows, :] = jnp.where(lane1 < 2 * PART, a, jnp.where(lane1 < 3 * PART, b, c))
        vec_out[...] = jnp.concatenate([bias, gain, shift, jnp.zeros((5, width), F32)], axis=0)
        step = 128

        def piece(i, carry):
            for rc, ref in ((1, osend), (0, okeep)):
                at = (info[8] ^ rc) * half + i * step
                right = att[:, pl.ds(pl.multiple_of(at, step), step)].astype(BF)
                res = nn(gt[...], right)
                put_shards(res, ref, info, lay_out, pl.ds(pl.multiple_of(i * step, step), step))
            return carry

        lax.fori_loop(0, half // step, piece, 0)


def attend_back_kernel(
    lay, info, q, k, v, g, qa, ka, ga, x_ref, vecs, bups,
    gq_out, gk_out, gv_out, send, keep, vec_out,
    gqt, gkt, gvt,
):
    width = q.shape[1]
    tok = q.shape[0]

    def pair(p, carry):
        sl = pl.ds(pl.multiple_of(p * LANES, LANES), LANES)
        qp, kp, vp, gp = q[:, sl], k[:, sl], v[:, sl], g[:, sl]
        qcat = jnp.concatenate([qp, qa[...]], axis=1)
        gcat = jnp.concatenate([gp, ga[...]], axis=1)
        kt = kp.T
        lane = lax.broadcasted_iota(jnp.int32, (1, LANES), 1)
        gk = jnp.zeros((tok, LANES), F32)
        gv = jnp.zeros((tok, LANES), F32)
        parts = []
        zero = jnp.zeros_like(kp)
        for h in range(2):
            mine = (lane < HD) == (h == 0)
            pick = head_lane(2 * p + h)
            kaug = jnp.where(pick, -jnp.ones((), BF), ka[...])
            vaug = jnp.where(pick, -jnp.ones((), BF), jnp.zeros((tok, LANES), BF))
            prob = jnp.exp(nt(jnp.concatenate([jnp.where(mine, kp, zero), kaug], axis=1), qcat))
            dp = nt(jnp.concatenate([jnp.where(mine, vp, zero), vaug], axis=1), gcat)
            ds = (prob * dp).astype(BF)
            gv += nn(prob.astype(BF), jnp.where(mine, gp, zero))
            gk += nn(ds, jnp.where(mine, qp, zero))
            parts.append(nn(kt[h * HD : (h + 1) * HD], ds))
        gqp = (jnp.concatenate(parts, axis=0) * (HD**-0.5)).astype(BF)
        gqt[sl, :] = gqp
        gq_out[:, sl] = gqp.T
        gkb, gvb = gk.astype(BF), gv.astype(BF)
        gk_out[:, sl] = gkb
        gv_out[:, sl] = gvb
        gkt[sl, :] = gkb.T
        gvt[sl, :] = gvb.T
        return carry

    lax.fori_loop(0, width // LANES, pair, 0)
    bq = jnp.sum(gq_out[...].astype(F32), axis=0, keepdims=True)
    bv = jnp.sum(gv_out[...].astype(F32), axis=0, keepdims=True)
    allv = jnp.concatenate([bq, bv, vecs[...]], axis=0)
    vec_out[...] = allv
    half = width // 2
    n, rs, ra, hb = lay
    rows_a = 3 * ra + 16
    if n > 1:
        lanes = rs
        for j in range(n):
            bup = bups[:, j * 4 * lanes : (j + 1) * 4 * lanes]
            block = jnp.concatenate(
                [allv[:8, j * lanes : (j + 1) * lanes]]
                + [bup[:, c * lanes : (c + 1) * lanes] for c in range(4)]
                + [jnp.zeros((4, lanes), F32)],
                axis=0,
            )
            block = jnp.concatenate([block, jnp.zeros((16, half - lanes), F32)], axis=1)
            pj = info[j]
            first = jnp.where(info[8] == 0, 1.0, 0.0)
            keep[pj, 3 * ra : rows_a, :] = (block * first).astype(BF)
            send[pj, 3 * ra : rows_a, :] = (block * (1.0 - first)).astype(BF)
    step = 128

    def piece(i, carry):
        cols = pl.ds(pl.multiple_of(i * step, step), step)
        for rc, ref in ((1, send), (0, keep)):
            at = (info[8] ^ rc) * half + i * step
            right = x_ref[:, pl.ds(pl.multiple_of(at, step), step)]
            for w, left in enumerate((gqt, gkt, gvt)):
                res = nn(left[...], right)
                for j in range(n):
                    pj = info[j]
                    base = j * rs
                    ref[pj, pl.ds(w * ra, ra), cols] = res[base : base + ra].astype(BF)
                    for a in range(2 if hb else 0):
                        yrow = rows_a + jnp.where(info[9] == a, 0, 3 * hb) + w * hb
                        s = base + ra + a * hb
                        ref[pj, pl.ds(pl.multiple_of(yrow, 16), hb), cols] = res[s : s + hb].astype(BF)
        return carry

    lax.fori_loop(0, half // step, piece, 0)


def input_kernel(r1, gq, gk, gv, wq, wk, wv, o0, o1, o2, o3):
    n = o0.shape[0]
    for r, o in enumerate((o0, o1, o2, o3)):
        rows = pl.ds(r * n, n)
        o[...] = (
            r1[rows, :]
            + nt(gq[rows, :], wq[...])
            + nt(gk[rows, :], wk[...])
            + nt(gv[rows, :], wv[...])
        ).astype(BF)


WHOLE = pl.BlockSpec(memory_space=pltpu.VMEM)
SCALARS = pl.BlockSpec(memory_space=pltpu.SMEM)


def shape(dims, dtype=BF):
    return jax.ShapeDtypeStruct(tuple(dims), dtype)


def params():
    return pltpu.CompilerParams(vmem_limit_bytes=VMEM_BYTES)


def call(kernel, outs, args, scalars=(), scratch=(), name=None, flops=0, nbytes=0):
    ins = [SCALARS if i in scalars else WHOLE for i in range(len(args))]
    return pl.pallas_call(
        kernel,
        out_shape=outs,
        in_specs=ins,
        out_specs=jax.tree.map(lambda _: WHOLE, outs),
        scratch_shapes=list(scratch),
        compiler_params=params(),
        cost_estimate=pl.CostEstimate(flops=flops, bytes_accessed=nbytes, transcendentals=0),
        name=name,
    )(*args)


def relative(x, axis_pairs):
    return lax.ppermute(x, "seq", axis_pairs)


def add(a, b):
    return (a.astype(F32) + b.astype(F32)).astype(BF)


def local(n_dp, n_seq, *args):
    (
        tokens, seg_lengths, w_query, b_query, w_key, w_value, b_value, w_out, b_out,
        gain_attn, shift_attn, w_up, b_up, w_down, b_down, gain_ffn, shift_ffn,
        grad_output, grad_pooled,
    ) = args
    me = lax.axis_index("seq")
    dp = lax.axis_index("dp")
    core, y = me % 2, me // 2
    rows, piece, width = tokens.shape
    tok = n_seq * piece
    ff = w_up.shape[1]
    fast = n_dp == 8
    n = n_dp if fast else 1
    rs = width // n
    half = width // 2
    xor = [[(i, i ^ r) for i in range(n_seq)] for r in range(n_seq)]

    if fast:
        j = jnp.arange(8, dtype=jnp.int32)
        pos = ((j % 2) ^ (dp % 2)) * 4 + ((j // 2) - (dp // 2)) % 4
    else:
        pos = jnp.zeros((8,), jnp.int32)
    info = jnp.concatenate([pos, jnp.stack([core, y, me]), jnp.zeros((5,), jnp.int32)]).astype(jnp.int32)

    pieces = call(
        split_kernel, [shape((piece, width))] * 8, (info, tokens, grad_output), scalars=(0,), name="split"
    )
    xs = [pieces[0]] + [lax.ppermute(pieces[r], "seq", xor[r]) for r in range(1, 4)]
    gs = [pieces[4]] + [lax.ppermute(pieces[4 + r], "seq", xor[r]) for r in range(1, 4)]

    lengths = lax.dynamic_index_in_dim(seg_lengths, me, 0, keepdims=False)
    ends = jnp.cumsum(lengths)
    order = me ^ jnp.arange(n_seq, dtype=jnp.int32)
    places = (order[:, None] * piece + jnp.arange(piece, dtype=jnp.int32)[None, :]).reshape(tok)
    seg = jnp.sum((places[:, None] >= ends[None, :]).astype(jnp.int32), axis=1)
    lane = jnp.arange(LANES, dtype=jnp.int32)
    hot = seg[:, None] == lane[None, :]
    onehot = hot.astype(BF)
    kaug = jnp.where((lane < SEGS)[None, :] & ~hot, NEG, 0.0).astype(BF)
    onehot_t = (seg[None, :] == jnp.arange(16, dtype=jnp.int32)[:, None]).astype(BF)
    length_col = lengths.astype(F32)[:, None]
    gpool = lax.dynamic_index_in_dim(grad_pooled, me, 0, keepdims=False).astype(F32) / length_col
    gp_hi = gpool.astype(BF)
    gp_low = (gpool - gp_hi.astype(F32)).astype(BF)
    zeros = jnp.zeros((LANES - SEGS, width), BF)
    gpl = jnp.concatenate([gp_hi, zeros, gp_low, zeros], axis=0)

    def vec(v):
        return v.astype(F32).reshape(1, -1)

    sq = shape((tok, width))
    sqf = shape((tok, width), F32)
    x, q, k, v, att, n1, inv, qaug = call(
        attend_kernel,
        [sq, sq, sq, sq, sqf, sqf, shape((tok, LANES), F32), shape((tok, LANES))],
        (*xs, onehot, kaug, w_query, vec(b_query), w_key, w_value, vec(b_value), w_out, vec(b_out)),
        scratch=[pltpu.VMEM((PART, tok), F32)],
        name="attend",
    )

    ra_d, hb_d = (64, 16) if fast else (width, 0)
    lay_d = (n, rs, ra_d, hb_d)
    rows_d = ra_d + 2 * hb_d
    tile = 768
    const = lambda *_: (0, 0)
    full = lambda a, b: pl.BlockSpec((a, b), const)
    vspec = full(1, width)
    pspec = full(piece, width)
    half_ff = ff // 2
    wire_d = shape((n, rows_d, half_ff))
    wire_spec = lambda dims: pl.BlockSpec(dims, lambda *_: (0,) * len(dims))
    *outs, pool, r2, gp, vec_b, d_send, d_keep = pl.pallas_call(
        functools.partial(ffn_kernel, lay_d),
        grid_spec=pltpu.PrefetchScalarGridSpec(
            num_scalar_prefetch=1,
            grid=(ff // tile,),
            in_specs=[
                full(tok, width), vspec, vspec,
                pl.BlockSpec((width, tile), lambda t, s: (0, t)),
                pl.BlockSpec((1, tile), lambda t, s: (0, t)),
                pl.BlockSpec((tile, width), lambda t, s: (t, 0)),
                vspec, vspec, vspec, pspec, pspec, pspec, pspec,
                full(tok, LANES), full(16, tok), full(2 * LANES, width),
            ],
            out_specs=[
                pspec, pspec, pspec, pspec, full(16, width), full(tok, width),
                pl.BlockSpec((tok, tile), lambda t, s: (0, t)),
                full(8, width), wire_spec(wire_d.shape), wire_spec(wire_d.shape),
            ],
            scratch_shapes=[
                pltpu.VMEM((tok, width), BF), pltpu.VMEM((tok, width), F32),
                pltpu.VMEM((tok, ff), BF), pltpu.VMEM((width, tok), BF),
            ],
        ),
        out_shape=[shape((piece, width))] * 4
        + [shape((16, width), F32), sqf, shape((tok, ff)), shape((8, width), F32), wire_d, wire_d],
        compiler_params=params(),
        name="ffn",
    )(
        info, n1, vec(gain_attn), vec(shift_attn), w_up, vec(b_up), w_down, vec(b_down),
        vec(gain_ffn), vec(shift_ffn), *gs, onehot, onehot_t, gpl,
    )

    ra_u, hb_u = (256, 64) if fast else (half, 0)
    lay_o = lay_d
    tile = 384
    steps = ff // tile
    wire_u = shape((n, half, ff // n))
    wire_o = shape((n, rows_d, half))
    if fast:
        up_spec = pl.BlockSpec((1, half, tile), lambda t, s: (s[t], 0, 0))
    else:
        up_spec = pl.BlockSpec((1, half, tile), lambda t, s: (0, 0, t))
    u_send, u_keep, bup, r1, gatt, gaug, vec_c, o_send, o_keep = pl.pallas_call(
        functools.partial(ffn_back_kernel, (ra_u, hb_u), lay_o),
        grid_spec=pltpu.PrefetchScalarGridSpec(
            num_scalar_prefetch=1,
            grid=(steps,),
            in_specs=[
                full(tok, width),
                pl.BlockSpec((tok, tile), lambda t, s: (0, t)),
                pl.BlockSpec((tile, width), lambda t, s: (t, 0)),
                pl.BlockSpec((width, tile), lambda t, s: (0, t)),
                full(tok, width), full(tok, LANES), vspec, vspec, full(width, width), full(tok, width),
            ],
            out_specs=[
                up_spec, up_spec, pl.BlockSpec((8, tile), lambda t, s: (0, t)),
                full(tok, width), full(tok, width), full(tok, LANES), full(8, width),
                wire_spec(wire_o.shape), wire_spec(wire_o.shape),
            ],
            scratch_shapes=[
                pltpu.VMEM((tok, width), BF), pltpu.VMEM((width, tok), BF),
                pltpu.VMEM((tok, width), F32), pltpu.VMEM((width, tok), BF),
            ],
        ),
        out_shape=[
            wire_u, wire_u, shape((8, ff), F32), sqf, sq, shape((tok, LANES)), shape((8, width), F32),
            wire_o, wire_o,
        ],
        compiler_params=params(),
        name="ffn_back",
    )(info, r2, gp, w_down, w_up, n1, inv, vec(gain_attn), vec(shift_attn), w_out, att)

    rows_q = 3 * rs + 16
    wire_q = shape((n, rows_q, half))
    vecs = jnp.concatenate([vec_c[:3], vec_b[:3], jnp.zeros((8, width), F32)], axis=0)
    gq, gk, gv, q_send, q_keep, vec_all = call(
        functools.partial(attend_back_kernel, lay_d),
        [sq, sq, sq, wire_q, wire_q, shape((16, width), F32)],
        (info, q, k, v, gatt, qaug, kaug, gaug, x, vecs, bup[:1]),
        scalars=(0,),
        scratch=[pltpu.VMEM((width, tok), BF)] * 3,
        name="attend_back",
    )
    ins = call(
        input_kernel, [shape((piece, width))] * 4, (r1, gq, gk, gv, w_query, w_key, w_value), name="input"
    )

    def back(parts, name):
        got = [parts[0]] + [lax.ppermute(parts[r], "seq", xor[r]) for r in range(1, 4)]
        return call(join_kernel, shape((rows, piece, width)), (info, *got), scalars=(0,), name=name)

    output = back(outs, "join_out")
    grad_tokens = back(ins, "join_in")
    own = pool[:SEGS] / length_col
    got = [own] + [lax.ppermute(own, "seq", xor[r]) for r in range(1, 4)]
    pooled = call(
        join_kernel, shape((rows, SEGS, width), F32), (info, *got), scalars=(0,), name="join_pool"
    )

    if fast:
        def reduce_all(send, keep, ra, hb):
            pp_core = lambda a: lax.ppermute(a, "seq", xor[1])
            pp_y = lambda a: lax.ppermute(a, "seq", xor[2])
            pp_x = lambda a: lax.ppermute(a, "dp", [(i, i ^ 1) for i in range(8)])
            pp_z = lambda a: lax.ppermute(a, "dp", [(i, (i + 2) % 8) for i in range(8)])

            def along_z(got, own):
                moving = add(got[3], own[3])
                for s in (2, 1, 0):
                    moving = (
                        got[s].astype(F32) + own[s].astype(F32) + pp_z(moving).astype(F32)
                    ).astype(BF)
                return moving

            r = pp_core(send)
            a1 = add(r[4:, :ra], keep[4:, :ra])
            b1 = add(r[:, ra + hb :], keep[:, ra + hb :])
            ax, by = pp_x(a1), pp_y(b1)
            a0 = add(r[:4, :ra], keep[:4, :ra])
            b0 = add(r[:, ra : ra + hb], keep[:, ra : ra + hb])
            a = along_z(ax, a0)
            b1 = add(by[4:], b0[4:])
            bx = pp_x(b1)
            b = along_z(bx, add(by[:4], b0[:4]))
            a = add(a, pp_y(a))
            b2 = pp_y(b)
            mine = jnp.concatenate([a, jnp.where(y == 0, b, b2), jnp.where(y == 0, b2, b)], axis=0)
            other = pp_core(mine)
            return jnp.where(core == 0, mine, other), jnp.where(core == 0, other, mine)

        dl, dh = reduce_all(d_send, d_keep, ra_d, hb_d)
        ul, uh = reduce_all(u_send, u_keep, ra_u, hb_u)
        ol, oh = reduce_all(o_send, o_keep, ra_d, hb_d)
        ql, qh = reduce_all(q_send, q_keep, 3 * ra_d + 16, 3 * hb_d)
        g_down = jnp.concatenate([dl, dh], axis=1).astype(F32).T
        g_up = jnp.concatenate([ul, uh], axis=0).astype(F32)
        g_out = jnp.concatenate([ol, oh], axis=1).astype(F32).T
        qf = jnp.concatenate([ql, qh], axis=1)
        at_b = 3 * ra_d + 16
        g_qkv = []
        for w in range(3):
            part = [qf[w * ra_d : (w + 1) * ra_d]] + [
                qf[at_b + (3 * a + w) * hb_d : at_b + (3 * a + w + 1) * hb_d] for a in range(2)
            ]
            g_qkv.append(jnp.concatenate(part, axis=0).astype(F32).T)
        vs = ql[3 * ra_d : 3 * ra_d + 16, :rs].astype(F32)
        small = [vs[i] for i in range(8)] + [vs[8:12].reshape(-1)]
    else:
        def total(send, keep, dim):
            h = keep.astype(F32) + lax.ppermute(send, "seq", xor[1]).astype(F32)
            h = (h + lax.ppermute(h.astype(BF), "seq", xor[2]).astype(F32))
            return lax.psum_scatter(h, "dp", scatter_dimension=dim, tiled=True).astype(BF)

        def whole(send, keep, dim, along):
            mine = total(send, keep, dim)
            other = lax.ppermute(mine, "seq", xor[1])
            lo, hi = jnp.where(core == 0, mine, other), jnp.where(core == 0, other, mine)
            return jnp.concatenate([lo, hi], axis=along).astype(F32)

        g_down = whole(d_send[0], d_keep[0], 0, 1).T
        g_up = whole(u_send[0], u_keep[0], 1, 0)
        g_out = whole(o_send[0], o_keep[0], 0, 1).T
        g_qkv = [
            whole(q_send[0, w * width : (w + 1) * width], q_keep[0, w * width : (w + 1) * width], 0, 1).T
            for w in range(3)
        ]
        flat = lax.psum(jnp.concatenate([vec_all[:8].reshape(-1), bup[0]]), ("dp", "seq"))
        mine = width // n_dp
        small = [
            lax.dynamic_slice_in_dim(flat, i * width + dp * mine, mine) for i in range(8)
        ] + [lax.dynamic_slice_in_dim(flat, 8 * width + dp * 4 * mine, 4 * mine)]

    bq, bv, b_o, gain1, shift1, b_d, gain2, shift2, b_u = small
    return (
        output, pooled, grad_tokens, g_qkv[0], bq, g_qkv[1], g_qkv[2], bv, g_out, b_o, gain1, shift1,
        g_up, b_u, g_down, b_d, gain2, shift2,
    )


def solution(mesh):
    rows = P("dp", "seq", None)
    placed = (rows, P("dp", None)) + (P(),) * 15 + (rows, P("dp", None, None))
    col, one = P(None, "dp"), P("dp")
    return jax.shard_map(
        functools.partial(local, mesh.shape["dp"], mesh.shape["seq"]),
        mesh=mesh,
        in_specs=placed,
        out_specs=(
            rows, P("dp", None, None), rows, col, one, col, col, one, col, one, one, one,
            col, one, col, one, one, one,
        ),
        check_vma=False,
    )
```

time: 1520 us -> 303 us (0.20)
  waiting for transfers between devices: 1230 us -> 126 us
  matrix products: 137 us -> 0 us
  Pallas kernels: 0 us -> 98.7 us
  local copies, waits for them, and re-layouts: 62 us -> 11.3 us
  starting transfers between devices: 1.09 us -> 43 us
  other arithmetic: 56.8 us -> 22 us
    reduce_scatter x8 -> x0, waiting for transfers between devices: 638 us -> none  [the longest x1 165 us: local(): lax.psum_scatter(grad_w_up, 'dp', scatter_dimension=1, tiled=True)]
    unnamed x29 -> x0, waiting for transfers between devices: 529 us -> none
    dot_general x26 -> x0, matrix products: 137 us -> none  [the longest x6 31.1 us: inner(): lax.dot_general(left, right, (((0,), (0,)), ((), ())), preferred_element_...]
    ppermute x0 -> x67, waiting for transfers between devices: none -> 126 us  [the longest x24 75.5 us: reduce_all(): pp_z = lambda a: lax.ppermute(a, 'dp', [(i, (i + 2) % 8) for i in range(8)])]
    pallas_call x0 -> x9, Pallas kernels: none -> 98.7 us  [the longest x7 51.5 us: call(): pl.pallas_call(kernel, out_shape=outs, in_specs=ins, out_specs=jax.tree.m...]
    ppermute x0 -> x67, starting transfers between devices: none -> 43 us  [the longest x12 13.3 us: reduce_all(): pp_y = lambda a: lax.ppermute(a, 'seq', xor[2])]
    psum x1 -> x0, waiting for transfers between devices: 32 us -> none  [local(): lax.psum(shares[0].astype(jnp.bfloat16), 'seq').astype(jnp.float32)]
    all_gather x2 -> x0, waiting for transfers between devices: 31.1 us -> none  [the longest x1 15.7 us: local(): key_piece = lax.all_gather(keys, 'seq', axis=1, tiled=True)]
  transfers between devices with their start and end apart: 20 -> 67, of which waited for: 19 -> 39; matrix products, arithmetic and copies ran while one was open for 9% -> 10% of each run, Pallas kernels for 0% -> 16%
where the time goes in v1:
time: 303 us; the launch traced here: 302 us
  waiting for transfers between devices  126 us (42%)
  Pallas kernels  98.7 us (33%)
  starting transfers between devices  43 us (14%)
  other arithmetic  22 us (7%)
  local copies, waits for them, and re-layouts  11.3 us (4%)
    ppermute x24, waiting for transfers between devices, reduce_all(): pp_z = lambda a: lax.ppermute(a, 'dp', [(i, (i + 2) % 8) for i in range(8)])  75.5 us
    pallas_call x7, Pallas kernels, call(): pl.pallas_call(kernel, out_shape=outs, in_specs=ins, out_specs=jax.tree.m...  51.5 us
    pallas_call x1, Pallas kernels, local(): pl.pallas_call(functools.partial(ffn_back_kernel, (ra_u, hb_u), lay_o), g...  24 us
    pallas_call x1, Pallas kernels, local(): pl.pallas_call(functools.partial(ffn_kernel, lay_d), grid_spec=pltpu.Pref...  23.2 us
    ppermute x8, waiting for transfers between devices, reduce_all(): pp_x = lambda a: lax.ppermute(a, 'dp', [(i, i ^ 1) for i in range(8)])  21.6 us
    ppermute x12, waiting for transfers between devices, reduce_all(): pp_y = lambda a: lax.ppermute(a, 'seq', xor[2])  18.6 us
    ppermute x12, starting transfers between devices, reduce_all(): pp_y = lambda a: lax.ppermute(a, 'seq', xor[2])  13.3 us
    ppermute x8, starting transfers between devices, reduce_all(): pp_x = lambda a: lax.ppermute(a, 'dp', [(i, i ^ 1) for i in range(8)])  10.7 us
  transfers between devices with their start and end apart: 67, of which 39 were waited for; matrix products, arithmetic and copies ran while one was open for 10% of the time, Pallas kernels for 16%

profile of v1, /device:TPU:0, one launch (start us, length us, event | category | flops | bytes accessed | tf_op | source)
XLA Modules:
  0.0 302.1 jit_solution(12410896747864716367)
XLA Ops:
  1.4 2.6 split.1
  4.5 2.5 collective-permute-start.1
  7.3 1.9 collective-permute-start.4
  20.1 14.9 %attend.1 = (bf16[512,768]{1,0:T(8,128)(2,1)}, bf16[512,768]{1,0:T(8,128)(2,1)}, bf16[512,768]{1,0:T(8,128)(2,1)}, bf16[512,768]{1,0:T(8,128)(2,1)}, f32[512,768...) custom-call(bf16[128,768]{1,0:T(8,128)(2,1)} %get-tuple-element.62.x0, ...), custom_call_target="tpu_custom_call" | custom-call | tf_op jit(solution)/shard_map/attend/pallas_call | solution.py:387
  35.8 23.2 %ffn.1 = (bf16[128,768]{1,0:T(8,128)(2,1)}, bf16[128,768]{1,0:T(8,128)(2,1)}, bf16[128,768]{1,0:T(8,128)(2,1)}, bf16[128,768]{1,0:T(8,128)(2,1)}, f32[16,768]{1,...) custom-call(s32[16]{0:T(128)} %concatenate.42.info, ...), custom_call_target="tpu_custom_call" | custom-call | tf_op jit(solution)/shard_map/ffn/pallas_call | solution.py:479
  59.0 24.0 %ffn_back.1 = (bf16[8,384,384]{2,1,0:T(8,128)(2,1)}, bf16[8,384,384]{2,1,0:T(8,128)(2,1)}, f32[8,3072]{1,0:T(8,128)}, f32[512,768]{1,0:T(8,128)}, bf16[512,768]{...) custom-call(s32[16]{0:T(128)} %concatenate.42.info, ...), custom_call_target="tpu_custom_call" | custom-call | tf_op jit(solution)/shard_map/ffn_back/pallas_call | solution.py:521
  84.1 1.5 slice.408.bups
  86.3 19.6 %attend_back.1 = (bf16[512,768]{1,0:T(8,128)(2,1)}, bf16[512,768]{1,0:T(8,128)(2,1)}, bf16[512,768]{1,0:T(8,128)(2,1)}, bf16[8,304,384]{2,1,0:T(8,128)(2,1)}, bf...) custom-call(s32[16]{0:T(128)} %concatenate.42.info, bf16[512,768]{1,0:T(8,128)(2,1)} %get-tuple-element.81.q, ...), custom_call_target="tpu_custom_call" | custom-call | tf_op jit(solution)/shard_map/attend_back/pallas_call | solution.py:387
  105.9 8.5 %input.1 = (bf16[128,768]{1,0:T(8,128)(2,1)}, bf16[128,768]{1,0:T(8,128)(2,1)}, bf16[128,768]{1,0:T(8,128)(2,1)}, bf16[128,768]{1,0:T(8,128)(2,1)}) custom-call(f32[512,768]{1,0:T(8,128)} %get-tuple-element.80.r1, bf16[512,768]{1,0:T(8,128)(2,1)} %get-tuple-element.91.gq, bf16[512,768]{1,0:T(8,128)(2,1)} %get-tuple-element.92.gk, ...), custom_call_target="tpu_custom_call" | custom-call | tf_op jit(solution)/shard_map/input/pallas_call | solution.py:387
  114.8 1.7 collective-permute-start.34
  118.7 2.0 collective-permute-done.10.refs_2_
  120.7 1.7 collective-permute-start.13
  122.9 1.8 collective-permute-start.7
  124.8 3.9 %collective-permute-done.13.refs_2_ = bf16[128,768]{1,0:T(8,128)(2,1)S(1)} collective-permute-done((bf16[128,768]{1,0:T(8,128)(2,1)}, bf16[128,768]{1,0:T(8,128)(2,1)S(1)}, u32[]{:S(2)}, u32[]{:S(2)}) %collective-permute-start.13) | collective-permute-done | bytes 196640 | tf_op jit(solution)/shard_map/ppermute | solution.py:567
  128.6 1.8 collective-permute-start.35
  130.5 1.5 join_pool.1
  133.0 2.2 join_in.1
  135.7 1.4 collective-permute-done.7.refs_2_
  137.1 2.0 collective-permute-done.8.refs_3_
  139.7 2.3 join_out.1
  142.0 1.6 collective-permute-start.36
  143.8 1.5 collective-permute-start.29
  145.3 2.3 collective-permute-done.36
  147.7 3.5 %collective-permute-done.29 = bf16[4,64,384]{2,1,0:T(8,128)(2,1)S(1)} collective-permute-done((bf16[4,64,384]{2,1,0:T(8,128)(2,1)S(1)}, bf16[4,64,384]{2,1,0:T(8,128)(2,1)S(1)}, u32[]{:S(2)}, u32[]{:S(2)}) %collective-permute-start.29) | collective-permute-done | bytes 196640 | tf_op jit(solution)/shard_map/ppermute | solution.py:582
  151.2 1.6 collective-permute-start.30
  153.2 1.3 collective-permute-start.38
  154.4 2.8 collective-permute-done.30
  159.7 3.8 %collective-permute-done.31 = bf16[64,384]{1,0:T(8,128)(2,1)S(1)} collective-permute-done((bf16[64,384]{1,0:T(8,128)(2,1)S(1)}, bf16[64,384]{1,0:T(8,128)(2,1)S(1)}, u32[]{:S(2)}, u32[]{:S(2)}) %collective-permute-start.31) | collective-permute-done | bytes 49184 | tf_op jit(solution)/shard_map/ppermute | solution.py:583
  163.6 5.8 %collective-permute-done.32 = bf16[64,384]{1,0:T(8,128)(2,1)S(1)} collective-permute-done((bf16[64,384]{1,0:T(8,128)(2,1)S(1)}, bf16[64,384]{1,0:T(8,128)(2,1)S(1)}, u32[]{:S(2)}, u32[]{:S(2)}) %collective-permute-start.32) | collective-permute-done | bytes 49184 | tf_op jit(solution)/shard_map/ppermute | solution.py:583
  169.4 1.2 collective-permute-start.33
  170.7 1.2 add_convert_fusion.11
  172.8 1.4 collective-permute-done.33
  174.3 4.4 %collective-permute-done.21 = bf16[8,48,384]{2,1,0:T(8,128)(2,1)S(1)} collective-permute-done((bf16[8,48,384]{2,1,0:T(8,128)(2,1)S(1)}, bf16[8,48,384]{2,1,0:T(8,128)(2,1)S(1)}, u32[]{:S(2)}, u32[]{:S(2)}) %collective-permute-start.21) | collective-permute-done | bytes 294944 | tf_op jit(solution)/shard_map/ppermute | solution.py:581
  178.7 1.5 collective-permute-start.22
  181.0 3.4 %collective-permute-done.22 = bf16[4,48,384]{2,1,0:T(8,128)(2,1)S(1)} collective-permute-done((bf16[4,48,384]{2,1,0:T(8,128)(2,1)S(1)}, bf16[4,48,384]{2,1,0:T(8,128)(2,1)S(1)}, u32[]{:S(2)}, u32[]{:S(2)}) %collective-permute-start.22) | collective-permute-done | bytes 147488 | tf_op jit(solution)/shard_map/ppermute | solution.py:582
  184.5 1.7 add_convert_fusion.5
  186.3 1.5 collective-permute-start.16
  187.8 2.5 collective-permute-done.23
  190.8 1.5 collective-permute-start.55
  194.7 1.4 collective-permute-done.24
  196.4 5.5 %collective-permute-done.25 = bf16[48,384]{1,0:T(8,128)(2,1)S(1)} collective-permute-done((bf16[48,384]{1,0:T(8,128)(2,1)S(1)}, bf16[48,384]{1,0:T(8,128)(2,1)S(1)}, u32[]{:S(2)}, u32[]{:S(2)}) %collective-permute-start.25) | collective-permute-done | bytes 36896 | tf_op jit(solution)/shard_map/ppermute | solution.py:583
  204.7 5.4 %collective-permute-done.26 = bf16[48,384]{1,0:T(8,128)(2,1)S(1)} collective-permute-done((bf16[48,384]{1,0:T(8,128)(2,1)S(1)}, bf16[48,384]{1,0:T(8,128)(2,1)S(1)}, u32[]{:S(2)}, u32[]{:S(2)}) %collective-permute-start.26) | collective-permute-done | bytes 36896 | tf_op jit(solution)/shard_map/ppermute | solution.py:581
  210.1 8.1 %collective-permute-done.17 = bf16[208,384]{1,0:T(8,128)(2,1)S(1)} collective-permute-done((bf16[208,384]{1,0:T(8,128)(2,1)S(1)}, bf16[208,384]{1,0:T(8,128)(2,1)S(1)}, u32[]{:S(2)}, u32[]{:S(2)}) %collective-permute-start.17) | collective-permute-done | bytes 159776 | tf_op jit(solution)/shard_map/ppermute | solution.py:583
  218.5 1.5 collective-permute-start.61
  220.7 4.9 %collective-permute-done.18 = bf16[208,384]{1,0:T(8,128)(2,1)S(1)} collective-permute-done((bf16[208,384]{1,0:T(8,128)(2,1)S(1)}, bf16[208,384]{1,0:T(8,128)(2,1)S(1)}, u32[]{:S(2)}, u32[]{:S(2)}) %collective-permute-start.18) | collective-permute-done | bytes 159776 | tf_op jit(solution)/shard_map/ppermute | solution.py:583
  225.7 11.9 %collective-permute-done.61 = bf16[4,16,1536]{2,1,0:T(8,128)(2,1)S(1)} collective-permute-done((bf16[4,16,1536]{2,1,0:T(8,128)(2,1)S(1)}, bf16[4,16,1536]{2,1,0:T(8,128)(2,1)S(1)}, u32[]{:S(2)}, u32[]{:S(2)}) %collective-permute-start.61) | collective-permute-done | bytes 196640 | tf_op jit(solution)/shard_map/ppermute | solution.py:582
  237.8 2.0 collective-permute-done.48
  240.9 3.2 %collective-permute-done.62 = bf16[16,1536]{1,0:T(8,128)(2,1)S(1)} collective-permute-done((bf16[16,1536]{1,0:T(8,128)(2,1)S(1)}, bf16[16,1536]{1,0:T(8,128)(2,1)S(1)}, u32[]{:S(2)}, u32[]{:S(2)}) %collective-permute-start.62) | collective-permute-done | bytes 49184 | tf_op jit(solution)/shard_map/ppermute | solution.py:583
  244.2 1.5 collective-permute-done.49
  245.8 4.3 %collective-permute-done.63 = bf16[16,1536]{1,0:T(8,128)(2,1)S(1)} collective-permute-done((bf16[16,1536]{1,0:T(8,128)(2,1)S(1)}, bf16[16,1536]{1,0:T(8,128)(2,1)S(1)}, u32[]{:S(2)}, u32[]{:S(2)}) %collective-permute-start.63) | collective-permute-done | bytes 49184 | tf_op jit(solution)/shard_map/ppermute | solution.py:583
  250.2 1.5 collective-permute-done.50
  251.8 4.3 %collective-permute-done.64 = bf16[16,1536]{1,0:T(8,128)(2,1)S(1)} collective-permute-done((bf16[16,1536]{1,0:T(8,128)(2,1)S(1)}, bf16[16,1536]{1,0:T(8,128)(2,1)S(1)}, u32[]{:S(2)}, u32[]{:S(2)}) %collective-permute-start.64) | collective-permute-done | bytes 49184 | tf_op jit(solution)/shard_map/ppermute | solution.py:583
  258.8 1.4 collective-permute-done.65
  260.2 1.6 collective-permute-done.52
  262.1 8.0 %collective-permute-done.56 = bf16[64,1536]{1,0:T(8,128)(2,1)S(1)} collective-permute-done((bf16[64,1536]{1,0:T(8,128)(2,1)S(1)}, bf16[64,1536]{1,0:T(8,128)(2,1)S(1)}, u32[]{:S(2)}, u32[]{:S(2)}) %collective-permute-start.56) | collective-permute-done | bytes 196640 | tf_op jit(solution)/shard_map/ppermute | solution.py:583
  270.3 3.9 %collective-permute-done.43 = bf16[256,384]{1,0:T(8,128)(2,1)S(1)} collective-permute-done((bf16[256,384]{1,0:T(8,128)(2,1)S(1)}, bf16[256,384]{1,0:T(8,128)(2,1)S(1)}, u32[]{:S(2)}, u32[]{:S(2)}) %collective-permute-start.43) | collective-permute-done | bytes 196640 | tf_op jit(solution)/shard_map/ppermute | solution.py:583
  276.4 1.5 convert_bitcast_fusion.4
  277.9 1.6 convert_bitcast_fusion.2
  281.2 3.6 %collective-permute-done.44 = bf16[256,384]{1,0:T(8,128)(2,1)} collective-permute-done((bf16[256,384]{1,0:T(8,128)(2,1)}, bf16[256,384]{1,0:T(8,128)(2,1)}, u32[]{:S(2)}, u32[]{:S(2)}) %collective-permute-start.44) | collective-permute-done | bytes 196640 | tf_op jit(solution)/shard_map/ppermute | solution.py:583
  285.9 2.7 collective-permute-done.58
  288.7 1.5 collective-permute-start.59
  290.2 3.1 %collective-permute-done.45 = bf16[256,384]{1,0:T(8,128)(2,1)S(1)} collective-permute-done((bf16[256,384]{1,0:T(8,128)(2,1)S(1)}, bf16[256,384]{1,0:T(8,128)(2,1)S(1)}, u32[]{:S(2)}, u32[]{:S(2)}) %collective-permute-start.45) | collective-permute-done | bytes 196640 | tf_op jit(solution)/shard_map/ppermute | solution.py:583
  293.4 1.2 collective-permute-start.46
  294.8 4.3 %collective-permute-done.46 = bf16[256,384]{1,0:T(8,128)(2,1)S(1)} collective-permute-done((bf16[256,384]{1,0:T(8,128)(2,1)S(1)}, bf16[256,384]{1,0:T(8,128)(2,1)S(1)}, u32[]{:S(2)}, u32[]{:S(2)}) %collective-permute-start.46) | collective-permute-done | bytes 196640 | tf_op jit(solution)/shard_map/ppermute | solution.py:581
  (253 shorter events, 44.9 us)
Async XLA Ops:
  4.0 14.7 %collective-permute-start = (bf16[128,768]{1,0:T(8,128)(2,1)}, bf16[128,768]{1,0:T(8,128)(2,1)S(1)}, u32[]{:S(2)}, u32[]{:S(2)}) collective-permute-start(bf16[128,768]{1,0:T(8,128)(2,1)} %get-tuple-element.63), channel_id=1, source_target_pairs={{0,1},{1,0},{2,3},{3,2},{4,5},{5,4},{6,7},{7,6},{8,9},{9,8},{10,11... | collective-permute-start | bytes 589832 | tf_op jit(solution)/shard_map/ppermute | solution.py:435
  4.5 14.9 %collective-permute-start.1 = (bf16[128,768]{1,0:T(8,128)(2,1)}, bf16[128,768]{1,0:T(8,128)(2,1)S(1)}, u32[]{:S(2)}, u32[]{:S(2)}) collective-permute-start(bf16[128,768]{1,0:T(8,128)(2,1)} %get-tuple-element.64), channel_id=1, source_target_pairs={{0,2},{1,3},{2,0},{3,1},{4,6},{5,7},{6,4},{7,5},{8,10},{9,11},{10,... | collective-permute-start | bytes 589832 | tf_op jit(solution)/shard_map/ppermute | solution.py:435
  7.0 12.3 %collective-permute-start.2 = (bf16[128,768]{1,0:T(8,128)(2,1)}, bf16[128,768]{1,0:T(8,128)(2,1)S(1)}, u32[]{:S(2)}, u32[]{:S(2)}) collective-permute-start(bf16[128,768]{1,0:T(8,128)(2,1)} %get-tuple-element.65), channel_id=1, source_target_pairs={{0,3},{1,2},{2,1},{3,0},{4,7},{5,6},{6,5},{7,4},{8,11},{9,10},{10,... | collective-permute-start | bytes 589832 | tf_op jit(solution)/shard_map/ppermute | solution.py:435
  7.2 27.9 %collective-permute-start.3 = (bf16[128,768]{1,0:T(8,128)(2,1)}, bf16[128,768]{1,0:T(8,128)(2,1)S(1)}, u32[]{:S(2)}, u32[]{:S(2)}) collective-permute-start(bf16[128,768]{1,0:T(8,128)(2,1)} %get-tuple-element.68), channel_id=1, source_target_pairs={{0,1},{1,0},{2,3},{3,2},{4,5},{5,4},{6,7},{7,6},{8,9},{9,8},{10,11... | collective-permute-start | bytes 589832 | tf_op jit(solution)/shard_map/ppermute | solution.py:436
  7.3 27.8 %collective-permute-start.4 = (bf16[128,768]{1,0:T(8,128)(2,1)}, bf16[128,768]{1,0:T(8,128)(2,1)S(1)}, u32[]{:S(2)}, u32[]{:S(2)}) collective-permute-start(bf16[128,768]{1,0:T(8,128)(2,1)} %get-tuple-element.69), channel_id=1, source_target_pairs={{0,2},{1,3},{2,0},{3,1},{4,6},{5,7},{6,4},{7,5},{8,10},{9,11},{10,... | collective-permute-start | bytes 589832 | tf_op jit(solution)/shard_map/ppermute | solution.py:436
  18.7 16.4 %collective-permute-start.5 = (bf16[128,768]{1,0:T(8,128)(2,1)}, bf16[128,768]{1,0:T(8,128)(2,1)S(1)}, u32[]{:S(2)}, u32[]{:S(2)}) collective-permute-start(bf16[128,768]{1,0:T(8,128)(2,1)} %get-tuple-element.70), channel_id=1, source_target_pairs={{0,3},{1,2},{2,1},{3,0},{4,7},{5,6},{6,5},{7,4},{8,11},{9,10},{10,... | collective-permute-start | bytes 589832 | tf_op jit(solution)/shard_map/ppermute | solution.py:436
  83.0 31.7 %collective-permute-start.28 = (bf16[8,96,384]{2,1,0:T(8,128)(2,1)}, bf16[8,96,384]{2,1,0:T(8,128)(2,1)S(1)}, u32[]{:S(2)}, u32[]{:S(2)}) collective-permute-start(bf16[8,96,384]{2,1,0:T(8,128)(2,1)} %get-tuple-element.100), channel_id=1, source_target_pairs={{0,1},{1,0},{2,3},{3,2},{4,5},{5,4},{6,7},{7,6},{8,9},{9,8},{10,11... | collective-permute-start | bytes 1769480 | tf_op jit(solution)/shard_map/ppermute | solution.py:580
  114.4 8.5 %collective-permute-start.12 = (bf16[128,768]{1,0:T(8,128)(2,1)}, bf16[128,768]{1,0:T(8,128)(2,1)S(1)}, u32[]{:S(2)}, u32[]{:S(2)}) collective-permute-start(bf16[128,768]{1,0:T(8,128)(2,1)} %get-tuple-element.95), channel_id=1, source_target_pairs={{0,1},{1,0},{2,3},{3,2},{4,5},{5,4},{6,7},{7,6},{8,9},{9,8},{10,11... | collective-permute-start | bytes 589832 | tf_op jit(solution)/shard_map/ppermute | solution.py:567
  114.8 9.9 %collective-permute-start.34 = (bf16[8,16,384]{2,1,0:T(8,128)(2,1)S(1)}, bf16[8,16,384]{2,1,0:T(8,128)(2,1)S(1)}, u32[]{:S(2)}, u32[]{:S(2)}) collective-permute-start(bf16[8,16,384]{2,1,0:T(8,128)(2,1)S(1)} %get-tuple-element.122), channel_id=1, source_target_pairs={{0,2},{1,3},{2,0},{3,1},{4,6},{5,7},{6,4},{7,5},{8,10},{9,11},{10,... | collective-permute-start | bytes 294920 | tf_op jit(solution)/shard_map/ppermute | solution.py:581
  116.5 4.2 %collective-permute-start.10 = (f32[8,768]{1,0:T(8,128)S(1)}, f32[8,768]{1,0:T(8,128)S(1)}, u32[]{:S(2)}, u32[]{:S(2)}) collective-permute-start(f32[8,768]{1,0:T(8,128)S(1)} %slice_divide_fusion.refs_0_), channel_id=1, source_target_pairs={{0,2},{1,3},{2,0},{3,1},{4,6},{5,7},{6,4},{7,5},{8,10},{9,11},{10,... | collective-permute-start | bytes 73736 | tf_op jit(solution)/shard_map/ppermute | solution.py:573
  117.0 5.5 %collective-permute-start.11 = (f32[8,768]{1,0:T(8,128)S(1)}, f32[8,768]{1,0:T(8,128)S(1)}, u32[]{:S(2)}, u32[]{:S(2)}) collective-permute-start(f32[8,768]{1,0:T(8,128)S(1)} %slice_divide_fusion.refs_0_), channel_id=1, source_target_pairs={{0,3},{1,2},{2,1},{3,0},{4,7},{5,6},{6,5},{7,4},{8,11},{9,10},{10,... | collective-permute-start | bytes 73736 | tf_op jit(solution)/shard_map/ppermute | solution.py:573
  118.1 4.3 %collective-permute-start.9 = (f32[8,768]{1,0:T(8,128)S(1)}, f32[8,768]{1,0:T(8,128)S(1)}, u32[]{:S(2)}, u32[]{:S(2)}) collective-permute-start(f32[8,768]{1,0:T(8,128)S(1)} %slice_divide_fusion.refs_0_), channel_id=1, source_target_pairs={{0,1},{1,0},{2,3},{3,2},{4,5},{5,4},{6,7},{7,6},{8,9},{9,8},{10,11... | collective-permute-start | bytes 73736 | tf_op jit(solution)/shard_map/ppermute | solution.py:573
  120.7 8.0 %collective-permute-start.13 = (bf16[128,768]{1,0:T(8,128)(2,1)}, bf16[128,768]{1,0:T(8,128)(2,1)S(1)}, u32[]{:S(2)}, u32[]{:S(2)}) collective-permute-start(bf16[128,768]{1,0:T(8,128)(2,1)} %get-tuple-element.96), channel_id=1, source_target_pairs={{0,2},{1,3},{2,0},{3,1},{4,6},{5,7},{6,4},{7,5},{8,10},{9,11},{10,... | collective-permute-start | bytes 589832 | tf_op jit(solution)/shard_map/ppermute | solution.py:567
  122.4 9.9 %collective-permute-start.14 = (bf16[128,768]{1,0:T(8,128)(2,1)}, bf16[128,768]{1,0:T(8,128)(2,1)S(1)}, u32[]{:S(2)}, u32[]{:S(2)}) collective-permute-start(bf16[128,768]{1,0:T(8,128)(2,1)} %get-tuple-element.97), channel_id=1, source_target_pairs={{0,3},{1,2},{2,1},{3,0},{4,7},{5,6},{6,5},{7,4},{8,11},{9,10},{10,... | collective-permute-start | bytes 589832 | tf_op jit(solution)/shard_map/ppermute | solution.py:567
  122.5 12.7 %collective-permute-start.6 = (bf16[128,768]{1,0:T(8,128)(2,1)S(1)}, bf16[128,768]{1,0:T(8,128)(2,1)S(1)}, u32[]{:S(2)}, u32[]{:S(2)}) collective-permute-start(bf16[128,768]{1,0:T(8,128)(2,1)S(1)} %copy-done.35), channel_id=1, source_target_pairs={{0,1},{1,0},{2,3},{3,2},{4,5},{5,4},{6,7},{7,6},{8,9},{9,8},{10,11... | collective-permute-start | bytes 589832 | tf_op jit(solution)/shard_map/ppermute | solution.py:567
  122.9 14.2 %collective-permute-start.7 = (bf16[128,768]{1,0:T(8,128)(2,1)S(1)}, bf16[128,768]{1,0:T(8,128)(2,1)S(1)}, u32[]{:S(2)}, u32[]{:S(2)}) collective-permute-start(bf16[128,768]{1,0:T(8,128)(2,1)S(1)} %copy-done.34), channel_id=1, source_target_pairs={{0,2},{1,3},{2,0},{3,1},{4,6},{5,7},{6,4},{7,5},{8,10},{9,11},{10,... | collective-permute-start | bytes 589832 | tf_op jit(solution)/shard_map/ppermute | solution.py:567
  124.7 14.3 %collective-permute-start.8 = (bf16[128,768]{1,0:T(8,128)(2,1)S(1)}, bf16[128,768]{1,0:T(8,128)(2,1)S(1)}, u32[]{:S(2)}, u32[]{:S(2)}) collective-permute-start(bf16[128,768]{1,0:T(8,128)(2,1)S(1)} %copy-done.33), channel_id=1, source_target_pairs={{0,3},{1,2},{2,1},{3,0},{4,7},{5,6},{6,5},{7,4},{8,11},{9,10},{10,... | collective-permute-start | bytes 589832 | tf_op jit(solution)/shard_map/ppermute | solution.py:567
  128.6 13.4 %collective-permute-start.35 = (bf16[4,16,384]{2,1,0:T(8,128)(2,1)S(1)}, bf16[4,16,384]{2,1,0:T(8,128)(2,1)S(1)}, u32[]{:S(2)}, u32[]{:S(2)}) collective-permute-start(bf16[4,16,384]{2,1,0:T(8,128)(2,1)S(1)} %get-tuple-element.144), channel_id=1, source_target_pairs={{0,4},{4,0},{8,12},{12,8},{16,20},{20,16},{24,28},{28,24},{1,5},{5... | collective-permute-start | bytes 147464 | tf_op jit(solution)/shard_map/ppermute | solution.py:582
  132.3 58.1 %collective-permute-start.54 = (bf16[8,96,1536]{2,1,0:T(8,128)(2,1)}, bf16[8,96,1536]{2,1,0:T(8,128)(2,1)S(1)}, u32[]{:S(2)}, u32[]{:S(2)}) collective-permute-start(bf16[8,96,1536]{2,1,0:T(8,128)(2,1)} %get-tuple-element.104), channel_id=1, source_target_pairs={{0,1},{1,0},{2,3},{3,2},{4,5},{5,4},{6,7},{7,6},{8,9},{9,8},{10,11... | collective-permute-start | bytes 7077896 | tf_op jit(solution)/shard_map/ppermute | solution.py:580
  135.2 58.5 %collective-permute-start.41 = (bf16[8,384,384]{2,1,0:T(8,128)(2,1)}, bf16[8,384,384]{2,1,0:T(8,128)(2,1)S(1)}, u32[]{:S(2)}, u32[]{:S(2)}) collective-permute-start(bf16[8,384,384]{2,1,0:T(8,128)(2,1)} %get-tuple-element.102), channel_id=1, source_target_pairs={{0,1},{1,0},{2,3},{3,2},{4,5},{5,4},{6,7},{7,6},{8,9},{9,8},{10,11... | collective-permute-start | bytes 7077896 | tf_op jit(solution)/shard_map/ppermute | solution.py:580
  137.1 33.6 %collective-permute-start.15 = (bf16[8,304,384]{2,1,0:T(8,128)(2,1)}, bf16[8,304,384]{2,1,0:T(8,128)(2,1)}, u32[]{:S(2)}, u32[]{:S(2)}) collective-permute-start(bf16[8,304,384]{2,1,0:T(8,128)(2,1)} %get-tuple-element.98), channel_id=1, source_target_pairs={{0,1},{1,0},{2,3},{3,2},{4,5},{5,4},{6,7},{7,6},{8,9},{9,8},{10,11... | collective-permute-start | bytes 5603336 | tf_op jit(solution)/shard_map/ppermute | solution.py:580
  142.0 5.6 %collective-permute-start.36 = (bf16[16,384]{1,0:T(8,128)(2,1)S(1)}, bf16[16,384]{1,0:T(8,128)(2,1)S(1)}, u32[]{:S(2)}, u32[]{:S(2)}) collective-permute-start(bf16[16,384]{1,0:T(8,128)(2,1)S(1)} %fusion.48), channel_id=1, source_target_pairs={{0,8},{4,12},{8,16},{12,20},{16,24},{20,28},{24,0},{28,4},{1,9},{5... | collective-permute-start | bytes 36872 | tf_op jit(solution)/shard_map/ppermute | solution.py:583
  143.8 7.4 %collective-permute-start.29 = (bf16[4,64,384]{2,1,0:T(8,128)(2,1)S(1)}, bf16[4,64,384]{2,1,0:T(8,128)(2,1)S(1)}, u32[]{:S(2)}, u32[]{:S(2)}) collective-permute-start(bf16[4,64,384]{2,1,0:T(8,128)(2,1)S(1)} %get-tuple-element.120), channel_id=1, source_target_pairs={{0,4},{4,0},{8,12},{12,8},{16,20},{20,16},{24,28},{28,24},{1,5},{5... | collective-permute-start | bytes 589832 | tf_op jit(solution)/shard_map/ppermute | solution.py:582
  147.6 5.5 %collective-permute-start.37 = (bf16[16,384]{1,0:T(8,128)(2,1)S(1)}, bf16[16,384]{1,0:T(8,128)(2,1)S(1)}, u32[]{:S(2)}, u32[]{:S(2)}) collective-permute-start(bf16[16,384]{1,0:T(8,128)(2,1)S(1)} %fusion.44), channel_id=1, source_target_pairs={{0,8},{4,12},{8,16},{12,20},{16,24},{20,28},{24,0},{28,4},{1,9},{5... | collective-permute-start | bytes 36872 | tf_op jit(solution)/shard_map/ppermute | solution.py:583
  151.2 6.1 %collective-permute-start.30 = (bf16[64,384]{1,0:T(8,128)(2,1)S(1)}, bf16[64,384]{1,0:T(8,128)(2,1)S(1)}, u32[]{:S(2)}, u32[]{:S(2)}) collective-permute-start(bf16[64,384]{1,0:T(8,128)(2,1)S(1)} %fusion.34), channel_id=1, source_target_pairs={{0,8},{4,12},{8,16},{12,20},{16,24},{20,28},{24,0},{28,4},{1,9},{5... | collective-permute-start | bytes 147464 | tf_op jit(solution)/shard_map/ppermute | solution.py:583
  153.2 5.5 %collective-permute-start.38 = (bf16[16,384]{1,0:T(8,128)(2,1)S(1)}, bf16[16,384]{1,0:T(8,128)(2,1)S(1)}, u32[]{:S(2)}, u32[]{:S(2)}) collective-permute-start(bf16[16,384]{1,0:T(8,128)(2,1)S(1)} %fusion.45), channel_id=1, source_target_pairs={{0,8},{4,12},{8,16},{12,20},{16,24},{20,28},{24,0},{28,4},{1,9},{5... | collective-permute-start | bytes 36872 | tf_op jit(solution)/shard_map/ppermute | solution.py:583
  157.3 6.2 %collective-permute-start.31 = (bf16[64,384]{1,0:T(8,128)(2,1)S(1)}, bf16[64,384]{1,0:T(8,128)(2,1)S(1)}, u32[]{:S(2)}, u32[]{:S(2)}) collective-permute-start(bf16[64,384]{1,0:T(8,128)(2,1)S(1)} %fusion.28), channel_id=1, source_target_pairs={{0,8},{4,12},{8,16},{12,20},{16,24},{20,28},{24,0},{28,4},{1,9},{5... | collective-permute-start | bytes 147464 | tf_op jit(solution)/shard_map/ppermute | solution.py:583
  158.7 4.8 %collective-permute-start.39 = (bf16[16,384]{1,0:T(8,128)(2,1)S(1)}, bf16[16,384]{1,0:T(8,128)(2,1)S(1)}, u32[]{:S(2)}, u32[]{:S(2)}) collective-permute-start(bf16[16,384]{1,0:T(8,128)(2,1)S(1)} %fusion.46), channel_id=1, source_target_pairs={{0,2},{1,3},{2,0},{3,1},{4,6},{5,7},{6,4},{7,5},{8,10},{9,11},{10,... | collective-permute-start | bytes 36872 | tf_op jit(solution)/shard_map/ppermute | solution.py:581
  163.5 5.9 %collective-permute-start.32 = (bf16[64,384]{1,0:T(8,128)(2,1)S(1)}, bf16[64,384]{1,0:T(8,128)(2,1)S(1)}, u32[]{:S(2)}, u32[]{:S(2)}) collective-permute-start(bf16[64,384]{1,0:T(8,128)(2,1)S(1)} %fusion.29), channel_id=1, source_target_pairs={{0,8},{4,12},{8,16},{12,20},{16,24},{20,28},{24,0},{28,4},{1,9},{5... | collective-permute-start | bytes 147464 | tf_op jit(solution)/shard_map/ppermute | solution.py:583
  169.4 4.7 %collective-permute-start.33 = (bf16[64,384]{1,0:T(8,128)(2,1)S(1)}, bf16[64,384]{1,0:T(8,128)(2,1)S(1)}, u32[]{:S(2)}, u32[]{:S(2)}) collective-permute-start(bf16[64,384]{1,0:T(8,128)(2,1)S(1)} %fusion.30), channel_id=1, source_target_pairs={{0,2},{1,3},{2,0},{3,1},{4,6},{5,7},{6,4},{7,5},{8,10},{9,11},{10,... | collective-permute-start | bytes 147464 | tf_op jit(solution)/shard_map/ppermute | solution.py:581
  171.9 6.8 %collective-permute-start.21 = (bf16[8,48,384]{2,1,0:T(8,128)(2,1)S(1)}, bf16[8,48,384]{2,1,0:T(8,128)(2,1)S(1)}, u32[]{:S(2)}, u32[]{:S(2)}) collective-permute-start(bf16[8,48,384]{2,1,0:T(8,128)(2,1)S(1)} %get-tuple-element.118), channel_id=1, source_target_pairs={{0,2},{1,3},{2,0},{3,1},{4,6},{5,7},{6,4},{7,5},{8,10},{9,11},{10,... | collective-permute-start | bytes 884744 | tf_op jit(solution)/shard_map/ppermute | solution.py:581
  174.2 6.1 %collective-permute-start.40 = (bf16[96,384]{1,0:T(8,128)(2,1)S(1)}, bf16[96,384]{1,0:T(8,128)(2,1)S(1)}, u32[]{:S(2)}, u32[]{:S(2)}) collective-permute-start(bf16[96,384]{1,0:T(8,128)(2,1)S(1)} %pad_maximum_fusion.4), channel_id=1, source_target_pairs={{0,1},{1,0},{2,3},{3,2},{4,5},{5,4},{6,7},{7,6},{8,9},{9,8},{10,11... | collective-permute-start | bytes 221192 | tf_op jit(solution)/shard_map/ppermute | solution.py:580
  178.7 5.7 %collective-permute-start.22 = (bf16[4,48,384]{2,1,0:T(8,128)(2,1)S(1)}, bf16[4,48,384]{2,1,0:T(8,128)(2,1)S(1)}, u32[]{:S(2)}, u32[]{:S(2)}) collective-permute-start(bf16[4,48,384]{2,1,0:T(8,128)(2,1)S(1)} %get-tuple-element.132), channel_id=1, source_target_pairs={{0,4},{4,0},{8,12},{12,8},{16,20},{20,16},{24,28},{28,24},{1,5},{5... | collective-permute-start | bytes 442376 | tf_op jit(solution)/shard_map/ppermute | solution.py:582
  184.5 5.8 %collective-permute-start.23 = (bf16[48,384]{1,0:T(8,128)(2,1)S(1)}, bf16[48,384]{1,0:T(8,128)(2,1)S(1)}, u32[]{:S(2)}, u32[]{:S(2)}) collective-permute-start(bf16[48,384]{1,0:T(8,128)(2,1)S(1)} %fusion.37), channel_id=1, source_target_pairs={{0,8},{4,12},{8,16},{12,20},{16,24},{20,28},{24,0},{28,4},{1,9},{5... | collective-permute-start | bytes 110600 | tf_op jit(solution)/shard_map/ppermute | solution.py:583
  186.3 17.4 %collective-permute-start.16 = (bf16[4,208,384]{2,1,0:T(8,128)(2,1)S(1)}, bf16[4,208,384]{2,1,0:T(8,128)(2,1)S(1)}, u32[]{:S(2)}, u32[]{:S(2)}) collective-permute-start(bf16[4,208,384]{2,1,0:T(8,128)(2,1)S(1)} %get-tuple-element.116), channel_id=1, source_target_pairs={{0,4},{4,0},{8,12},{12,8},{16,20},{20,16},{24,28},{28,24},{1,5},{5... | collective-permute-start | bytes 1916936 | tf_op jit(solution)/shard_map/ppermute | solution.py:582
  190.3 5.8 %collective-permute-start.24 = (bf16[48,384]{1,0:T(8,128)(2,1)S(1)}, bf16[48,384]{1,0:T(8,128)(2,1)S(1)}, u32[]{:S(2)}, u32[]{:S(2)}) collective-permute-start(bf16[48,384]{1,0:T(8,128)(2,1)S(1)} %fusion.31), channel_id=1, source_target_pairs={{0,8},{4,12},{8,16},{12,20},{16,24},{20,28},{24,0},{28,4},{1,9},{5... | collective-permute-start | bytes 110600 | tf_op jit(solution)/shard_map/ppermute | solution.py:583
  190.8 71.0 %collective-permute-start.55 = (bf16[4,64,1536]{2,1,0:T(8,128)(2,1)S(1)}, bf16[4,64,1536]{2,1,0:T(8,128)(2,1)S(1)}, u32[]{:S(2)}, u32[]{:S(2)}) collective-permute-start(bf16[4,64,1536]{2,1,0:T(8,128)(2,1)S(1)} %get-tuple-element.108), channel_id=1, source_target_pairs={{0,4},{4,0},{8,12},{12,8},{16,20},{20,16},{24,28},{28,24},{1,5},{5... | collective-permute-start | bytes 2359304 | tf_op jit(solution)/shard_map/ppermute | solution.py:582
  192.6 25.8 %collective-permute-start.60 = (bf16[8,16,1536]{2,1,0:T(8,128)(2,1)S(1)}, bf16[8,16,1536]{2,1,0:T(8,128)(2,1)S(1)}, u32[]{:S(2)}, u32[]{:S(2)}) collective-permute-start(bf16[8,16,1536]{2,1,0:T(8,128)(2,1)S(1)} %get-tuple-element.110), channel_id=1, source_target_pairs={{0,2},{1,3},{2,0},{3,1},{4,6},{5,7},{6,4},{7,5},{8,10},{9,11},{10,... | collective-permute-start | bytes 1179656 | tf_op jit(solution)/shard_map/ppermute | solution.py:581
  194.1 67.9 %collective-permute-start.42 = (bf16[4,256,384]{2,1,0:T(8,128)(2,1)S(1)}, bf16[4,256,384]{2,1,0:T(8,128)(2,1)S(1)}, u32[]{:S(2)}, u32[]{:S(2)}) collective-permute-start(bf16[4,256,384]{2,1,0:T(8,128)(2,1)S(1)} %get-tuple-element.112), channel_id=1, source_target_pairs={{0,4},{4,0},{8,12},{12,8},{16,20},{20,16},{24,28},{28,24},{1,5},{5... | collective-permute-start | bytes 2359304 | tf_op jit(solution)/shard_map/ppermute | solution.py:582
  196.1 5.8 %collective-permute-start.25 = (bf16[48,384]{1,0:T(8,128)(2,1)S(1)}, bf16[48,384]{1,0:T(8,128)(2,1)S(1)}, u32[]{:S(2)}, u32[]{:S(2)}) collective-permute-start(bf16[48,384]{1,0:T(8,128)(2,1)S(1)} %fusion.32), channel_id=1, source_target_pairs={{0,8},{4,12},{8,16},{12,20},{16,24},{20,28},{24,0},{28,4},{1,9},{5... | collective-permute-start | bytes 110600 | tf_op jit(solution)/shard_map/ppermute | solution.py:583
  201.9 18.0 %collective-permute-start.47 = (bf16[8,64,384]{2,1,0:T(8,128)(2,1)S(1)}, bf16[8,64,384]{2,1,0:T(8,128)(2,1)S(1)}, u32[]{:S(2)}, u32[]{:S(2)}) collective-permute-start(bf16[8,64,384]{2,1,0:T(8,128)(2,1)S(1)} %get-tuple-element.114), channel_id=1, source_target_pairs={{0,2},{1,3},{2,0},{3,1},{4,6},{5,7},{6,4},{7,5},{8,10},{9,11},{10,... | collective-permute-start | bytes 1179656 | tf_op jit(solution)/shard_map/ppermute | solution.py:581
  203.7 6.4 %collective-permute-start.26 = (bf16[48,384]{1,0:T(8,128)(2,1)S(1)}, bf16[48,384]{1,0:T(8,128)(2,1)S(1)}, u32[]{:S(2)}, u32[]{:S(2)}) collective-permute-start(bf16[48,384]{1,0:T(8,128)(2,1)S(1)} %fusion.33), channel_id=1, source_target_pairs={{0,2},{1,3},{2,0},{3,1},{4,6},{5,7},{6,4},{7,5},{8,10},{9,11},{10,... | collective-permute-start | bytes 110600 | tf_op jit(solution)/shard_map/ppermute | solution.py:581
  210.1 8.1 %collective-permute-start.17 = (bf16[208,384]{1,0:T(8,128)(2,1)S(1)}, bf16[208,384]{1,0:T(8,128)(2,1)S(1)}, u32[]{:S(2)}, u32[]{:S(2)}) collective-permute-start(bf16[208,384]{1,0:T(8,128)(2,1)S(1)} %fusion.16), channel_id=1, source_target_pairs={{0,8},{4,12},{8,16},{12,20},{16,24},{20,28},{24,0},{28,4},{1,9},{5... | collective-permute-start | bytes 479240 | tf_op jit(solution)/shard_map/ppermute | solution.py:583
  218.3 7.3 %collective-permute-start.18 = (bf16[208,384]{1,0:T(8,128)(2,1)S(1)}, bf16[208,384]{1,0:T(8,128)(2,1)S(1)}, u32[]{:S(2)}, u32[]{:S(2)}) collective-permute-start(bf16[208,384]{1,0:T(8,128)(2,1)S(1)} %fusion.6), channel_id=1, source_target_pairs={{0,8},{4,12},{8,16},{12,20},{16,24},{20,28},{24,0},{28,4},{1,9},{5... | collective-permute-start | bytes 479240 | tf_op jit(solution)/shard_map/ppermute | solution.py:583
  218.5 19.2 %collective-permute-start.61 = (bf16[4,16,1536]{2,1,0:T(8,128)(2,1)S(1)}, bf16[4,16,1536]{2,1,0:T(8,128)(2,1)S(1)}, u32[]{:S(2)}, u32[]{:S(2)}) collective-permute-start(bf16[4,16,1536]{2,1,0:T(8,128)(2,1)S(1)} %get-tuple-element.124), channel_id=1, source_target_pairs={{0,4},{4,0},{8,12},{12,8},{16,20},{20,16},{24,28},{28,24},{1,5},{5... | collective-permute-start | bytes 589832 | tf_op jit(solution)/shard_map/ppermute | solution.py:582
  220.0 19.7 %collective-permute-start.48 = (bf16[4,64,384]{2,1,0:T(8,128)(2,1)S(1)}, bf16[4,64,384]{2,1,0:T(8,128)(2,1)S(1)}, u32[]{:S(2)}, u32[]{:S(2)}) collective-permute-start(bf16[4,64,384]{2,1,0:T(8,128)(2,1)S(1)} %get-tuple-element.126), channel_id=1, source_target_pairs={{0,4},{4,0},{8,12},{12,8},{16,20},{20,16},{24,28},{28,24},{1,5},{5... | collective-permute-start | bytes 589832 | tf_op jit(solution)/shard_map/ppermute | solution.py:582
  225.7 14.2 %collective-permute-start.19 = (bf16[208,384]{1,0:T(8,128)(2,1)S(1)}, bf16[208,384]{1,0:T(8,128)(2,1)S(1)}, u32[]{:S(2)}, u32[]{:S(2)}) collective-permute-start(bf16[208,384]{1,0:T(8,128)(2,1)S(1)} %fusion.7), channel_id=1, source_target_pairs={{0,8},{4,12},{8,16},{12,20},{16,24},{20,28},{24,0},{28,4},{1,9},{5... | collective-permute-start | bytes 479240 | tf_op jit(solution)/shard_map/ppermute | solution.py:583
  237.7 6.4 %collective-permute-start.62 = (bf16[16,1536]{1,0:T(8,128)(2,1)S(1)}, bf16[16,1536]{1,0:T(8,128)(2,1)S(1)}, u32[]{:S(2)}, u32[]{:S(2)}) collective-permute-start(bf16[16,1536]{1,0:T(8,128)(2,1)S(1)} %fusion.36), channel_id=1, source_target_pairs={{0,8},{4,12},{8,16},{12,20},{16,24},{20,28},{24,0},{28,4},{1,9},{5... | collective-permute-start | bytes 147464 | tf_op jit(solution)/shard_map/ppermute | solution.py:583
  239.8 5.9 %collective-permute-start.49 = (bf16[64,384]{1,0:T(8,128)(2,1)S(1)}, bf16[64,384]{1,0:T(8,128)(2,1)S(1)}, u32[]{:S(2)}, u32[]{:S(2)}) collective-permute-start(bf16[64,384]{1,0:T(8,128)(2,1)S(1)} %fusion.35), channel_id=1, source_target_pairs={{0,8},{4,12},{8,16},{12,20},{16,24},{20,28},{24,0},{28,4},{1,9},{5... | collective-permute-start | bytes 147464 | tf_op jit(solution)/shard_map/ppermute | solution.py:583
  239.9 18.7 %collective-permute-start.20 = (bf16[208,384]{1,0:T(8,128)(2,1)S(1)}, bf16[208,384]{1,0:T(8,128)(2,1)S(1)}, u32[]{:S(2)}, u32[]{:S(2)}) collective-permute-start(bf16[208,384]{1,0:T(8,128)(2,1)S(1)} %fusion.8), channel_id=1, source_target_pairs={{0,2},{1,3},{2,0},{3,1},{4,6},{5,7},{6,4},{7,5},{8,10},{9,11},{10,... | collective-permute-start | bytes 479240 | tf_op jit(solution)/shard_map/ppermute | solution.py:581
  244.1 5.9 %collective-permute-start.63 = (bf16[16,1536]{1,0:T(8,128)(2,1)S(1)}, bf16[16,1536]{1,0:T(8,128)(2,1)S(1)}, u32[]{:S(2)}, u32[]{:S(2)}) collective-permute-start(bf16[16,1536]{1,0:T(8,128)(2,1)S(1)} %fusion.22), channel_id=1, source_target_pairs={{0,8},{4,12},{8,16},{12,20},{16,24},{20,28},{24,0},{28,4},{1,9},{5... | collective-permute-start | bytes 147464 | tf_op jit(solution)/shard_map/ppermute | solution.py:583
  245.8 5.9 %collective-permute-start.50 = (bf16[64,384]{1,0:T(8,128)(2,1)S(1)}, bf16[64,384]{1,0:T(8,128)(2,1)S(1)}, u32[]{:S(2)}, u32[]{:S(2)}) collective-permute-start(bf16[64,384]{1,0:T(8,128)(2,1)S(1)} %fusion.25), channel_id=1, source_target_pairs={{0,8},{4,12},{8,16},{12,20},{16,24},{20,28},{24,0},{28,4},{1,9},{5... | collective-permute-start | bytes 147464 | tf_op jit(solution)/shard_map/ppermute | solution.py:583
  250.1 5.9 %collective-permute-start.64 = (bf16[16,1536]{1,0:T(8,128)(2,1)S(1)}, bf16[16,1536]{1,0:T(8,128)(2,1)S(1)}, u32[]{:S(2)}, u32[]{:S(2)}) collective-permute-start(bf16[16,1536]{1,0:T(8,128)(2,1)S(1)} %fusion.23), channel_id=1, source_target_pairs={{0,8},{4,12},{8,16},{12,20},{16,24},{20,28},{24,0},{28,4},{1,9},{5... | collective-permute-start | bytes 147464 | tf_op jit(solution)/shard_map/ppermute | solution.py:583
  251.7 5.9 %collective-permute-start.51 = (bf16[64,384]{1,0:T(8,128)(2,1)S(1)}, bf16[64,384]{1,0:T(8,128)(2,1)S(1)}, u32[]{:S(2)}, u32[]{:S(2)}) collective-permute-start(bf16[64,384]{1,0:T(8,128)(2,1)S(1)} %fusion.26), channel_id=1, source_target_pairs={{0,8},{4,12},{8,16},{12,20},{16,24},{20,28},{24,0},{28,4},{1,9},{5... | collective-permute-start | bytes 147464 | tf_op jit(solution)/shard_map/ppermute | solution.py:583
  258.7 16.2 %collective-permute-start.27 = (bf16[304,384]{1,0:T(8,128)(2,1)S(1)}, bf16[304,384]{1,0:T(8,128)(2,1)S(1)}, u32[]{:S(2)}, u32[]{:S(2)}) collective-permute-start(bf16[304,384]{1,0:T(8,128)(2,1)S(1)} %pad_maximum_fusion.3), channel_id=1, source_target_pairs={{0,1},{1,0},{2,3},{3,2},{4,5},{5,4},{6,7},{7,6},{8,9},{9,8},{10,11... | collective-permute-start | bytes 700424 | tf_op jit(solution)/shard_map/ppermute | solution.py:580
  261.9 8.2 %collective-permute-start.56 = (bf16[64,1536]{1,0:T(8,128)(2,1)S(1)}, bf16[64,1536]{1,0:T(8,128)(2,1)S(1)}, u32[]{:S(2)}, u32[]{:S(2)}) collective-permute-start(bf16[64,1536]{1,0:T(8,128)(2,1)S(1)} %fusion.15), channel_id=1, source_target_pairs={{0,8},{4,12},{8,16},{12,20},{16,24},{20,28},{24,0},{28,4},{1,9},{5... | collective-permute-start | bytes 589832 | tf_op jit(solution)/shard_map/ppermute | solution.py:583
  262.1 12.1 %collective-permute-start.43 = (bf16[256,384]{1,0:T(8,128)(2,1)S(1)}, bf16[256,384]{1,0:T(8,128)(2,1)S(1)}, u32[]{:S(2)}, u32[]{:S(2)}) collective-permute-start(bf16[256,384]{1,0:T(8,128)(2,1)S(1)} %fusion.14), channel_id=1, source_target_pairs={{0,8},{4,12},{8,16},{12,20},{16,24},{20,28},{24,0},{28,4},{1,9},{5... | collective-permute-start | bytes 589832 | tf_op jit(solution)/shard_map/ppermute | solution.py:583
  270.2 9.9 %collective-permute-start.57 = (bf16[64,1536]{1,0:T(8,128)(2,1)S(1)}, bf16[64,1536]{1,0:T(8,128)(2,1)}, u32[]{:S(2)}, u32[]{:S(2)}) collective-permute-start(bf16[64,1536]{1,0:T(8,128)(2,1)S(1)} %fusion), channel_id=1, source_target_pairs={{0,8},{4,12},{8,16},{12,20},{16,24},{20,28},{24,0},{28,4},{1,9},{5... | collective-permute-start | bytes 589832 | tf_op jit(solution)/shard_map/ppermute | solution.py:583
  274.9 9.9 %collective-permute-start.44 = (bf16[256,384]{1,0:T(8,128)(2,1)}, bf16[256,384]{1,0:T(8,128)(2,1)}, u32[]{:S(2)}, u32[]{:S(2)}) collective-permute-start(bf16[256,384]{1,0:T(8,128)(2,1)} %fusion.3), channel_id=1, source_target_pairs={{0,8},{4,12},{8,16},{12,20},{16,24},{20,28},{24,0},{28,4},{1,9},{5... | collective-permute-start | bytes 589832 | tf_op jit(solution)/shard_map/ppermute | solution.py:583
  281.1 7.5 %collective-permute-start.58 = (bf16[64,1536]{1,0:T(8,128)(2,1)S(1)}, bf16[64,1536]{1,0:T(8,128)(2,1)S(1)}, u32[]{:S(2)}, u32[]{:S(2)}) collective-permute-start(bf16[64,1536]{1,0:T(8,128)(2,1)S(1)} %fusion.1), channel_id=1, source_target_pairs={{0,8},{4,12},{8,16},{12,20},{16,24},{20,28},{24,0},{28,4},{1,9},{5... | collective-permute-start | bytes 589832 | tf_op jit(solution)/shard_map/ppermute | solution.py:583
  285.8 7.5 %collective-permute-start.45 = (bf16[256,384]{1,0:T(8,128)(2,1)S(1)}, bf16[256,384]{1,0:T(8,128)(2,1)S(1)}, u32[]{:S(2)}, u32[]{:S(2)}) collective-permute-start(bf16[256,384]{1,0:T(8,128)(2,1)S(1)} %fusion.4), channel_id=1, source_target_pairs={{0,8},{4,12},{8,16},{12,20},{16,24},{20,28},{24,0},{28,4},{1,9},{5... | collective-permute-start | bytes 589832 | tf_op jit(solution)/shard_map/ppermute | solution.py:583
  288.7 6.0 %collective-permute-start.59 = (bf16[64,1536]{1,0:T(8,128)(2,1)S(1)}, bf16[64,1536]{1,0:T(8,128)(2,1)S(1)}, u32[]{:S(2)}, u32[]{:S(2)}) collective-permute-start(bf16[64,1536]{1,0:T(8,128)(2,1)S(1)} %fusion.2), channel_id=1, source_target_pairs={{0,2},{1,3},{2,0},{3,1},{4,6},{5,7},{6,4},{7,5},{8,10},{9,11},{10,... | collective-permute-start | bytes 589832 | tf_op jit(solution)/shard_map/ppermute | solution.py:581
  293.4 5.7 %collective-permute-start.46 = (bf16[256,384]{1,0:T(8,128)(2,1)S(1)}, bf16[256,384]{1,0:T(8,128)(2,1)S(1)}, u32[]{:S(2)}, u32[]{:S(2)}) collective-permute-start(bf16[256,384]{1,0:T(8,128)(2,1)S(1)} %fusion.5), channel_id=1, source_target_pairs={{0,2},{1,3},{2,0},{3,1},{4,6},{5,7},{6,4},{7,5},{8,10},{9,11},{10,... | collective-permute-start | bytes 589832 | tf_op jit(solution)/shard_map/ppermute | solution.py:581
  294.8 4.6 %collective-permute-start.66 = (bf16[96,1536]{1,0:T(8,128)(2,1)S(1)}, bf16[96,1536]{1,0:T(8,128)(2,1)S(1)}, u32[]{:S(2)}, u32[]{:S(2)}) collective-permute-start(bf16[96,1536]{1,0:T(8,128)(2,1)S(1)} %pad_maximum_fusion.2), channel_id=1, source_target_pairs={{0,1},{1,0},{2,3},{3,2},{4,5},{5,4},{6,7},{7,6},{8,9},{9,8},{10,11... | collective-permute-start | bytes 884744 | tf_op jit(solution)/shard_map/ppermute | solution.py:580
  (39 other events, 341.2 us)

commit v2 on v1

v2 whole, which is shorter than its diff:
```python
import functools

import jax
import jax.numpy as jnp
from jax import lax
from jax.experimental import pallas as pl
from jax.experimental.pallas import tpu as pltpu
from jax.sharding import PartitionSpec as P

HD = 64
SEGS = 8
BF = jnp.bfloat16
F32 = jnp.float32
EPS = 1e-06
NEG = -1e30
LANES = 128

PART = 16


def nn(a, b):
    return jnp.dot(a, b, preferred_element_type=F32)


def nt(a, b):
    return lax.dot_general(a, b, (((1,), (1,)), ((), ())), preferred_element_type=F32)


def three_parts(v):
    hi = v.astype(BF)
    rest = v - hi.astype(F32)
    mid = rest.astype(BF)
    low = (rest - mid.astype(F32)).astype(BF)
    return hi, mid, low


def two_parts(v):
    hi = v.astype(BF)
    return hi, (v - hi.astype(F32)).astype(BF)


def norm(value):
    centre = value - jnp.mean(value, axis=-1, keepdims=True)
    inverse = lax.rsqrt(jnp.mean(centre * centre, axis=-1, keepdims=True) + EPS)
    return centre * inverse, inverse


def norm_back(grad, normed, inverse):
    a = jnp.mean(grad, axis=-1, keepdims=True)
    b = jnp.mean(grad * normed, axis=-1, keepdims=True)
    return (grad - a - normed * b) * inverse


def gelu_both(x):
    phi = 0.5 + 0.5 * lax.erf(x * (0.5**0.5))
    density = 0.3989422804014327 * jnp.exp(x * x * -0.5)
    return x * phi, phi + x * density


def head_lane(h):
    lane = lax.broadcasted_iota(jnp.int32, (1, LANES), 1)
    return (lane % PART == h) & (lane >= PART) & (lane < 4 * PART)


def put_rows(out_ref, lead, y, rows, halves, cols, value):
    n = value.shape[0] // halves
    for a in range(halves):
        side = jnp.where(y == a, 0, 1) if halves > 1 else 0
        out_ref[side, lead, pl.ds(rows, n), cols] = value[a * n : (a + 1) * n].astype(BF)


def put_shards(out_ref, info, lay, cols, value, rows=0, first=0):
    n, halves, rs = lay
    count = value.shape[0] // rs
    for i in range(count):
        lead = info[first * count + i] if n > 1 else 0
        put_rows(out_ref, lead, info[9], rows, halves, cols, value[i * rs : (i + 1) * rs])


def copies(pairs, sems, first=0):
    out = []
    for i, (src, dst) in enumerate(pairs):
        out.append(pltpu.make_async_copy(src, dst, sems.at[first + i]))
        out[-1].start()
    return out


def wait(moves):
    for m in moves:
        m.wait()


def split_kernel(info, x_ref, *refs):
    outs, sems = refs[:-1], refs[-1]
    wait(copies([(x_ref.at[info[10] ^ r], outs[r]) for r in range(len(outs))], sems))


def join_kernel(info, *refs):
    me = info[10]
    out = refs[-1]
    for r in range(4):
        out[me ^ r] = refs[r][...]


def attend_kernel(
    x0, x1, x2, x3, wq_h, wk_h, wv_h, wo_h, oh_ref, ka_ref, bq, bv, bo,
    x_h, q_h, k_h, v_h, att_h, inv_h, qa_h, n1_out,
    x_out, q_out, k_out, v_out, att_out, inv_out, qa_out, wq, wk, wv, wo, stat, sems,
):
    n = x0.shape[0]
    ws = copies([(wq_h, wq), (wk_h, wk), (wv_h, wv), (wo_h, wo)], sems, 4)
    for r, ref in enumerate((x0, x1, x2, x3)):
        x_out[r * n : (r + 1) * n] = ref[...]
    outs = copies([(x_out, x_h)], sems, 8)
    x = x_out[...]
    ws[0].wait()
    q_out[...] = ((nn(x, wq[...]) + bq[...]).astype(BF).astype(F32) * (HD**-0.5)).astype(BF)
    outs += copies([(q_out, q_h)], sems, 9)
    ws[1].wait()
    k_out[...] = nn(x, wk[...]).astype(BF)
    outs += copies([(k_out, k_h)], sems, 10)
    ws[2].wait()
    v_out[...] = (nn(x, wv[...]) + bv[...]).astype(BF)
    outs += copies([(v_out, v_h)], sems, 11)
    tok, width = x.shape
    stat[...] = jnp.zeros_like(stat)
    ones = jnp.ones((16, tok), BF)

    def pair(p, carry):
        sl = pl.ds(pl.multiple_of(p * LANES, LANES), LANES)
        qcat = jnp.concatenate([q_out[:, sl], oh_ref[...]], axis=1)
        kp = k_out[:, sl]
        vt = v_out[:, sl].T
        lane = lax.broadcasted_iota(jnp.int32, (1, LANES), 1)
        parts = []
        for h in range(2):
            kh = jnp.where((lane < HD) == (h == 0), kp, jnp.zeros_like(kp))
            st = nt(jnp.concatenate([kh, ka_ref[...]], axis=1), qcat)
            m = jnp.max(st, axis=0, keepdims=True)
            pb = jnp.exp(st - m).astype(BF)
            ot = nn(jnp.concatenate([vt[h * HD : (h + 1) * HD], ones], axis=0), pb)
            total = ot[HD : HD + 1]
            stat[pl.ds(2 * p + h, 1), :] = m + jnp.log(total)
            parts.append(ot[:HD] / total)
        att_out[:, sl] = jnp.concatenate(parts, axis=0).T
        return carry

    lax.fori_loop(0, width // LANES, pair, 0)
    outs += copies([(att_out, att_h)], sems, 12)
    hi, mid, low = three_parts(stat[...])
    zero = jnp.zeros((PART, tok), BF)
    qa_out[...] = jnp.concatenate([zero, hi, mid, low, zero, zero, zero, zero], axis=0).T + oh_ref[...]
    outs += copies([(qa_out, qa_h)], sems, 13)
    ws[3].wait()
    mixed = nn(att_out[...].astype(BF), wo[...]) + bo[...]
    n1, inv = norm(x.astype(F32) + mixed)
    n1_out[...] = n1
    inv_out[...] = jnp.broadcast_to(inv, inv_out.shape)
    outs += copies([(inv_out, inv_h)], sems, 14)
    wait(outs)


def ffn_kernel(
    lay, info, n1_ref, ga, sa, wu, bu, wd, bd, gf, sf, g0, g1, g2, g3, oh_ref, oht_ref, gpl,
    o0, o1, o2, o3, gp_h, send, keep, pool_out, r2_out, vec_out,
    hl, acc, act, gt, gp_out, sem_g,
):
    n = g0.shape[0]
    tok, width = acc.shape
    ff = act.shape[1]
    tile = width
    steps = ff // tile

    def slopes(t):
        cols = pl.ds(pl.multiple_of(t * tile, tile), tile)
        return pltpu.make_async_copy(gp_out.at[:, cols], gp_h.at[:, cols], sem_g.at[t])

    hl[...] = (n1_ref[...] * ga[...] + sa[...]).astype(BF)
    acc[...] = jnp.zeros_like(acc)

    def step(t, carry):
        cols = pl.ds(pl.multiple_of(t * tile, tile), tile)
        for r in range(4):
            rows = pl.ds(r * n, n)
            a, d = gelu_both(nn(hl[rows, :], wu[:, cols]) + bu[:, cols])
            ab = a.astype(BF)
            act[rows, cols] = ab
            gp_out[rows, cols] = d.astype(BF)
            acc[rows, :] += nn(ab, wd[cols, :])
        slopes(t).start()
        return carry

    lax.fori_loop(0, steps, step, 0)
    gain = jnp.zeros((1, width), F32)
    shift = jnp.zeros((1, width), F32)
    bias = jnp.zeros((1, width), F32)
    pool = jnp.zeros(pool_out.shape, F32)
    for r, (o, g) in enumerate(((o0, g0), (o1, g1), (o2, g2), (o3, g3))):
        rows = pl.ds(r * n, n)
        hidden = n1_ref[rows, :] * ga[...] + sa[...]
        n2, inv = norm(hidden + (acc[rows, :] + bd[...]))
        result = n2 * gf[...] + sf[...]
        o[...] = result.astype(BF)
        hi, low = two_parts(result)
        oht = oht_ref[:, r * n : (r + 1) * n]
        pool += nn(oht, hi) + nn(oht, low)
        oh = oh_ref[rows, :]
        gout = g[...].astype(F32) + nn(jnp.concatenate([oh, oh], axis=1), gpl[...])
        gain += jnp.sum(gout * n2, axis=0, keepdims=True)
        shift += jnp.sum(gout, axis=0, keepdims=True)
        gr2 = norm_back(gout * gf[...], n2, inv)
        r2_out[rows, :] = gr2
        low_g = gr2.astype(BF)
        bias += jnp.sum(low_g.astype(F32), axis=0, keepdims=True)
        gt[:, r * n : (r + 1) * n] = low_g.T
    pool_out[...] = pool
    vec_out[...] = jnp.concatenate([bias, gain, shift, jnp.zeros((5, width), F32)], axis=0)
    half = ff // 2
    part = 512

    def piece(i, carry):
        for rc, ref in ((1, send), (0, keep)):
            at = (info[8] ^ rc) * half + i * part
            res = nn(gt[...], act[:, pl.ds(pl.multiple_of(at, part), part)])
            put_shards(ref, info, lay, pl.ds(pl.multiple_of(i * part, part), part), res)
        return carry

    lax.fori_loop(0, half // part, piece, 0)
    for t in range(steps):
        slopes(t).wait()


def ffn_back_kernel(
    lay, info, r2_ref, gp_h, wd, n1_ref, ga, sa,
    send, keep, bup_out, gpre_out,
    gl, hlt, gp, sem_w,
):
    width = hlt.shape[0]
    half = width // 2
    ff = gp.shape[1]
    tile = width
    steps = ff // tile

    def load(t):
        cols = pl.ds(pl.multiple_of(t * tile, tile), tile)
        return pltpu.make_async_copy(gp_h.at[:, cols], gp.at[:, cols], sem_w.at[t])

    for t in range(steps):
        load(t).start()
    gl[...] = r2_ref[...].astype(BF)
    hlt[...] = (n1_ref[...] * ga[...] + sa[...]).astype(BF).T
    per = 2 if lay[0] > 1 else 1

    def step(t, carry):
        cols = pl.ds(pl.multiple_of(t * tile, tile), tile)
        load(t).wait()
        gpre = (nt(gl[...], wd[cols, :]) * gp[:, cols].astype(F32)).astype(BF)
        gpre_out[:, cols] = gpre
        bup_out[:, cols] = jnp.broadcast_to(
            jnp.sum(gpre.astype(F32), axis=0, keepdims=True), (bup_out.shape[0], tile)
        )
        for rc, ref in ((1, send), (0, keep)):
            at = pl.multiple_of((info[8] ^ rc) * half, half)
            res = nn(hlt[pl.ds(at, half), :], gpre)
            for i in range(per):
                if lay[0] > 1:
                    put_rows(ref, info[per * t + i], info[9], 0, lay[1], slice(None), res[:, i * half : (i + 1) * half])
                else:
                    put_rows(ref, 0, info[9], 0, lay[1], cols, res)
        return carry

    lax.fori_loop(0, steps, step, 0)


def norm_back_kernel(
    lay, info, r2_ref, gpre, wu, n1_ref, inv_ref, ga, wo, att,
    r1_h, gatt_out, gaug_out, vec_out, osend, okeep,
    gt, r1_out, acc, sems,
):
    tok, width = r2_ref.shape
    half = width // 2
    n = tok // 4
    gain = jnp.zeros((1, width), F32)
    shift = jnp.zeros((1, width), F32)
    bias = jnp.zeros((1, width), F32)
    row = lax.broadcasted_iota(jnp.int32, (width, LANES), 0) // HD
    lane = lax.broadcasted_iota(jnp.int32, (width, LANES), 1)
    pick = ((lane % PART == row) & (lane >= PART) & (lane < 4 * PART)).astype(BF)
    lane1 = lax.broadcasted_iota(jnp.int32, (1, LANES), 1)
    outs = []

    def step(t, carry):
        cols = pl.ds(pl.multiple_of(t * width, width), width)
        acc[...] += nt(gpre[:, cols], wu[:, cols])
        return carry

    acc[...] = r2_ref[...]
    lax.fori_loop(0, gpre.shape[1] // width, step, 0)
    for r in range(4):
        rows = pl.ds(r * n, n)
        gh = acc[rows, :]
        n1 = n1_ref[rows, :]
        gain += jnp.sum(gh * n1, axis=0, keepdims=True)
        shift += jnp.sum(gh, axis=0, keepdims=True)
        gr1 = norm_back(gh * ga[...], n1, inv_ref[rows, :1])
        r1_out[rows, :] = gr1
        outs += copies([(r1_out.at[rows, :], r1_h.at[rows, :])], sems, r)
        gm = gr1.astype(BF)
        bias += jnp.sum(gm.astype(F32), axis=0, keepdims=True)
        gt[:, r * n : (r + 1) * n] = gm.T
        gatt = nt(gm, wo[...]).astype(BF)
        gatt_out[rows, :] = gatt
        a, b, c = three_parts(gatt.astype(F32) * att[rows, :])
        delta = nn(a, pick) + nn(b, pick) + nn(c, pick)
        a, b, c = three_parts(delta)
        gaug_out[rows, :] = jnp.where(lane1 < 2 * PART, a, jnp.where(lane1 < 3 * PART, b, c))
    vec_out[...] = jnp.concatenate([bias, gain, shift, jnp.zeros((5, width), F32)], axis=0)
    sides = [att[:, pl.ds(pl.multiple_of((info[8] ^ rc) * half, half), half)].astype(BF) for rc in (1, 0)]
    res = nn(gt[...], jnp.concatenate(sides, axis=1))
    put_shards(osend, info, lay, slice(None), res[:, :half])
    put_shards(okeep, info, lay, slice(None), res[:, half:])
    wait(outs)


def attend_back_kernel(
    q, k, v, g, qa, ka, ga,
    gq, gk, gv, gqt, gkt, gvt, vec_out,
):
    tok, width = q.shape

    def pair(p, carry):
        sl = pl.ds(pl.multiple_of(p * LANES, LANES), LANES)
        qp, kp, vp, gp = q[:, sl], k[:, sl], v[:, sl], g[:, sl]
        qcat = jnp.concatenate([qp, qa[...]], axis=1)
        gcat = jnp.concatenate([gp, ga[...]], axis=1)
        kt = kp.T
        lane = lax.broadcasted_iota(jnp.int32, (1, LANES), 1)
        gkp = jnp.zeros((tok, LANES), F32)
        gvp = jnp.zeros((tok, LANES), F32)
        parts = []
        zero = jnp.zeros_like(kp)
        for h in range(2):
            mine = (lane < HD) == (h == 0)
            pick = head_lane(2 * p + h)
            kaug = jnp.where(pick, -jnp.ones((), BF), ka[...])
            vaug = jnp.where(pick, -jnp.ones((), BF), jnp.zeros((tok, LANES), BF))
            prob = jnp.exp(nt(jnp.concatenate([jnp.where(mine, kp, zero), kaug], axis=1), qcat))
            dp = nt(jnp.concatenate([jnp.where(mine, vp, zero), vaug], axis=1), gcat)
            ds = (prob * dp).astype(BF)
            gvp += nn(prob.astype(BF), jnp.where(mine, gp, zero))
            gkp += nn(ds, jnp.where(mine, qp, zero))
            parts.append(nn(kt[h * HD : (h + 1) * HD], ds))
        gqp = (jnp.concatenate(parts, axis=0) * (HD**-0.5)).astype(BF)
        gqt[sl, :] = gqp
        gq[:, sl] = gqp.T
        gkb, gvb = gkp.astype(BF), gvp.astype(BF)
        gk[:, sl] = gkb
        gv[:, sl] = gvb
        gkt[sl, :] = gkb.T
        gvt[sl, :] = gvb.T
        return carry

    lax.fori_loop(0, width // LANES, pair, 0)
    bq = jnp.sum(gq[...].astype(F32), axis=0, keepdims=True)
    bv = jnp.sum(gv[...].astype(F32), axis=0, keepdims=True)
    vec_out[...] = jnp.concatenate([bq, bv, jnp.zeros((6, width), F32)], axis=0)


def project_back_kernel(
    lay, info, gq, gk, gv, gqt, gkt, gvt, x_ref, r1, wq, wk, wv, vecs, bups,
    send, keep, o0, o1, o2, o3,
):
    width = x_ref.shape[1]
    n, halves, rs = lay
    half = width // 2
    sides = [x_ref[:, pl.ds(pl.multiple_of((info[8] ^ rc) * half, half), half)] for rc in (1, 0)]
    right = jnp.concatenate(sides, axis=1)
    for m, left in enumerate((gqt, gkt, gvt)):
        both = nn(left[...], right)
        for rc, ref in ((1, send), (0, keep)):
            res = both[:, :half] if rc else both[:, half:]
            if n > 1:
                for j in range(n):
                    lead, at = info[j], j * rs
                    if m == 1:
                        put_rows(ref, lead, info[9], 48, halves, slice(None), res[at : at + 32])
                        put_rows(ref, lead, info[9], 128, halves, slice(None), res[at + 32 : at + rs])
                    else:
                        put_rows(ref, lead, info[9], 40 * m, halves, slice(None), res[at : at + rs])
            else:
                ref[0, 0, pl.ds(m * width, width), :] = res.astype(BF)
    if n > 1:
        for j in range(n):
            bup = bups[:1, j * 4 * rs : (j + 1) * 4 * rs]
            block = jnp.concatenate(
                [vecs[:, j * rs : (j + 1) * rs], jnp.zeros((8, rs), F32)]
                + [bup[:, c * rs : (c + 1) * rs] for c in range(4)]
                + [jnp.zeros((12, rs), F32)],
                axis=0,
            )
            block = jnp.concatenate([block, jnp.zeros((32, half - rs), F32)], axis=1)
            for rc, ref in ((1, send), (0, keep)):
                mine = jnp.where((info[8] ^ rc) == 0, 1.0, 0.0)
                put_rows(ref, info[j], info[9], 64, halves, slice(None), block * mine)

    total = r1[...] + nt(gq[...], wq[...]) + nt(gk[...], wk[...]) + nt(gv[...], wv[...])
    for r, o in enumerate((o0, o1, o2, o3)):
        c = o.shape[0]
        o[...] = total[r * c : (r + 1) * c].astype(BF)


WHOLE = pl.BlockSpec(memory_space=pltpu.VMEM)
SCALARS = pl.BlockSpec(memory_space=pltpu.SMEM)
FAR = pl.BlockSpec(memory_space=pltpu.HBM)


def shape(dims, dtype=BF):
    return jax.ShapeDtypeStruct(tuple(dims), dtype)


def buf(dims, dtype=BF):
    return pltpu.VMEM(tuple(dims), dtype)


def sems(count):
    return pltpu.SemaphoreType.DMA((count,))


def params(mib):
    return pltpu.CompilerParams(vmem_limit_bytes=mib * 1024 * 1024)


COST = pl.CostEstimate(flops=10**9, bytes_accessed=10**6, transcendentals=0)


class Line:
    def __init__(self):
        self.token = None

    def call(self, kernel, outs, args, scalars=(), scratch=(), name=None, mib=8, far_in=(), far_out=()):
        args = [pltpu.with_memory_space_constraint(a, pltpu.HBM) if i in far_in else a for i, a in enumerate(args)]
        ins = [SCALARS if i in scalars else FAR if i in far_in else WHOLE for i in range(len(args))]
        to = [FAR if i in far_out else WHOLE for i in range(len(outs))]
        outs = [pltpu.HBM(o.shape, o.dtype) if i in far_out else o for i, o in enumerate(outs)]
        tokens = [] if self.token is None else [self.token]
        n_in, n_tok, n_out = len(args), len(tokens), len(outs)

        def body(*refs):
            left, right = refs[:n_in], refs[n_in + n_tok :]
            kernel(*left, *right[:n_out], *right[n_out + 1 :])
            right[n_out][...] = jnp.zeros((8, LANES), F32)

        *got, self.token = pl.pallas_call(
            body,
            out_shape=[*outs, shape((8, LANES), F32)],
            in_specs=ins + [WHOLE] * n_tok,
            out_specs=[*to, WHOLE],
            scratch_shapes=list(scratch),
            compiler_params=params(mib),
            cost_estimate=COST,
            name=name,
        )(*args, *tokens)
        return got


def kernel_name(kernel):
    return getattr(kernel, "func", kernel).__name__.split("_")[0]


def plus(a, b):
    return (a.astype(F32) + b.astype(F32)).astype(BF)


def view(ref, cut):
    return ref[:, :, slice(*cut[0]), slice(*cut[1])]


def one_kernel(cuts_a, cuts_b, count, *refs):
    got, kept = refs[:count], refs[count : 2 * count]
    sa, sb, ka, kb = refs[2 * count :]
    at = 0
    for i, cut in cuts_a:
        total = plus(view(got[i], cut), view(kept[i], cut))
        m = total.shape[2]
        sa[:, :, at : at + m, :] = total[:, 4:]
        ka[:, :, at : at + m, :] = total[:, :4]
        at += m
    at = 0
    for i, cut in cuts_b:
        total = plus(view(got[i], cut), view(kept[i], cut))
        m = total.shape[2]
        sb[:, at : at + m, :] = total[1]
        kb[:, at : at + m, :] = total[0]
        at += m


def two_kernel(ga, gb, ka, kb, sa, sb, la, lb):
    a = plus(ga[...], ka[...])
    sa[...] = a[1]
    la[...] = a[0]
    b = plus(gb[...], kb[...])
    sb[...] = b[4:]
    lb[...] = b[:4]


def three_kernel(ga, gb, ka, kb, send, keep):
    m = ga.shape[1]
    a, b = plus(ga[...], ka[...]), plus(gb[...], kb[...])
    send[:, :m, :] = a[2:]
    keep[:, :m, :] = a[:2]
    send[:, m:, :] = b[2:]
    keep[:, m:, :] = b[:2]


def four_kernel(got, kept, send, keep):
    total = plus(got[...], kept[...])
    send[...] = total[1]
    keep[...] = total[0]


def five_kernel(got, kept, mine):
    mine[...] = plus(got[...], kept[...])


def six_kernel(info, mine, other, both):
    both[info[9]] = mine[...]
    both[1 - info[9]] = other[...]


def down_kernel(info, mine, other, out):
    m = mine.shape[1] // 2
    cols = mine.shape[2]
    for rc, ref in ((0, mine), (1, other)):
        for p in range(2):
            block = jnp.concatenate([ref[0, p * m : (p + 1) * m], ref[1, p * m : (p + 1) * m]], axis=0)
            at = (info[8] ^ rc) * 2 * cols + p * cols
            out[:, pl.ds(pl.multiple_of(at, cols), cols)] = block.astype(F32)


def up_kernel(info, mine, other, out):
    half = out.shape[0] // 2
    m = half // 2
    for rc, ref in ((0, mine), (1, other)):
        for a in range(2):
            at = (info[8] ^ rc) * half + a * m
            out[pl.ds(pl.multiple_of(at, m), m), :] = ref[a].astype(F32)


def qkv_kernel(info, mine, other, gq, gk, gv, go, vec):
    half = gq.shape[1] // 2
    for rc, ref in ((0, mine), (1, other)):
        at = pl.ds(pl.multiple_of((info[8] ^ rc) * half, half), half)

        def put(out, *spans):
            parts = [ref[a, i : i + m] for i, m in spans for a in range(2)]
            out[:, at] = jnp.concatenate(parts, axis=0).astype(F32)

        put(gq, (0, 48))
        put(gk, (48, 16), (176, 32))
        put(gv, (128, 48))
        put(go, (80, 48))
    rs = vec.shape[1]
    low = jnp.where(info[8] == 0, mine[:, 64:80, :].astype(F32), other[:, 64:80, :].astype(F32))
    vec[...] = jnp.concatenate([low[0, :8, :rs], low[1, :8, :rs]], axis=0)


def local(n_dp, n_seq, *args):
    (
        tokens, seg_lengths, w_query, b_query, w_key, w_value, b_value, w_out, b_out,
        gain_attn, shift_attn, w_up, b_up, w_down, b_down, gain_ffn, shift_ffn,
        grad_output, grad_pooled,
    ) = args
    line = Line()
    me = lax.axis_index("seq")
    dp = lax.axis_index("dp")
    core, y = me % 2, me // 2
    rows, piece, width = tokens.shape
    tok = n_seq * piece
    ff = w_up.shape[1]
    fast = n_dp == 8
    n = n_dp if fast else 1
    rs = width // n
    half = width // 2
    xor = [[(i, i ^ r) for i in range(n_seq)] for r in range(n_seq)]

    if fast:
        j = jnp.arange(8, dtype=jnp.int32) ^ dp
        pos = (j % 2) * 4 + (j // 2 % 2) * 2 + j // 4
    else:
        pos = jnp.zeros((8,), jnp.int32)
    info = jnp.concatenate([pos, jnp.stack([core, y, me]), jnp.zeros((5,), jnp.int32)]).astype(jnp.int32)

    def rel(a, name):
        parts = line.call(
            split_kernel, [shape((piece, width))] * n_seq, (info, a), scalars=(0,), scratch=[sems(n_seq)],
            name=name, far_in=(1,),
        )
        return [parts[0]] + [lax.ppermute(parts[r], "seq", xor[r]) for r in range(1, n_seq)]

    xs = rel(tokens, "split_tokens")
    gs = rel(grad_output, "split_grads")

    lengths = lax.dynamic_index_in_dim(seg_lengths, me, 0, keepdims=False)
    ends = jnp.cumsum(lengths)
    order = me ^ jnp.arange(n_seq, dtype=jnp.int32)
    places = (order[:, None] * piece + jnp.arange(piece, dtype=jnp.int32)[None, :]).reshape(tok)
    seg = jnp.sum((places[:, None] >= ends[None, :]).astype(jnp.int32), axis=1)
    lane = jnp.arange(LANES, dtype=jnp.int32)
    hot = seg[:, None] == lane[None, :]
    onehot = hot.astype(BF)
    kaug = jnp.where((lane < SEGS)[None, :] & ~hot, NEG, 0.0).astype(BF)
    onehot_t = (seg[None, :] == jnp.arange(16, dtype=jnp.int32)[:, None]).astype(BF)
    length_col = lengths.astype(F32)[:, None]
    gpool = lax.dynamic_index_in_dim(grad_pooled, me, 0, keepdims=False).astype(F32) / length_col
    gp_hi = gpool.astype(BF)
    gp_low = (gpool - gp_hi.astype(F32)).astype(BF)
    zeros = jnp.zeros((LANES - SEGS, width), BF)
    gpl = jnp.concatenate([gp_hi, zeros, gp_low, zeros], axis=0)

    def vec(v):
        return v.astype(F32).reshape(1, -1)

    sq = shape((tok, width))
    sqf = shape((tok, width), F32)
    lanes = shape((tok, LANES))
    lanes_f = shape((tok, LANES), F32)
    x, q, k, v, att, inv, qaug, n1 = line.call(
        attend_kernel,
        [sq, sq, sq, sq, sqf, lanes_f, lanes, sqf],
        (*xs, w_query, w_key, w_value, w_out, onehot, kaug, vec(b_query), vec(b_value), vec(b_out)),
        scratch=[buf((tok, width))] * 4
        + [buf((tok, width), F32), buf((tok, LANES), F32), buf((tok, LANES))]
        + [buf((width, width))] * 4
        + [buf((PART, tok), F32), sems(15)],
        name="attend",
        mib=20,
        far_in=range(4, 8),
        far_out=range(7),
    )

    halves = 2 if fast else 1
    lay = (n, halves, rs)
    wire_d = shape((halves, n, rs // halves, ff // 2))
    steps = ff // width
    *outs, gp, d_send, d_keep, pool, r2, vec_b = line.call(
        functools.partial(ffn_kernel, lay),
        [shape((piece, width))] * 4
        + [shape((tok, ff)), wire_d, wire_d, shape((16, width), F32), sqf, shape((8, width), F32)],
        (
            info, n1, vec(gain_attn), vec(shift_attn), w_up, vec(b_up), w_down, vec(b_down),
            vec(gain_ffn), vec(shift_ffn), *gs, onehot, onehot_t, gpl,
        ),
        scalars=(0,),
        scratch=[
            buf((tok, width)), buf((tok, width), F32), buf((tok, ff)), buf((width, tok)), buf((tok, ff)), sems(steps),
        ],
        name="ffn",
        mib=18,
        far_out=(4,),
    )

    pp_core = lambda a: lax.ppermute(a, "seq", xor[1])
    pp_y = lambda a: lax.ppermute(a, "seq", xor[2])

    def pp_dp(bit):
        return lambda a: lax.ppermute(a, "dp", [(i, i ^ bit) for i in range(n_dp)])

    pp_x, pp_z1, pp_z2 = pp_dp(1), pp_dp(2), pp_dp(4)

    def join_rows(parts):
        return parts[0] if len(parts) == 1 else jnp.concatenate(parts, axis=-2)

    class Sum:
        def __init__(self, name, got, kept, cuts_a, cuts_b):
            self.name, self.got, self.kept = name, got, kept
            self.cuts = cuts_a, cuts_b

        def run(self, kernel, outs, args, scalars=()):
            return line.call(
                kernel, [shape(o) for o in outs], args, scalars=scalars, name=self.name + kernel_name(kernel), mib=16
            )

        def one(self):
            a, b = (sum(r1 - r0 for _, ((r0, r1), _) in cut) for cut in self.cuts)
            c = self.cuts[0][0][1][1]
            c = c[1] - c[0]
            sa, sb, ka, kb = self.run(
                functools.partial(one_kernel, *self.cuts, len(self.got)),
                [(2, 4, a, c), (8, b, c), (2, 4, a, c), (8, b, c)],
                (*self.got, *self.kept),
            )
            self.got, self.kept = (pp_x(sa), pp_y(sb)), (ka, kb)
            self.dims = a, b, c

        def two(self):
            a, b, c = self.dims
            sa, sb, ka, kb = self.run(two_kernel, [(4, a, c), (4, b, c)] * 2, (*self.got, *self.kept))
            self.got, self.kept = (pp_y(sa), pp_x(sb)), (ka, kb)

        def three(self):
            a, b, c = self.dims
            send, keep = self.run(three_kernel, [(2, a + b, c)] * 2, (*self.got, *self.kept))
            self.got, self.kept = pp_z1(send), keep

        def four(self):
            a, b, c = self.dims
            send, keep = self.run(four_kernel, [(a + b, c)] * 2, (self.got, self.kept))
            self.got, self.kept = pp_z2(send), keep

        def five(self):
            a, b, c = self.dims
            (mine,) = self.run(five_kernel, [(a + b, c)], (self.got, self.kept))
            self.got, self.kept = pp_y(mine), mine

        def six(self):
            a, b, c = self.dims
            (both,) = self.run(six_kernel, [(2, a + b, c)], (info, self.kept, self.got), scalars=(0,))
            self.got, self.kept = pp_core(both), both

        def end(self, kernel, outs):
            return line.call(
                kernel, outs, (info, self.kept, self.got), scalars=(0,), name=self.name + "end", mib=16
            )

    def there(parts):
        return [parts[0]] + [lax.ppermute(parts[r], "seq", xor[r]) for r in range(1, 4)]

    def joined(got, name):
        (whole,) = line.call(
            join_kernel, [shape((rows, *got[0].shape), got[0].dtype)], (info, *got), scalars=(0,), name=name
        )
        return whole

    out_got = there(outs)
    pool_got = there([pool[:SEGS] / length_col] * n_seq)

    wire_u = shape((halves, n, half // halves, ff // n))
    if fast:
        d_got = pp_core(d_send)
    u_send, u_keep, bup, gpre = line.call(
        functools.partial(ffn_back_kernel, lay),
        [wire_u, wire_u, shape((8, ff), F32), shape((tok, ff))],
        (info, r2, gp, w_down, n1, vec(gain_attn), vec(shift_attn)),
        scalars=(0,),
        scratch=[buf((tok, width)), buf((width, tok)), buf((tok, ff)), sems(steps)],
        name="ffn_back",
        mib=12,
        far_in=(2,),
    )
    if fast:
        u_got = pp_core(u_send)
        c, m = ff // 4, rs // 2
        down = Sum("down_", [d_got], [d_keep], [(0, ((0, m), (0, c)))], [(0, ((0, m), (c, 2 * c)))])
        down.one()
    wire_o = shape((halves, n, rs // halves, half))
    r1, gatt, gaug, vec_c, o_send, o_keep = line.call(
        functools.partial(norm_back_kernel, lay),
        [sqf, sq, shape((tok, LANES)), shape((8, width), F32), wire_o, wire_o],
        (info, r2, gpre, w_up, n1, inv, vec(gain_attn), w_out, att),
        scalars=(0,),
        scratch=[buf((width, tok)), buf((tok, width), F32), buf((tok, width), F32), sems(4)],
        name="norm_back",
        mib=14,
        far_out=(0,),
    )
    output = joined(out_got, "join_out")
    pooled = joined(pool_got, "join_pool")
    if fast:
        o_got = pp_core(o_send)
        m = half // 2
        up = Sum("up_", [u_got], [u_keep], [(0, ((0, m // 2), (0, half)))], [(0, ((m // 2, m), (0, half)))])
        up.one()

    gq, gk, gv, gqt, gkt, gvt, vec_d = line.call(
        attend_back_kernel,
        [sq] * 3 + [shape((width, tok))] * 3 + [shape((8, width), F32)],
        (q, k, v, gatt, qaug, kaug, gaug),
        name="attend_back",
        mib=10,
    )
    vecs = jnp.concatenate([vec_d[:2], vec_c[:3], vec_b[:3]], axis=0)
    if fast:
        down.two()
        up.two()
    rows_q = 160 if fast else 3 * width
    wire_q = shape((halves, n, rows_q, half))
    q_send, q_keep, *ins = line.call(
        functools.partial(project_back_kernel, lay),
        [wire_q, wire_q] + [shape((piece, width))] * 4,
        (info, gq, gk, gv, gqt, gkt, gvt, x, r1, w_query, w_key, w_value, vecs, bup),
        scalars=(0,),
        name="project_back",
        mib=16,
    )
    in_got = there(ins)
    if fast:
        q_got = pp_core(q_send)
        qkv = Sum(
            "qkv_", [q_got, o_got], [q_keep, o_keep],
            [(0, ((0, 80), (0, half))), (1, ((0, 48), (0, half)))],
            [(0, ((80, 160), (0, half)))],
        )
        f32 = lambda *d: shape(d, F32)
        down.three()
        qkv.one()
        up.three()
        down.four()
        qkv.two()
        up.four()
        down.five()
        qkv.three()
        down.six()
        up.five()
        grad_tokens = joined(in_got, "join_in")
        qkv.four()
        up.six()
        (g_down,) = down.end(down_kernel, [f32(rs, ff)])
        qkv.five()
        (g_up,) = up.end(up_kernel, [f32(width, ff // n)])
        qkv.six()
        *g_qkv, g_out, vs = qkv.end(qkv_kernel, [f32(rs, width)] * 4 + [f32(16, rs)])
        g_down, g_out, g_qkv = g_down.T, g_out.T, [g.T for g in g_qkv]
        small = [vs[i] for i in range(8)] + [vs[8:12].reshape(-1)]
    else:
        grad_tokens = joined(in_got, "join_in")

        def total(send, keep, dim):
            h = keep.astype(F32) + pp_core(send).astype(F32)
            h = h + pp_y(h.astype(BF)).astype(F32)
            return lax.psum_scatter(h, "dp", scatter_dimension=dim, tiled=True).astype(BF)

        def whole(send, keep, dim, along):
            mine = total(send, keep, dim)
            other = pp_core(mine)
            lo, hi = jnp.where(core == 0, mine, other), jnp.where(core == 0, other, mine)
            return jnp.concatenate([lo, hi], axis=along).astype(F32)

        g_down = whole(d_send[0, 0], d_keep[0, 0], 0, 1).T
        g_up = whole(u_send[0, 0], u_keep[0, 0], 1, 0)
        g_out = whole(o_send[0, 0], o_keep[0, 0], 0, 1).T
        g_qkv = [
            whole(q_send[0, 0, w * width : (w + 1) * width], q_keep[0, 0, w * width : (w + 1) * width], 0, 1).T
            for w in range(3)
        ]
        flat = lax.psum(jnp.concatenate([vecs.reshape(-1), bup[0]]), ("dp", "seq"))
        mine = width // n_dp
        small = [
            lax.dynamic_slice_in_dim(flat, i * width + dp * mine, mine) for i in range(8)
        ] + [lax.dynamic_slice_in_dim(flat, 8 * width + dp * 4 * mine, 4 * mine)]

    bq, bv, b_o, gain1, shift1, b_d, gain2, shift2, b_u = small
    return (
        output, pooled, grad_tokens, g_qkv[0], bq, g_qkv[1], g_qkv[2], bv, g_out, b_o, gain1, shift1,
        g_up, b_u, g_down, b_d, gain2, shift2,
    )


def solution(mesh):
    rows = P("dp", "seq", None)
    placed = (rows, P("dp", None)) + (P(),) * 15 + (rows, P("dp", None, None))
    col, one = P(None, "dp"), P("dp")
    return jax.shard_map(
        functools.partial(local, mesh.shape["dp"], mesh.shape["seq"]),
        mesh=mesh,
        in_specs=placed,
        out_specs=(
            rows, P("dp", None, None), rows, col, one, col, col, one, col, one, one, one,
            col, one, col, one, one, one,
        ),
        check_vma=False,
    )
```

time: 303 us -> 194 us (0.64)
  waiting for transfers between devices: 126 us -> 66.3 us
  other arithmetic: 22 us -> 2.25 us
  Pallas kernels: 98.7 us -> 79 us
  local copies, waits for them, and re-layouts: 11.3 us -> 4.94 us
  starting transfers between devices: 43 us -> 39.5 us
    ppermute x67 -> x43, waiting for transfers between devices: 126 us -> 66.3 us  [the longest x9 27.8 us: local(): pp_y = lambda a: lax.ppermute(a, 'seq', xor[2])]
    pallas_call x9 -> x32, Pallas kernels: 98.7 us -> 79 us  [call(): pl.pallas_call(body, out_shape=[*outs, shape((8, LANES), F32)], in_specs=...]
    convert_element_type x50 -> x0, other arithmetic: 9.62 us -> none  [the longest x24 5.04 us: add(): return (a.astype(F32) + b.astype(F32)).astype(BF)]
    transpose x4 -> x0, other arithmetic: 5.02 us -> none  [the longest x2 3.17 us: local(): g_qkv.append(jnp.concatenate(part, axis=0).astype(F32).T)]
    reshape x8, local copies, waits for them, and re-layouts: 4.73 us -> 0.04 us  [vec(): return v.astype(F32).reshape(1, -1)]
    ppermute x67 -> x43, starting transfers between devices: 43 us -> 39.5 us  [the longest x12 16.9 us: pp_dp(): return lambda a: lax.ppermute(a, 'dp', [(i, i ^ bit) for i in range(n_dp)])]
  transfers between devices with their start and end apart: 67 -> 43, of which waited for: 39 -> 15; matrix products, arithmetic and copies ran while one was open for 10% -> 1% of each run, Pallas kernels for 16% -> 28%
where the time goes in v2:
time: 194 us; the launch traced here: 193 us
  Pallas kernels  79 us (41%)
  waiting for transfers between devices  66.3 us (34%)
  starting transfers between devices  39.5 us (20%)
  local copies, waits for them, and re-layouts  4.94 us (3%)
  other arithmetic  2.25 us (1%)
    pallas_call x32, Pallas kernels, call(): pl.pallas_call(body, out_shape=[*outs, shape((8, LANES), F32)], in_specs=...  79 us
    ppermute x9, waiting for transfers between devices, local(): pp_y = lambda a: lax.ppermute(a, 'seq', xor[2])  27.8 us
    ppermute x12, waiting for transfers between devices, pp_dp(): return lambda a: lax.ppermute(a, 'dp', [(i, i ^ bit) for i in range(n_dp)])  26.7 us
    ppermute x12, starting transfers between devices, pp_dp(): return lambda a: lax.ppermute(a, 'dp', [(i, i ^ bit) for i in range(n_dp)])  16.9 us
    ppermute x9, starting transfers between devices, local(): pp_y = lambda a: lax.ppermute(a, 'seq', xor[2])  9.53 us
    ppermute x9, waiting for transfers between devices, there(): lax.ppermute(parts[r], 'seq', xor[r])  7.32 us
    ppermute x9, starting transfers between devices, there(): lax.ppermute(parts[r], 'seq', xor[r])  6.37 us
    ppermute x6, starting transfers between devices, rel(): lax.ppermute(parts[r], 'seq', xor[r])  5.39 us
  transfers between devices with their start and end apart: 43, of which 15 were waited for; matrix products, arithmetic and copies ran while one was open for 1% of the time, Pallas kernels for 28%

profile of v2, /device:TPU:0, one launch (start us, length us, event | category | flops | bytes accessed | tf_op | source)
XLA Modules:
  0.0 193.4 jit_solution(13101732428255016048)
XLA Ops:
  0.8 1.8 split_tokens.1
  3.1 2.6 %collective-permute-start.1 = (bf16[128,768]{1,0:T(8,128)(2,1)S(1)}, bf16[128,768]{1,0:T(8,128)(2,1)S(1)}, u32[]{:S(2)}, u32[]{:S(2)}) collective-permute-start(bf16[128,768]{1,0:T(8,128)(2,1)S(1)} %get-tuple-element.152), channel_id=1, source_target_pairs={{0,2},{1,3},{2,0},{3,1},{4,6},{5,7},{6,4},{7,5},{8,10},{9,11},{10,... | collective-permute-start | bytes 589832 | tf_op jit(solution)/shard_map/ppermute | solution.py:598
  5.9 1.8 split_grads.1
  7.9 1.9 collective-permute-start.4
  9.8 0.7 convert_bitcast_fusion
  11.1 0.8 subtract_convert_fusion
  12.3 2.9 %collective-permute-done.2.refs_3_ = bf16[128,768]{1,0:T(8,128)(2,1)S(1)} collective-permute-done((bf16[128,768]{1,0:T(8,128)(2,1)S(1)}, bf16[128,768]{1,0:T(8,128)(2,1)S(1)}, u32[]{:S(2)}, u32[]{:S(2)}) %collective-permute-start.2) | collective-permute-done | bytes 196640 | tf_op jit(solution)/shard_map/ppermute | solution.py:598
  15.2 14.4 %attend.1 = (bf16[512,768]{1,0:T(8,128)(2,1)}, bf16[512,768]{1,0:T(8,128)(2,1)}, bf16[512,768]{1,0:T(8,128)(2,1)}, bf16[512,768]{1,0:T(8,128)(2,1)}, f32[512,768...) custom-call(bf16[128,768]{1,0:T(8,128)(2,1)S(1)} %get-tuple-element., ...), custom_call_target="tpu_custom_call" | custom-call | flops 1000000000 | bytes 1000000 | tf_op jit(solution)/shard_map/attend/pallas_call | solution.py:453
  29.6 2.3 %copy-done.1 = bf16[768,3072]{1,0:T(8,128)(2,1)S(1)} copy-done((bf16[768,3072]{1,0:T(8,128)(2,1)S(1)}, bf16[768,3072]{1,0:T(8,128)(2,1)}, u32[]{:S(2)}) %copy-start.1) | copy-done | bytes 4718616
  32.0 14.6 %ffn.1 = (bf16[128,768]{1,0:T(8,128)(2,1)S(1)}, bf16[128,768]{1,0:T(8,128)(2,1)S(1)}, bf16[128,768]{1,0:T(8,128)(2,1)S(1)}, bf16[128,768]{1,0:T(8,128)(2,1)S(1)}...) custom-call(s32[16]{0:T(128)S(1)} %concatenate.9.refs_0_, ...), custom_call_target="tpu_custom_call" | custom-call | flops 1000000000 | bytes 1000000 | tf_op jit(solution)/shard_map/ffn/pallas_call | solution.py:453
  47.0 7.8 %ffn_back.1 = (bf16[2,8,192,384]{3,2,1,0:T(8,128)(2,1)S(1)}, bf16[2,8,192,384]{3,2,1,0:T(8,128)(2,1)S(1)}, f32[8,3072]{1,0:T(8,128)S(1)}, bf16[512,3072]{1,0:T(8,128)(2,1)S(1)}, f32[8,128]{1,0:T(8,128)S(1)}) custom-call(s32[16]{0:T(128)S(1)} %concatenate.9.refs_0_, f32[512,768]{1,0:T(8,128)S(1)} %get-tuple-element.166.refs_1_, ...), custom_call_target="tpu_custom_call" | custom-call | flops 1000000000 | bytes 1000000 | tf_op jit(solution)/shard_map/ffn_back/pallas_call | solution.py:453
  55.4 1.9 %collective-permute-start.7 = (bf16[128,768]{1,0:T(8,128)(2,1)S(1)}, bf16[128,768]{1,0:T(8,128)(2,1)S(1)}, u32[]{:S(2)}, u32[]{:S(2)}) collective-permute-start(bf16[128,768]{1,0:T(8,128)(2,1)S(1)} %get-tuple-element.164), channel_id=1, source_target_pairs={{0,2},{1,3},{2,0},{3,1},{4,6},{5,7},{6,4},{7,5},{8,10},{9,11},{10,... | collective-permute-start | bytes 589832 | tf_op jit(solution)/shard_map/ppermute | solution.py:726
  57.6 0.6 down_one.1
  58.2 0.6 copy-done.2
  59.4 9.3 %norm_back.1 = (f32[512,768]{1,0:T(8,128)}, bf16[512,768]{1,0:T(8,128)(2,1)S(1)}, bf16[512,128]{1,0:T(8,128)(2,1)S(1)}, f32[8,768]{1,0:T(8,128)S(1)}, bf16[2,8,4...) custom-call(s32[16]{0:T(128)S(1)} %concatenate.9.refs_0_, ...), custom_call_target="tpu_custom_call" | custom-call | flops 1000000000 | bytes 1000000 | tf_op jit(solution)/shard_map/norm_back/pallas_call | solution.py:453
  68.7 2.0 %collective-permute-start.11 = (f32[8,768]{1,0:T(8,128)S(1)}, f32[8,768]{1,0:T(8,128)S(1)}, u32[]{:S(2)}, u32[]{:S(2)}) collective-permute-start(f32[8,768]{1,0:T(8,128)S(1)} %slice_divide_fusion.refs_1_), channel_id=1, source_target_pairs={{0,2},{1,3},{2,0},{3,1},{4,6},{5,7},{6,4},{7,5},{8,10},{9,11},{10,... | collective-permute-start | bytes 73736 | tf_op jit(solution)/shard_map/ppermute | solution.py:726
  70.7 1.6 collective-permute-start.16
  72.2 1.5 join_out.1
  73.7 1.3 collective-permute-start.17
  75.0 1.2 join_pool.1
  76.2 0.6 up_one.1
  76.8 0.6 collective-permute-start.14
  77.5 0.7 collective-permute-start.15
  78.2 10.6 %attend_back.1 = (bf16[512,768]{1,0:T(8,128)(2,1)S(1)}, bf16[512,768]{1,0:T(8,128)(2,1)S(1)}, bf16[512,768]{1,0:T(8,128)(2,1)S(1)}, bf16[768,512]{1,0:T(8,128)(2...) custom-call(bf16[512,768]{1,0:T(8,128)(2,1)S(1)} %copy-done.10, ...), custom_call_target="tpu_custom_call" | custom-call | flops 1000000000 | bytes 1000000 | tf_op jit(solution)/shard_map/attend_back/pallas_call | solution.py:453
  88.9 1.0 collective-permute-done.17.refs_1_
  90.2 8.7 %collective-permute-done.14.refs_0_ = bf16[2,4,96,384]{3,2,1,0:T(8,128)(2,1)S(1)} collective-permute-done((bf16[2,4,96,384]{3,2,1,0:T(8,128)(2,1)S(1)}, bf16[2,4,96,384]{3,2,1,0:T(8,128)(2,1)S(1)}, u32[]{:S(2)}, u32[]{:S(2)}) %collective-permute-start.14) | collective-permute-done | bytes 589856 | tf_op jit(solution)/shard_map/ppermute | solution.py:666
  98.9 2.9 %collective-permute-done.15.refs_1_ = bf16[8,96,384]{2,1,0:T(8,128)(2,1)S(1)} collective-permute-done((bf16[8,96,384]{2,1,0:T(8,128)(2,1)S(1)}, bf16[8,96,384]{2,1,0:T(8,128)(2,1)S(1)}, u32[]{:S(2)}, u32[]{:S(2)}) %collective-permute-start.15) | collective-permute-done | bytes 589856 | tf_op jit(solution)/shard_map/ppermute | solution.py:663
  102.2 4.5 %project_back.1 = (bf16[2,8,160,384]{3,2,1,0:T(8,128)(2,1)S(1)}, bf16[2,8,160,384]{3,2,1,0:T(8,128)(2,1)S(1)}, bf16[128,768]{1,0:T(8,128)(2,1)S(1)}, bf16[128,76...) custom-call(s32[16]{0:T(128)S(1)} %concatenate.9.refs_0_, ...), custom_call_target="tpu_custom_call" | custom-call | flops 1000000000 | bytes 1000000 | tf_op jit(solution)/shard_map/project_back/pallas_call | solution.py:453
  107.3 1.5 collective-permute-start.25
  109.3 6.9 %collective-permute-done.25.refs_0_ = bf16[4,48,768]{2,1,0:T(8,128)(2,1)S(1)} collective-permute-done((bf16[4,48,768]{2,1,0:T(8,128)(2,1)S(1)}, bf16[4,48,768]{2,1,0:T(8,128)(2,1)S(1)}, u32[]{:S(2)}, u32[]{:S(2)}) %collective-permute-start.25) | collective-permute-done | bytes 294944 | tf_op jit(solution)/shard_map/ppermute | solution.py:663
  116.3 1.2 collective-permute-done.26.refs_1_
  117.7 0.6 qkv_one.1
  118.3 0.6 collective-permute-start.28
  119.2 1.7 collective-permute-start.21
  120.9 1.5 collective-permute-start.22
  122.4 1.6 collective-permute-start.30
  124.0 13.0 %collective-permute-done.21.refs_0_ = bf16[4,96,384]{2,1,0:T(8,128)(2,1)S(1)} collective-permute-done((bf16[4,96,384]{2,1,0:T(8,128)(2,1)S(1)}, bf16[4,96,384]{2,1,0:T(8,128)(2,1)S(1)}, u32[]{:S(2)}, u32[]{:S(2)}) %collective-permute-start.21) | collective-permute-done | bytes 294944 | tf_op jit(solution)/shard_map/ppermute | solution.py:663
  137.0 6.1 %collective-permute-done.22.refs_1_ = bf16[4,96,384]{2,1,0:T(8,128)(2,1)S(1)} collective-permute-done((bf16[4,96,384]{2,1,0:T(8,128)(2,1)S(1)}, bf16[4,96,384]{2,1,0:T(8,128)(2,1)S(1)}, u32[]{:S(2)}, u32[]{:S(2)}) %collective-permute-start.22) | collective-permute-done | bytes 294944 | tf_op jit(solution)/shard_map/ppermute | solution.py:666
  143.2 1.6 collective-permute-start.27
  145.2 0.7 collective-permute-start.34
  145.9 2.6 %collective-permute-start.32 = (bf16[96,768]{1,0:T(8,128)(2,1)S(1)}, bf16[96,768]{1,0:T(8,128)(2,1)S(1)}, u32[]{:S(2)}, u32[]{:S(2)}) collective-permute-start(bf16[96,768]{1,0:T(8,128)(2,1)S(1)} %get-tuple-element.246), channel_id=1, source_target_pairs={{0,16},{4,20},{8,24},{12,28},{16,0},{20,4},{24,8},{28,12},{1,17},{... | collective-permute-start | bytes 442376 | tf_op jit(solution)/shard_map/ppermute | solution.py:666
  149.0 4.3 %collective-permute-done.27.refs_0_ = bf16[2,192,384]{2,1,0:T(8,128)(2,1)S(1)} collective-permute-done((bf16[2,192,384]{2,1,0:T(8,128)(2,1)S(1)}, bf16[2,192,384]{2,1,0:T(8,128)(2,1)S(1)}, u32[]{:S(2)}, u32[]{:S(2)}) %collective-permute-start.27) | collective-permute-done | bytes 294944 | tf_op jit(solution)/shard_map/ppermute | solution.py:666
  153.4 0.7 collective-permute-start.33
  154.1 2.6 %collective-permute-start.31 = (bf16[192,384]{1,0:T(8,128)(2,1)S(1)}, bf16[192,384]{1,0:T(8,128)(2,1)S(1)}, u32[]{:S(2)}, u32[]{:S(2)}) collective-permute-start(bf16[192,384]{1,0:T(8,128)(2,1)S(1)} %get-tuple-element.244), channel_id=1, source_target_pairs={{0,16},{4,20},{8,24},{12,28},{16,0},{20,4},{24,8},{28,12},{1,17},{... | collective-permute-start | bytes 442376 | tf_op jit(solution)/shard_map/ppermute | solution.py:666
  156.9 1.8 collective-permute-start.36
  158.7 1.3 collective-permute-start.19
  159.9 0.6 collective-permute-start.20
  160.5 0.6 down_six.1
  161.2 1.3 collective-permute-start.39
  162.5 3.9 %collective-permute-done.19.refs_3_ = bf16[128,768]{1,0:T(8,128)(2,1)S(1)} collective-permute-done((bf16[128,768]{1,0:T(8,128)(2,1)S(1)}, bf16[128,768]{1,0:T(8,128)(2,1)S(1)}, u32[]{:S(2)}, u32[]{:S(2)}) %collective-permute-start.19) | collective-permute-done | bytes 196640 | tf_op jit(solution)/shard_map/ppermute | solution.py:726
  166.4 3.4 %collective-permute-done.20.refs_4_ = bf16[128,768]{1,0:T(8,128)(2,1)S(1)} collective-permute-done((bf16[128,768]{1,0:T(8,128)(2,1)S(1)}, bf16[128,768]{1,0:T(8,128)(2,1)S(1)}, u32[]{:S(2)}, u32[]{:S(2)}) %collective-permute-start.20) | collective-permute-done | bytes 196640 | tf_op jit(solution)/shard_map/ppermute | solution.py:726
  169.8 1.5 join_in.1
  171.4 1.3 collective-permute-start.37
  172.7 0.6 collective-permute-done.39.refs_2_
  173.4 0.6 up_six.1
  174.0 1.6 down_end.1
  175.7 6.4 %collective-permute-done.37.refs_0_ = bf16[208,384]{1,0:T(8,128)(2,1)S(1)} collective-permute-done((bf16[208,384]{1,0:T(8,128)(2,1)S(1)}, bf16[208,384]{1,0:T(8,128)(2,1)S(1)}, u32[]{:S(2)}, u32[]{:S(2)}) %collective-permute-start.37) | collective-permute-done | bytes 159776 | tf_op jit(solution)/shard_map/ppermute | solution.py:666
  182.1 1.3 collective-permute-start.40
  183.4 1.6 up_end.1
  185.1 3.2 %collective-permute-done.40.refs_2_ = bf16[208,384]{1,0:T(8,128)(2,1)S(1)} collective-permute-done((bf16[208,384]{1,0:T(8,128)(2,1)S(1)}, bf16[208,384]{1,0:T(8,128)(2,1)S(1)}, u32[]{:S(2)}, u32[]{:S(2)}) %collective-permute-start.40) | collective-permute-done | bytes 159776 | tf_op jit(solution)/shard_map/ppermute | solution.py:663
  188.3 0.6 qkv_six.1
  189.0 1.6 collective-permute-done.42.refs_2_
  190.6 1.6 qkv_end.1
  192.7 0.7 reshape.165
  (137 shorter events, 8.0 us)
Async XLA Ops:
  2.6 9.5 %collective-permute-start = (bf16[128,768]{1,0:T(8,128)(2,1)S(1)}, bf16[128,768]{1,0:T(8,128)(2,1)S(1)}, u32[]{:S(2)}, u32[]{:S(2)}) collective-permute-start(bf16[128,768]{1,0:T(8,128)(2,1)S(1)} %get-tuple-element.151), channel_id=1, source_target_pairs={{0,1},{1,0},{2,3},{3,2},{4,5},{5,4},{6,7},{7,6},{8,9},{9,8},{10,11... | collective-permute-start | bytes 589832 | tf_op jit(solution)/shard_map/ppermute | solution.py:598
  3.1 9.2 %collective-permute-start.1 = (bf16[128,768]{1,0:T(8,128)(2,1)S(1)}, bf16[128,768]{1,0:T(8,128)(2,1)S(1)}, u32[]{:S(2)}, u32[]{:S(2)}) collective-permute-start(bf16[128,768]{1,0:T(8,128)(2,1)S(1)} %get-tuple-element.152), channel_id=1, source_target_pairs={{0,2},{1,3},{2,0},{3,1},{4,6},{5,7},{6,4},{7,5},{8,10},{9,11},{10,... | collective-permute-start | bytes 589832 | tf_op jit(solution)/shard_map/ppermute | solution.py:598
  5.7 9.4 %collective-permute-start.2 = (bf16[128,768]{1,0:T(8,128)(2,1)S(1)}, bf16[128,768]{1,0:T(8,128)(2,1)S(1)}, u32[]{:S(2)}, u32[]{:S(2)}) collective-permute-start(bf16[128,768]{1,0:T(8,128)(2,1)S(1)} %get-tuple-element.153), channel_id=1, source_target_pairs={{0,3},{1,2},{2,1},{3,0},{4,7},{5,6},{6,5},{7,4},{8,11},{9,10},{10,... | collective-permute-start | bytes 589832 | tf_op jit(solution)/shard_map/ppermute | solution.py:598
  5.8 6.1 %copy-start.15 = (bf16[768]{0:T(1024)(128)(2,1)S(1)}, bf16[768]{0:T(1024)(128)(2,1)}, u32[]{:S(2)}) copy-start(bf16[768]{0:T(1024)(128)(2,1)} %param.22) | copy-start | bytes 4612
  5.8 6.2 %copy-start.16 = (bf16[768]{0:T(1024)(128)(2,1)S(1)}, bf16[768]{0:T(1024)(128)(2,1)}, u32[]{:S(2)}) copy-start(bf16[768]{0:T(1024)(128)(2,1)} %param.25) | copy-start | bytes 4612
  5.8 6.2 %copy-start.17 = (bf16[768]{0:T(1024)(128)(2,1)S(1)}, bf16[768]{0:T(1024)(128)(2,1)}, u32[]{:S(2)}) copy-start(bf16[768]{0:T(1024)(128)(2,1)} %param.27) | copy-start | bytes 4612
  5.8 6.2 %copy-start.18 = (bf16[768]{0:T(1024)(128)(2,1)S(1)}, bf16[768]{0:T(1024)(128)(2,1)}, u32[]{:S(2)}) copy-start(bf16[768]{0:T(1024)(128)(2,1)} %param.28) | copy-start | bytes 4612
  5.8 6.2 %copy-start.19 = (bf16[768]{0:T(1024)(128)(2,1)S(1)}, bf16[768]{0:T(1024)(128)(2,1)}, u32[]{:S(2)}) copy-start(bf16[768]{0:T(1024)(128)(2,1)} %param.29) | copy-start | bytes 4612
  5.8 6.2 %copy-start.14 = (bf16[3072]{0:T(1024)(128)(2,1)S(1)}, bf16[3072]{0:T(1024)(128)(2,1)}, u32[]{:S(2)}) copy-start(bf16[3072]{0:T(1024)(128)(2,1)} %param.31) | copy-start | bytes 18436
  5.8 6.2 %copy-start.20 = (bf16[768]{0:T(1024)(128)(2,1)S(1)}, bf16[768]{0:T(1024)(128)(2,1)}, u32[]{:S(2)}) copy-start(bf16[768]{0:T(1024)(128)(2,1)} %param.33) | copy-start | bytes 4612
  5.8 6.3 %copy-start.21 = (bf16[768]{0:T(1024)(128)(2,1)S(1)}, bf16[768]{0:T(1024)(128)(2,1)}, u32[]{:S(2)}) copy-start(bf16[768]{0:T(1024)(128)(2,1)} %param.34) | copy-start | bytes 4612
  5.9 6.3 %copy-start.22 = (bf16[768]{0:T(1024)(128)(2,1)S(1)}, bf16[768]{0:T(1024)(128)(2,1)}, u32[]{:S(2)}) copy-start(bf16[768]{0:T(1024)(128)(2,1)} %param.35) | copy-start | bytes 4612
  7.7 21.9 %collective-permute-start.3 = (bf16[128,768]{1,0:T(8,128)(2,1)S(1)}, bf16[128,768]{1,0:T(8,128)(2,1)S(1)}, u32[]{:S(2)}, u32[]{:S(2)}) collective-permute-start(bf16[128,768]{1,0:T(8,128)(2,1)S(1)} %get-tuple-element.158), channel_id=1, source_target_pairs={{0,1},{1,0},{2,3},{3,2},{4,5},{5,4},{6,7},{7,6},{8,9},{9,8},{10,11... | collective-permute-start | bytes 589832 | tf_op jit(solution)/shard_map/ppermute | solution.py:598
  7.9 21.7 %collective-permute-start.4 = (bf16[128,768]{1,0:T(8,128)(2,1)S(1)}, bf16[128,768]{1,0:T(8,128)(2,1)S(1)}, u32[]{:S(2)}, u32[]{:S(2)}) collective-permute-start(bf16[128,768]{1,0:T(8,128)(2,1)S(1)} %get-tuple-element.159), channel_id=1, source_target_pairs={{0,2},{1,3},{2,0},{3,1},{4,6},{5,7},{6,4},{7,5},{8,10},{9,11},{10,... | collective-permute-start | bytes 589832 | tf_op jit(solution)/shard_map/ppermute | solution.py:598
  12.2 17.5 %collective-permute-start.5 = (bf16[128,768]{1,0:T(8,128)(2,1)S(1)}, bf16[128,768]{1,0:T(8,128)(2,1)S(1)}, u32[]{:S(2)}, u32[]{:S(2)}) collective-permute-start(bf16[128,768]{1,0:T(8,128)(2,1)S(1)} %get-tuple-element.160), channel_id=1, source_target_pairs={{0,3},{1,2},{2,1},{3,0},{4,7},{5,6},{6,5},{7,4},{8,11},{9,10},{10,... | collective-permute-start | bytes 589832 | tf_op jit(solution)/shard_map/ppermute | solution.py:598
  15.2 14.5 %copy-start = (bf16[3072,768]{1,0:T(8,128)(2,1)S(1)}, bf16[3072,768]{1,0:T(8,128)(2,1)}, u32[]{:S(2)}) copy-start(bf16[3072,768]{1,0:T(8,128)(2,1)} %refs_3_.2) | copy-start | bytes 14155780
  29.6 2.3 %copy-start.1 = (bf16[768,3072]{1,0:T(8,128)(2,1)S(1)}, bf16[768,3072]{1,0:T(8,128)(2,1)}, u32[]{:S(2)}) copy-start(bf16[768,3072]{1,0:T(8,128)(2,1)} %refs_3_.3) | copy-start | bytes 14155780
  32.0 26.2 %slice-start = ((s8[4718592]{0:T(1024)(128)(4,1)}), s8[4194304]{0:T(1024)(128)(4,1)S(1)}, s32[]{:S(2)}) async-start(s8[4718592]{0:T(1024)(128)(4,1)} %bitcast.37), calls=%async_computation | async-start | bytes 8388608
  46.5 10.9 %collective-permute-start.9 = (bf16[2,8,48,1536]{3,2,1,0:T(8,128)(2,1)S(1)}, bf16[2,8,48,1536]{3,2,1,0:T(8,128)(2,1)S(1)}, u32[]{:S(2)}, u32[]{:S(2)}) collective-permute-start(bf16[2,8,48,1536]{3,2,1,0:T(8,128)(2,1)S(1)} %get-tuple-element.172), channel_id=1, source_target_pairs={{0,1},{1,0},{2,3},{3,2},{4,5},{5,4},{6,7},{7,6},{8,9},{9,8},{10,11... | collective-permute-start | bytes 7077896 | tf_op jit(solution)/shard_map/ppermute | solution.py:662
  47.0 11.3 %slice-start.1 = ((s8[4718592]{0:T(1024)(128)(4,1)}), s8[524288]{0:T(1024)(128)(4,1)S(1)}, s32[]{:S(2)}) async-start(s8[4718592]{0:T(1024)(128)(4,1)} %bitcast.37), calls=%async_computation.1 | async-start | bytes 1048576
  54.8 21.4 %collective-permute-start.13 = (bf16[2,8,192,384]{3,2,1,0:T(8,128)(2,1)S(1)}, bf16[2,8,192,384]{3,2,1,0:T(8,128)(2,1)S(1)}, u32[]{:S(2)}, u32[]{:S(2)}) collective-permute-start(bf16[2,8,192,384]{3,2,1,0:T(8,128)(2,1)S(1)} %get-tuple-element.187), channel_id=1, source_target_pairs={{0,1},{1,0},{2,3},{3,2},{4,5},{5,4},{6,7},{7,6},{8,9},{9,8},{10,11... | collective-permute-start | bytes 7077896 | tf_op jit(solution)/shard_map/ppermute | solution.py:662
  55.0 13.6 %collective-permute-start.6 = (bf16[128,768]{1,0:T(8,128)(2,1)S(1)}, bf16[128,768]{1,0:T(8,128)(2,1)S(1)}, u32[]{:S(2)}, u32[]{:S(2)}) collective-permute-start(bf16[128,768]{1,0:T(8,128)(2,1)S(1)} %get-tuple-element.163), channel_id=1, source_target_pairs={{0,1},{1,0},{2,3},{3,2},{4,5},{5,4},{6,7},{7,6},{8,9},{9,8},{10,11... | collective-permute-start | bytes 589832 | tf_op jit(solution)/shard_map/ppermute | solution.py:726
  55.4 15.3 %collective-permute-start.7 = (bf16[128,768]{1,0:T(8,128)(2,1)S(1)}, bf16[128,768]{1,0:T(8,128)(2,1)S(1)}, u32[]{:S(2)}, u32[]{:S(2)}) collective-permute-start(bf16[128,768]{1,0:T(8,128)(2,1)S(1)} %get-tuple-element.164), channel_id=1, source_target_pairs={{0,2},{1,3},{2,0},{3,1},{4,6},{5,7},{6,4},{7,5},{8,10},{9,11},{10,... | collective-permute-start | bytes 589832 | tf_op jit(solution)/shard_map/ppermute | solution.py:726
  57.3 13.4 %collective-permute-start.8 = (bf16[128,768]{1,0:T(8,128)(2,1)S(1)}, bf16[128,768]{1,0:T(8,128)(2,1)S(1)}, u32[]{:S(2)}, u32[]{:S(2)}) collective-permute-start(bf16[128,768]{1,0:T(8,128)(2,1)S(1)} %get-tuple-element.165), channel_id=1, source_target_pairs={{0,3},{1,2},{2,1},{3,0},{4,7},{5,6},{6,5},{7,4},{8,11},{9,10},{10,... | collective-permute-start | bytes 589832 | tf_op jit(solution)/shard_map/ppermute | solution.py:726
  57.4 16.3 %collective-permute-start.10 = (f32[8,768]{1,0:T(8,128)S(1)}, f32[8,768]{1,0:T(8,128)S(1)}, u32[]{:S(2)}, u32[]{:S(2)}) collective-permute-start(f32[8,768]{1,0:T(8,128)S(1)} %slice_divide_fusion.refs_1_), channel_id=1, source_target_pairs={{0,1},{1,0},{2,3},{3,2},{4,5},{5,4},{6,7},{7,6},{8,9},{9,8},{10,11... | collective-permute-start | bytes 73736 | tf_op jit(solution)/shard_map/ppermute | solution.py:726
  68.7 6.4 %collective-permute-start.11 = (f32[8,768]{1,0:T(8,128)S(1)}, f32[8,768]{1,0:T(8,128)S(1)}, u32[]{:S(2)}, u32[]{:S(2)}) collective-permute-start(f32[8,768]{1,0:T(8,128)S(1)} %slice_divide_fusion.refs_1_), channel_id=1, source_target_pairs={{0,2},{1,3},{2,0},{3,1},{4,6},{5,7},{6,4},{7,5},{8,10},{9,11},{10,... | collective-permute-start | bytes 73736 | tf_op jit(solution)/shard_map/ppermute | solution.py:726
  70.7 4.3 %collective-permute-start.12 = (f32[8,768]{1,0:T(8,128)S(1)}, f32[8,768]{1,0:T(8,128)S(1)}, u32[]{:S(2)}, u32[]{:S(2)}) collective-permute-start(f32[8,768]{1,0:T(8,128)S(1)} %slice_divide_fusion.refs_1_), channel_id=1, source_target_pairs={{0,3},{1,2},{2,1},{3,0},{4,7},{5,6},{6,5},{7,4},{8,11},{9,10},{10,... | collective-permute-start | bytes 73736 | tf_op jit(solution)/shard_map/ppermute | solution.py:726
  70.7 18.2 %collective-permute-start.16 = (bf16[2,4,48,768]{3,2,1,0:T(8,128)(2,1)S(1)}, bf16[2,4,48,768]{3,2,1,0:T(8,128)(2,1)S(1)}, u32[]{:S(2)}, u32[]{:S(2)}) collective-permute-start(bf16[2,4,48,768]{3,2,1,0:T(8,128)(2,1)S(1)} %get-tuple-element.207), channel_id=1, source_target_pairs={{0,4},{4,0},{8,12},{12,8},{16,20},{20,16},{24,28},{28,24},{1,5},{5... | collective-permute-start | bytes 1769480 | tf_op jit(solution)/shard_map/ppermute | solution.py:666
  73.7 16.2 %collective-permute-start.17 = (bf16[8,48,768]{2,1,0:T(8,128)(2,1)S(1)}, bf16[8,48,768]{2,1,0:T(8,128)(2,1)S(1)}, u32[]{:S(2)}, u32[]{:S(2)}) collective-permute-start(bf16[8,48,768]{2,1,0:T(8,128)(2,1)S(1)} %get-tuple-element.208), channel_id=1, source_target_pairs={{0,2},{1,3},{2,0},{3,1},{4,6},{5,7},{6,4},{7,5},{8,10},{9,11},{10,... | collective-permute-start | bytes 1769480 | tf_op jit(solution)/shard_map/ppermute | solution.py:663
  76.2 1.9 copy-start.11
  76.2 1.9 copy-start.12
  76.2 1.9 copy-start.13
  76.8 22.1 %collective-permute-start.14 = (bf16[2,4,96,384]{3,2,1,0:T(8,128)(2,1)S(1)}, bf16[2,4,96,384]{3,2,1,0:T(8,128)(2,1)S(1)}, u32[]{:S(2)}, u32[]{:S(2)}) collective-permute-start(bf16[2,4,96,384]{3,2,1,0:T(8,128)(2,1)S(1)} %get-tuple-element.203), channel_id=1, source_target_pairs={{0,4},{4,0},{8,12},{12,8},{16,20},{20,16},{24,28},{28,24},{1,5},{5... | collective-permute-start | bytes 1769480 | tf_op jit(solution)/shard_map/ppermute | solution.py:666
  77.5 24.4 %collective-permute-start.15 = (bf16[8,96,384]{2,1,0:T(8,128)(2,1)S(1)}, bf16[8,96,384]{2,1,0:T(8,128)(2,1)S(1)}, u32[]{:S(2)}, u32[]{:S(2)}) collective-permute-start(bf16[8,96,384]{2,1,0:T(8,128)(2,1)S(1)} %get-tuple-element.204), channel_id=1, source_target_pairs={{0,2},{1,3},{2,0},{3,1},{4,6},{5,7},{6,4},{7,5},{8,10},{9,11},{10,... | collective-permute-start | bytes 1769480 | tf_op jit(solution)/shard_map/ppermute | solution.py:663
  89.9 12.3 %copy-start.7 = (f32[512,768]{1,0:T(8,128)S(1)}, f32[512,768]{1,0:T(8,128)}, u32[]{:S(2)}) copy-start(f32[512,768]{1,0:T(8,128)} %get-tuple-element.198.refs_8_) | copy-start | bytes 4718596
  89.9 12.3 %copy-start.8 = (bf16[512,768]{1,0:T(8,128)(2,1)S(1)}, bf16[512,768]{1,0:T(8,128)(2,1)}, u32[]{:S(2)}) copy-start(bf16[512,768]{1,0:T(8,128)(2,1)} %get-tuple-element.197.refs_7_) | copy-start | bytes 2359300
  90.2 12.0 %copy-start.3 = (bf16[768,768]{1,0:T(8,128)(2,1)S(1)}, bf16[768,768]{1,0:T(8,128)(2,1)}, u32[]{:S(2)}) copy-start(bf16[768,768]{1,0:T(8,128)(2,1)} %refs_9_.1) | copy-start | bytes 3538948
  90.2 12.0 %copy-start.4 = (bf16[768,768]{1,0:T(8,128)(2,1)S(1)}, bf16[768,768]{1,0:T(8,128)(2,1)}, u32[]{:S(2)}) copy-start(bf16[768,768]{1,0:T(8,128)(2,1)} %refs_10_.1) | copy-start | bytes 3538948
  90.2 12.0 %copy-start.5 = (bf16[768,768]{1,0:T(8,128)(2,1)S(1)}, bf16[768,768]{1,0:T(8,128)(2,1)}, u32[]{:S(2)}) copy-start(bf16[768,768]{1,0:T(8,128)(2,1)} %refs_11_.1) | copy-start | bytes 3538948
  106.7 11.0 %collective-permute-start.23 = (bf16[2,8,160,384]{3,2,1,0:T(8,128)(2,1)S(1)}, bf16[2,8,160,384]{3,2,1,0:T(8,128)(2,1)S(1)}, u32[]{:S(2)}, u32[]{:S(2)}) collective-permute-start(bf16[2,8,160,384]{3,2,1,0:T(8,128)(2,1)S(1)} %get-tuple-element.222), channel_id=1, source_target_pairs={{0,1},{1,0},{2,3},{3,2},{4,5},{5,4},{6,7},{7,6},{8,9},{9,8},{10,11... | collective-permute-start | bytes 5898248 | tf_op jit(solution)/shard_map/ppermute | solution.py:662
  106.8 10.9 %collective-permute-start.24 = (bf16[2,8,48,384]{3,2,1,0:T(8,128)(2,1)S(1)}, bf16[2,8,48,384]{3,2,1,0:T(8,128)(2,1)S(1)}, u32[]{:S(2)}, u32[]{:S(2)}) collective-permute-start(bf16[2,8,48,384]{3,2,1,0:T(8,128)(2,1)S(1)} %get-tuple-element.223), channel_id=1, source_target_pairs={{0,1},{1,0},{2,3},{3,2},{4,5},{5,4},{6,7},{7,6},{8,9},{9,8},{10,11... | collective-permute-start | bytes 1769480 | tf_op jit(solution)/shard_map/ppermute | solution.py:662
  107.3 9.0 %collective-permute-start.25 = (bf16[4,48,768]{2,1,0:T(8,128)(2,1)S(1)}, bf16[4,48,768]{2,1,0:T(8,128)(2,1)S(1)}, u32[]{:S(2)}, u32[]{:S(2)}) collective-permute-start(bf16[4,48,768]{2,1,0:T(8,128)(2,1)S(1)} %get-tuple-element.226), channel_id=1, source_target_pairs={{0,2},{1,3},{2,0},{3,1},{4,6},{5,7},{6,4},{7,5},{8,10},{9,11},{10,... | collective-permute-start | bytes 884744 | tf_op jit(solution)/shard_map/ppermute | solution.py:663
  108.8 8.7 %collective-permute-start.26 = (bf16[4,48,768]{2,1,0:T(8,128)(2,1)S(1)}, bf16[4,48,768]{2,1,0:T(8,128)(2,1)S(1)}, u32[]{:S(2)}, u32[]{:S(2)}) collective-permute-start(bf16[4,48,768]{2,1,0:T(8,128)(2,1)S(1)} %get-tuple-element.227), channel_id=1, source_target_pairs={{0,4},{4,0},{8,12},{12,8},{16,20},{20,16},{24,28},{28,24},{1,5},{5... | collective-permute-start | bytes 884744 | tf_op jit(solution)/shard_map/ppermute | solution.py:666
  118.3 26.6 %collective-permute-start.28 = (bf16[2,4,128,384]{3,2,1,0:T(8,128)(2,1)S(1)}, bf16[2,4,128,384]{3,2,1,0:T(8,128)(2,1)S(1)}, u32[]{:S(2)}, u32[]{:S(2)}) collective-permute-start(bf16[2,4,128,384]{3,2,1,0:T(8,128)(2,1)S(1)} %get-tuple-element.235), channel_id=1, source_target_pairs={{0,4},{4,0},{8,12},{12,8},{16,20},{20,16},{24,28},{28,24},{1,5},{5... | collective-permute-start | bytes 2359304 | tf_op jit(solution)/shard_map/ppermute | solution.py:666
  118.9 26.0 %collective-permute-start.29 = (bf16[8,80,384]{2,1,0:T(8,128)(2,1)S(1)}, bf16[8,80,384]{2,1,0:T(8,128)(2,1)S(1)}, u32[]{:S(2)}, u32[]{:S(2)}) collective-permute-start(bf16[8,80,384]{2,1,0:T(8,128)(2,1)S(1)} %get-tuple-element.236), channel_id=1, source_target_pairs={{0,2},{1,3},{2,0},{3,1},{4,6},{5,7},{6,4},{7,5},{8,10},{9,11},{10,... | collective-permute-start | bytes 1474568 | tf_op jit(solution)/shard_map/ppermute | solution.py:663
  119.2 17.8 %collective-permute-start.21 = (bf16[4,96,384]{2,1,0:T(8,128)(2,1)S(1)}, bf16[4,96,384]{2,1,0:T(8,128)(2,1)S(1)}, u32[]{:S(2)}, u32[]{:S(2)}) collective-permute-start(bf16[4,96,384]{2,1,0:T(8,128)(2,1)S(1)} %get-tuple-element.218), channel_id=1, source_target_pairs={{0,2},{1,3},{2,0},{3,1},{4,6},{5,7},{6,4},{7,5},{8,10},{9,11},{10,... | collective-permute-start | bytes 884744 | tf_op jit(solution)/shard_map/ppermute | solution.py:663
  120.9 22.1 %collective-permute-start.22 = (bf16[4,96,384]{2,1,0:T(8,128)(2,1)S(1)}, bf16[4,96,384]{2,1,0:T(8,128)(2,1)S(1)}, u32[]{:S(2)}, u32[]{:S(2)}) collective-permute-start(bf16[4,96,384]{2,1,0:T(8,128)(2,1)S(1)} %get-tuple-element.219), channel_id=1, source_target_pairs={{0,4},{4,0},{8,12},{12,8},{16,20},{20,16},{24,28},{28,24},{1,5},{5... | collective-permute-start | bytes 884744 | tf_op jit(solution)/shard_map/ppermute | solution.py:666
  122.4 22.4 %collective-permute-start.30 = (bf16[2,96,768]{2,1,0:T(8,128)(2,1)S(1)}, bf16[2,96,768]{2,1,0:T(8,128)(2,1)S(1)}, u32[]{:S(2)}, u32[]{:S(2)}) collective-permute-start(bf16[2,96,768]{2,1,0:T(8,128)(2,1)S(1)} %get-tuple-element.239), channel_id=1, source_target_pairs={{0,8},{4,12},{8,0},{12,4},{16,24},{20,28},{24,16},{28,20},{1,9},{5... | collective-permute-start | bytes 884744 | tf_op jit(solution)/shard_map/ppermute | solution.py:666
  143.2 10.1 %collective-permute-start.27 = (bf16[2,192,384]{2,1,0:T(8,128)(2,1)S(1)}, bf16[2,192,384]{2,1,0:T(8,128)(2,1)S(1)}, u32[]{:S(2)}, u32[]{:S(2)}) collective-permute-start(bf16[2,192,384]{2,1,0:T(8,128)(2,1)S(1)} %get-tuple-element.233), channel_id=1, source_target_pairs={{0,8},{4,12},{8,0},{12,4},{16,24},{20,28},{24,16},{28,20},{1,9},{5... | collective-permute-start | bytes 884744 | tf_op jit(solution)/shard_map/ppermute | solution.py:666
  145.2 11.4 %collective-permute-start.34 = (bf16[4,128,384]{2,1,0:T(8,128)(2,1)S(1)}, bf16[4,128,384]{2,1,0:T(8,128)(2,1)S(1)}, u32[]{:S(2)}, u32[]{:S(2)}) collective-permute-start(bf16[4,128,384]{2,1,0:T(8,128)(2,1)S(1)} %get-tuple-element.250), channel_id=1, source_target_pairs={{0,2},{1,3},{2,0},{3,1},{4,6},{5,7},{6,4},{7,5},{8,10},{9,11},{10,... | collective-permute-start | bytes 1179656 | tf_op jit(solution)/shard_map/ppermute | solution.py:663
  145.9 7.5 %collective-permute-start.32 = (bf16[96,768]{1,0:T(8,128)(2,1)S(1)}, bf16[96,768]{1,0:T(8,128)(2,1)S(1)}, u32[]{:S(2)}, u32[]{:S(2)}) collective-permute-start(bf16[96,768]{1,0:T(8,128)(2,1)S(1)} %get-tuple-element.246), channel_id=1, source_target_pairs={{0,16},{4,20},{8,24},{12,28},{16,0},{20,4},{24,8},{28,12},{1,17},{... | collective-permute-start | bytes 442376 | tf_op jit(solution)/shard_map/ppermute | solution.py:666
  148.5 8.2 %collective-permute-start.35 = (bf16[4,80,384]{2,1,0:T(8,128)(2,1)S(1)}, bf16[4,80,384]{2,1,0:T(8,128)(2,1)S(1)}, u32[]{:S(2)}, u32[]{:S(2)}) collective-permute-start(bf16[4,80,384]{2,1,0:T(8,128)(2,1)S(1)} %get-tuple-element.251), channel_id=1, source_target_pairs={{0,4},{4,0},{8,12},{12,8},{16,20},{20,16},{24,28},{28,24},{1,5},{5... | collective-permute-start | bytes 737288 | tf_op jit(solution)/shard_map/ppermute | solution.py:666
  153.4 6.5 %collective-permute-start.33 = (bf16[96,768]{1,0:T(8,128)(2,1)S(1)}, bf16[96,768]{1,0:T(8,128)(2,1)S(1)}, u32[]{:S(2)}, u32[]{:S(2)}) collective-permute-start(bf16[96,768]{1,0:T(8,128)(2,1)S(1)} %get-tuple-element.249.refs_1_), channel_id=1, source_target_pairs={{0,2},{1,3},{2,0},{3,1},{4,6},{5,7},{6,4},{7,5},{8,10},{9,11},{10,... | collective-permute-start | bytes 442376 | tf_op jit(solution)/shard_map/ppermute | solution.py:663
  154.1 7.0 %collective-permute-start.31 = (bf16[192,384]{1,0:T(8,128)(2,1)S(1)}, bf16[192,384]{1,0:T(8,128)(2,1)S(1)}, u32[]{:S(2)}, u32[]{:S(2)}) collective-permute-start(bf16[192,384]{1,0:T(8,128)(2,1)S(1)} %get-tuple-element.244), channel_id=1, source_target_pairs={{0,16},{4,20},{8,24},{12,28},{16,0},{20,4},{24,8},{28,12},{1,17},{... | collective-permute-start | bytes 442376 | tf_op jit(solution)/shard_map/ppermute | solution.py:666
  156.9 14.4 %collective-permute-start.36 = (bf16[2,208,384]{2,1,0:T(8,128)(2,1)S(1)}, bf16[2,208,384]{2,1,0:T(8,128)(2,1)S(1)}, u32[]{:S(2)}, u32[]{:S(2)}) collective-permute-start(bf16[2,208,384]{2,1,0:T(8,128)(2,1)S(1)} %get-tuple-element.259), channel_id=1, source_target_pairs={{0,8},{4,12},{8,0},{12,4},{16,24},{20,28},{24,16},{28,20},{1,9},{5... | collective-permute-start | bytes 958472 | tf_op jit(solution)/shard_map/ppermute | solution.py:666
  158.7 3.8 %collective-permute-start.18 = (bf16[128,768]{1,0:T(8,128)(2,1)S(1)}, bf16[128,768]{1,0:T(8,128)(2,1)S(1)}, u32[]{:S(2)}, u32[]{:S(2)}) collective-permute-start(bf16[128,768]{1,0:T(8,128)(2,1)S(1)} %get-tuple-element.215), channel_id=1, source_target_pairs={{0,1},{1,0},{2,3},{3,2},{4,5},{5,4},{6,7},{7,6},{8,9},{9,8},{10,11... | collective-permute-start | bytes 589832 | tf_op jit(solution)/shard_map/ppermute | solution.py:726
  158.7 7.7 %collective-permute-start.19 = (bf16[128,768]{1,0:T(8,128)(2,1)S(1)}, bf16[128,768]{1,0:T(8,128)(2,1)S(1)}, u32[]{:S(2)}, u32[]{:S(2)}) collective-permute-start(bf16[128,768]{1,0:T(8,128)(2,1)S(1)} %get-tuple-element.216), channel_id=1, source_target_pairs={{0,2},{1,3},{2,0},{3,1},{4,6},{5,7},{6,4},{7,5},{8,10},{9,11},{10,... | collective-permute-start | bytes 589832 | tf_op jit(solution)/shard_map/ppermute | solution.py:726
  159.9 9.9 %collective-permute-start.20 = (bf16[128,768]{1,0:T(8,128)(2,1)S(1)}, bf16[128,768]{1,0:T(8,128)(2,1)S(1)}, u32[]{:S(2)}, u32[]{:S(2)}) collective-permute-start(bf16[128,768]{1,0:T(8,128)(2,1)S(1)} %get-tuple-element.217), channel_id=1, source_target_pairs={{0,3},{1,2},{2,1},{3,0},{4,7},{5,6},{6,5},{7,4},{8,11},{9,10},{10,... | collective-permute-start | bytes 589832 | tf_op jit(solution)/shard_map/ppermute | solution.py:726
  161.2 12.2 %collective-permute-start.39 = (bf16[192,384]{1,0:T(8,128)(2,1)S(1)}, bf16[192,384]{1,0:T(8,128)(2,1)S(1)}, u32[]{:S(2)}, u32[]{:S(2)}) collective-permute-start(bf16[192,384]{1,0:T(8,128)(2,1)S(1)} %get-tuple-element.265.refs_1_), channel_id=1, source_target_pairs={{0,2},{1,3},{2,0},{3,1},{4,6},{5,7},{6,4},{7,5},{8,10},{9,11},{10,... | collective-permute-start | bytes 442376 | tf_op jit(solution)/shard_map/ppermute | solution.py:663
  162.5 11.5 %collective-permute-start.38 = (bf16[2,96,768]{2,1,0:T(8,128)(2,1)S(1)}, bf16[2,96,768]{2,1,0:T(8,128)(2,1)S(1)}, u32[]{:S(2)}, u32[]{:S(2)}) collective-permute-start(bf16[2,96,768]{2,1,0:T(8,128)(2,1)S(1)} %get-tuple-element.264.refs_1_), channel_id=1, source_target_pairs={{0,1},{1,0},{2,3},{3,2},{4,5},{5,4},{6,7},{7,6},{8,9},{9,8},{10,11... | collective-permute-start | bytes 884744 | tf_op jit(solution)/shard_map/ppermute | solution.py:662
  171.4 10.7 %collective-permute-start.37 = (bf16[208,384]{1,0:T(8,128)(2,1)S(1)}, bf16[208,384]{1,0:T(8,128)(2,1)S(1)}, u32[]{:S(2)}, u32[]{:S(2)}) collective-permute-start(bf16[208,384]{1,0:T(8,128)(2,1)S(1)} %get-tuple-element.262), channel_id=1, source_target_pairs={{0,16},{4,20},{8,24},{12,28},{16,0},{20,4},{24,8},{28,12},{1,17},{... | collective-permute-start | bytes 479240 | tf_op jit(solution)/shard_map/ppermute | solution.py:666
  173.9 9.5 %collective-permute-start.41 = (bf16[2,192,384]{2,1,0:T(8,128)(2,1)S(1)}, bf16[2,192,384]{2,1,0:T(8,128)(2,1)S(1)}, u32[]{:S(2)}, u32[]{:S(2)}) collective-permute-start(bf16[2,192,384]{2,1,0:T(8,128)(2,1)S(1)} %get-tuple-element.270.refs_1_), channel_id=1, source_target_pairs={{0,1},{1,0},{2,3},{3,2},{4,5},{5,4},{6,7},{7,6},{8,9},{9,8},{10,11... | collective-permute-start | bytes 884744 | tf_op jit(solution)/shard_map/ppermute | solution.py:662
  182.1 6.2 %collective-permute-start.40 = (bf16[208,384]{1,0:T(8,128)(2,1)S(1)}, bf16[208,384]{1,0:T(8,128)(2,1)S(1)}, u32[]{:S(2)}, u32[]{:S(2)}) collective-permute-start(bf16[208,384]{1,0:T(8,128)(2,1)S(1)} %get-tuple-element.269.refs_1_), channel_id=1, source_target_pairs={{0,2},{1,3},{2,0},{3,1},{4,6},{5,7},{6,4},{7,5},{8,10},{9,11},{10,... | collective-permute-start | bytes 479240 | tf_op jit(solution)/shard_map/ppermute | solution.py:663
  188.9 1.7 collective-permute-start.42
  (4 other events, 6.7 us)

commit v3 on v2

--- a/solution.py
+++ b/solution.py
@@ -57,6 +57,10 @@
     return x * phi, phi + x * density
 
 
+def row(ref):
+    return ref[...].astype(F32).reshape(1, ref.shape[0])
+
+
 def head_lane(h):
     lane = lax.broadcasted_iota(jnp.int32, (1, LANES), 1)
     return (lane % PART == h) & (lane >= PART) & (lane < 4 * PART)
@@ -95,32 +99,46 @@
     wait(copies([(x_ref.at[info[10] ^ r], outs[r]) for r in range(len(outs))], sems))
 
 
-def join_kernel(info, *refs):
+def pack_kernel(o0, o1, o2, o3, i0, i1, i2, i3, pool, p0, p1, p2, p3):
+    n = o0.shape[0]
+    hi, low = two_parts(pool[:SEGS, :])
+    for p, o, i in ((p0, o0, i0), (p1, o1, i1), (p2, o2, i2), (p3, o3, i3)):
+        p[:n, :] = o[...]
+        p[n : 2 * n, :] = i[...]
+        p[2 * n : 2 * n + SEGS, :] = hi
+        p[2 * n + SEGS :, :] = low
+
+
+def unpack_kernel(info, lengths, p0, p1, p2, p3, out, grad, pool):
     me = info[10]
-    out = refs[-1]
-    for r in range(4):
-        out[me ^ r] = refs[r][...]
+    n = out.shape[1]
+    for r, p in enumerate((p0, p1, p2, p3)):
+        out[me ^ r] = p[:n, :]
+        grad[me ^ r] = p[n : 2 * n, :]
+        sums = p[2 * n :, :].astype(F32)
+        pool[me ^ r] = (sums[:SEGS] + sums[SEGS:]) / lengths[me ^ r][:, :1]
 
 
 def attend_kernel(
-    x0, x1, x2, x3, wq_h, wk_h, wv_h, wo_h, oh_ref, ka_ref, bq, bv, bo,
+    x0, x1, x2, x3, wq_h, wk_h, wv_h, wo_h, oh_ref, ka_ref, bq_ref, bv_ref, bo_ref,
     x_h, q_h, k_h, v_h, att_h, inv_h, qa_h, n1_out,
     x_out, q_out, k_out, v_out, att_out, inv_out, qa_out, wq, wk, wv, wo, stat, sems,
 ):
     n = x0.shape[0]
+    bq, bv, bo = row(bq_ref), row(bv_ref), row(bo_ref)
     ws = copies([(wq_h, wq), (wk_h, wk), (wv_h, wv), (wo_h, wo)], sems, 4)
     for r, ref in enumerate((x0, x1, x2, x3)):
         x_out[r * n : (r + 1) * n] = ref[...]
     outs = copies([(x_out, x_h)], sems, 8)
     x = x_out[...]
     ws[0].wait()
-    q_out[...] = ((nn(x, wq[...]) + bq[...]).astype(BF).astype(F32) * (HD**-0.5)).astype(BF)
+    q_out[...] = ((nn(x, wq[...]) + bq).astype(BF).astype(F32) * (HD**-0.5)).astype(BF)
     outs += copies([(q_out, q_h)], sems, 9)
     ws[1].wait()
     k_out[...] = nn(x, wk[...]).astype(BF)
     outs += copies([(k_out, k_h)], sems, 10)
     ws[2].wait()
-    v_out[...] = (nn(x, wv[...]) + bv[...]).astype(BF)
+    v_out[...] = (nn(x, wv[...]) + bv).astype(BF)
     outs += copies([(v_out, v_h)], sems, 11)
     tok, width = x.shape
     stat[...] = jnp.zeros_like(stat)
@@ -152,7 +170,7 @@
     qa_out[...] = jnp.concatenate([zero, hi, mid, low, zero, zero, zero, zero], axis=0).T + oh_ref[...]
     outs += copies([(qa_out, qa_h)], sems, 13)
     ws[3].wait()
-    mixed = nn(att_out[...].astype(BF), wo[...]) + bo[...]
+    mixed = nn(att_out[...].astype(BF), wo[...]) + bo
     n1, inv = norm(x.astype(F32) + mixed)
     n1_out[...] = n1
     inv_out[...] = jnp.broadcast_to(inv, inv_out.shape)
@@ -161,11 +179,13 @@
 
 
 def ffn_kernel(
-    lay, info, n1_ref, ga, sa, wu, bu, wd, bd, gf, sf, g0, g1, g2, g3, oh_ref, oht_ref, gpl,
+    lay, info, n1_ref, ga_ref, sa_ref, bd_ref, gf_ref, sf_ref, wu, bu_ref, wd_h, g0, g1, g2, g3, oh_ref, oht_ref, gpl,
     o0, o1, o2, o3, gp_h, send, keep, pool_out, r2_out, vec_out,
-    hl, acc, act, gt, gp_out, sem_g,
+    hl, acc, act, gt, gp_out, wd, bu, sem_g, sem_w,
 ):
     n = g0.shape[0]
+    ga, sa, bd, gf, sf = row(ga_ref), row(sa_ref), row(bd_ref), row(gf_ref), row(sf_ref)
+    bu[...] = row(bu_ref)
     tok, width = acc.shape
     ff = act.shape[1]
     tile = width
@@ -175,11 +195,18 @@
         cols = pl.ds(pl.multiple_of(t * tile, tile), tile)
         return pltpu.make_async_copy(gp_out.at[:, cols], gp_h.at[:, cols], sem_g.at[t])
 
-    hl[...] = (n1_ref[...] * ga[...] + sa[...]).astype(BF)
+    def weights(t):
+        rows = pl.ds(pl.multiple_of(t * tile, tile), tile)
+        return pltpu.make_async_copy(wd_h.at[rows, :], wd.at[rows, :], sem_w.at[t])
+
+    for t in range(steps):
+        weights(t).start()
+    hl[...] = (n1_ref[...] * ga + sa).astype(BF)
     acc[...] = jnp.zeros_like(acc)
 
     def step(t, carry):
         cols = pl.ds(pl.multiple_of(t * tile, tile), tile)
+        weights(t).wait()
         for r in range(4):
             rows = pl.ds(r * n, n)
             a, d = gelu_both(nn(hl[rows, :], wu[:, cols]) + bu[:, cols])
@@ -197,9 +224,9 @@
     pool = jnp.zeros(pool_out.shape, F32)
     for r, (o, g) in enumerate(((o0, g0), (o1, g1), (o2, g2), (o3, g3))):
         rows = pl.ds(r * n, n)
-        hidden = n1_ref[rows, :] * ga[...] + sa[...]
-        n2, inv = norm(hidden + (acc[rows, :] + bd[...]))
-        result = n2 * gf[...] + sf[...]
+        hidden = n1_ref[rows, :] * ga + sa
+        n2, inv = norm(hidden + (acc[rows, :] + bd))
+        result = n2 * gf + sf
         o[...] = result.astype(BF)
         hi, low = two_parts(result)
         oht = oht_ref[:, r * n : (r + 1) * n]
@@ -208,7 +235,7 @@
         gout = g[...].astype(F32) + nn(jnp.concatenate([oh, oh], axis=1), gpl[...])
         gain += jnp.sum(gout * n2, axis=0, keepdims=True)
         shift += jnp.sum(gout, axis=0, keepdims=True)
-        gr2 = norm_back(gout * gf[...], n2, inv)
+        gr2 = norm_back(gout * gf, n2, inv)
         r2_out[rows, :] = gr2
         low_g = gr2.astype(BF)
         bias += jnp.sum(low_g.astype(F32), axis=0, keepdims=True)
@@ -231,10 +258,11 @@
 
 
 def ffn_back_kernel(
-    lay, info, r2_ref, gp_h, wd, n1_ref, ga, sa,
+    lay, info, r2_ref, gp_h, wd, n1_ref, ga_ref, sa_ref,
     send, keep, bup_out, gpre_out,
     gl, hlt, gp, sem_w,
 ):
+    ga, sa = row(ga_ref), row(sa_ref)
     width = hlt.shape[0]
     half = width // 2
     ff = gp.shape[1]
@@ -248,7 +276,7 @@
     for t in range(steps):
         load(t).start()
     gl[...] = r2_ref[...].astype(BF)
-    hlt[...] = (n1_ref[...] * ga[...] + sa[...]).astype(BF).T
+    hlt[...] = (n1_ref[...] * ga + sa).astype(BF).T
     per = 2 if lay[0] > 1 else 1
 
     def step(t, carry):
@@ -273,19 +301,20 @@
 
 
 def norm_back_kernel(
-    lay, info, r2_ref, gpre, wu, n1_ref, inv_ref, ga, wo, att,
+    lay, info, r2_ref, gpre, wu, n1_ref, inv_ref, ga_ref, wo, att,
     r1_h, gatt_out, gaug_out, vec_out, osend, okeep,
     gt, r1_out, acc, sems,
 ):
+    ga = row(ga_ref)
     tok, width = r2_ref.shape
     half = width // 2
     n = tok // 4
     gain = jnp.zeros((1, width), F32)
     shift = jnp.zeros((1, width), F32)
     bias = jnp.zeros((1, width), F32)
-    row = lax.broadcasted_iota(jnp.int32, (width, LANES), 0) // HD
+    head = lax.broadcasted_iota(jnp.int32, (width, LANES), 0) // HD
     lane = lax.broadcasted_iota(jnp.int32, (width, LANES), 1)
-    pick = ((lane % PART == row) & (lane >= PART) & (lane < 4 * PART)).astype(BF)
+    pick = ((lane % PART == head) & (lane >= PART) & (lane < 4 * PART)).astype(BF)
     lane1 = lax.broadcasted_iota(jnp.int32, (1, LANES), 1)
     outs = []
 
@@ -302,7 +331,7 @@
         n1 = n1_ref[rows, :]
         gain += jnp.sum(gh * n1, axis=0, keepdims=True)
         shift += jnp.sum(gh, axis=0, keepdims=True)
-        gr1 = norm_back(gh * ga[...], n1, inv_ref[rows, :1])
+        gr1 = norm_back(gh * ga, n1, inv_ref[rows, :1])
         r1_out[rows, :] = gr1
         outs += copies([(r1_out.at[rows, :], r1_h.at[rows, :])], sems, r)
         gm = gr1.astype(BF)
@@ -368,27 +397,33 @@
 
 def project_back_kernel(
     lay, info, gq, gk, gv, gqt, gkt, gvt, x_ref, r1, wq, wk, wv, vecs, bups,
-    send, keep, o0, o1, o2, o3,
+    send_a, send_b, keep_a, keep_b, o0, o1, o2, o3,
 ):
     width = x_ref.shape[1]
     n, halves, rs = lay
     half = width // 2
     sides = [x_ref[:, pl.ds(pl.multiple_of((info[8] ^ rc) * half, half), half)] for rc in (1, 0)]
     right = jnp.concatenate(sides, axis=1)
+    wires = ((1, (send_a, send_b)), (0, (keep_a, keep_b)))
     for m, left in enumerate((gqt, gkt, gvt)):
         both = nn(left[...], right)
-        for rc, ref in ((1, send), (0, keep)):
+        for rc, (wa, wb) in wires:
             res = both[:, :half] if rc else both[:, half:]
             if n > 1:
                 for j in range(n):
-                    lead, at = info[j], j * rs
-                    if m == 1:
-                        put_rows(ref, lead, info[9], 48, halves, slice(None), res[at : at + 32])
-                        put_rows(ref, lead, info[9], 128, halves, slice(None), res[at + 32 : at + rs])
+                    rows = res[j * rs : (j + 1) * rs]
+                    put = functools.partial(put_rows, lead=info[j], y=info[9], halves=halves, cols=slice(None))
+                    if m == 0:
+                        put(wa, rows=0, value=rows)
+                    elif m == 1:
+                        put(wa, rows=48, value=rows[:32])
+                        put(wb, rows=48, value=rows[32:])
                     else:
-                        put_rows(ref, lead, info[9], 40 * m, halves, slice(None), res[at : at + rs])
+                        put(wb, rows=0, value=rows)
+            elif m < 2:
+                wa[0, 0, pl.ds(m * width, width), :] = res.astype(BF)
             else:
-                ref[0, 0, pl.ds(m * width, width), :] = res.astype(BF)
+                wb[0, 0] = res.astype(BF)
     if n > 1:
         for j in range(n):
             bup = bups[:1, j * 4 * rs : (j + 1) * 4 * rs]
@@ -399,9 +434,9 @@
                 axis=0,
             )
             block = jnp.concatenate([block, jnp.zeros((32, half - rs), F32)], axis=1)
-            for rc, ref in ((1, send), (0, keep)):
+            for rc, (wa, _) in wires:
                 mine = jnp.where((info[8] ^ rc) == 0, 1.0, 0.0)
-                put_rows(ref, info[j], info[9], 64, halves, slice(None), block * mine)
+                put_rows(wa, info[j], info[9], 64, halves, slice(None), block * mine)
 
     total = r1[...] + nt(gq[...], wq[...]) + nt(gk[...], wk[...]) + nt(gv[...], wv[...])
     for r, o in enumerate((o0, o1, o2, o3)):
@@ -430,14 +465,21 @@
     return pltpu.CompilerParams(vmem_limit_bytes=mib * 1024 * 1024)
 
 
-COST = pl.CostEstimate(flops=10**9, bytes_accessed=10**6, transcendentals=0)
+def cost(us):
+    return pl.CostEstimate(flops=int(us * 10**9) + 1, bytes_accessed=1, transcendentals=0)
+
+
+COSTS = {
+    "down_one": 0.1, "up_one": 0.1, "down_two": 0.1, "up_two": 1.0, "down_three": 8.0, "qkv_one": 0.1, "up_three": 3.0,
+    "down_four": 1.0, "down_end": 0.02, "up_end": 0.02,
+}
 
 
 class Line:
     def __init__(self):
         self.token = None
 
-    def call(self, kernel, outs, args, scalars=(), scratch=(), name=None, mib=8, far_in=(), far_out=()):
+    def call(self, kernel, outs, args, scalars=(), scratch=(), name=None, mib=8, far_in=(), far_out=(), us=0.0):
         args = [pltpu.with_memory_space_constraint(a, pltpu.HBM) if i in far_in else a for i, a in enumerate(args)]
         ins = [SCALARS if i in scalars else FAR if i in far_in else WHOLE for i in range(len(args))]
         to = [FAR if i in far_out else WHOLE for i in range(len(outs))]
@@ -457,7 +499,7 @@
             out_specs=[*to, WHOLE],
             scratch_shapes=list(scratch),
             compiler_params=params(mib),
-            cost_estimate=COST,
+            cost_estimate=cost(us),
             name=name,
         )(*args, *tokens)
         return got
@@ -503,9 +545,32 @@
     lb[...] = b[:4]
 
 
+def two_with_out_kernel(split, ga, gb, ka, kb, go, ko, sa, sb, la, lb, lx, ly):
+    ma, mb, mo = ka.shape[2], kb.shape[1], ko.shape[2]
+    two_kernel(ga, gb, ka, kb, sa.at[:, :ma, :], sb.at[:, :mb, :], la, lb)
+    total = plus(go[...], ko[...])
+    rest = mo - split
+    sb[:, mb : mb + split, :] = total[0, 4:, :split]
+    sb[:, mb + split :, :] = total[1, 4:, :split]
+    lx[...] = total[:, :4, :split]
+    sa[:, ma : ma + rest, :] = total[1, :4, split:]
+    sa[:, ma + rest :, :] = total[1, 4:, split:]
+    ly[...] = total[0, :, split:]
+
+
+def two_from_out_kernel(ga, gb, ka, kb, gx, gy, kx, ky, sa, sb, la, lb):
+    ma, mb, nx, ny = ka.shape[2], kb.shape[1], kx.shape[2], ky.shape[1]
+    two_kernel(ga, gb, ka, kb, sa.at[:, :ma, :], sb.at[:, :mb, :], la.at[:, :ma, :], lb.at[:, :mb, :])
+    x0, y0 = gx.shape[1] - 2 * nx, gy.shape[1] - 2 * ny
+    la[:, ma:, :] = plus(gx[:, x0 : x0 + nx, :], kx[0])
+    sa[:, ma:, :] = plus(gx[:, x0 + nx :, :], kx[1])
+    lb[:, mb:, :] = plus(gy[:, y0 : y0 + ny, :], ky[:4])
+    sb[:, mb:, :] = plus(gy[:, y0 + ny :, :], ky[4:])
+
+
 def three_kernel(ga, gb, ka, kb, send, keep):
-    m = ga.shape[1]
-    a, b = plus(ga[...], ka[...]), plus(gb[...], kb[...])
+    m, mb = ka.shape[1], kb.shape[1]
+    a, b = plus(ga[:, :m, :], ka[...]), plus(gb[:, :mb, :], kb[...])
     send[:, :m, :] = a[2:]
     keep[:, :m, :] = a[:2]
     send[:, m:, :] = b[2:]
@@ -546,22 +611,25 @@
             out[pl.ds(pl.multiple_of(at, m), m), :] = ref[a].astype(F32)
 
 
-def qkv_kernel(info, mine, other, gq, gk, gv, go, vec):
+def qkv_kernel(info, mine, other, gq, gk, gv, go, *vecs):
     half = gq.shape[1] // 2
     for rc, ref in ((0, mine), (1, other)):
         at = pl.ds(pl.multiple_of((info[8] ^ rc) * half, half), half)
 
         def put(out, *spans):
-            parts = [ref[a, i : i + m] for i, m in spans for a in range(2)]
+            parts = [ref[a, i : i + m] for a, i, m in spans]
             out[:, at] = jnp.concatenate(parts, axis=0).astype(F32)
 
-        put(gq, (0, 48))
-        put(gk, (48, 16), (176, 32))
-        put(gv, (128, 48))
-        put(go, (80, 48))
-    rs = vec.shape[1]
+        put(gq, (0, 0, 48), (1, 0, 48))
+        put(gk, (0, 48, 16), (1, 48, 16), (0, 160, 32), (1, 160, 32))
+        put(gv, (0, 112, 48), (1, 112, 48))
+        put(go, (0, 80, 32), (0, 192, 16), (1, 80, 32), (1, 192, 16))
+    rs = vecs[0].shape[0]
     low = jnp.where(info[8] == 0, mine[:, 64:80, :].astype(F32), other[:, 64:80, :].astype(F32))
-    vec[...] = jnp.concatenate([low[0, :8, :rs], low[1, :8, :rs]], axis=0)
+    for i, out in enumerate(vecs[:8]):
+        out[...] = low[0, i, :rs]
+    for c in range(4):
+        vecs[8][pl.ds(c * rs, rs)] = low[1, c, :rs]
 
 
 def local(n_dp, n_seq, *args):
@@ -617,17 +685,16 @@
     zeros = jnp.zeros((LANES - SEGS, width), BF)
     gpl = jnp.concatenate([gp_hi, zeros, gp_low, zeros], axis=0)
 
-    def vec(v):
-        return v.astype(F32).reshape(1, -1)
 
     sq = shape((tok, width))
     sqf = shape((tok, width), F32)
+    row_lengths = jnp.broadcast_to(seg_lengths.astype(F32)[:, :, None], (rows, SEGS, LANES))
     lanes = shape((tok, LANES))
     lanes_f = shape((tok, LANES), F32)
     x, q, k, v, att, inv, qaug, n1 = line.call(
         attend_kernel,
         [sq, sq, sq, sq, sqf, lanes_f, lanes, sqf],
-        (*xs, w_query, w_key, w_value, w_out, onehot, kaug, vec(b_query), vec(b_value), vec(b_out)),
+        (*xs, w_query, w_key, w_value, w_out, onehot, kaug, b_query, b_value, b_out),
         scratch=[buf((tok, width))] * 4
         + [buf((tok, width), F32), buf((tok, LANES), F32), buf((tok, LANES))]
         + [buf((width, width))] * 4
@@ -647,15 +714,16 @@
         [shape((piece, width))] * 4
         + [shape((tok, ff)), wire_d, wire_d, shape((16, width), F32), sqf, shape((8, width), F32)],
         (
-            info, n1, vec(gain_attn), vec(shift_attn), w_up, vec(b_up), w_down, vec(b_down),
-            vec(gain_ffn), vec(shift_ffn), *gs, onehot, onehot_t, gpl,
+            info, n1, gain_attn, shift_attn, b_down, gain_ffn, shift_ffn, w_up, b_up, w_down, *gs, onehot, onehot_t, gpl,
         ),
         scalars=(0,),
         scratch=[
-            buf((tok, width)), buf((tok, width), F32), buf((tok, ff)), buf((width, tok)), buf((tok, ff)), sems(steps),
+            buf((tok, width)), buf((tok, width), F32), buf((tok, ff)), buf((width, tok)), buf((tok, ff)), buf((ff, width)),
+            buf((1, ff), F32), sems(steps), sems(steps),
         ],
         name="ffn",
-        mib=18,
+        mib=24,
+        far_in=(9,),
         far_out=(4,),
     )
 
@@ -676,8 +744,9 @@
             self.cuts = cuts_a, cuts_b
 
         def run(self, kernel, outs, args, scalars=()):
+            name = self.name + kernel_name(kernel)
             return line.call(
-                kernel, [shape(o) for o in outs], args, scalars=scalars, name=self.name + kernel_name(kernel), mib=16
+                kernel, [shape(o) for o in outs], args, scalars=scalars, name=name, mib=16, us=COSTS.get(name, 0.3)
             )
 
         def one(self):
@@ -697,6 +766,27 @@
             sa, sb, ka, kb = self.run(two_kernel, [(4, a, c), (4, b, c)] * 2, (*self.got, *self.kept))
             self.got, self.kept = (pp_y(sa), pp_x(sb)), (ka, kb)
 
+        def two_with_out(self, got, kept, split):
+            a, b, c = self.dims
+            m = kept.shape[2]
+            rest = m - split
+            sa, sb, ka, kb, kx, ky = self.run(
+                functools.partial(two_with_out_kernel, split),
+                [(4, a + 2 * rest, c), (4, b + 2 * split, c), (4, a, c), (4, b, c), (2, 4, split, c), (8, rest, c)],
+                (*self.got, *self.kept, got, kept),
+            )
+            self.got, self.kept = (pp_y(sa), pp_x(sb)), (ka, kb)
+            return self.got[1], self.got[0], kx, ky
+
+        def two_from_out(self, gx, gy, kx, ky):
+            a, b, c = self.dims
+            a, b = a + kx.shape[2], b + ky.shape[1]
+            self.dims = a, b, c
+            sa, sb, ka, kb = self.run(
+                two_from_out_kernel, [(4, a, c), (4, b, c)] * 2, (*self.got, *self.kept, gx, gy, kx, ky)
+            )
+            self.got, self.kept = (pp_y(sa), pp_x(sb)), (ka, kb)
+
         def three(self):
             a, b, c = self.dims
             send, keep = self.run(three_kernel, [(2, a + b, c)] * 2, (*self.got, *self.kept))
@@ -721,18 +811,6 @@
             return line.call(
                 kernel, outs, (info, self.kept, self.got), scalars=(0,), name=self.name + "end", mib=16
             )
-
-    def there(parts):
-        return [parts[0]] + [lax.ppermute(parts[r], "seq", xor[r]) for r in range(1, 4)]
-
-    def joined(got, name):
-        (whole,) = line.call(
-            join_kernel, [shape((rows, *got[0].shape), got[0].dtype)], (info, *got), scalars=(0,), name=name
-        )
-        return whole
-
-    out_got = there(outs)
-    pool_got = there([pool[:SEGS] / length_col] * n_seq)
 
     wire_u = shape((halves, n, half // halves, ff // n))
     if fast:
@@ -740,7 +818,7 @@
     u_send, u_keep, bup, gpre = line.call(
         functools.partial(ffn_back_kernel, lay),
         [wire_u, wire_u, shape((8, ff), F32), shape((tok, ff))],
-        (info, r2, gp, w_down, n1, vec(gain_attn), vec(shift_attn)),
+        (info, r2, gp, w_down, n1, gain_attn, shift_attn),
         scalars=(0,),
         scratch=[buf((tok, width)), buf((width, tok)), buf((tok, ff)), sems(steps)],
         name="ffn_back",
@@ -756,15 +834,13 @@
     r1, gatt, gaug, vec_c, o_send, o_keep = line.call(
         functools.partial(norm_back_kernel, lay),
         [sqf, sq, shape((tok, LANES)), shape((8, width), F32), wire_o, wire_o],
-        (info, r2, gpre, w_up, n1, inv, vec(gain_attn), w_out, att),
+        (info, r2, gpre, w_up, n1, inv, gain_attn, w_out, att),
         scalars=(0,),
         scratch=[buf((width, tok)), buf((tok, width), F32), buf((tok, width), F32), sems(4)],
         name="norm_back",
         mib=14,
         far_out=(0,),
     )
-    output = joined(out_got, "join_out")
-    pooled = joined(pool_got, "join_pool")
     if fast:
         o_got = pp_core(o_send)
         m = half // 2
@@ -781,48 +857,65 @@
     vecs = jnp.concatenate([vec_d[:2], vec_c[:3], vec_b[:3]], axis=0)
     if fast:
         down.two()
-        up.two()
-    rows_q = 160 if fast else 3 * width
-    wire_q = shape((halves, n, rows_q, half))
-    q_send, q_keep, *ins = line.call(
+    rows_a, rows_b = (80, 80) if fast else (2 * width, width)
+    wire_a, wire_b = shape((halves, n, rows_a, half)), shape((halves, n, rows_b, half))
+    qa_send, qb_send, qa_keep, qb_keep, *ins = line.call(
         functools.partial(project_back_kernel, lay),
-        [wire_q, wire_q] + [shape((piece, width))] * 4,
+        [wire_a, wire_b, wire_a, wire_b] + [shape((piece, width))] * 4,
         (info, gq, gk, gv, gqt, gkt, gvt, x, r1, w_query, w_key, w_value, vecs, bup),
         scalars=(0,),
         name="project_back",
         mib=16,
     )
-    in_got = there(ins)
+
+    def send_back():
+        packs = line.call(
+            pack_kernel, [shape((2 * piece + 2 * SEGS, width))] * n_seq, (*outs, *ins, pool), name="pack"
+        )
+        return [packs[0]] + [lax.ppermute(packs[r], "seq", xor[r]) for r in range(1, n_seq)]
+
+    def take_back(packs):
+        return line.call(
+            unpack_kernel,
+            [shape((rows, piece, width)), shape((rows, piece, width)), shape((rows, SEGS, width), F32)],
+            (info, row_lengths, *packs),
+            scalars=(0,),
+            name="unpack",
+        )
+
     if fast:
-        q_got = pp_core(q_send)
         qkv = Sum(
-            "qkv_", [q_got, o_got], [q_keep, o_keep],
-            [(0, ((0, 80), (0, half))), (1, ((0, 48), (0, half)))],
-            [(0, ((80, 160), (0, half)))],
+            "qkv_", [pp_core(qa_send), pp_core(qb_send)], [qa_keep, qb_keep],
+            [(0, ((0, 80), (0, half)))],
+            [(1, ((0, 80), (0, half)))],
         )
         f32 = lambda *d: shape(d, F32)
+        out_sum = up.two_with_out(o_got, o_keep, 32)
         down.three()
         qkv.one()
+        packs = send_back()
         up.three()
         down.four()
-        qkv.two()
+        qkv.two_from_out(*out_sum)
         up.four()
         down.five()
+        down.six()
         qkv.three()
-        down.six()
         up.five()
-        grad_tokens = joined(in_got, "join_in")
+        up.six()
         qkv.four()
-        up.six()
         (g_down,) = down.end(down_kernel, [f32(rs, ff)])
+        (g_up,) = up.end(up_kernel, [f32(width, ff // n)])
         qkv.five()
-        (g_up,) = up.end(up_kernel, [f32(width, ff // n)])
+        output, grad_tokens, pooled = take_back(packs)
         qkv.six()
-        *g_qkv, g_out, vs = qkv.end(qkv_kernel, [f32(rs, width)] * 4 + [f32(16, rs)])
+        *g_qkv, g_out, v0, v1, v2, v3, v4, v5, v6, v7, v8 = qkv.end(
+            qkv_kernel, [f32(rs, width)] * 4 + [f32(rs)] * 8 + [f32(4 * rs)]
+        )
         g_down, g_out, g_qkv = g_down.T, g_out.T, [g.T for g in g_qkv]
-        small = [vs[i] for i in range(8)] + [vs[8:12].reshape(-1)]
+        small = [v0, v1, v2, v3, v4, v5, v6, v7, v8]
     else:
-        grad_tokens = joined(in_got, "join_in")
+        output, grad_tokens, pooled = take_back(send_back())
 
         def total(send, keep, dim):
             h = keep.astype(F32) + pp_core(send).astype(F32)
@@ -839,8 +932,12 @@
         g_up = whole(u_send[0, 0], u_keep[0, 0], 1, 0)
         g_out = whole(o_send[0, 0], o_keep[0, 0], 0, 1).T
         g_qkv = [
-            whole(q_send[0, 0, w * width : (w + 1) * width], q_keep[0, 0, w * width : (w + 1) * width], 0, 1).T
-            for w in range(3)
+            whole(send, keep, 0, 1).T
+            for send, keep in (
+                (qa_send[0, 0, :width], qa_keep[0, 0, :width]),
+                (qa_send[0, 0, width:], qa_keep[0, 0, width:]),
+                (qb_send[0, 0], qb_keep[0, 0]),
+            )
         ]
         flat = lax.psum(jnp.concatenate([vecs.reshape(-1), bup[0]]), ("dp", "seq"))
         mine = width // n_dp

time: 194 us -> 162 us (0.84)
  waiting for transfers between devices: 66.3 us -> 43.8 us
  local copies, waits for them, and re-layouts: 4.94 us -> 0.32 us
  starting transfers between devices: 39.5 us -> 36.5 us
    ppermute x12, waiting for transfers between devices: 26.7 us -> 10.2 us  [pp_dp(): return lambda a: lax.ppermute(a, 'dp', [(i, i ^ bit) for i in range(n_dp)])]
    ppermute x9, waiting for transfers between devices: 27.8 us -> 22.4 us  [local(): pp_y = lambda a: lax.ppermute(a, 'seq', xor[2])]
    ppermute x9 -> x3, starting transfers between devices: 6.37 us -> 1.93 us  [send_back(): lax.ppermute(packs[r], 'seq', xor[r])]
    unnamed x50, local copies, waits for them, and re-layouts: 3.58 us -> 0.14 us
    ppermute x12, starting transfers between devices: 16.9 us -> 19.1 us  [pp_dp(): return lambda a: lax.ppermute(a, 'dp', [(i, i ^ bit) for i in range(n_dp)])]
    pallas_call x32 -> x31, Pallas kernels: 79 us -> 77.9 us  [call(): pl.pallas_call(body, out_shape=[*outs, shape((8, LANES), F32)], in_specs=...]
    ppermute x9 -> x3, waiting for transfers between devices: 7.32 us -> 6.39 us  [send_back(): lax.ppermute(packs[r], 'seq', xor[r])]
  transfers between devices with their start and end apart: 43 -> 38, of which waited for: 15 -> 10; matrix products, arithmetic and copies ran while one was open for 1% -> 1% of each run, Pallas kernels for 28% -> 36%
where the time goes in v3:
time: 162 us
  Pallas kernels  77.9 us (48%)
  waiting for transfers between devices  43.8 us (27%)
  starting transfers between devices  36.5 us (23%)
  other arithmetic  2.17 us (1%)
    pallas_call x31, Pallas kernels, call(): pl.pallas_call(body, out_shape=[*outs, shape((8, LANES), F32)], in_specs=...  77.9 us
    ppermute x9, waiting for transfers between devices, local(): pp_y = lambda a: lax.ppermute(a, 'seq', xor[2])  22.4 us
    ppermute x12, starting transfers between devices, pp_dp(): return lambda a: lax.ppermute(a, 'dp', [(i, i ^ bit) for i in range(n_dp)])  19.1 us
    ppermute x12, waiting for transfers between devices, pp_dp(): return lambda a: lax.ppermute(a, 'dp', [(i, i ^ bit) for i in range(n_dp)])  10.2 us
    ppermute x9, starting transfers between devices, local(): pp_y = lambda a: lax.ppermute(a, 'seq', xor[2])  8.73 us
    ppermute x3, waiting for transfers between devices, send_back(): lax.ppermute(packs[r], 'seq', xor[r])  6.39 us
    ppermute x6, starting transfers between devices, rel(): lax.ppermute(parts[r], 'seq', xor[r])  5.39 us
  transfers between devices with their start and end apart: 38, of which 10 were waited for; matrix products, arithmetic and copies ran while one was open for 1% of the time, Pallas kernels for 36%

profile of v3, /device:TPU:0, one launch (start us, length us, event | category | flops | bytes accessed | tf_op | source)
XLA Modules:
  0.0 162.2 jit_solution(15541297098831996872)
XLA Ops:
  0.8 1.8 %split_tokens.1 = (bf16[128,768]{1,0:T(8,128)(2,1)S(1)}, bf16[128,768]{1,0:T(8,128)(2,1)S(1)}, bf16[128,768]{1,0:T(8,128)(2,1)S(1)}, bf16[128,768]{1,0:T(8,128)(2,1)S(1)}, f32[8,128]{1,0:T(8,128)S(1)}) custom-call(s32[16]{0:T(128)S(1)} %concatenate.9.refs_0_, bf16[4,128,768]{2,1,0:T(8,128)(2,1)} %refs_1_.2), custom_call_target="tpu_custom_call" | custom-call | flops 1 | bytes 1 | tf_op jit(solution)/shard_map/split_tokens/pallas_call | solution.py:495
  2.6 0.5 collective-permute-start
  3.2 2.6 %collective-permute-start.1 = (bf16[128,768]{1,0:T(8,128)(2,1)S(1)}, bf16[128,768]{1,0:T(8,128)(2,1)S(1)}, u32[]{:S(2)}, u32[]{:S(2)}) collective-permute-start(bf16[128,768]{1,0:T(8,128)(2,1)S(1)} %get-tuple-element.167), channel_id=1, source_target_pairs={{0,2},{1,3},{2,0},{3,1},{4,6},{5,7},{6,4},{7,5},{8,10},{9,11},{10,... | collective-permute-start | bytes 589832 | tf_op jit(solution)/shard_map/ppermute | solution.py:666
  5.8 1.8 %split_grads.1 = (bf16[128,768]{1,0:T(8,128)(2,1)S(1)}, bf16[128,768]{1,0:T(8,128)(2,1)S(1)}, bf16[128,768]{1,0:T(8,128)(2,1)S(1)}, bf16[128,768]{1,0:T(8,128)(2,1)S(1)}, f32[8,128]{1,0:T(8,128)S(1)}) custom-call(s32[16]{0:T(128)S(1)} %concatenate.9.refs_0_, bf16[4,128,768]{2,1,0:T(8,128)(2,1)} %refs_1_.3, f32[8,128]{1,0:T(8,128)S(1)} %get-tuple-element.169.refs_2_), custom_call_target="tpu_custom_call" | custom-call | flops 1 | bytes 1 | tf_op jit(solution)/shard_map/split_grads/pallas_call | solution.py:495
  7.6 0.2 collective-permute-start.3
  7.8 1.9 %collective-permute-start.4 = (bf16[128,768]{1,0:T(8,128)(2,1)S(1)}, bf16[128,768]{1,0:T(8,128)(2,1)S(1)}, u32[]{:S(2)}, u32[]{:S(2)}) collective-permute-start(bf16[128,768]{1,0:T(8,128)(2,1)S(1)} %get-tuple-element.174), channel_id=1, source_target_pairs={{0,2},{1,3},{2,0},{3,1},{4,6},{5,7},{6,4},{7,5},{8,10},{9,11},{10,... | collective-permute-start | bytes 589832 | tf_op jit(solution)/shard_map/ppermute | solution.py:666
  9.8 0.7 convert_bitcast_fusion
  11.0 0.8 subtract_convert_fusion
  12.1 3.1 %collective-permute-done.2.refs_3_ = bf16[128,768]{1,0:T(8,128)(2,1)S(1)} collective-permute-done((bf16[128,768]{1,0:T(8,128)(2,1)S(1)}, bf16[128,768]{1,0:T(8,128)(2,1)S(1)}, u32[]{:S(2)}, u32[]{:S(2)}) %collective-permute-start.2) | collective-permute-done | bytes 196640 | tf_op jit(solution)/shard_map/ppermute | solution.py:666
  15.3 14.4 %attend.1 = (bf16[512,768]{1,0:T(8,128)(2,1)}, bf16[512,768]{1,0:T(8,128)(2,1)}, bf16[512,768]{1,0:T(8,128)(2,1)}, bf16[512,768]{1,0:T(8,128)(2,1)}, f32[512,768...) custom-call(bf16[128,768]{1,0:T(8,128)(2,1)S(1)} %get-tuple-element., ...), custom_call_target="tpu_custom_call" | custom-call | flops 1 | bytes 1 | tf_op jit(solution)/shard_map/attend/pallas_call | solution.py:495
  29.8 15.7 %ffn.1 = (bf16[128,768]{1,0:T(8,128)(2,1)S(1)}, bf16[128,768]{1,0:T(8,128)(2,1)S(1)}, bf16[128,768]{1,0:T(8,128)(2,1)S(1)}, bf16[128,768]{1,0:T(8,128)(2,1)S(1)}...) custom-call(s32[16]{0:T(128)S(1)} %concatenate.9.refs_0_, ...), custom_call_target="tpu_custom_call" | custom-call | flops 1 | bytes 1 | tf_op jit(solution)/shard_map/ffn/pallas_call | solution.py:495
  45.6 0.4 collective-permute-start.6
  46.0 7.8 %ffn_back.1 = (bf16[2,8,192,384]{3,2,1,0:T(8,128)(2,1)S(1)}, bf16[2,8,192,384]{3,2,1,0:T(8,128)(2,1)S(1)}, f32[8,3072]{1,0:T(8,128)S(1)}, bf16[512,3072]{1,0:T(8,128)(2,1)S(1)}, f32[8,128]{1,0:T(8,128)S(1)}) custom-call(s32[16]{0:T(128)S(1)} %concatenate.9.refs_0_, f32[512,768]{1,0:T(8,128)S(1)} %get-tuple-element.184.refs_1_, ...), custom_call_target="tpu_custom_call" | custom-call | flops 1 | bytes 1 | tf_op jit(solution)/shard_map/ffn_back/pallas_call | solution.py:495
  53.8 0.2 collective-permute-start.7
  54.0 0.6 down_one.1
  54.7 1.9 %collective-permute-start.8 = (bf16[2,4,48,768]{3,2,1,0:T(8,128)(2,1)S(1)}, bf16[2,4,48,768]{3,2,1,0:T(8,128)(2,1)S(1)}, u32[]{:S(2)}, u32[]{:S(2)}) collective-permute-start(bf16[2,4,48,768]{3,2,1,0:T(8,128)(2,1)S(1)} %get-tuple-element.213), channel_id=1, source_target_pairs={{0,4},{4,0},{8,12},{12,8},{16,20},{20,16},{24,28},{28,24},{1,5},{5... | collective-permute-start | bytes 1769480 | tf_op jit(solution)/shard_map/ppermute | solution.py:734
  56.5 1.5 collective-permute-start.9
  58.1 9.2 %norm_back.1 = (f32[512,768]{1,0:T(8,128)}, bf16[512,768]{1,0:T(8,128)(2,1)S(1)}, bf16[512,128]{1,0:T(8,128)(2,1)S(1)}, f32[8,768]{1,0:T(8,128)S(1)}, bf16[2,8,4...) custom-call(s32[16]{0:T(128)S(1)} %concatenate.9.refs_0_, ...), custom_call_target="tpu_custom_call" | custom-call | flops 1 | bytes 1 | tf_op jit(solution)/shard_map/norm_back/pallas_call | solution.py:495
  67.3 0.6 up_one.1
  67.9 0.6 collective-permute-start.14
  68.5 0.5 collective-permute-start.15
  69.2 10.7 %attend_back.1 = (bf16[512,768]{1,0:T(8,128)(2,1)S(1)}, bf16[512,768]{1,0:T(8,128)(2,1)S(1)}, bf16[512,768]{1,0:T(8,128)(2,1)S(1)}, bf16[768,512]{1,0:T(8,128)(2...) custom-call(bf16[512,768]{1,0:T(8,128)(2,1)S(1)} %copy-done.8, ...), custom_call_target="tpu_custom_call" | custom-call | flops 1 | bytes 1 | tf_op jit(solution)/shard_map/attend_back/pallas_call | solution.py:495
  79.9 0.3 down_two.1
  80.2 1.6 collective-permute-start.12
  81.7 1.5 collective-permute-start.13
  83.3 4.5 %project_back.1 = (bf16[2,8,80,384]{3,2,1,0:T(8,128)(2,1)S(1)}, bf16[2,8,80,384]{3,2,1,0:T(8,128)(2,1)S(1)}, bf16[2,8,80,384]{3,2,1,0:T(8,128)(2,1)S(1)}, bf16[2...) custom-call(s32[16]{0:T(128)S(1)} %concatenate.9.refs_0_, ...), custom_call_target="tpu_custom_call" | custom-call | flops 1 | bytes 1 | tf_op jit(solution)/shard_map/project_back/pallas_call | solution.py:495
  87.8 0.5 collective-permute-start.11
  88.3 0.4 up_two.1
  88.8 0.6 collective-permute-start.22
  89.4 1.5 collective-permute-done.12.refs_0_
  90.9 1.5 collective-permute-start.23
  92.6 0.5 qkv_one.1
  93.1 0.6 collective-permute-start.20
  93.7 0.3 collective-permute-start.21
  94.0 1.7 %collective-permute-start.24 = (bf16[2,96,768]{2,1,0:T(8,128)(2,1)S(1)}, bf16[2,96,768]{2,1,0:T(8,128)(2,1)S(1)}, u32[]{:S(2)}, u32[]{:S(2)}) collective-permute-start(bf16[2,96,768]{2,1,0:T(8,128)(2,1)S(1)} %get-tuple-element.254), channel_id=1, source_target_pairs={{0,8},{4,12},{8,0},{12,4},{16,24},{20,28},{24,16},{28,20},{1,9},{5... | collective-permute-start | bytes 884744 | tf_op jit(solution)/shard_map/ppermute | solution.py:734
  95.9 7.1 %collective-permute-done.23.refs_0_.refs_5_ = bf16[4,128,384]{2,1,0:T(8,128)(2,1)S(1)} collective-permute-done((bf16[4,128,384]{2,1,0:T(8,128)(2,1)S(1)}, bf16[4,128,384]{2,1,0:T(8,128)(2,1)S(1)}, u32[]{:S(2)}, u32[]{:S(2)}) %collective-permute-start.23) | collective-permute-done | bytes 393248 | tf_op jit(solution)/shard_map/ppermute | solution.py:731
  103.1 1.7 %collective-permute-start.28 = (bf16[2,192,384]{2,1,0:T(8,128)(2,1)S(1)}, bf16[2,192,384]{2,1,0:T(8,128)(2,1)S(1)}, u32[]{:S(2)}, u32[]{:S(2)}) collective-permute-start(bf16[2,192,384]{2,1,0:T(8,128)(2,1)S(1)} %get-tuple-element.267), channel_id=1, source_target_pairs={{0,8},{4,12},{8,0},{12,4},{16,24},{20,28},{24,16},{28,20},{1,9},{5... | collective-permute-start | bytes 884744 | tf_op jit(solution)/shard_map/ppermute | solution.py:734
  104.9 2.6 %collective-permute-start.27 = (bf16[96,768]{1,0:T(8,128)(2,1)S(1)}, bf16[96,768]{1,0:T(8,128)(2,1)S(1)}, u32[]{:S(2)}, u32[]{:S(2)}) collective-permute-start(bf16[96,768]{1,0:T(8,128)(2,1)S(1)} %get-tuple-element.265), channel_id=1, source_target_pairs={{0,16},{4,20},{8,24},{12,28},{16,0},{20,4},{24,8},{28,12},{1,17},{... | collective-permute-start | bytes 442376 | tf_op jit(solution)/shard_map/ppermute | solution.py:734
  107.5 5.1 %collective-permute-done.20.refs_0_ = bf16[2,4,80,384]{3,2,1,0:T(8,128)(2,1)S(1)} collective-permute-done((bf16[2,4,80,384]{3,2,1,0:T(8,128)(2,1)S(1)}, bf16[2,4,80,384]{3,2,1,0:T(8,128)(2,1)S(1)}, u32[]{:S(2)}, u32[]{:S(2)}) %collective-permute-start.20) | collective-permute-done | bytes 491552 | tf_op jit(solution)/shard_map/ppermute | solution.py:734
  112.6 0.3 qkv_two.1
  112.9 0.8 collective-permute-start.25
  113.7 1.0 collective-permute-start.26
  114.9 1.1 collective-permute-start.29
  116.0 2.6 %collective-permute-start.31 = (bf16[192,384]{1,0:T(8,128)(2,1)S(1)}, bf16[192,384]{1,0:T(8,128)(2,1)S(1)}, u32[]{:S(2)}, u32[]{:S(2)}) collective-permute-start(bf16[192,384]{1,0:T(8,128)(2,1)S(1)} %get-tuple-element.276), channel_id=1, source_target_pairs={{0,16},{4,20},{8,24},{12,28},{16,0},{20,4},{24,8},{28,12},{1,17},{... | collective-permute-start | bytes 442376 | tf_op jit(solution)/shard_map/ppermute | solution.py:734
  118.6 6.7 %collective-permute-done.29.refs_2_ = bf16[96,768]{1,0:T(8,128)(2,1)S(1)} collective-permute-done((bf16[96,768]{1,0:T(8,128)(2,1)S(1)}, bf16[96,768]{1,0:T(8,128)(2,1)S(1)}, u32[]{:S(2)}, u32[]{:S(2)}) %collective-permute-start.29) | collective-permute-done | bytes 147488 | tf_op jit(solution)/shard_map/ppermute | solution.py:731
  125.3 0.6 down_six.1
  126.1 1.6 %collective-permute-start.30 = (bf16[2,208,384]{2,1,0:T(8,128)(2,1)S(1)}, bf16[2,208,384]{2,1,0:T(8,128)(2,1)S(1)}, u32[]{:S(2)}, u32[]{:S(2)}) collective-permute-start(bf16[2,208,384]{2,1,0:T(8,128)(2,1)S(1)} %get-tuple-element.274), channel_id=1, source_target_pairs={{0,8},{4,12},{8,0},{12,4},{16,24},{20,28},{24,16},{28,20},{1,9},{5... | collective-permute-start | bytes 958472 | tf_op jit(solution)/shard_map/ppermute | solution.py:734
  127.8 0.6 collective-permute-start.32
  128.4 4.6 %collective-permute-done.32.refs_2_ = bf16[192,384]{1,0:T(8,128)(2,1)S(1)} collective-permute-done((bf16[192,384]{1,0:T(8,128)(2,1)S(1)}, bf16[192,384]{1,0:T(8,128)(2,1)S(1)}, u32[]{:S(2)}, u32[]{:S(2)}) %collective-permute-start.32) | collective-permute-done | bytes 147488 | tf_op jit(solution)/shard_map/ppermute | solution.py:731
  133.0 0.6 up_six.1
  133.7 0.5 collective-permute-start.17
  134.2 0.5 collective-permute-start.18
  134.7 0.9 collective-permute-start.19
  135.7 2.7 %collective-permute-start.33 = (bf16[208,384]{1,0:T(8,128)(2,1)S(1)}, bf16[208,384]{1,0:T(8,128)(2,1)S(1)}, u32[]{:S(2)}, u32[]{:S(2)}) collective-permute-start(bf16[208,384]{1,0:T(8,128)(2,1)S(1)} %get-tuple-element.282), channel_id=1, source_target_pairs={{0,16},{4,20},{8,24},{12,28},{16,0},{20,4},{24,8},{28,12},{1,17},{... | collective-permute-start | bytes 479240 | tf_op jit(solution)/shard_map/ppermute | solution.py:734
  138.3 1.6 %down_end.1 = (f32[96,3072]{1,0:T(8,128)}, f32[8,128]{1,0:T(8,128)S(1)}) custom-call(s32[16]{0:T(128)S(1)} %concatenate.9.refs_0_, bf16[2,96,768]{2,1,0:T(8,128)(2,1)S(1)} %get-tuple-element.285.refs_1_, bf16[2,96,768]{2,1,0:T(8,128)(2,1)S(1)} %collective-permute-done.35.refs_2_, f32[8,128]{1,0:T(8,128)S(1)} %get-tuple-element.286.refs_3_), custom_call_target="tpu_custom_call" | custom-call | flops 1 | bytes 1 | tf_op jit(solution)/shard_map/down_end/pallas_call | solution.py:495
  140.0 1.6 %up_end.1 = (f32[768,384]{1,0:T(8,128)}, f32[8,128]{1,0:T(8,128)S(1)}) custom-call(s32[16]{0:T(128)S(1)} %concatenate.9.refs_0_, bf16[2,192,384]{2,1,0:T(8,128)(2,1)S(1)} %get-tuple-element.284.refs_1_, bf16[2,192,384]{2,1,0:T(8,128)(2,1)S(1)} %collective-permute-done.34.refs_2_, f32[8,128]{1,0:T(8,128)S(1)} %get-tuple-element.287.refs_3_), custom_call_target="tpu_custom_call" | custom-call | flops 1 | bytes 1 | tf_op jit(solution)/shard_map/up_end/pallas_call | solution.py:495
  141.6 5.1 %collective-permute-done.33.refs_0_ = bf16[208,384]{1,0:T(8,128)(2,1)S(1)} collective-permute-done((bf16[208,384]{1,0:T(8,128)(2,1)S(1)}, bf16[208,384]{1,0:T(8,128)(2,1)S(1)}, u32[]{:S(2)}, u32[]{:S(2)}) %collective-permute-start.33) | collective-permute-done | bytes 159776 | tf_op jit(solution)/shard_map/ppermute | solution.py:734
  146.7 0.7 collective-permute-start.36
  147.5 6.4 %collective-permute-done.19.refs_5_ = bf16[272,768]{1,0:T(8,128)(2,1)S(1)} collective-permute-done((bf16[272,768]{1,0:T(8,128)(2,1)S(1)}, bf16[272,768]{1,0:T(8,128)(2,1)S(1)}, u32[]{:S(2)}, u32[]{:S(2)}) %collective-permute-start.19) | collective-permute-done | bytes 417824 | tf_op jit(solution)/shard_map/ppermute | solution.py:875
  153.9 1.8 %unpack.1 = (bf16[4,128,768]{2,1,0:T(8,128)(2,1)}, bf16[4,128,768]{2,1,0:T(8,128)(2,1)}, f32[4,8,768]{2,1,0:T(8,128)}, f32[8,128]{1,0:T(8,128)S(1)}) custom-call(s32[16]{0:T(128)S(1)} %concatenate.9.refs_0_, f32[4,8,128]{2,1,0:T(8,128)S(1)} %broadcast_in_dim.12.refs_1_, bf16[272,768]{1,0:T(8,128)(2,1)S(1)} %get-tuple-element.242.refs_2_, ...), custom_call_target="tpu_custom_call" | custom-call | flops 1 | bytes 1 | tf_op jit(solution)/shard_map/unpack/pallas_call | solution.py:495
  155.7 2.5 %collective-permute-done.36.refs_2_ = bf16[208,384]{1,0:T(8,128)(2,1)S(1)} collective-permute-done((bf16[208,384]{1,0:T(8,128)(2,1)S(1)}, bf16[208,384]{1,0:T(8,128)(2,1)S(1)}, u32[]{:S(2)}, u32[]{:S(2)}) %collective-permute-start.36) | collective-permute-done | bytes 159776 | tf_op jit(solution)/shard_map/ppermute | solution.py:731
  158.2 0.6 qkv_six.1
  158.8 1.6 collective-permute-done.37.refs_2_
  160.4 1.6 qkv_end.1
  (115 shorter events, 2.4 us)
Async XLA Ops:
  0.7 14.5 %copy-start.16 = (bf16[768]{0:T(1024)(128)(2,1)S(1)}, bf16[768]{0:T(1024)(128)(2,1)}, u32[]{:S(2)}) copy-start(bf16[768]{0:T(1024)(128)(2,1)} %refs_10_.2) | copy-start | bytes 4612
  0.7 14.5 %copy-start.17 = (bf16[768]{0:T(1024)(128)(2,1)S(1)}, bf16[768]{0:T(1024)(128)(2,1)}, u32[]{:S(2)}) copy-start(bf16[768]{0:T(1024)(128)(2,1)} %refs_11_.2) | copy-start | bytes 4612
  0.7 14.5 %copy-start.18 = (bf16[768]{0:T(1024)(128)(2,1)S(1)}, bf16[768]{0:T(1024)(128)(2,1)}, u32[]{:S(2)}) copy-start(bf16[768]{0:T(1024)(128)(2,1)} %refs_12_.1) | copy-start | bytes 4612
  2.6 9.3 %collective-permute-start = (bf16[128,768]{1,0:T(8,128)(2,1)S(1)}, bf16[128,768]{1,0:T(8,128)(2,1)S(1)}, u32[]{:S(2)}, u32[]{:S(2)}) collective-permute-start(bf16[128,768]{1,0:T(8,128)(2,1)S(1)} %get-tuple-element.166), channel_id=1, source_target_pairs={{0,1},{1,0},{2,3},{3,2},{4,5},{5,4},{6,7},{7,6},{8,9},{9,8},{10,11... | collective-permute-start | bytes 589832 | tf_op jit(solution)/shard_map/ppermute | solution.py:666
  3.2 8.9 %collective-permute-start.1 = (bf16[128,768]{1,0:T(8,128)(2,1)S(1)}, bf16[128,768]{1,0:T(8,128)(2,1)S(1)}, u32[]{:S(2)}, u32[]{:S(2)}) collective-permute-start(bf16[128,768]{1,0:T(8,128)(2,1)S(1)} %get-tuple-element.167), channel_id=1, source_target_pairs={{0,2},{1,3},{2,0},{3,1},{4,6},{5,7},{6,4},{7,5},{8,10},{9,11},{10,... | collective-permute-start | bytes 589832 | tf_op jit(solution)/shard_map/ppermute | solution.py:666
  5.8 9.4 %collective-permute-start.2 = (bf16[128,768]{1,0:T(8,128)(2,1)S(1)}, bf16[128,768]{1,0:T(8,128)(2,1)S(1)}, u32[]{:S(2)}, u32[]{:S(2)}) collective-permute-start(bf16[128,768]{1,0:T(8,128)(2,1)S(1)} %get-tuple-element.168), channel_id=1, source_target_pairs={{0,3},{1,2},{2,1},{3,0},{4,7},{5,6},{6,5},{7,4},{8,11},{9,10},{10,... | collective-permute-start | bytes 589832 | tf_op jit(solution)/shard_map/ppermute | solution.py:666
  7.6 22.1 %collective-permute-start.3 = (bf16[128,768]{1,0:T(8,128)(2,1)S(1)}, bf16[128,768]{1,0:T(8,128)(2,1)S(1)}, u32[]{:S(2)}, u32[]{:S(2)}) collective-permute-start(bf16[128,768]{1,0:T(8,128)(2,1)S(1)} %get-tuple-element.173), channel_id=1, source_target_pairs={{0,1},{1,0},{2,3},{3,2},{4,5},{5,4},{6,7},{7,6},{8,9},{9,8},{10,11... | collective-permute-start | bytes 589832 | tf_op jit(solution)/shard_map/ppermute | solution.py:666
  7.8 21.9 %collective-permute-start.4 = (bf16[128,768]{1,0:T(8,128)(2,1)S(1)}, bf16[128,768]{1,0:T(8,128)(2,1)S(1)}, u32[]{:S(2)}, u32[]{:S(2)}) collective-permute-start(bf16[128,768]{1,0:T(8,128)(2,1)S(1)} %get-tuple-element.174), channel_id=1, source_target_pairs={{0,2},{1,3},{2,0},{3,1},{4,6},{5,7},{6,4},{7,5},{8,10},{9,11},{10,... | collective-permute-start | bytes 589832 | tf_op jit(solution)/shard_map/ppermute | solution.py:666
  12.0 17.8 %collective-permute-start.5 = (bf16[128,768]{1,0:T(8,128)(2,1)S(1)}, bf16[128,768]{1,0:T(8,128)(2,1)S(1)}, u32[]{:S(2)}, u32[]{:S(2)}) collective-permute-start(bf16[128,768]{1,0:T(8,128)(2,1)S(1)} %get-tuple-element.175), channel_id=1, source_target_pairs={{0,3},{1,2},{2,1},{3,0},{4,7},{5,6},{6,5},{7,4},{8,11},{9,10},{10,... | collective-permute-start | bytes 589832 | tf_op jit(solution)/shard_map/ppermute | solution.py:666
  15.2 14.5 %copy-start = (bf16[768,3072]{1,0:T(8,128)(2,1)S(1)}, bf16[768,3072]{1,0:T(8,128)(2,1)}, u32[]{:S(2)}) copy-start(bf16[768,3072]{1,0:T(8,128)(2,1)} %refs_3_.5) | copy-start | bytes 14155780
  15.2 14.5 %copy-start.13 = (bf16[768]{0:T(1024)(128)(2,1)S(1)}, bf16[768]{0:T(1024)(128)(2,1)}, u32[]{:S(2)}) copy-start(bf16[768]{0:T(1024)(128)(2,1)} %refs_6_.7) | copy-start | bytes 4612
  15.2 14.5 %copy-start.14 = (bf16[768]{0:T(1024)(128)(2,1)S(1)}, bf16[768]{0:T(1024)(128)(2,1)}, u32[]{:S(2)}) copy-start(bf16[768]{0:T(1024)(128)(2,1)} %refs_6_.6) | copy-start | bytes 4612
  15.2 14.5 %copy-start.15 = (bf16[3072]{0:T(1024)(128)(2,1)S(1)}, bf16[3072]{0:T(1024)(128)(2,1)}, u32[]{:S(2)}) copy-start(bf16[3072]{0:T(1024)(128)(2,1)} %refs_8_.1) | copy-start | bytes 18436
  15.3 14.5 %copy-start.19 = (bf16[768]{0:T(1024)(128)(2,1)S(1)}, bf16[768]{0:T(1024)(128)(2,1)}, u32[]{:S(2)}) copy-start(bf16[768]{0:T(1024)(128)(2,1)} %refs_4_.3) | copy-start | bytes 4612
  15.3 14.5 %copy-start.20 = (bf16[768]{0:T(1024)(128)(2,1)S(1)}, bf16[768]{0:T(1024)(128)(2,1)}, u32[]{:S(2)}) copy-start(bf16[768]{0:T(1024)(128)(2,1)} %refs_5_.4) | copy-start | bytes 4612
  15.3 14.5 %copy-start.21 = (bf16[768]{0:T(1024)(128)(2,1)S(1)}, bf16[768]{0:T(1024)(128)(2,1)}, u32[]{:S(2)}) copy-start(bf16[768]{0:T(1024)(128)(2,1)} %refs_6_.5) | copy-start | bytes 4612
  29.7 16.2 %slice-start = ((s8[4718592]{0:T(1024)(128)(4,1)}), s8[4194304]{0:T(1024)(128)(4,1)S(1)}, s32[]{:S(2)}) async-start(s8[4718592]{0:T(1024)(128)(4,1)} %bitcast.20), calls=%async_computation | async-start | bytes 8388608
  29.8 16.2 %slice-start.1 = ((s8[4718592]{0:T(1024)(128)(4,1)}), s8[524288]{0:T(1024)(128)(4,1)S(1)}, s32[]{:S(2)}) async-start(s8[4718592]{0:T(1024)(128)(4,1)} %bitcast.20), calls=%async_computation.1 | async-start | bytes 1048576
  45.6 8.5 %collective-permute-start.6 = (bf16[2,8,48,1536]{3,2,1,0:T(8,128)(2,1)S(1)}, bf16[2,8,48,1536]{3,2,1,0:T(8,128)(2,1)S(1)}, u32[]{:S(2)}, u32[]{:S(2)}) collective-permute-start(bf16[2,8,48,1536]{3,2,1,0:T(8,128)(2,1)S(1)} %get-tuple-element.190), channel_id=1, source_target_pairs={{0,1},{1,0},{2,3},{3,2},{4,5},{5,4},{6,7},{7,6},{8,9},{9,8},{10,11... | collective-permute-start | bytes 7077896 | tf_op jit(solution)/shard_map/ppermute | solution.py:730
  53.8 13.5 %collective-permute-start.7 = (bf16[2,8,192,384]{3,2,1,0:T(8,128)(2,1)S(1)}, bf16[2,8,192,384]{3,2,1,0:T(8,128)(2,1)S(1)}, u32[]{:S(2)}, u32[]{:S(2)}) collective-permute-start(bf16[2,8,192,384]{3,2,1,0:T(8,128)(2,1)S(1)} %get-tuple-element.197), channel_id=1, source_target_pairs={{0,1},{1,0},{2,3},{3,2},{4,5},{5,4},{6,7},{7,6},{8,9},{9,8},{10,11... | collective-permute-start | bytes 7077896 | tf_op jit(solution)/shard_map/ppermute | solution.py:730
  54.0 4.0 %copy-start.4 = (bf16[768,768]{1,0:T(8,128)(2,1)S(1)}, bf16[768,768]{1,0:T(8,128)(2,1)}, u32[]{:S(2)}) copy-start(bf16[768,768]{1,0:T(8,128)(2,1)} %refs_7_.5) | copy-start | bytes 3538948
  54.0 4.0 %copy-start.6 = (f32[512,768]{1,0:T(8,128)S(1)}, f32[512,768]{1,0:T(8,128)}, u32[]{:S(2)}) copy-start(f32[512,768]{1,0:T(8,128)} %get-tuple-element.189.refs_8_) | copy-start | bytes 4718596
  54.0 4.0 %copy-start.11 = (f32[512,128]{1,0:T(8,128)S(1)}, f32[512,128]{1,0:T(8,128)}, u32[]{:S(2)}) copy-start(f32[512,128]{1,0:T(8,128)} %get-tuple-element.188.refs_5_) | copy-start | bytes 786436
  54.7 25.2 %collective-permute-start.8 = (bf16[2,4,48,768]{3,2,1,0:T(8,128)(2,1)S(1)}, bf16[2,4,48,768]{3,2,1,0:T(8,128)(2,1)S(1)}, u32[]{:S(2)}, u32[]{:S(2)}) collective-permute-start(bf16[2,4,48,768]{3,2,1,0:T(8,128)(2,1)S(1)} %get-tuple-element.213), channel_id=1, source_target_pairs={{0,4},{4,0},{8,12},{12,8},{16,20},{20,16},{24,28},{28,24},{1,5},{5... | collective-permute-start | bytes 1769480 | tf_op jit(solution)/shard_map/ppermute | solution.py:734
  56.5 23.4 %collective-permute-start.9 = (bf16[8,48,768]{2,1,0:T(8,128)(2,1)S(1)}, bf16[8,48,768]{2,1,0:T(8,128)(2,1)S(1)}, u32[]{:S(2)}, u32[]{:S(2)}) collective-permute-start(bf16[8,48,768]{2,1,0:T(8,128)(2,1)S(1)} %get-tuple-element.214), channel_id=1, source_target_pairs={{0,2},{1,3},{2,0},{3,1},{4,6},{5,7},{6,4},{7,5},{8,10},{9,11},{10,... | collective-permute-start | bytes 1769480 | tf_op jit(solution)/shard_map/ppermute | solution.py:731
  67.3 1.8 %copy-start.8 = (bf16[512,768]{1,0:T(8,128)(2,1)S(1)}, bf16[512,768]{1,0:T(8,128)(2,1)}, u32[]{:S(2)}) copy-start(bf16[512,768]{1,0:T(8,128)(2,1)} %get-tuple-element.181.refs_0_) | copy-start | bytes 2359300
  67.3 1.8 %copy-start.9 = (bf16[512,768]{1,0:T(8,128)(2,1)S(1)}, bf16[512,768]{1,0:T(8,128)(2,1)}, u32[]{:S(2)}) copy-start(bf16[512,768]{1,0:T(8,128)(2,1)} %get-tuple-element.182.refs_1_) | copy-start | bytes 2359300
  67.3 1.8 %copy-start.10 = (bf16[512,768]{1,0:T(8,128)(2,1)S(1)}, bf16[512,768]{1,0:T(8,128)(2,1)}, u32[]{:S(2)}) copy-start(bf16[512,768]{1,0:T(8,128)(2,1)} %get-tuple-element.183.refs_2_) | copy-start | bytes 2359300
  67.3 1.8 %copy-start.12 = (bf16[512,128]{1,0:T(8,128)(2,1)S(1)}, bf16[512,128]{1,0:T(8,128)(2,1)}, u32[]{:S(2)}) copy-start(bf16[512,128]{1,0:T(8,128)(2,1)} %get-tuple-element.195.refs_4_) | copy-start | bytes 393220
  67.9 19.8 %collective-permute-start.14 = (bf16[2,4,96,384]{3,2,1,0:T(8,128)(2,1)S(1)}, bf16[2,4,96,384]{3,2,1,0:T(8,128)(2,1)S(1)}, u32[]{:S(2)}, u32[]{:S(2)}) collective-permute-start(bf16[2,4,96,384]{3,2,1,0:T(8,128)(2,1)S(1)} %get-tuple-element.232), channel_id=1, source_target_pairs={{0,4},{4,0},{8,12},{12,8},{16,20},{20,16},{24,28},{28,24},{1,5},{5... | collective-permute-start | bytes 1769480 | tf_op jit(solution)/shard_map/ppermute | solution.py:734
  68.5 19.3 %collective-permute-start.15 = (bf16[8,96,384]{2,1,0:T(8,128)(2,1)S(1)}, bf16[8,96,384]{2,1,0:T(8,128)(2,1)S(1)}, u32[]{:S(2)}, u32[]{:S(2)}) collective-permute-start(bf16[8,96,384]{2,1,0:T(8,128)(2,1)S(1)} %get-tuple-element.233), channel_id=1, source_target_pairs={{0,2},{1,3},{2,0},{3,1},{4,6},{5,7},{6,4},{7,5},{8,10},{9,11},{10,... | collective-permute-start | bytes 1769480 | tf_op jit(solution)/shard_map/ppermute | solution.py:731
  69.1 19.3 %collective-permute-start.16 = (bf16[2,8,48,384]{3,2,1,0:T(8,128)(2,1)S(1)}, bf16[2,8,48,384]{3,2,1,0:T(8,128)(2,1)S(1)}, u32[]{:S(2)}, u32[]{:S(2)}) collective-permute-start(bf16[2,8,48,384]{3,2,1,0:T(8,128)(2,1)S(1)} %get-tuple-element.236), channel_id=1, source_target_pairs={{0,1},{1,0},{2,3},{3,2},{4,5},{5,4},{6,7},{7,6},{8,9},{9,8},{10,11... | collective-permute-start | bytes 1769480 | tf_op jit(solution)/shard_map/ppermute | solution.py:730
  69.1 14.1 %copy-start.1 = (bf16[768,768]{1,0:T(8,128)(2,1)S(1)}, bf16[768,768]{1,0:T(8,128)(2,1)}, u32[]{:S(2)}) copy-start(bf16[768,768]{1,0:T(8,128)(2,1)} %refs_9_.3) | copy-start | bytes 3538948
  69.1 14.1 %copy-start.2 = (bf16[768,768]{1,0:T(8,128)(2,1)S(1)}, bf16[768,768]{1,0:T(8,128)(2,1)}, u32[]{:S(2)}) copy-start(bf16[768,768]{1,0:T(8,128)(2,1)} %refs_10_.3) | copy-start | bytes 3538948
  69.1 14.1 %copy-start.3 = (bf16[768,768]{1,0:T(8,128)(2,1)S(1)}, bf16[768,768]{1,0:T(8,128)(2,1)}, u32[]{:S(2)}) copy-start(bf16[768,768]{1,0:T(8,128)(2,1)} %refs_11_.3) | copy-start | bytes 3538948
  69.1 14.1 %copy-start.5 = (f32[512,768]{1,0:T(8,128)S(1)}, f32[512,768]{1,0:T(8,128)}, u32[]{:S(2)}) copy-start(f32[512,768]{1,0:T(8,128)} %get-tuple-element.208.refs_8_) | copy-start | bytes 4718596
  69.2 14.1 %copy-start.7 = (bf16[512,768]{1,0:T(8,128)(2,1)S(1)}, bf16[512,768]{1,0:T(8,128)(2,1)}, u32[]{:S(2)}) copy-start(bf16[512,768]{1,0:T(8,128)(2,1)} %get-tuple-element.207.refs_7_) | copy-start | bytes 2359300
  80.2 10.7 %collective-permute-start.12 = (bf16[4,48,768]{2,1,0:T(8,128)(2,1)S(1)}, bf16[4,48,768]{2,1,0:T(8,128)(2,1)S(1)}, u32[]{:S(2)}, u32[]{:S(2)}) collective-permute-start(bf16[4,48,768]{2,1,0:T(8,128)(2,1)S(1)} %get-tuple-element.228), channel_id=1, source_target_pairs={{0,2},{1,3},{2,0},{3,1},{4,6},{5,7},{6,4},{7,5},{8,10},{9,11},{10,... | collective-permute-start | bytes 884744 | tf_op jit(solution)/shard_map/ppermute | solution.py:731
  81.7 10.7 %collective-permute-start.13 = (bf16[4,48,768]{2,1,0:T(8,128)(2,1)S(1)}, bf16[4,48,768]{2,1,0:T(8,128)(2,1)S(1)}, u32[]{:S(2)}, u32[]{:S(2)}) collective-permute-start(bf16[4,48,768]{2,1,0:T(8,128)(2,1)S(1)} %get-tuple-element.229), channel_id=1, source_target_pairs={{0,4},{4,0},{8,12},{12,8},{16,20},{20,16},{24,28},{28,24},{1,5},{5... | collective-permute-start | bytes 884744 | tf_op jit(solution)/shard_map/ppermute | solution.py:734
  87.8 4.8 %collective-permute-start.10 = (bf16[2,8,80,384]{3,2,1,0:T(8,128)(2,1)S(1)}, bf16[2,8,80,384]{3,2,1,0:T(8,128)(2,1)S(1)}, u32[]{:S(2)}, u32[]{:S(2)}) collective-permute-start(bf16[2,8,80,384]{3,2,1,0:T(8,128)(2,1)S(1)} %get-tuple-element.224), channel_id=1, source_target_pairs={{0,1},{1,0},{2,3},{3,2},{4,5},{5,4},{6,7},{7,6},{8,9},{9,8},{10,11... | collective-permute-start | bytes 2949128 | tf_op jit(solution)/shard_map/ppermute | solution.py:730
  87.8 4.7 %collective-permute-start.11 = (bf16[2,8,80,384]{3,2,1,0:T(8,128)(2,1)S(1)}, bf16[2,8,80,384]{3,2,1,0:T(8,128)(2,1)S(1)}, u32[]{:S(2)}, u32[]{:S(2)}) collective-permute-start(bf16[2,8,80,384]{3,2,1,0:T(8,128)(2,1)S(1)} %get-tuple-element.225), channel_id=1, source_target_pairs={{0,1},{1,0},{2,3},{3,2},{4,5},{5,4},{6,7},{7,6},{8,9},{9,8},{10,11... | collective-permute-start | bytes 2949128 | tf_op jit(solution)/shard_map/ppermute | solution.py:730
  88.8 14.2 %collective-permute-start.22 = (bf16[4,160,384]{2,1,0:T(8,128)(2,1)S(1)}, bf16[4,160,384]{2,1,0:T(8,128)(2,1)S(1)}, u32[]{:S(2)}, u32[]{:S(2)}) collective-permute-start(bf16[4,160,384]{2,1,0:T(8,128)(2,1)S(1)} %get-tuple-element.250), channel_id=1, source_target_pairs={{0,4},{4,0},{8,12},{12,8},{16,20},{20,16},{24,28},{28,24},{1,5},{5... | collective-permute-start | bytes 1474568 | tf_op jit(solution)/shard_map/ppermute | solution.py:734
  90.9 12.1 %collective-permute-start.23 = (bf16[4,128,384]{2,1,0:T(8,128)(2,1)S(1)}, bf16[4,128,384]{2,1,0:T(8,128)(2,1)S(1)}, u32[]{:S(2)}, u32[]{:S(2)}) collective-permute-start(bf16[4,128,384]{2,1,0:T(8,128)(2,1)S(1)} %get-tuple-element.251), channel_id=1, source_target_pairs={{0,2},{1,3},{2,0},{3,1},{4,6},{5,7},{6,4},{7,5},{8,10},{9,11},{10,... | collective-permute-start | bytes 1179656 | tf_op jit(solution)/shard_map/ppermute | solution.py:731
  93.1 19.5 %collective-permute-start.20 = (bf16[2,4,80,384]{3,2,1,0:T(8,128)(2,1)S(1)}, bf16[2,4,80,384]{3,2,1,0:T(8,128)(2,1)S(1)}, u32[]{:S(2)}, u32[]{:S(2)}) collective-permute-start(bf16[2,4,80,384]{3,2,1,0:T(8,128)(2,1)S(1)} %get-tuple-element.246), channel_id=1, source_target_pairs={{0,4},{4,0},{8,12},{12,8},{16,20},{20,16},{24,28},{28,24},{1,5},{5... | collective-permute-start | bytes 1474568 | tf_op jit(solution)/shard_map/ppermute | solution.py:734
  93.7 18.9 %collective-permute-start.21 = (bf16[8,80,384]{2,1,0:T(8,128)(2,1)S(1)}, bf16[8,80,384]{2,1,0:T(8,128)(2,1)S(1)}, u32[]{:S(2)}, u32[]{:S(2)}) collective-permute-start(bf16[8,80,384]{2,1,0:T(8,128)(2,1)S(1)} %get-tuple-element.247), channel_id=1, source_target_pairs={{0,2},{1,3},{2,0},{3,1},{4,6},{5,7},{6,4},{7,5},{8,10},{9,11},{10,... | collective-permute-start | bytes 1474568 | tf_op jit(solution)/shard_map/ppermute | solution.py:731
  94.0 10.8 %collective-permute-start.24 = (bf16[2,96,768]{2,1,0:T(8,128)(2,1)S(1)}, bf16[2,96,768]{2,1,0:T(8,128)(2,1)S(1)}, u32[]{:S(2)}, u32[]{:S(2)}) collective-permute-start(bf16[2,96,768]{2,1,0:T(8,128)(2,1)S(1)} %get-tuple-element.254), channel_id=1, source_target_pairs={{0,8},{4,12},{8,0},{12,4},{16,24},{20,28},{24,16},{28,20},{1,9},{5... | collective-permute-start | bytes 884744 | tf_op jit(solution)/shard_map/ppermute | solution.py:734
  103.1 11.6 %collective-permute-start.28 = (bf16[2,192,384]{2,1,0:T(8,128)(2,1)S(1)}, bf16[2,192,384]{2,1,0:T(8,128)(2,1)S(1)}, u32[]{:S(2)}, u32[]{:S(2)}) collective-permute-start(bf16[2,192,384]{2,1,0:T(8,128)(2,1)S(1)} %get-tuple-element.267), channel_id=1, source_target_pairs={{0,8},{4,12},{8,0},{12,4},{16,24},{20,28},{24,16},{28,20},{1,9},{5... | collective-permute-start | bytes 884744 | tf_op jit(solution)/shard_map/ppermute | solution.py:734
  104.9 10.0 %collective-permute-start.27 = (bf16[96,768]{1,0:T(8,128)(2,1)S(1)}, bf16[96,768]{1,0:T(8,128)(2,1)S(1)}, u32[]{:S(2)}, u32[]{:S(2)}) collective-permute-start(bf16[96,768]{1,0:T(8,128)(2,1)S(1)} %get-tuple-element.265), channel_id=1, source_target_pairs={{0,16},{4,20},{8,24},{12,28},{16,0},{20,4},{24,8},{28,12},{1,17},{... | collective-permute-start | bytes 442376 | tf_op jit(solution)/shard_map/ppermute | solution.py:734
  112.9 13.0 %collective-permute-start.25 = (bf16[4,112,384]{2,1,0:T(8,128)(2,1)S(1)}, bf16[4,112,384]{2,1,0:T(8,128)(2,1)S(1)}, u32[]{:S(2)}, u32[]{:S(2)}) collective-permute-start(bf16[4,112,384]{2,1,0:T(8,128)(2,1)S(1)} %get-tuple-element.261), channel_id=1, source_target_pairs={{0,2},{1,3},{2,0},{3,1},{4,6},{5,7},{6,4},{7,5},{8,10},{9,11},{10,... | collective-permute-start | bytes 1032200 | tf_op jit(solution)/shard_map/ppermute | solution.py:731
  113.7 12.2 %collective-permute-start.26 = (bf16[4,96,384]{2,1,0:T(8,128)(2,1)S(1)}, bf16[4,96,384]{2,1,0:T(8,128)(2,1)S(1)}, u32[]{:S(2)}, u32[]{:S(2)}) collective-permute-start(bf16[4,96,384]{2,1,0:T(8,128)(2,1)S(1)} %get-tuple-element.262), channel_id=1, source_target_pairs={{0,4},{4,0},{8,12},{12,8},{16,20},{20,16},{24,28},{28,24},{1,5},{5... | collective-permute-start | bytes 884744 | tf_op jit(solution)/shard_map/ppermute | solution.py:734
  114.9 10.5 %collective-permute-start.29 = (bf16[96,768]{1,0:T(8,128)(2,1)S(1)}, bf16[96,768]{1,0:T(8,128)(2,1)S(1)}, u32[]{:S(2)}, u32[]{:S(2)}) collective-permute-start(bf16[96,768]{1,0:T(8,128)(2,1)S(1)} %get-tuple-element.271.refs_1_), channel_id=1, source_target_pairs={{0,2},{1,3},{2,0},{3,1},{4,6},{5,7},{6,4},{7,5},{8,10},{9,11},{10,... | collective-permute-start | bytes 442376 | tf_op jit(solution)/shard_map/ppermute | solution.py:731
  116.0 11.7 %collective-permute-start.31 = (bf16[192,384]{1,0:T(8,128)(2,1)S(1)}, bf16[192,384]{1,0:T(8,128)(2,1)S(1)}, u32[]{:S(2)}, u32[]{:S(2)}) collective-permute-start(bf16[192,384]{1,0:T(8,128)(2,1)S(1)} %get-tuple-element.276), channel_id=1, source_target_pairs={{0,16},{4,20},{8,24},{12,28},{16,0},{20,4},{24,8},{28,12},{1,17},{... | collective-permute-start | bytes 442376 | tf_op jit(solution)/shard_map/ppermute | solution.py:734
  126.1 8.6 %collective-permute-start.30 = (bf16[2,208,384]{2,1,0:T(8,128)(2,1)S(1)}, bf16[2,208,384]{2,1,0:T(8,128)(2,1)S(1)}, u32[]{:S(2)}, u32[]{:S(2)}) collective-permute-start(bf16[2,208,384]{2,1,0:T(8,128)(2,1)S(1)} %get-tuple-element.274), channel_id=1, source_target_pairs={{0,8},{4,12},{8,0},{12,4},{16,24},{20,28},{24,16},{28,20},{1,9},{5... | collective-permute-start | bytes 958472 | tf_op jit(solution)/shard_map/ppermute | solution.py:734
  127.8 19.7 %copy-start.22 = (s32[4,8]{1,0:T(4,128)S(1)}, s32[4,8]{1,0:T(4,128)}, u32[]{:S(2)}) copy-start(s32[4,8]{1,0:T(4,128)} %param.20) | copy-start | bytes 388
  127.8 5.2 %collective-permute-start.32 = (bf16[192,384]{1,0:T(8,128)(2,1)S(1)}, bf16[192,384]{1,0:T(8,128)(2,1)S(1)}, u32[]{:S(2)}, u32[]{:S(2)}) collective-permute-start(bf16[192,384]{1,0:T(8,128)(2,1)S(1)} %get-tuple-element.279.refs_1_), channel_id=1, source_target_pairs={{0,2},{1,3},{2,0},{3,1},{4,6},{5,7},{6,4},{7,5},{8,10},{9,11},{10,... | collective-permute-start | bytes 442376 | tf_op jit(solution)/shard_map/ppermute | solution.py:731
  128.4 7.3 %collective-permute-start.35 = (bf16[2,96,768]{2,1,0:T(8,128)(2,1)S(1)}, bf16[2,96,768]{2,1,0:T(8,128)(2,1)S(1)}, u32[]{:S(2)}, u32[]{:S(2)}) collective-permute-start(bf16[2,96,768]{2,1,0:T(8,128)(2,1)S(1)} %get-tuple-element.285.refs_1_), channel_id=1, source_target_pairs={{0,1},{1,0},{2,3},{3,2},{4,5},{5,4},{6,7},{7,6},{8,9},{9,8},{10,11... | collective-permute-start | bytes 884744 | tf_op jit(solution)/shard_map/ppermute | solution.py:730
  133.6 6.4 %collective-permute-start.34 = (bf16[2,192,384]{2,1,0:T(8,128)(2,1)S(1)}, bf16[2,192,384]{2,1,0:T(8,128)(2,1)S(1)}, u32[]{:S(2)}, u32[]{:S(2)}) collective-permute-start(bf16[2,192,384]{2,1,0:T(8,128)(2,1)S(1)} %get-tuple-element.284.refs_1_), channel_id=1, source_target_pairs={{0,1},{1,0},{2,3},{3,2},{4,5},{5,4},{6,7},{7,6},{8,9},{9,8},{10,11... | collective-permute-start | bytes 884744 | tf_op jit(solution)/shard_map/ppermute | solution.py:730
  133.7 13.8 %collective-permute-start.17 = (bf16[272,768]{1,0:T(8,128)(2,1)S(1)}, bf16[272,768]{1,0:T(8,128)(2,1)S(1)}, u32[]{:S(2)}, u32[]{:S(2)}) collective-permute-start(bf16[272,768]{1,0:T(8,128)(2,1)S(1)} %get-tuple-element.243), channel_id=1, source_target_pairs={{0,1},{1,0},{2,3},{3,2},{4,5},{5,4},{6,7},{7,6},{8,9},{9,8},{10,11... | collective-permute-start | bytes 1253384 | tf_op jit(solution)/shard_map/ppermute | solution.py:875
  134.2 13.3 %collective-permute-start.18 = (bf16[272,768]{1,0:T(8,128)(2,1)S(1)}, bf16[272,768]{1,0:T(8,128)(2,1)S(1)}, u32[]{:S(2)}, u32[]{:S(2)}) collective-permute-start(bf16[272,768]{1,0:T(8,128)(2,1)S(1)} %get-tuple-element.244), channel_id=1, source_target_pairs={{0,2},{1,3},{2,0},{3,1},{4,6},{5,7},{6,4},{7,5},{8,10},{9,11},{10,... | collective-permute-start | bytes 1253384 | tf_op jit(solution)/shard_map/ppermute | solution.py:875
  134.7 19.2 %collective-permute-start.19 = (bf16[272,768]{1,0:T(8,128)(2,1)S(1)}, bf16[272,768]{1,0:T(8,128)(2,1)S(1)}, u32[]{:S(2)}, u32[]{:S(2)}) collective-permute-start(bf16[272,768]{1,0:T(8,128)(2,1)S(1)} %get-tuple-element.245), channel_id=1, source_target_pairs={{0,3},{1,2},{2,1},{3,0},{4,7},{5,6},{6,5},{7,4},{8,11},{9,10},{10,... | collective-permute-start | bytes 1253384 | tf_op jit(solution)/shard_map/ppermute | solution.py:875
  135.7 11.0 %collective-permute-start.33 = (bf16[208,384]{1,0:T(8,128)(2,1)S(1)}, bf16[208,384]{1,0:T(8,128)(2,1)S(1)}, u32[]{:S(2)}, u32[]{:S(2)}) collective-permute-start(bf16[208,384]{1,0:T(8,128)(2,1)S(1)} %get-tuple-element.282), channel_id=1, source_target_pairs={{0,16},{4,20},{8,24},{12,28},{16,0},{20,4},{24,8},{28,12},{1,17},{... | collective-permute-start | bytes 479240 | tf_op jit(solution)/shard_map/ppermute | solution.py:734
  146.7 11.4 %collective-permute-start.36 = (bf16[208,384]{1,0:T(8,128)(2,1)S(1)}, bf16[208,384]{1,0:T(8,128)(2,1)S(1)}, u32[]{:S(2)}, u32[]{:S(2)}) collective-permute-start(bf16[208,384]{1,0:T(8,128)(2,1)S(1)} %get-tuple-element.293.refs_1_), channel_id=1, source_target_pairs={{0,2},{1,3},{2,0},{3,1},{4,6},{5,7},{6,4},{7,5},{8,10},{9,11},{10,... | collective-permute-start | bytes 479240 | tf_op jit(solution)/shard_map/ppermute | solution.py:731
  158.7 1.7 %collective-permute-start.37 = (bf16[2,208,384]{2,1,0:T(8,128)(2,1)S(1)}, bf16[2,208,384]{2,1,0:T(8,128)(2,1)S(1)}, u32[]{:S(2)}, u32[]{:S(2)}) collective-permute-start(bf16[2,208,384]{2,1,0:T(8,128)(2,1)S(1)} %get-tuple-element.295.refs_1_), channel_id=1, source_target_pairs={{0,1},{1,0},{2,3},{3,2},{4,5},{5,4},{6,7},{7,6},{8,9},{9,8},{10,11... | collective-permute-start | bytes 958472 | tf_op jit(solution)/shard_map/ppermute | solution.py:730

commit v4 on v3

--- a/solution.py
+++ b/solution.py
@@ -16,6 +16,7 @@
 LANES = 128
 
 PART = 16
+ROWS = 32
 
 
 def nn(a, b):
@@ -61,6 +62,17 @@
     return ref[...].astype(F32).reshape(1, ref.shape[0])
 
 
+def fold(v):
+    out = v[:8]
+    for i in range(8, v.shape[0], 8):
+        out += v[i : i + 8]
+    return out
+
+
+def total(v):
+    return jnp.sum(v, axis=0, keepdims=True)
+
+
 def head_lane(h):
     lane = lax.broadcasted_iota(jnp.int32, (1, LANES), 1)
     return (lane % PART == h) & (lane >= PART) & (lane < 4 * PART)
@@ -97,6 +109,10 @@
 def split_kernel(info, x_ref, *refs):
     outs, sems = refs[:-1], refs[-1]
     wait(copies([(x_ref.at[info[10] ^ r], outs[r]) for r in range(len(outs))], sems))
+
+
+def fetch_kernel(a, b, c, x, y, z, sems):
+    wait(copies([(a, x), (b, y), (c, z)], sems))
 
 
 def pack_kernel(o0, o1, o2, o3, i0, i1, i2, i3, pool, p0, p1, p2, p3):
@@ -120,24 +136,21 @@
 
 
 def attend_kernel(
-    x0, x1, x2, x3, wq_h, wk_h, wv_h, wo_h, oh_ref, ka_ref, bq_ref, bv_ref, bo_ref,
+    x0, x1, x2, x3, wq, wk, wv, wo_h, oh_ref, ka_ref, bq_ref, bv_ref, bo_ref,
     x_h, q_h, k_h, v_h, att_h, inv_h, qa_h, n1_out,
-    x_out, q_out, k_out, v_out, att_out, inv_out, qa_out, wq, wk, wv, wo, stat, sems,
+    x_out, q_out, k_out, v_out, att_out, inv_out, qa_out, wo, stat, sems,
 ):
     n = x0.shape[0]
     bq, bv, bo = row(bq_ref), row(bv_ref), row(bo_ref)
-    ws = copies([(wq_h, wq), (wk_h, wk), (wv_h, wv), (wo_h, wo)], sems, 4)
+    last = copies([(wo_h, wo)], sems, 4)
     for r, ref in enumerate((x0, x1, x2, x3)):
         x_out[r * n : (r + 1) * n] = ref[...]
     outs = copies([(x_out, x_h)], sems, 8)
     x = x_out[...]
-    ws[0].wait()
     q_out[...] = ((nn(x, wq[...]) + bq).astype(BF).astype(F32) * (HD**-0.5)).astype(BF)
     outs += copies([(q_out, q_h)], sems, 9)
-    ws[1].wait()
     k_out[...] = nn(x, wk[...]).astype(BF)
     outs += copies([(k_out, k_h)], sems, 10)
-    ws[2].wait()
     v_out[...] = (nn(x, wv[...]) + bv).astype(BF)
     outs += copies([(v_out, v_h)], sems, 11)
     tok, width = x.shape
@@ -163,25 +176,27 @@
         att_out[:, sl] = jnp.concatenate(parts, axis=0).T
         return carry
 
-    lax.fori_loop(0, width // LANES, pair, 0)
+    lax.fori_loop(0, width // LANES, pair, 0, unroll=2)
     outs += copies([(att_out, att_h)], sems, 12)
     hi, mid, low = three_parts(stat[...])
     zero = jnp.zeros((PART, tok), BF)
     qa_out[...] = jnp.concatenate([zero, hi, mid, low, zero, zero, zero, zero], axis=0).T + oh_ref[...]
     outs += copies([(qa_out, qa_h)], sems, 13)
-    ws[3].wait()
-    mixed = nn(att_out[...].astype(BF), wo[...]) + bo
-    n1, inv = norm(x.astype(F32) + mixed)
-    n1_out[...] = n1
-    inv_out[...] = jnp.broadcast_to(inv, inv_out.shape)
+    wait(last)
+    n1_out[...] = nn(att_out[...].astype(BF), wo[...])
+    for at in range(0, tok, ROWS):
+        rows = slice(at, at + ROWS)
+        n1, inv = norm(x_out[rows, :].astype(F32) + (n1_out[rows, :] + bo))
+        n1_out[rows, :] = n1
+        inv_out[rows, :] = jnp.broadcast_to(inv, (ROWS, LANES))
     outs += copies([(inv_out, inv_h)], sems, 14)
     wait(outs)
 
 
 def ffn_kernel(
     lay, info, n1_ref, ga_ref, sa_ref, bd_ref, gf_ref, sf_ref, wu, bu_ref, wd_h, g0, g1, g2, g3, oh_ref, oht_ref, gpl,
-    o0, o1, o2, o3, gp_h, send, keep, pool_out, r2_out, vec_out,
-    hl, acc, act, gt, gp_out, wd, bu, sem_g, sem_w,
+    o0, o1, o2, o3, gp_out, send, keep, pool_out, r2_out, vec_out,
+    hl, acc, act, gt, wd, bu, gsum, hi, low, gl, sem_w,
 ):
     n = g0.shape[0]
     ga, sa, bd, gf, sf = row(ga_ref), row(sa_ref), row(bd_ref), row(gf_ref), row(sf_ref)
@@ -191,10 +206,6 @@
     tile = width
     steps = ff // tile
 
-    def slopes(t):
-        cols = pl.ds(pl.multiple_of(t * tile, tile), tile)
-        return pltpu.make_async_copy(gp_out.at[:, cols], gp_h.at[:, cols], sem_g.at[t])
-
     def weights(t):
         rows = pl.ds(pl.multiple_of(t * tile, tile), tile)
         return pltpu.make_async_copy(wd_h.at[rows, :], wd.at[rows, :], sem_w.at[t])
@@ -207,43 +218,41 @@
     def step(t, carry):
         cols = pl.ds(pl.multiple_of(t * tile, tile), tile)
         weights(t).wait()
-        for r in range(4):
-            rows = pl.ds(r * n, n)
+        for r in range(2):
+            rows = pl.ds(r * 2 * n, 2 * n)
             a, d = gelu_both(nn(hl[rows, :], wu[:, cols]) + bu[:, cols])
             ab = a.astype(BF)
             act[rows, cols] = ab
             gp_out[rows, cols] = d.astype(BF)
             acc[rows, :] += nn(ab, wd[cols, :])
-        slopes(t).start()
         return carry
 
     lax.fori_loop(0, steps, step, 0)
-    gain = jnp.zeros((1, width), F32)
-    shift = jnp.zeros((1, width), F32)
-    bias = jnp.zeros((1, width), F32)
-    pool = jnp.zeros(pool_out.shape, F32)
-    for r, (o, g) in enumerate(((o0, g0), (o1, g1), (o2, g2), (o3, g3))):
-        rows = pl.ds(r * n, n)
+    oh = oh_ref[...]
+    gsum[...] = nn(jnp.concatenate([oh, oh], axis=1), gpl[...])
+    gain, shift, bias = (jnp.zeros((8, width), F32) for _ in range(3))
+    gs, os = (g0, g1, g2, g3), (o0, o1, o2, o3)
+    for at in range(0, tok, ROWS):
+        rows = slice(at, at + ROWS)
+        r, of = at // n, slice(at % n, at % n + ROWS)
         hidden = n1_ref[rows, :] * ga + sa
         n2, inv = norm(hidden + (acc[rows, :] + bd))
         result = n2 * gf + sf
-        o[...] = result.astype(BF)
-        hi, low = two_parts(result)
-        oht = oht_ref[:, r * n : (r + 1) * n]
-        pool += nn(oht, hi) + nn(oht, low)
-        oh = oh_ref[rows, :]
-        gout = g[...].astype(F32) + nn(jnp.concatenate([oh, oh], axis=1), gpl[...])
-        gain += jnp.sum(gout * n2, axis=0, keepdims=True)
-        shift += jnp.sum(gout, axis=0, keepdims=True)
+        os[r][of, :] = result.astype(BF)
+        hi[rows, :], low[rows, :] = two_parts(result)
+        gout = gs[r][of, :].astype(F32) + gsum[rows, :]
+        gain += fold(gout * n2)
+        shift += fold(gout)
         gr2 = norm_back(gout * gf, n2, inv)
         r2_out[rows, :] = gr2
         low_g = gr2.astype(BF)
-        bias += jnp.sum(low_g.astype(F32), axis=0, keepdims=True)
-        gt[:, r * n : (r + 1) * n] = low_g.T
-    pool_out[...] = pool
-    vec_out[...] = jnp.concatenate([bias, gain, shift, jnp.zeros((5, width), F32)], axis=0)
+        bias += fold(low_g.astype(F32))
+        gl[rows, :] = low_g
+    gt[...] = gl[...].T
+    pool_out[...] = nn(oht_ref[...], hi[...]) + nn(oht_ref[...], low[...])
+    vec_out[...] = jnp.concatenate([total(v) for v in (bias, gain, shift)] + [jnp.zeros((5, width), F32)], axis=0)
     half = ff // 2
-    part = 512
+    part = 768
 
     def piece(i, carry):
         for rc, ref in ((1, send), (0, keep)):
@@ -253,14 +262,12 @@
         return carry
 
     lax.fori_loop(0, half // part, piece, 0)
-    for t in range(steps):
-        slopes(t).wait()
 
 
 def ffn_back_kernel(
-    lay, info, r2_ref, gp_h, wd, n1_ref, ga_ref, sa_ref,
+    lay, info, r2_ref, gp, wd, n1_ref, ga_ref, sa_ref,
     send, keep, bup_out, gpre_out,
-    gl, hlt, gp, sem_w,
+    gl, hlt,
 ):
     ga, sa = row(ga_ref), row(sa_ref)
     width = hlt.shape[0]
@@ -269,19 +276,12 @@
     tile = width
     steps = ff // tile
 
-    def load(t):
-        cols = pl.ds(pl.multiple_of(t * tile, tile), tile)
-        return pltpu.make_async_copy(gp_h.at[:, cols], gp.at[:, cols], sem_w.at[t])
-
-    for t in range(steps):
-        load(t).start()
     gl[...] = r2_ref[...].astype(BF)
     hlt[...] = (n1_ref[...] * ga + sa).astype(BF).T
     per = 2 if lay[0] > 1 else 1
 
     def step(t, carry):
         cols = pl.ds(pl.multiple_of(t * tile, tile), tile)
-        load(t).wait()
         gpre = (nt(gl[...], wd[cols, :]) * gp[:, cols].astype(F32)).astype(BF)
         gpre_out[:, cols] = gpre
         bup_out[:, cols] = jnp.broadcast_to(
@@ -302,21 +302,16 @@
 
 def norm_back_kernel(
     lay, info, r2_ref, gpre, wu, n1_ref, inv_ref, ga_ref, wo, att,
-    r1_h, gatt_out, gaug_out, vec_out, osend, okeep,
-    gt, r1_out, acc, sems,
+    r1_out, gatt_out, gaug_out, vec_out, osend, okeep,
+    gt, acc, gm, hi, low,
 ):
     ga = row(ga_ref)
     tok, width = r2_ref.shape
     half = width // 2
-    n = tok // 4
-    gain = jnp.zeros((1, width), F32)
-    shift = jnp.zeros((1, width), F32)
-    bias = jnp.zeros((1, width), F32)
     head = lax.broadcasted_iota(jnp.int32, (width, LANES), 0) // HD
     lane = lax.broadcasted_iota(jnp.int32, (width, LANES), 1)
     pick = ((lane % PART == head) & (lane >= PART) & (lane < 4 * PART)).astype(BF)
     lane1 = lax.broadcasted_iota(jnp.int32, (1, LANES), 1)
-    outs = []
 
     def step(t, carry):
         cols = pl.ds(pl.multiple_of(t * width, width), width)
@@ -325,30 +320,30 @@
 
     acc[...] = r2_ref[...]
     lax.fori_loop(0, gpre.shape[1] // width, step, 0)
-    for r in range(4):
-        rows = pl.ds(r * n, n)
+    gain, shift, bias = (jnp.zeros((8, width), F32) for _ in range(3))
+    for at in range(0, tok, ROWS):
+        rows = slice(at, at + ROWS)
         gh = acc[rows, :]
         n1 = n1_ref[rows, :]
-        gain += jnp.sum(gh * n1, axis=0, keepdims=True)
-        shift += jnp.sum(gh, axis=0, keepdims=True)
+        gain += fold(gh * n1)
+        shift += fold(gh)
         gr1 = norm_back(gh * ga, n1, inv_ref[rows, :1])
         r1_out[rows, :] = gr1
-        outs += copies([(r1_out.at[rows, :], r1_h.at[rows, :])], sems, r)
-        gm = gr1.astype(BF)
-        bias += jnp.sum(gm.astype(F32), axis=0, keepdims=True)
-        gt[:, r * n : (r + 1) * n] = gm.T
-        gatt = nt(gm, wo[...]).astype(BF)
-        gatt_out[rows, :] = gatt
-        a, b, c = three_parts(gatt.astype(F32) * att[rows, :])
-        delta = nn(a, pick) + nn(b, pick) + nn(c, pick)
-        a, b, c = three_parts(delta)
-        gaug_out[rows, :] = jnp.where(lane1 < 2 * PART, a, jnp.where(lane1 < 3 * PART, b, c))
-    vec_out[...] = jnp.concatenate([bias, gain, shift, jnp.zeros((5, width), F32)], axis=0)
+        low_g = gr1.astype(BF)
+        bias += fold(low_g.astype(F32))
+        gm[rows, :] = low_g
+    gt[...] = gm[...].T
+    gatt_out[...] = nt(gm[...], wo[...]).astype(BF)
+    for at in range(0, tok, ROWS):
+        rows = slice(at, at + ROWS)
+        hi[rows, :], low[rows, :] = two_parts(gatt_out[rows, :].astype(F32) * att[rows, :])
+    a, b, c = three_parts(nn(hi[...], pick) + nn(low[...], pick))
+    gaug_out[...] = jnp.where(lane1 < 2 * PART, a, jnp.where(lane1 < 3 * PART, b, c))
+    vec_out[...] = jnp.concatenate([total(v) for v in (bias, gain, shift)] + [jnp.zeros((5, width), F32)], axis=0)
     sides = [att[:, pl.ds(pl.multiple_of((info[8] ^ rc) * half, half), half)].astype(BF) for rc in (1, 0)]
     res = nn(gt[...], jnp.concatenate(sides, axis=1))
     put_shards(osend, info, lay, slice(None), res[:, :half])
     put_shards(okeep, info, lay, slice(None), res[:, half:])
-    wait(outs)
 
 
 def attend_back_kernel(
@@ -389,16 +384,13 @@
         gvt[sl, :] = gvb.T
         return carry
 
-    lax.fori_loop(0, width // LANES, pair, 0)
+    lax.fori_loop(0, width // LANES, pair, 0, unroll=6)
     bq = jnp.sum(gq[...].astype(F32), axis=0, keepdims=True)
     bv = jnp.sum(gv[...].astype(F32), axis=0, keepdims=True)
     vec_out[...] = jnp.concatenate([bq, bv, jnp.zeros((6, width), F32)], axis=0)
 
 
-def project_back_kernel(
-    lay, info, gq, gk, gv, gqt, gkt, gvt, x_ref, r1, wq, wk, wv, vecs, bups,
-    send_a, send_b, keep_a, keep_b, o0, o1, o2, o3,
-):
+def weights_back_kernel(lay, info, gqt, gkt, gvt, x_ref, vecs, bups, send_a, send_b, keep_a, keep_b):
     width = x_ref.shape[1]
     n, halves, rs = lay
     half = width // 2
@@ -438,10 +430,12 @@
                 mine = jnp.where((info[8] ^ rc) == 0, 1.0, 0.0)
                 put_rows(wa, info[j], info[9], 64, halves, slice(None), block * mine)
 
-    total = r1[...] + nt(gq[...], wq[...]) + nt(gk[...], wk[...]) + nt(gv[...], wv[...])
+
+def input_back_kernel(gq, gk, gv, r1, wq, wk, wv, o0, o1, o2, o3):
+    whole = r1[...] + nt(gq[...], wq[...]) + nt(gk[...], wk[...]) + nt(gv[...], wv[...])
     for r, o in enumerate((o0, o1, o2, o3)):
         c = o.shape[0]
-        o[...] = total[r * c : (r + 1) * c].astype(BF)
+        o[...] = whole[r * c : (r + 1) * c].astype(BF)
 
 
 WHOLE = pl.BlockSpec(memory_space=pltpu.VMEM)
@@ -611,13 +605,17 @@
             out[pl.ds(pl.multiple_of(at, m), m), :] = ref[a].astype(F32)
 
 
-def qkv_kernel(info, mine, other, gq, gk, gv, go, *vecs):
+def qkv_kernel(info, here, over_y, over_core, over_both, gq, gk, gv, go, *vecs):
     half = gq.shape[1] // 2
+    y0 = info[9] == 0
+    mine, other = (
+        [jnp.where(y0, a[...], b[...]), jnp.where(y0, b[...], a[...])] for a, b in ((here, over_y), (over_core, over_both))
+    )
     for rc, ref in ((0, mine), (1, other)):
         at = pl.ds(pl.multiple_of((info[8] ^ rc) * half, half), half)
 
         def put(out, *spans):
-            parts = [ref[a, i : i + m] for a, i, m in spans]
+            parts = [ref[a][i : i + m] for a, i, m in spans]
             out[:, at] = jnp.concatenate(parts, axis=0).astype(F32)
 
         put(gq, (0, 0, 48), (1, 0, 48))
@@ -625,11 +623,11 @@
         put(gv, (0, 112, 48), (1, 112, 48))
         put(go, (0, 80, 32), (0, 192, 16), (1, 80, 32), (1, 192, 16))
     rs = vecs[0].shape[0]
-    low = jnp.where(info[8] == 0, mine[:, 64:80, :].astype(F32), other[:, 64:80, :].astype(F32))
+    low = [jnp.where(info[8] == 0, m[64:80].astype(F32), o[64:80].astype(F32)) for m, o in zip(mine, other)]
     for i, out in enumerate(vecs[:8]):
-        out[...] = low[0, i, :rs]
+        out[...] = low[0][i, :rs]
     for c in range(4):
-        vecs[8][pl.ds(c * rs, rs)] = low[1, c, :rs]
+        vecs[8][pl.ds(c * rs, rs)] = low[1][c, :rs]
 
 
 def local(n_dp, n_seq, *args):
@@ -689,19 +687,22 @@
     sq = shape((tok, width))
     sqf = shape((tok, width), F32)
     row_lengths = jnp.broadcast_to(seg_lengths.astype(F32)[:, :, None], (rows, SEGS, LANES))
+    near = line.call(
+        fetch_kernel, [shape((width, width))] * 3, (w_query, w_key, w_value), scratch=[sems(3)], name="fetch",
+        far_in=range(3),
+    )
     lanes = shape((tok, LANES))
     lanes_f = shape((tok, LANES), F32)
     x, q, k, v, att, inv, qaug, n1 = line.call(
         attend_kernel,
         [sq, sq, sq, sq, sqf, lanes_f, lanes, sqf],
-        (*xs, w_query, w_key, w_value, w_out, onehot, kaug, b_query, b_value, b_out),
+        (*xs, *near, w_out, onehot, kaug, b_query, b_value, b_out),
         scratch=[buf((tok, width))] * 4
         + [buf((tok, width), F32), buf((tok, LANES), F32), buf((tok, LANES))]
-        + [buf((width, width))] * 4
-        + [buf((PART, tok), F32), sems(15)],
+        + [buf((width, width)), buf((PART, tok), F32), sems(15)],
         name="attend",
         mib=20,
-        far_in=range(4, 8),
+        far_in=(7,),
         far_out=range(7),
     )
 
@@ -718,13 +719,13 @@
         ),
         scalars=(0,),
         scratch=[
-            buf((tok, width)), buf((tok, width), F32), buf((tok, ff)), buf((width, tok)), buf((tok, ff)), buf((ff, width)),
-            buf((1, ff), F32), sems(steps), sems(steps),
+            buf((tok, width)), buf((tok, width), F32), buf((tok, ff)), buf((width, tok)), buf((ff, width)),
+            buf((1, ff), F32), buf((tok, width), F32), buf((tok, width)), buf((tok, width)), buf((tok, width)),
+            sems(steps),
         ],
         name="ffn",
         mib=24,
         far_in=(9,),
-        far_out=(4,),
     )
 
     pp_core = lambda a: lax.ppermute(a, "seq", xor[1])
@@ -802,6 +803,10 @@
             (mine,) = self.run(five_kernel, [(a + b, c)], (self.got, self.kept))
             self.got, self.kept = pp_y(mine), mine
 
+        def five_all(self):
+            (mine,) = self.run(five_kernel, [(self.dims[0] + self.dims[1], self.dims[2])], (self.got, self.kept))
+            self.kept, self.got = mine, [pp_y(mine), pp_core(mine), lax.ppermute(mine, "seq", xor[3])]
+
         def six(self):
             a, b, c = self.dims
             (both,) = self.run(six_kernel, [(2, a + b, c)], (info, self.kept, self.got), scalars=(0,))
@@ -809,7 +814,8 @@
 
         def end(self, kernel, outs):
             return line.call(
-                kernel, outs, (info, self.kept, self.got), scalars=(0,), name=self.name + "end", mib=16
+                kernel, outs, (info, self.kept, *(self.got if isinstance(self.got, list) else [self.got])), scalars=(0,),
+                name=self.name + "end", mib=16,
             )
 
     wire_u = shape((halves, n, half // halves, ff // n))
@@ -820,10 +826,9 @@
         [wire_u, wire_u, shape((8, ff), F32), shape((tok, ff))],
         (info, r2, gp, w_down, n1, gain_attn, shift_attn),
         scalars=(0,),
-        scratch=[buf((tok, width)), buf((width, tok)), buf((tok, ff)), sems(steps)],
+        scratch=[buf((tok, width)), buf((width, tok))],
         name="ffn_back",
         mib=12,
-        far_in=(2,),
     )
     if fast:
         u_got = pp_core(u_send)
@@ -836,10 +841,9 @@
         [sqf, sq, shape((tok, LANES)), shape((8, width), F32), wire_o, wire_o],
         (info, r2, gpre, w_up, n1, inv, gain_attn, w_out, att),
         scalars=(0,),
-        scratch=[buf((width, tok)), buf((tok, width), F32), buf((tok, width), F32), sems(4)],
+        scratch=[buf((width, tok)), buf((tok, width), F32)] + [buf((tok, width))] * 3,
         name="norm_back",
         mib=14,
-        far_out=(0,),
     )
     if fast:
         o_got = pp_core(o_send)
@@ -859,16 +863,20 @@
         down.two()
     rows_a, rows_b = (80, 80) if fast else (2 * width, width)
     wire_a, wire_b = shape((halves, n, rows_a, half)), shape((halves, n, rows_b, half))
-    qa_send, qb_send, qa_keep, qb_keep, *ins = line.call(
-        functools.partial(project_back_kernel, lay),
-        [wire_a, wire_b, wire_a, wire_b] + [shape((piece, width))] * 4,
-        (info, gq, gk, gv, gqt, gkt, gvt, x, r1, w_query, w_key, w_value, vecs, bup),
+    qa_send, qb_send, qa_keep, qb_keep = line.call(
+        functools.partial(weights_back_kernel, lay),
+        [wire_a, wire_b, wire_a, wire_b],
+        (info, gqt, gkt, gvt, x, vecs, bup),
         scalars=(0,),
-        name="project_back",
+        name="weights_back",
         mib=16,
     )
 
     def send_back():
+        ins = line.call(
+            input_back_kernel, [shape((piece, width))] * 4, (gq, gk, gv, r1, w_query, w_key, w_value),
+            name="input_back", mib=16,
+        )
         packs = line.call(
             pack_kernel, [shape((2 * piece + 2 * SEGS, width))] * n_seq, (*outs, *ins, pool), name="pack"
         )
@@ -881,6 +889,7 @@
             (info, row_lengths, *packs),
             scalars=(0,),
             name="unpack",
+            us=1.0,
         )
 
     if fast:
@@ -906,9 +915,8 @@
         qkv.four()
         (g_down,) = down.end(down_kernel, [f32(rs, ff)])
         (g_up,) = up.end(up_kernel, [f32(width, ff // n)])
-        qkv.five()
+        qkv.five_all()
         output, grad_tokens, pooled = take_back(packs)
-        qkv.six()
         *g_qkv, g_out, v0, v1, v2, v3, v4, v5, v6, v7, v8 = qkv.end(
             qkv_kernel, [f32(rs, width)] * 4 + [f32(rs)] * 8 + [f32(4 * rs)]
         )

time: 162 us -> 152 us (0.938)
  Pallas kernels: 77.9 us -> 70.7 us
  waiting for transfers between devices: 43.8 us -> 38.1 us
  starting transfers between devices: 36.5 us -> 39.9 us
    pallas_call x31 -> x32, Pallas kernels: 77.9 us -> 70.7 us  [call(): pl.pallas_call(body, out_shape=[*outs, shape((8, LANES), F32)], in_specs=...]
    ppermute x3, waiting for transfers between devices: 6.39 us -> 1.93 us  [send_back(): lax.ppermute(packs[r], 'seq', xor[r])]
    ppermute x0 -> x1, waiting for transfers between devices: none -> 2.35 us  [five_all(): lax.ppermute(mine, 'seq', xor[3])]
    ppermute x8, starting transfers between devices: 1.35 us -> 3.31 us  [local(): pp_core = lambda a: lax.ppermute(a, 'seq', xor[1])]
    ppermute x0 -> x1, starting transfers between devices: none -> 1.76 us  [five_all(): lax.ppermute(mine, 'seq', xor[3])]
    ppermute x12, waiting for transfers between devices: 10.2 us -> 8.51 us  [pp_dp(): return lambda a: lax.ppermute(a, 'dp', [(i, i ^ bit) for i in range(n_dp)])]
  transfers between devices with their start and end apart: 38 -> 39, of which waited for: 10 -> 13; matrix products, arithmetic and copies ran while one was open for 1% -> 1% of each run, Pallas kernels for 36% -> 35%
where the time goes in v4:
time: 152 us
  Pallas kernels  70.7 us (47%)
  starting transfers between devices  39.9 us (26%)
  waiting for transfers between devices  38.1 us (25%)
  between operations  1.57 us (1%)
    pallas_call x32, Pallas kernels, call(): pl.pallas_call(body, out_shape=[*outs, shape((8, LANES), F32)], in_specs=...  70.7 us
    ppermute x9, waiting for transfers between devices, local(): pp_y = lambda a: lax.ppermute(a, 'seq', xor[2])  23.7 us
    ppermute x12, starting transfers between devices, pp_dp(): return lambda a: lax.ppermute(a, 'dp', [(i, i ^ bit) for i in range(n_dp)])  18.8 us
    ppermute x9, starting transfers between devices, local(): pp_y = lambda a: lax.ppermute(a, 'seq', xor[2])  9.61 us
    ppermute x12, waiting for transfers between devices, pp_dp(): return lambda a: lax.ppermute(a, 'dp', [(i, i ^ bit) for i in range(n_dp)])  8.51 us
    ppermute x6, starting transfers between devices, rel(): lax.ppermute(parts[r], 'seq', xor[r])  5.39 us
    ppermute x8, starting transfers between devices, local(): pp_core = lambda a: lax.ppermute(a, 'seq', xor[1])  3.31 us
  transfers between devices with their start and end apart: 39, of which 13 were waited for; matrix products, arithmetic and copies ran while one was open for 1% of the time, Pallas kernels for 35%

profile of v4, /device:TPU:0, one launch (start us, length us, event | category | flops | bytes accessed | tf_op | source)
XLA Modules:
  0.0 152.1 jit_solution(6698786700689831325)
XLA Ops:
  0.8 1.8 %split_tokens.1 = (bf16[128,768]{1,0:T(8,128)(2,1)S(1)}, bf16[128,768]{1,0:T(8,128)(2,1)S(1)}, bf16[128,768]{1,0:T(8,128)(2,1)S(1)}, bf16[128,768]{1,0:T(8,128)(2,1)S(1)}, f32[8,128]{1,0:T(8,128)S(1)}) custom-call(s32[16]{0:T(128)S(1)} %concatenate.9.refs_0_, bf16[4,128,768]{2,1,0:T(8,128)(2,1)} %refs_1_.3), custom_call_target="tpu_custom_call" | custom-call | flops 1 | bytes 1 | tf_op jit(solution)/shard_map/split_tokens/pallas_call | solution.py:489
  2.6 0.5 collective-permute-start
  3.1 2.6 %collective-permute-start.1 = (bf16[128,768]{1,0:T(8,128)(2,1)S(1)}, bf16[128,768]{1,0:T(8,128)(2,1)S(1)}, u32[]{:S(2)}, u32[]{:S(2)}) collective-permute-start(bf16[128,768]{1,0:T(8,128)(2,1)S(1)} %get-tuple-element.170), channel_id=1, source_target_pairs={{0,2},{1,3},{2,0},{3,1},{4,6},{5,7},{6,4},{7,5},{8,10},{9,11},{10,... | collective-permute-start | bytes 589832 | tf_op jit(solution)/shard_map/ppermute | solution.py:664
  5.8 1.8 %split_grads.1 = (bf16[128,768]{1,0:T(8,128)(2,1)S(1)}, bf16[128,768]{1,0:T(8,128)(2,1)S(1)}, bf16[128,768]{1,0:T(8,128)(2,1)S(1)}, bf16[128,768]{1,0:T(8,128)(2,1)S(1)}, f32[8,128]{1,0:T(8,128)S(1)}) custom-call(s32[16]{0:T(128)S(1)} %concatenate.9.refs_0_, bf16[4,128,768]{2,1,0:T(8,128)(2,1)} %refs_1_.4, f32[8,128]{1,0:T(8,128)S(1)} %get-tuple-element.172.refs_2_), custom_call_target="tpu_custom_call" | custom-call | flops 1 | bytes 1 | tf_op jit(solution)/shard_map/split_grads/pallas_call | solution.py:489
  7.8 1.9 %collective-permute-start.4 = (bf16[128,768]{1,0:T(8,128)(2,1)S(1)}, bf16[128,768]{1,0:T(8,128)(2,1)S(1)}, u32[]{:S(2)}, u32[]{:S(2)}) collective-permute-start(bf16[128,768]{1,0:T(8,128)(2,1)S(1)} %get-tuple-element.181), channel_id=1, source_target_pairs={{0,2},{1,3},{2,0},{3,1},{4,6},{5,7},{6,4},{7,5},{8,10},{9,11},{10,... | collective-permute-start | bytes 589832 | tf_op jit(solution)/shard_map/ppermute | solution.py:664
  10.3 0.8 subtract_convert_fusion
  11.2 2.2 %fetch.1 = (bf16[768,768]{1,0:T(8,128)(2,1)S(1)}, bf16[768,768]{1,0:T(8,128)(2,1)S(1)}, bf16[768,768]{1,0:T(8,128)(2,1)S(1)}, f32[8,128]{1,0:T(8,128)S(1)}) custom-call(bf16[768,768]{1,0:T(8,128)(2,1)} %refs_4_.3, bf16[768,768]{1,0:T(8,128)(2,1)} %refs_5_.5, bf16[768,768]{1,0:T(8,128)(2,1)} %refs_6_.7, f32[8,128]{1,0:T(8,128)S(1)} %get-tuple-element.173.refs_3_), custom_call_target="tpu_custom_call" | custom-call | flops 1 | bytes 1 | tf_op jit(solution)/shard_map/fetch/pallas_call | solution.py:489
  13.6 1.6 %collective-permute-done.2.refs_3_ = bf16[128,768]{1,0:T(8,128)(2,1)S(1)} collective-permute-done((bf16[128,768]{1,0:T(8,128)(2,1)S(1)}, bf16[128,768]{1,0:T(8,128)(2,1)S(1)}, u32[]{:S(2)}, u32[]{:S(2)}) %collective-permute-start.2) | collective-permute-done | bytes 196640 | tf_op jit(solution)/shard_map/ppermute | solution.py:664
  15.3 11.2 %attend.1 = (bf16[512,768]{1,0:T(8,128)(2,1)}, bf16[512,768]{1,0:T(8,128)(2,1)}, bf16[512,768]{1,0:T(8,128)(2,1)}, bf16[512,768]{1,0:T(8,128)(2,1)}, f32[512,768...) custom-call(bf16[128,768]{1,0:T(8,128)(2,1)S(1)} %get-tuple-element., ...), custom_call_target="tpu_custom_call" | custom-call | flops 1 | bytes 1 | tf_op jit(solution)/shard_map/attend/pallas_call | solution.py:489
  26.7 14.2 %ffn.1 = (bf16[128,768]{1,0:T(8,128)(2,1)S(1)}, bf16[128,768]{1,0:T(8,128)(2,1)S(1)}, bf16[128,768]{1,0:T(8,128)(2,1)S(1)}, bf16[128,768]{1,0:T(8,128)(2,1)S(1)}...) custom-call(s32[16]{0:T(128)S(1)} %concatenate.9.refs_0_, ...), custom_call_target="tpu_custom_call" | custom-call | flops 1 | bytes 1 | tf_op jit(solution)/shard_map/ffn/pallas_call | solution.py:489
  40.9 0.4 collective-permute-start.6
  41.3 6.9 %ffn_back.1 = (bf16[2,8,192,384]{3,2,1,0:T(8,128)(2,1)S(1)}, bf16[2,8,192,384]{3,2,1,0:T(8,128)(2,1)S(1)}, f32[8,3072]{1,0:T(8,128)S(1)}, bf16[512,3072]{1,0:T(8,128)(2,1)S(1)}, f32[8,128]{1,0:T(8,128)S(1)}) custom-call(s32[16]{0:T(128)S(1)} %concatenate.9.refs_0_, f32[512,768]{1,0:T(8,128)S(1)} %get-tuple-element.191.refs_1_, ...), custom_call_target="tpu_custom_call" | custom-call | flops 1 | bytes 1 | tf_op jit(solution)/shard_map/ffn_back/pallas_call | solution.py:489
  48.5 0.6 down_one.1
  49.1 1.9 %collective-permute-start.8 = (bf16[2,4,48,768]{3,2,1,0:T(8,128)(2,1)S(1)}, bf16[2,4,48,768]{3,2,1,0:T(8,128)(2,1)S(1)}, u32[]{:S(2)}, u32[]{:S(2)}) collective-permute-start(bf16[2,4,48,768]{3,2,1,0:T(8,128)(2,1)S(1)} %get-tuple-element.220), channel_id=1, source_target_pairs={{0,4},{4,0},{8,12},{12,8},{16,20},{20,16},{24,28},{28,24},{1,5},{5... | collective-permute-start | bytes 1769480 | tf_op jit(solution)/shard_map/ppermute | solution.py:735
  50.9 1.5 collective-permute-start.9
  52.5 7.0 %norm_back.1 = (f32[512,768]{1,0:T(8,128)S(1)}, bf16[512,768]{1,0:T(8,128)(2,1)S(1)}, bf16[512,128]{1,0:T(8,128)(2,1)S(1)}, f32[8,768]{1,0:T(8,128)S(1)}, bf16[2...) custom-call(s32[16]{0:T(128)S(1)} %concatenate.9.refs_0_, ...), custom_call_target="tpu_custom_call" | custom-call | flops 1 | bytes 1 | tf_op jit(solution)/shard_map/norm_back/pallas_call | solution.py:489
  59.5 0.6 up_one.1
  60.2 0.6 collective-permute-start.14
  60.8 0.5 collective-permute-start.15
  61.3 9.3 %attend_back.1 = (bf16[512,768]{1,0:T(8,128)(2,1)S(1)}, bf16[512,768]{1,0:T(8,128)(2,1)S(1)}, bf16[512,768]{1,0:T(8,128)(2,1)S(1)}, bf16[768,512]{1,0:T(8,128)(2...) custom-call(bf16[512,768]{1,0:T(8,128)(2,1)S(1)} %copy-done.6, ...), custom_call_target="tpu_custom_call" | custom-call | flops 1 | bytes 1 | tf_op jit(solution)/shard_map/attend_back/pallas_call | solution.py:489
  70.9 1.6 %collective-permute-start.12 = (bf16[4,48,768]{2,1,0:T(8,128)(2,1)S(1)}, bf16[4,48,768]{2,1,0:T(8,128)(2,1)S(1)}, u32[]{:S(2)}, u32[]{:S(2)}) collective-permute-start(bf16[4,48,768]{2,1,0:T(8,128)(2,1)S(1)} %get-tuple-element.230), channel_id=1, source_target_pairs={{0,2},{1,3},{2,0},{3,1},{4,6},{5,7},{6,4},{7,5},{8,10},{9,11},{10,... | collective-permute-start | bytes 884744 | tf_op jit(solution)/shard_map/ppermute | solution.py:732
  72.5 1.5 collective-permute-start.13
  74.0 2.8 %weights_back.1 = (bf16[2,8,80,384]{3,2,1,0:T(8,128)(2,1)S(1)}, bf16[2,8,80,384]{3,2,1,0:T(8,128)(2,1)S(1)}, bf16[2,8,80,384]{3,2,1,0:T(8,128)(2,1)S(1)}, bf16[2...) custom-call(s32[16]{0:T(128)S(1)} %concatenate.9.refs_0_, bf16[768,512]{1,0:T(8,128)(2,1)S(1)} %get-tuple-element.212.refs_1_, ...), custom_call_target="tpu_custom_call" | custom-call | flops 1 | bytes 1 | tf_op jit(solution)/shard_map/weights_back/pallas_call | solution.py:489
  76.9 1.0 collective-permute-done.14.refs_0_
  77.9 1.9 %collective-permute-done.15.refs_1_ = bf16[8,96,384]{2,1,0:T(8,128)(2,1)S(1)} collective-permute-done((bf16[8,96,384]{2,1,0:T(8,128)(2,1)S(1)}, bf16[8,96,384]{2,1,0:T(8,128)(2,1)S(1)}, u32[]{:S(2)}, u32[]{:S(2)}) %collective-permute-start.15) | collective-permute-done | bytes 589856 | tf_op jit(solution)/shard_map/ppermute | solution.py:732
  79.8 0.4 up_two.1
  80.2 0.5 collective-permute-start.22
  80.7 4.6 %collective-permute-done.12.refs_0_ = bf16[4,48,768]{2,1,0:T(8,128)(2,1)S(1)} collective-permute-done((bf16[4,48,768]{2,1,0:T(8,128)(2,1)S(1)}, bf16[4,48,768]{2,1,0:T(8,128)(2,1)S(1)}, u32[]{:S(2)}, u32[]{:S(2)}) %collective-permute-start.12) | collective-permute-done | bytes 294944 | tf_op jit(solution)/shard_map/ppermute | solution.py:732
  85.3 1.5 collective-permute-start.23
  87.0 0.5 qkv_one.1
  87.5 0.6 collective-permute-start.20
  88.1 0.3 collective-permute-start.21
  88.5 1.8 %collective-permute-start.24 = (bf16[2,96,768]{2,1,0:T(8,128)(2,1)S(1)}, bf16[2,96,768]{2,1,0:T(8,128)(2,1)S(1)}, u32[]{:S(2)}, u32[]{:S(2)}) collective-permute-start(bf16[2,96,768]{2,1,0:T(8,128)(2,1)S(1)} %get-tuple-element.262), channel_id=1, source_target_pairs={{0,8},{4,12},{8,0},{12,4},{16,24},{20,28},{24,16},{28,20},{1,9},{5... | collective-permute-start | bytes 884744 | tf_op jit(solution)/shard_map/ppermute | solution.py:735
  90.2 2.1 %input_back.1 = (bf16[128,768]{1,0:T(8,128)(2,1)S(1)}, bf16[128,768]{1,0:T(8,128)(2,1)S(1)}, bf16[128,768]{1,0:T(8,128)(2,1)S(1)}, bf16[128,768]{1,0:T(8,128)(2,1)S(1)}, f32[8,128]{1,0:T(8,128)S(1)}) custom-call(bf16[512,768]{1,0:T(8,128)(2,1)S(1)} %get-tuple-element.208.refs_0_, bf16[512,768]{1,0:T(8,128)(2,1)S(1)} %get-tuple-element.209.refs_1_, ...), custom_call_target="tpu_custom_call" | custom-call | flops 1 | bytes 1 | tf_op jit(solution)/shard_map/input_back/pallas_call | solution.py:489
  92.4 4.9 %collective-permute-done.23.refs_0_.refs_5_ = bf16[4,128,384]{2,1,0:T(8,128)(2,1)S(1)} collective-permute-done((bf16[4,128,384]{2,1,0:T(8,128)(2,1)S(1)}, bf16[4,128,384]{2,1,0:T(8,128)(2,1)S(1)}, u32[]{:S(2)}, u32[]{:S(2)}) %collective-permute-start.23) | collective-permute-done | bytes 393248 | tf_op jit(solution)/shard_map/ppermute | solution.py:732
  97.5 1.6 %collective-permute-start.28 = (bf16[2,192,384]{2,1,0:T(8,128)(2,1)S(1)}, bf16[2,192,384]{2,1,0:T(8,128)(2,1)S(1)}, u32[]{:S(2)}, u32[]{:S(2)}) collective-permute-start(bf16[2,192,384]{2,1,0:T(8,128)(2,1)S(1)} %get-tuple-element.275), channel_id=1, source_target_pairs={{0,8},{4,12},{8,0},{12,4},{16,24},{20,28},{24,16},{28,20},{1,9},{5... | collective-permute-start | bytes 884744 | tf_op jit(solution)/shard_map/ppermute | solution.py:735
  99.3 2.7 %collective-permute-start.27 = (bf16[96,768]{1,0:T(8,128)(2,1)S(1)}, bf16[96,768]{1,0:T(8,128)(2,1)S(1)}, u32[]{:S(2)}, u32[]{:S(2)}) collective-permute-start(bf16[96,768]{1,0:T(8,128)(2,1)S(1)} %get-tuple-element.273), channel_id=1, source_target_pairs={{0,16},{4,20},{8,24},{12,28},{16,0},{20,4},{24,8},{28,12},{1,17},{... | collective-permute-start | bytes 442376 | tf_op jit(solution)/shard_map/ppermute | solution.py:735
  101.9 3.0 %collective-permute-done.20.refs_0_ = bf16[2,4,80,384]{3,2,1,0:T(8,128)(2,1)S(1)} collective-permute-done((bf16[2,4,80,384]{3,2,1,0:T(8,128)(2,1)S(1)}, bf16[2,4,80,384]{3,2,1,0:T(8,128)(2,1)S(1)}, u32[]{:S(2)}, u32[]{:S(2)}) %collective-permute-start.20) | collective-permute-done | bytes 491552 | tf_op jit(solution)/shard_map/ppermute | solution.py:735
  104.9 1.3 collective-permute-done.21.refs_1_
  106.2 0.3 qkv_two.1
  106.6 1.6 %collective-permute-start.25 = (bf16[4,112,384]{2,1,0:T(8,128)(2,1)S(1)}, bf16[4,112,384]{2,1,0:T(8,128)(2,1)S(1)}, u32[]{:S(2)}, u32[]{:S(2)}) collective-permute-start(bf16[4,112,384]{2,1,0:T(8,128)(2,1)S(1)} %get-tuple-element.269), channel_id=1, source_target_pairs={{0,2},{1,3},{2,0},{3,1},{4,6},{5,7},{6,4},{7,5},{8,10},{9,11},{10,... | collective-permute-start | bytes 1032200 | tf_op jit(solution)/shard_map/ppermute | solution.py:732
  108.1 0.5 collective-permute-start.26
  108.8 0.6 collective-permute-start.29
  109.4 2.6 %collective-permute-start.31 = (bf16[192,384]{1,0:T(8,128)(2,1)S(1)}, bf16[192,384]{1,0:T(8,128)(2,1)S(1)}, u32[]{:S(2)}, u32[]{:S(2)}) collective-permute-start(bf16[192,384]{1,0:T(8,128)(2,1)S(1)} %get-tuple-element.284), channel_id=1, source_target_pairs={{0,16},{4,20},{8,24},{12,28},{16,0},{20,4},{24,8},{28,12},{1,17},{... | collective-permute-start | bytes 442376 | tf_op jit(solution)/shard_map/ppermute | solution.py:735
  112.0 6.2 %collective-permute-done.29.refs_2_ = bf16[96,768]{1,0:T(8,128)(2,1)S(1)} collective-permute-done((bf16[96,768]{1,0:T(8,128)(2,1)S(1)}, bf16[96,768]{1,0:T(8,128)(2,1)S(1)}, u32[]{:S(2)}, u32[]{:S(2)}) %collective-permute-start.29) | collective-permute-done | bytes 147488 | tf_op jit(solution)/shard_map/ppermute | solution.py:732
  118.2 0.6 down_six.1
  119.0 1.8 %collective-permute-start.30 = (bf16[2,208,384]{2,1,0:T(8,128)(2,1)S(1)}, bf16[2,208,384]{2,1,0:T(8,128)(2,1)S(1)}, u32[]{:S(2)}, u32[]{:S(2)}) collective-permute-start(bf16[2,208,384]{2,1,0:T(8,128)(2,1)S(1)} %get-tuple-element.282), channel_id=1, source_target_pairs={{0,8},{4,12},{8,0},{12,4},{16,24},{20,28},{24,16},{28,20},{1,9},{5... | collective-permute-start | bytes 958472 | tf_op jit(solution)/shard_map/ppermute | solution.py:735
  120.8 1.6 %collective-permute-start.32 = (bf16[192,384]{1,0:T(8,128)(2,1)S(1)}, bf16[192,384]{1,0:T(8,128)(2,1)S(1)}, u32[]{:S(2)}, u32[]{:S(2)}) collective-permute-start(bf16[192,384]{1,0:T(8,128)(2,1)S(1)} %get-tuple-element.287.refs_1_), channel_id=1, source_target_pairs={{0,2},{1,3},{2,0},{3,1},{4,6},{5,7},{6,4},{7,5},{8,10},{9,11},{10,... | collective-permute-start | bytes 442376 | tf_op jit(solution)/shard_map/ppermute | solution.py:732
  122.4 0.5 collective-permute-start.17
  122.9 0.5 collective-permute-start.18
  123.4 3.2 %collective-permute-done.32.refs_2_ = bf16[192,384]{1,0:T(8,128)(2,1)S(1)} collective-permute-done((bf16[192,384]{1,0:T(8,128)(2,1)S(1)}, bf16[192,384]{1,0:T(8,128)(2,1)S(1)}, u32[]{:S(2)}, u32[]{:S(2)}) %collective-permute-start.32) | collective-permute-done | bytes 147488 | tf_op jit(solution)/shard_map/ppermute | solution.py:732
  126.6 0.6 up_six.1
  127.2 2.7 %collective-permute-start.34 = (bf16[2,192,384]{2,1,0:T(8,128)(2,1)S(1)}, bf16[2,192,384]{2,1,0:T(8,128)(2,1)S(1)}, u32[]{:S(2)}, u32[]{:S(2)}) collective-permute-start(bf16[2,192,384]{2,1,0:T(8,128)(2,1)S(1)} %get-tuple-element.292.refs_1_), channel_id=1, source_target_pairs={{0,1},{1,0},{2,3},{3,2},{4,5},{5,4},{6,7},{7,6},{8,9},{9,8},{10,11... | collective-permute-start | bytes 884744 | tf_op jit(solution)/shard_map/ppermute | solution.py:731
  129.9 2.7 %collective-permute-start.33 = (bf16[208,384]{1,0:T(8,128)(2,1)S(1)}, bf16[208,384]{1,0:T(8,128)(2,1)S(1)}, u32[]{:S(2)}, u32[]{:S(2)}) collective-permute-start(bf16[208,384]{1,0:T(8,128)(2,1)S(1)} %get-tuple-element.290), channel_id=1, source_target_pairs={{0,16},{4,20},{8,24},{12,28},{16,0},{20,4},{24,8},{28,12},{1,17},{... | collective-permute-start | bytes 479240 | tf_op jit(solution)/shard_map/ppermute | solution.py:735
  132.6 1.6 %down_end.1 = (f32[96,3072]{1,0:T(8,128)}, f32[8,128]{1,0:T(8,128)S(1)}) custom-call(s32[16]{0:T(128)S(1)} %concatenate.9.refs_0_, bf16[2,96,768]{2,1,0:T(8,128)(2,1)S(1)} %get-tuple-element.293.refs_1_, bf16[2,96,768]{2,1,0:T(8,128)(2,1)S(1)} %collective-permute-done.35.refs_2_, f32[8,128]{1,0:T(8,128)S(1)} %get-tuple-element.294.refs_3_), custom_call_target="tpu_custom_call" | custom-call | flops 1 | bytes 1 | tf_op jit(solution)/shard_map/down_end/pallas_call | solution.py:489
  134.2 1.6 %up_end.1 = (f32[768,384]{1,0:T(8,128)}, f32[8,128]{1,0:T(8,128)S(1)}) custom-call(s32[16]{0:T(128)S(1)} %concatenate.9.refs_0_, bf16[2,192,384]{2,1,0:T(8,128)(2,1)S(1)} %get-tuple-element.292.refs_1_, bf16[2,192,384]{2,1,0:T(8,128)(2,1)S(1)} %collective-permute-done.34.refs_2_, f32[8,128]{1,0:T(8,128)S(1)} %get-tuple-element.295.refs_3_), custom_call_target="tpu_custom_call" | custom-call | flops 1 | bytes 1 | tf_op jit(solution)/shard_map/up_end/pallas_call | solution.py:489
  135.9 4.5 %collective-permute-done.33.refs_0_ = bf16[208,384]{1,0:T(8,128)(2,1)S(1)} collective-permute-done((bf16[208,384]{1,0:T(8,128)(2,1)S(1)}, bf16[208,384]{1,0:T(8,128)(2,1)S(1)}, u32[]{:S(2)}, u32[]{:S(2)}) %collective-permute-start.33) | collective-permute-done | bytes 159776 | tf_op jit(solution)/shard_map/ppermute | solution.py:735
  140.4 0.4 collective-permute-start.36
  140.8 1.8 %collective-permute-start.38 = (bf16[208,384]{1,0:T(8,128)(2,1)S(1)}, bf16[208,384]{1,0:T(8,128)(2,1)S(1)}, u32[]{:S(2)}, u32[]{:S(2)}) collective-permute-start(bf16[208,384]{1,0:T(8,128)(2,1)S(1)} %get-tuple-element.301.refs_1_), channel_id=1, source_target_pairs={{0,3},{1,2},{2,1},{3,0},{4,7},{5,6},{6,5},{7,4},{8,11},{9,10},{10,... | collective-permute-start | bytes 479240 | tf_op jit(solution)/shard_map/ppermute | solution.py:808
  142.6 1.9 %collective-permute-done.19.refs_5_ = bf16[272,768]{1,0:T(8,128)(2,1)S(1)} collective-permute-done((bf16[272,768]{1,0:T(8,128)(2,1)S(1)}, bf16[272,768]{1,0:T(8,128)(2,1)S(1)}, u32[]{:S(2)}, u32[]{:S(2)}) %collective-permute-start.19) | collective-permute-done | bytes 417824 | tf_op jit(solution)/shard_map/ppermute | solution.py:883
  144.6 1.8 %unpack.1 = (bf16[4,128,768]{2,1,0:T(8,128)(2,1)}, bf16[4,128,768]{2,1,0:T(8,128)(2,1)}, f32[4,8,768]{2,1,0:T(8,128)}, f32[8,128]{1,0:T(8,128)S(1)}) custom-call(s32[16]{0:T(128)S(1)} %concatenate.9.refs_0_, f32[4,8,128]{2,1,0:T(8,128)S(1)} %broadcast_in_dim.12.refs_1_, bf16[272,768]{1,0:T(8,128)(2,1)S(1)} %get-tuple-element.250.refs_2_, ...), custom_call_target="tpu_custom_call" | custom-call | flops 1000000000 | bytes 1 | tf_op jit(solution)/shard_map/unpack/pallas_call | solution.py:489
  146.3 1.6 %collective-permute-done.36.refs_2_ = bf16[208,384]{1,0:T(8,128)(2,1)S(1)} collective-permute-done((bf16[208,384]{1,0:T(8,128)(2,1)S(1)}, bf16[208,384]{1,0:T(8,128)(2,1)S(1)}, u32[]{:S(2)}, u32[]{:S(2)}) %collective-permute-start.36) | collective-permute-done | bytes 159776 | tf_op jit(solution)/shard_map/ppermute | solution.py:732
  147.9 2.4 %collective-permute-done.38.refs_4_ = bf16[208,384]{1,0:T(8,128)(2,1)S(1)} collective-permute-done((bf16[208,384]{1,0:T(8,128)(2,1)S(1)}, bf16[208,384]{1,0:T(8,128)(2,1)S(1)}, u32[]{:S(2)}, u32[]{:S(2)}) %collective-permute-start.38) | collective-permute-done | bytes 159776 | tf_op jit(solution)/shard_map/ppermute | solution.py:808
  150.3 1.6 %qkv_end.1 = (f32[96,768]{1,0:T(8,128)}, f32[96,768]{1,0:T(8,128)}, f32[96,768]{1,0:T(8,128)}, f32[96,768]{1,0:T(8,128)}, f32[96]{0:T(128)}, /*index=5*/f32[96]{...) custom-call(s32[16]{0:T(128)S(1)} %concatenate.9.refs_0_, ...), custom_call_target="tpu_custom_call" | custom-call | flops 1 | bytes 1 | tf_op jit(solution)/shard_map/qkv_end/pallas_call | solution.py:489
  (119 shorter events, 2.9 us)
Async XLA Ops:
  0.7 9.1 %copy-start.20 = (s32[4,8]{1,0:T(4,128)S(1)}, s32[4,8]{1,0:T(4,128)}, u32[]{:S(2)}) copy-start(s32[4,8]{1,0:T(4,128)} %param.20) | copy-start | bytes 388
  0.8 25.7 %slice-start.2 = ((s8[4718592]{0:T(1024)(128)(4,1)}), s8[524288]{0:T(1024)(128)(4,1)S(1)}, s32[]{:S(2)}) async-start(s8[4718592]{0:T(1024)(128)(4,1)} %bitcast.22), calls=%async_computation.2 | async-start | bytes 1048576
  2.6 10.9 %collective-permute-start = (bf16[128,768]{1,0:T(8,128)(2,1)S(1)}, bf16[128,768]{1,0:T(8,128)(2,1)S(1)}, u32[]{:S(2)}, u32[]{:S(2)}) collective-permute-start(bf16[128,768]{1,0:T(8,128)(2,1)S(1)} %get-tuple-element.169), channel_id=1, source_target_pairs={{0,1},{1,0},{2,3},{3,2},{4,5},{5,4},{6,7},{7,6},{8,9},{9,8},{10,11... | collective-permute-start | bytes 589832 | tf_op jit(solution)/shard_map/ppermute | solution.py:664
  3.1 10.4 %collective-permute-start.1 = (bf16[128,768]{1,0:T(8,128)(2,1)S(1)}, bf16[128,768]{1,0:T(8,128)(2,1)S(1)}, u32[]{:S(2)}, u32[]{:S(2)}) collective-permute-start(bf16[128,768]{1,0:T(8,128)(2,1)S(1)} %get-tuple-element.170), channel_id=1, source_target_pairs={{0,2},{1,3},{2,0},{3,1},{4,6},{5,7},{6,4},{7,5},{8,10},{9,11},{10,... | collective-permute-start | bytes 589832 | tf_op jit(solution)/shard_map/ppermute | solution.py:664
  5.7 9.4 %collective-permute-start.2 = (bf16[128,768]{1,0:T(8,128)(2,1)S(1)}, bf16[128,768]{1,0:T(8,128)(2,1)S(1)}, u32[]{:S(2)}, u32[]{:S(2)}) collective-permute-start(bf16[128,768]{1,0:T(8,128)(2,1)S(1)} %get-tuple-element.171), channel_id=1, source_target_pairs={{0,3},{1,2},{2,1},{3,0},{4,7},{5,6},{6,5},{7,4},{8,11},{9,10},{10,... | collective-permute-start | bytes 589832 | tf_op jit(solution)/shard_map/ppermute | solution.py:664
  7.6 18.9 %collective-permute-start.3 = (bf16[128,768]{1,0:T(8,128)(2,1)S(1)}, bf16[128,768]{1,0:T(8,128)(2,1)S(1)}, u32[]{:S(2)}, u32[]{:S(2)}) collective-permute-start(bf16[128,768]{1,0:T(8,128)(2,1)S(1)} %get-tuple-element.180), channel_id=1, source_target_pairs={{0,1},{1,0},{2,3},{3,2},{4,5},{5,4},{6,7},{7,6},{8,9},{9,8},{10,11... | collective-permute-start | bytes 589832 | tf_op jit(solution)/shard_map/ppermute | solution.py:664
  7.8 18.7 %collective-permute-start.4 = (bf16[128,768]{1,0:T(8,128)(2,1)S(1)}, bf16[128,768]{1,0:T(8,128)(2,1)S(1)}, u32[]{:S(2)}, u32[]{:S(2)}) collective-permute-start(bf16[128,768]{1,0:T(8,128)(2,1)S(1)} %get-tuple-element.181), channel_id=1, source_target_pairs={{0,2},{1,3},{2,0},{3,1},{4,6},{5,7},{6,4},{7,5},{8,10},{9,11},{10,... | collective-permute-start | bytes 589832 | tf_op jit(solution)/shard_map/ppermute | solution.py:664
  11.1 4.1 %copy-start.14 = (bf16[768]{0:T(1024)(128)(2,1)S(1)}, bf16[768]{0:T(1024)(128)(2,1)}, u32[]{:S(2)}) copy-start(bf16[768]{0:T(1024)(128)(2,1)} %refs_10_.1) | copy-start | bytes 4612
  11.1 4.1 %copy-start.15 = (bf16[768]{0:T(1024)(128)(2,1)S(1)}, bf16[768]{0:T(1024)(128)(2,1)}, u32[]{:S(2)}) copy-start(bf16[768]{0:T(1024)(128)(2,1)} %refs_11_.1) | copy-start | bytes 4612
  11.1 4.1 %copy-start.16 = (bf16[768]{0:T(1024)(128)(2,1)S(1)}, bf16[768]{0:T(1024)(128)(2,1)}, u32[]{:S(2)}) copy-start(bf16[768]{0:T(1024)(128)(2,1)} %refs_12_.1) | copy-start | bytes 4612
  11.2 15.4 %slice-start.3 = ((s8[4718592]{0:T(1024)(128)(4,1)}), s8[4194304]{0:T(1024)(128)(4,1)S(1)}, s32[]{:S(2)}) async-start(s8[4718592]{0:T(1024)(128)(4,1)} %bitcast.22), calls=%async_computation.3 | async-start | bytes 8388608
  13.5 13.1 %collective-permute-start.5 = (bf16[128,768]{1,0:T(8,128)(2,1)S(1)}, bf16[128,768]{1,0:T(8,128)(2,1)S(1)}, u32[]{:S(2)}, u32[]{:S(2)}) collective-permute-start(bf16[128,768]{1,0:T(8,128)(2,1)S(1)} %get-tuple-element.182), channel_id=1, source_target_pairs={{0,3},{1,2},{2,1},{3,0},{4,7},{5,6},{6,5},{7,4},{8,11},{9,10},{10,... | collective-permute-start | bytes 589832 | tf_op jit(solution)/shard_map/ppermute | solution.py:664
  15.2 11.4 %copy-start.11 = (bf16[768]{0:T(1024)(128)(2,1)S(1)}, bf16[768]{0:T(1024)(128)(2,1)}, u32[]{:S(2)}) copy-start(bf16[768]{0:T(1024)(128)(2,1)} %refs_6_.6) | copy-start | bytes 4612
  15.2 11.4 %copy-start.12 = (bf16[768]{0:T(1024)(128)(2,1)S(1)}, bf16[768]{0:T(1024)(128)(2,1)}, u32[]{:S(2)}) copy-start(bf16[768]{0:T(1024)(128)(2,1)} %refs_6_.5) | copy-start | bytes 4612
  15.2 11.4 %copy-start.13 = (bf16[3072]{0:T(1024)(128)(2,1)S(1)}, bf16[3072]{0:T(1024)(128)(2,1)}, u32[]{:S(2)}) copy-start(bf16[3072]{0:T(1024)(128)(2,1)} %refs_8_.1) | copy-start | bytes 18436
  15.2 11.4 %copy-start.17 = (bf16[768]{0:T(1024)(128)(2,1)S(1)}, bf16[768]{0:T(1024)(128)(2,1)}, u32[]{:S(2)}) copy-start(bf16[768]{0:T(1024)(128)(2,1)} %refs_4_.2) | copy-start | bytes 4612
  15.2 11.4 %copy-start.18 = (bf16[768]{0:T(1024)(128)(2,1)S(1)}, bf16[768]{0:T(1024)(128)(2,1)}, u32[]{:S(2)}) copy-start(bf16[768]{0:T(1024)(128)(2,1)} %refs_5_.3) | copy-start | bytes 4612
  15.3 11.4 %copy-start.19 = (bf16[768]{0:T(1024)(128)(2,1)S(1)}, bf16[768]{0:T(1024)(128)(2,1)}, u32[]{:S(2)}) copy-start(bf16[768]{0:T(1024)(128)(2,1)} %refs_6_.4) | copy-start | bytes 4612
  26.6 14.7 %slice-start = ((s8[4718592]{0:T(1024)(128)(4,1)}), s8[4194304]{0:T(1024)(128)(4,1)S(1)}, s32[]{:S(2)}) async-start(s8[4718592]{0:T(1024)(128)(4,1)} %bitcast.20), calls=%async_computation | async-start | bytes 8388608
  26.7 14.6 %slice-start.1 = ((s8[4718592]{0:T(1024)(128)(4,1)}), s8[524288]{0:T(1024)(128)(4,1)S(1)}, s32[]{:S(2)}) async-start(s8[4718592]{0:T(1024)(128)(4,1)} %bitcast.20), calls=%async_computation.1 | async-start | bytes 1048576
  40.9 7.6 %collective-permute-start.6 = (bf16[2,8,48,1536]{3,2,1,0:T(8,128)(2,1)S(1)}, bf16[2,8,48,1536]{3,2,1,0:T(8,128)(2,1)S(1)}, u32[]{:S(2)}, u32[]{:S(2)}) collective-permute-start(bf16[2,8,48,1536]{3,2,1,0:T(8,128)(2,1)S(1)} %get-tuple-element.197), channel_id=1, source_target_pairs={{0,1},{1,0},{2,3},{3,2},{4,5},{5,4},{6,7},{7,6},{8,9},{9,8},{10,11... | collective-permute-start | bytes 7077896 | tf_op jit(solution)/shard_map/ppermute | solution.py:731
  48.2 11.3 %collective-permute-start.7 = (bf16[2,8,192,384]{3,2,1,0:T(8,128)(2,1)S(1)}, bf16[2,8,192,384]{3,2,1,0:T(8,128)(2,1)S(1)}, u32[]{:S(2)}, u32[]{:S(2)}) collective-permute-start(bf16[2,8,192,384]{3,2,1,0:T(8,128)(2,1)S(1)} %get-tuple-element.204), channel_id=1, source_target_pairs={{0,1},{1,0},{2,3},{3,2},{4,5},{5,4},{6,7},{7,6},{8,9},{9,8},{10,11... | collective-permute-start | bytes 7077896 | tf_op jit(solution)/shard_map/ppermute | solution.py:731
  48.4 4.0 %copy-start.3 = (bf16[768,768]{1,0:T(8,128)(2,1)S(1)}, bf16[768,768]{1,0:T(8,128)(2,1)}, u32[]{:S(2)}) copy-start(bf16[768,768]{1,0:T(8,128)(2,1)} %refs_7_.5) | copy-start | bytes 3538948
  48.5 4.0 %copy-start.4 = (f32[512,768]{1,0:T(8,128)S(1)}, f32[512,768]{1,0:T(8,128)}, u32[]{:S(2)}) copy-start(f32[512,768]{1,0:T(8,128)} %get-tuple-element.196.refs_8_) | copy-start | bytes 4718596
  48.5 4.0 %copy-start.9 = (f32[512,128]{1,0:T(8,128)S(1)}, f32[512,128]{1,0:T(8,128)}, u32[]{:S(2)}) copy-start(f32[512,128]{1,0:T(8,128)} %get-tuple-element.195.refs_5_) | copy-start | bytes 786436
  49.1 21.6 %collective-permute-start.8 = (bf16[2,4,48,768]{3,2,1,0:T(8,128)(2,1)S(1)}, bf16[2,4,48,768]{3,2,1,0:T(8,128)(2,1)S(1)}, u32[]{:S(2)}, u32[]{:S(2)}) collective-permute-start(bf16[2,4,48,768]{3,2,1,0:T(8,128)(2,1)S(1)} %get-tuple-element.220), channel_id=1, source_target_pairs={{0,4},{4,0},{8,12},{12,8},{16,20},{20,16},{24,28},{28,24},{1,5},{5... | collective-permute-start | bytes 1769480 | tf_op jit(solution)/shard_map/ppermute | solution.py:735
  50.9 19.7 %collective-permute-start.9 = (bf16[8,48,768]{2,1,0:T(8,128)(2,1)S(1)}, bf16[8,48,768]{2,1,0:T(8,128)(2,1)S(1)}, u32[]{:S(2)}, u32[]{:S(2)}) collective-permute-start(bf16[8,48,768]{2,1,0:T(8,128)(2,1)S(1)} %get-tuple-element.221), channel_id=1, source_target_pairs={{0,2},{1,3},{2,0},{3,1},{4,6},{5,7},{6,4},{7,5},{8,10},{9,11},{10,... | collective-permute-start | bytes 1769480 | tf_op jit(solution)/shard_map/ppermute | solution.py:732
  59.5 1.8 %copy-start.6 = (bf16[512,768]{1,0:T(8,128)(2,1)S(1)}, bf16[512,768]{1,0:T(8,128)(2,1)}, u32[]{:S(2)}) copy-start(bf16[512,768]{1,0:T(8,128)(2,1)} %get-tuple-element.188.refs_0_) | copy-start | bytes 2359300
  59.5 1.8 %copy-start.7 = (bf16[512,768]{1,0:T(8,128)(2,1)S(1)}, bf16[512,768]{1,0:T(8,128)(2,1)}, u32[]{:S(2)}) copy-start(bf16[512,768]{1,0:T(8,128)(2,1)} %get-tuple-element.189.refs_1_) | copy-start | bytes 2359300
  59.5 1.8 %copy-start.8 = (bf16[512,768]{1,0:T(8,128)(2,1)S(1)}, bf16[512,768]{1,0:T(8,128)(2,1)}, u32[]{:S(2)}) copy-start(bf16[512,768]{1,0:T(8,128)(2,1)} %get-tuple-element.190.refs_2_) | copy-start | bytes 2359300
  59.5 1.8 %copy-start.10 = (bf16[512,128]{1,0:T(8,128)(2,1)S(1)}, bf16[512,128]{1,0:T(8,128)(2,1)}, u32[]{:S(2)}) copy-start(bf16[512,128]{1,0:T(8,128)(2,1)} %get-tuple-element.202.refs_4_) | copy-start | bytes 393220
  60.2 17.7 %collective-permute-start.14 = (bf16[2,4,96,384]{3,2,1,0:T(8,128)(2,1)S(1)}, bf16[2,4,96,384]{3,2,1,0:T(8,128)(2,1)S(1)}, u32[]{:S(2)}, u32[]{:S(2)}) collective-permute-start(bf16[2,4,96,384]{3,2,1,0:T(8,128)(2,1)S(1)} %get-tuple-element.234), channel_id=1, source_target_pairs={{0,4},{4,0},{8,12},{12,8},{16,20},{20,16},{24,28},{28,24},{1,5},{5... | collective-permute-start | bytes 1769480 | tf_op jit(solution)/shard_map/ppermute | solution.py:735
  60.8 19.0 %collective-permute-start.15 = (bf16[8,96,384]{2,1,0:T(8,128)(2,1)S(1)}, bf16[8,96,384]{2,1,0:T(8,128)(2,1)S(1)}, u32[]{:S(2)}, u32[]{:S(2)}) collective-permute-start(bf16[8,96,384]{2,1,0:T(8,128)(2,1)S(1)} %get-tuple-element.235), channel_id=1, source_target_pairs={{0,2},{1,3},{2,0},{3,1},{4,6},{5,7},{6,4},{7,5},{8,10},{9,11},{10,... | collective-permute-start | bytes 1769480 | tf_op jit(solution)/shard_map/ppermute | solution.py:732
  61.3 18.5 %collective-permute-start.16 = (bf16[2,8,48,384]{3,2,1,0:T(8,128)(2,1)S(1)}, bf16[2,8,48,384]{3,2,1,0:T(8,128)(2,1)S(1)}, u32[]{:S(2)}, u32[]{:S(2)}) collective-permute-start(bf16[2,8,48,384]{3,2,1,0:T(8,128)(2,1)S(1)} %get-tuple-element.238), channel_id=1, source_target_pairs={{0,1},{1,0},{2,3},{3,2},{4,5},{5,4},{6,7},{7,6},{8,9},{9,8},{10,11... | collective-permute-start | bytes 1769480 | tf_op jit(solution)/shard_map/ppermute | solution.py:731
  70.6 3.4 %copy-start.5 = (bf16[512,768]{1,0:T(8,128)(2,1)S(1)}, bf16[512,768]{1,0:T(8,128)(2,1)}, u32[]{:S(2)}) copy-start(bf16[512,768]{1,0:T(8,128)(2,1)} %get-tuple-element.215.refs_4_) | copy-start | bytes 2359300
  70.9 14.4 %collective-permute-start.12 = (bf16[4,48,768]{2,1,0:T(8,128)(2,1)S(1)}, bf16[4,48,768]{2,1,0:T(8,128)(2,1)S(1)}, u32[]{:S(2)}, u32[]{:S(2)}) collective-permute-start(bf16[4,48,768]{2,1,0:T(8,128)(2,1)S(1)} %get-tuple-element.230), channel_id=1, source_target_pairs={{0,2},{1,3},{2,0},{3,1},{4,6},{5,7},{6,4},{7,5},{8,10},{9,11},{10,... | collective-permute-start | bytes 884744 | tf_op jit(solution)/shard_map/ppermute | solution.py:732
  72.5 14.3 %collective-permute-start.13 = (bf16[4,48,768]{2,1,0:T(8,128)(2,1)S(1)}, bf16[4,48,768]{2,1,0:T(8,128)(2,1)S(1)}, u32[]{:S(2)}, u32[]{:S(2)}) collective-permute-start(bf16[4,48,768]{2,1,0:T(8,128)(2,1)S(1)} %get-tuple-element.231), channel_id=1, source_target_pairs={{0,4},{4,0},{8,12},{12,8},{16,20},{20,16},{24,28},{28,24},{1,5},{5... | collective-permute-start | bytes 884744 | tf_op jit(solution)/shard_map/ppermute | solution.py:735
  77.9 9.1 %collective-permute-start.10 = (bf16[2,8,80,384]{3,2,1,0:T(8,128)(2,1)S(1)}, bf16[2,8,80,384]{3,2,1,0:T(8,128)(2,1)S(1)}, u32[]{:S(2)}, u32[]{:S(2)}) collective-permute-start(bf16[2,8,80,384]{3,2,1,0:T(8,128)(2,1)S(1)} %get-tuple-element.226), channel_id=1, source_target_pairs={{0,1},{1,0},{2,3},{3,2},{4,5},{5,4},{6,7},{7,6},{8,9},{9,8},{10,11... | collective-permute-start | bytes 2949128 | tf_op jit(solution)/shard_map/ppermute | solution.py:731
  79.8 7.2 %collective-permute-start.11 = (bf16[2,8,80,384]{3,2,1,0:T(8,128)(2,1)S(1)}, bf16[2,8,80,384]{3,2,1,0:T(8,128)(2,1)S(1)}, u32[]{:S(2)}, u32[]{:S(2)}) collective-permute-start(bf16[2,8,80,384]{3,2,1,0:T(8,128)(2,1)S(1)} %get-tuple-element.227), channel_id=1, source_target_pairs={{0,1},{1,0},{2,3},{3,2},{4,5},{5,4},{6,7},{7,6},{8,9},{9,8},{10,11... | collective-permute-start | bytes 2949128 | tf_op jit(solution)/shard_map/ppermute | solution.py:731
  80.2 17.2 %collective-permute-start.22 = (bf16[4,160,384]{2,1,0:T(8,128)(2,1)S(1)}, bf16[4,160,384]{2,1,0:T(8,128)(2,1)S(1)}, u32[]{:S(2)}, u32[]{:S(2)}) collective-permute-start(bf16[4,160,384]{2,1,0:T(8,128)(2,1)S(1)} %get-tuple-element.258), channel_id=1, source_target_pairs={{0,4},{4,0},{8,12},{12,8},{16,20},{20,16},{24,28},{28,24},{1,5},{5... | collective-permute-start | bytes 1474568 | tf_op jit(solution)/shard_map/ppermute | solution.py:735
  85.3 12.1 %collective-permute-start.23 = (bf16[4,128,384]{2,1,0:T(8,128)(2,1)S(1)}, bf16[4,128,384]{2,1,0:T(8,128)(2,1)S(1)}, u32[]{:S(2)}, u32[]{:S(2)}) collective-permute-start(bf16[4,128,384]{2,1,0:T(8,128)(2,1)S(1)} %get-tuple-element.259), channel_id=1, source_target_pairs={{0,2},{1,3},{2,0},{3,1},{4,6},{5,7},{6,4},{7,5},{8,10},{9,11},{10,... | collective-permute-start | bytes 1179656 | tf_op jit(solution)/shard_map/ppermute | solution.py:732
  87.0 3.2 %copy-start = (bf16[768,768]{1,0:T(8,128)(2,1)S(1)}, bf16[768,768]{1,0:T(8,128)(2,1)}, u32[]{:S(2)}) copy-start(bf16[768,768]{1,0:T(8,128)(2,1)} %refs_4_.3) | copy-start | bytes 3538948
  87.0 3.2 %copy-start.1 = (bf16[768,768]{1,0:T(8,128)(2,1)S(1)}, bf16[768,768]{1,0:T(8,128)(2,1)}, u32[]{:S(2)}) copy-start(bf16[768,768]{1,0:T(8,128)(2,1)} %refs_5_.5) | copy-start | bytes 3538948
  87.0 3.2 %copy-start.2 = (bf16[768,768]{1,0:T(8,128)(2,1)S(1)}, bf16[768,768]{1,0:T(8,128)(2,1)}, u32[]{:S(2)}) copy-start(bf16[768,768]{1,0:T(8,128)(2,1)} %refs_6_.7) | copy-start | bytes 3538948
  87.5 17.4 %collective-permute-start.20 = (bf16[2,4,80,384]{3,2,1,0:T(8,128)(2,1)S(1)}, bf16[2,4,80,384]{3,2,1,0:T(8,128)(2,1)S(1)}, u32[]{:S(2)}, u32[]{:S(2)}) collective-permute-start(bf16[2,4,80,384]{3,2,1,0:T(8,128)(2,1)S(1)} %get-tuple-element.254), channel_id=1, source_target_pairs={{0,4},{4,0},{8,12},{12,8},{16,20},{20,16},{24,28},{28,24},{1,5},{5... | collective-permute-start | bytes 1474568 | tf_op jit(solution)/shard_map/ppermute | solution.py:735
  88.1 18.1 %collective-permute-start.21 = (bf16[8,80,384]{2,1,0:T(8,128)(2,1)S(1)}, bf16[8,80,384]{2,1,0:T(8,128)(2,1)S(1)}, u32[]{:S(2)}, u32[]{:S(2)}) collective-permute-start(bf16[8,80,384]{2,1,0:T(8,128)(2,1)S(1)} %get-tuple-element.255), channel_id=1, source_target_pairs={{0,2},{1,3},{2,0},{3,1},{4,6},{5,7},{6,4},{7,5},{8,10},{9,11},{10,... | collective-permute-start | bytes 1474568 | tf_op jit(solution)/shard_map/ppermute | solution.py:732
  88.5 10.7 %collective-permute-start.24 = (bf16[2,96,768]{2,1,0:T(8,128)(2,1)S(1)}, bf16[2,96,768]{2,1,0:T(8,128)(2,1)S(1)}, u32[]{:S(2)}, u32[]{:S(2)}) collective-permute-start(bf16[2,96,768]{2,1,0:T(8,128)(2,1)S(1)} %get-tuple-element.262), channel_id=1, source_target_pairs={{0,8},{4,12},{8,0},{12,4},{16,24},{20,28},{24,16},{28,20},{1,9},{5... | collective-permute-start | bytes 884744 | tf_op jit(solution)/shard_map/ppermute | solution.py:735
  97.5 11.1 %collective-permute-start.28 = (bf16[2,192,384]{2,1,0:T(8,128)(2,1)S(1)}, bf16[2,192,384]{2,1,0:T(8,128)(2,1)S(1)}, u32[]{:S(2)}, u32[]{:S(2)}) collective-permute-start(bf16[2,192,384]{2,1,0:T(8,128)(2,1)S(1)} %get-tuple-element.275), channel_id=1, source_target_pairs={{0,8},{4,12},{8,0},{12,4},{16,24},{20,28},{24,16},{28,20},{1,9},{5... | collective-permute-start | bytes 884744 | tf_op jit(solution)/shard_map/ppermute | solution.py:735
  99.3 9.5 %collective-permute-start.27 = (bf16[96,768]{1,0:T(8,128)(2,1)S(1)}, bf16[96,768]{1,0:T(8,128)(2,1)S(1)}, u32[]{:S(2)}, u32[]{:S(2)}) collective-permute-start(bf16[96,768]{1,0:T(8,128)(2,1)S(1)} %get-tuple-element.273), channel_id=1, source_target_pairs={{0,16},{4,20},{8,24},{12,28},{16,0},{20,4},{24,8},{28,12},{1,17},{... | collective-permute-start | bytes 442376 | tf_op jit(solution)/shard_map/ppermute | solution.py:735
  106.6 12.2 %collective-permute-start.25 = (bf16[4,112,384]{2,1,0:T(8,128)(2,1)S(1)}, bf16[4,112,384]{2,1,0:T(8,128)(2,1)S(1)}, u32[]{:S(2)}, u32[]{:S(2)}) collective-permute-start(bf16[4,112,384]{2,1,0:T(8,128)(2,1)S(1)} %get-tuple-element.269), channel_id=1, source_target_pairs={{0,2},{1,3},{2,0},{3,1},{4,6},{5,7},{6,4},{7,5},{8,10},{9,11},{10,... | collective-permute-start | bytes 1032200 | tf_op jit(solution)/shard_map/ppermute | solution.py:732
  108.1 10.6 %collective-permute-start.26 = (bf16[4,96,384]{2,1,0:T(8,128)(2,1)S(1)}, bf16[4,96,384]{2,1,0:T(8,128)(2,1)S(1)}, u32[]{:S(2)}, u32[]{:S(2)}) collective-permute-start(bf16[4,96,384]{2,1,0:T(8,128)(2,1)S(1)} %get-tuple-element.270), channel_id=1, source_target_pairs={{0,4},{4,0},{8,12},{12,8},{16,20},{20,16},{24,28},{28,24},{1,5},{5... | collective-permute-start | bytes 884744 | tf_op jit(solution)/shard_map/ppermute | solution.py:735
  108.8 9.4 %collective-permute-start.29 = (bf16[96,768]{1,0:T(8,128)(2,1)S(1)}, bf16[96,768]{1,0:T(8,128)(2,1)S(1)}, u32[]{:S(2)}, u32[]{:S(2)}) collective-permute-start(bf16[96,768]{1,0:T(8,128)(2,1)S(1)} %get-tuple-element.279.refs_1_), channel_id=1, source_target_pairs={{0,2},{1,3},{2,0},{3,1},{4,6},{5,7},{6,4},{7,5},{8,10},{9,11},{10,... | collective-permute-start | bytes 442376 | tf_op jit(solution)/shard_map/ppermute | solution.py:732
  109.4 11.4 %collective-permute-start.31 = (bf16[192,384]{1,0:T(8,128)(2,1)S(1)}, bf16[192,384]{1,0:T(8,128)(2,1)S(1)}, u32[]{:S(2)}, u32[]{:S(2)}) collective-permute-start(bf16[192,384]{1,0:T(8,128)(2,1)S(1)} %get-tuple-element.284), channel_id=1, source_target_pairs={{0,16},{4,20},{8,24},{12,28},{16,0},{20,4},{24,8},{28,12},{1,17},{... | collective-permute-start | bytes 442376 | tf_op jit(solution)/shard_map/ppermute | solution.py:735
  119.0 8.2 %collective-permute-start.30 = (bf16[2,208,384]{2,1,0:T(8,128)(2,1)S(1)}, bf16[2,208,384]{2,1,0:T(8,128)(2,1)S(1)}, u32[]{:S(2)}, u32[]{:S(2)}) collective-permute-start(bf16[2,208,384]{2,1,0:T(8,128)(2,1)S(1)} %get-tuple-element.282), channel_id=1, source_target_pairs={{0,8},{4,12},{8,0},{12,4},{16,24},{20,28},{24,16},{28,20},{1,9},{5... | collective-permute-start | bytes 958472 | tf_op jit(solution)/shard_map/ppermute | solution.py:735
  120.8 5.8 %collective-permute-start.32 = (bf16[192,384]{1,0:T(8,128)(2,1)S(1)}, bf16[192,384]{1,0:T(8,128)(2,1)S(1)}, u32[]{:S(2)}, u32[]{:S(2)}) collective-permute-start(bf16[192,384]{1,0:T(8,128)(2,1)S(1)} %get-tuple-element.287.refs_1_), channel_id=1, source_target_pairs={{0,2},{1,3},{2,0},{3,1},{4,6},{5,7},{6,4},{7,5},{8,10},{9,11},{10,... | collective-permute-start | bytes 442376 | tf_op jit(solution)/shard_map/ppermute | solution.py:732
  122.4 7.5 %collective-permute-start.35 = (bf16[2,96,768]{2,1,0:T(8,128)(2,1)S(1)}, bf16[2,96,768]{2,1,0:T(8,128)(2,1)S(1)}, u32[]{:S(2)}, u32[]{:S(2)}) collective-permute-start(bf16[2,96,768]{2,1,0:T(8,128)(2,1)S(1)} %get-tuple-element.293.refs_1_), channel_id=1, source_target_pairs={{0,1},{1,0},{2,3},{3,2},{4,5},{5,4},{6,7},{7,6},{8,9},{9,8},{10,11... | collective-permute-start | bytes 884744 | tf_op jit(solution)/shard_map/ppermute | solution.py:731
  122.4 18.4 %collective-permute-start.17 = (bf16[272,768]{1,0:T(8,128)(2,1)S(1)}, bf16[272,768]{1,0:T(8,128)(2,1)S(1)}, u32[]{:S(2)}, u32[]{:S(2)}) collective-permute-start(bf16[272,768]{1,0:T(8,128)(2,1)S(1)} %get-tuple-element.251), channel_id=1, source_target_pairs={{0,1},{1,0},{2,3},{3,2},{4,5},{5,4},{6,7},{7,6},{8,9},{9,8},{10,11... | collective-permute-start | bytes 1253384 | tf_op jit(solution)/shard_map/ppermute | solution.py:883
  122.9 19.7 %collective-permute-start.18 = (bf16[272,768]{1,0:T(8,128)(2,1)S(1)}, bf16[272,768]{1,0:T(8,128)(2,1)S(1)}, u32[]{:S(2)}, u32[]{:S(2)}) collective-permute-start(bf16[272,768]{1,0:T(8,128)(2,1)S(1)} %get-tuple-element.252), channel_id=1, source_target_pairs={{0,2},{1,3},{2,0},{3,1},{4,6},{5,7},{6,4},{7,5},{8,10},{9,11},{10,... | collective-permute-start | bytes 1253384 | tf_op jit(solution)/shard_map/ppermute | solution.py:883
  126.6 17.9 %collective-permute-start.19 = (bf16[272,768]{1,0:T(8,128)(2,1)S(1)}, bf16[272,768]{1,0:T(8,128)(2,1)S(1)}, u32[]{:S(2)}, u32[]{:S(2)}) collective-permute-start(bf16[272,768]{1,0:T(8,128)(2,1)S(1)} %get-tuple-element.253), channel_id=1, source_target_pairs={{0,3},{1,2},{2,1},{3,0},{4,7},{5,6},{6,5},{7,4},{8,11},{9,10},{10,... | collective-permute-start | bytes 1253384 | tf_op jit(solution)/shard_map/ppermute | solution.py:883
  127.2 7.0 %collective-permute-start.34 = (bf16[2,192,384]{2,1,0:T(8,128)(2,1)S(1)}, bf16[2,192,384]{2,1,0:T(8,128)(2,1)S(1)}, u32[]{:S(2)}, u32[]{:S(2)}) collective-permute-start(bf16[2,192,384]{2,1,0:T(8,128)(2,1)S(1)} %get-tuple-element.292.refs_1_), channel_id=1, source_target_pairs={{0,1},{1,0},{2,3},{3,2},{4,5},{5,4},{6,7},{7,6},{8,9},{9,8},{10,11... | collective-permute-start | bytes 884744 | tf_op jit(solution)/shard_map/ppermute | solution.py:731
  129.9 10.4 %collective-permute-start.33 = (bf16[208,384]{1,0:T(8,128)(2,1)S(1)}, bf16[208,384]{1,0:T(8,128)(2,1)S(1)}, u32[]{:S(2)}, u32[]{:S(2)}) collective-permute-start(bf16[208,384]{1,0:T(8,128)(2,1)S(1)} %get-tuple-element.290), channel_id=1, source_target_pairs={{0,16},{4,20},{8,24},{12,28},{16,0},{20,4},{24,8},{28,12},{1,17},{... | collective-permute-start | bytes 479240 | tf_op jit(solution)/shard_map/ppermute | solution.py:735
  140.4 7.6 %collective-permute-start.36 = (bf16[208,384]{1,0:T(8,128)(2,1)S(1)}, bf16[208,384]{1,0:T(8,128)(2,1)S(1)}, u32[]{:S(2)}, u32[]{:S(2)}) collective-permute-start(bf16[208,384]{1,0:T(8,128)(2,1)S(1)} %get-tuple-element.301.refs_1_), channel_id=1, source_target_pairs={{0,2},{1,3},{2,0},{3,1},{4,6},{5,7},{6,4},{7,5},{8,10},{9,11},{10,... | collective-permute-start | bytes 479240 | tf_op jit(solution)/shard_map/ppermute | solution.py:732
  140.8 7.1 %collective-permute-start.37 = (bf16[208,384]{1,0:T(8,128)(2,1)S(1)}, bf16[208,384]{1,0:T(8,128)(2,1)S(1)}, u32[]{:S(2)}, u32[]{:S(2)}) collective-permute-start(bf16[208,384]{1,0:T(8,128)(2,1)S(1)} %get-tuple-element.301.refs_1_), channel_id=1, source_target_pairs={{0,1},{1,0},{2,3},{3,2},{4,5},{5,4},{6,7},{7,6},{8,9},{9,8},{10,11... | collective-permute-start | bytes 479240 | tf_op jit(solution)/shard_map/ppermute | solution.py:731
  140.8 9.5 %collective-permute-start.38 = (bf16[208,384]{1,0:T(8,128)(2,1)S(1)}, bf16[208,384]{1,0:T(8,128)(2,1)S(1)}, u32[]{:S(2)}, u32[]{:S(2)}) collective-permute-start(bf16[208,384]{1,0:T(8,128)(2,1)S(1)} %get-tuple-element.301.refs_1_), channel_id=1, source_target_pairs={{0,3},{1,2},{2,1},{3,0},{4,7},{5,6},{6,5},{7,4},{8,11},{9,10},{10,... | collective-permute-start | bytes 479240 | tf_op jit(solution)/shard_map/ppermute | solution.py:808

commit v5 on v4

--- a/solution.py
+++ b/solution.py
@@ -176,7 +176,7 @@
         att_out[:, sl] = jnp.concatenate(parts, axis=0).T
         return carry
 
-    lax.fori_loop(0, width // LANES, pair, 0, unroll=2)
+    lax.fori_loop(0, width // LANES, pair, 0, unroll=3)
     outs += copies([(att_out, att_h)], sems, 12)
     hi, mid, low = three_parts(stat[...])
     zero = jnp.zeros((PART, tok), BF)
@@ -261,7 +261,7 @@
             put_shards(ref, info, lay, pl.ds(pl.multiple_of(i * part, part), part), res)
         return carry
 
-    lax.fori_loop(0, half // part, piece, 0)
+    lax.fori_loop(0, half // part, piece, 0, unroll=2)
 
 
 def ffn_back_kernel(
@@ -297,7 +297,7 @@
                     put_rows(ref, 0, info[9], 0, lay[1], cols, res)
         return carry
 
-    lax.fori_loop(0, steps, step, 0)
+    lax.fori_loop(0, steps, step, 0, unroll=4)
 
 
 def norm_back_kernel(
@@ -384,13 +384,13 @@
         gvt[sl, :] = gvb.T
         return carry
 
-    lax.fori_loop(0, width // LANES, pair, 0, unroll=6)
+    lax.fori_loop(0, width // LANES, pair, 0, unroll=2)
     bq = jnp.sum(gq[...].astype(F32), axis=0, keepdims=True)
     bv = jnp.sum(gv[...].astype(F32), axis=0, keepdims=True)
     vec_out[...] = jnp.concatenate([bq, bv, jnp.zeros((6, width), F32)], axis=0)
 
 
-def weights_back_kernel(lay, info, gqt, gkt, gvt, x_ref, vecs, bups, send_a, send_b, keep_a, keep_b):
+def weights_back_kernel(lay, info, gqt, gkt, gvt, x_ref, vecs, bups, osend, okeep, send_a, send_b, keep_a, keep_b):
     width = x_ref.shape[1]
     n, halves, rs = lay
     half = width // 2
@@ -417,6 +417,9 @@
             else:
                 wb[0, 0] = res.astype(BF)
     if n > 1:
+        for o, (wa, wb) in ((osend, (send_a, send_b)), (okeep, (keep_a, keep_b))):
+            wa[:, :, 80:, :] = o[:, :, :16, :]
+            wb[:, :, 80:, :] = o[:, :, 16:, :]
         for j in range(n):
             bup = bups[:1, j * 4 * rs : (j + 1) * 4 * rs]
             block = jnp.concatenate(
@@ -463,10 +466,7 @@
     return pl.CostEstimate(flops=int(us * 10**9) + 1, bytes_accessed=1, transcendentals=0)
 
 
-COSTS = {
-    "down_one": 0.1, "up_one": 0.1, "down_two": 0.1, "up_two": 1.0, "down_three": 8.0, "qkv_one": 0.1, "up_three": 3.0,
-    "down_four": 1.0, "down_end": 0.02, "up_end": 0.02,
-}
+COSTS = {'down_one': 0.1, 'up_one': 0.1, 'down_two': 0.1, 'up_two': 1.0, 'down_three': 14.0, 'qkv_one': 0.1, 'up_three': 3.0, 'down_four': 1.0, 'down_end': 0.02, 'up_end': 0.02}
 
 
 class Line:
@@ -499,82 +499,28 @@
         return got
 
 
-def kernel_name(kernel):
-    return getattr(kernel, "func", kernel).__name__.split("_")[0]
-
-
 def plus(a, b):
     return (a.astype(F32) + b.astype(F32)).astype(BF)
 
 
-def view(ref, cut):
-    return ref[:, :, slice(*cut[0]), slice(*cut[1])]
-
-
-def one_kernel(cuts_a, cuts_b, count, *refs):
-    got, kept = refs[:count], refs[count : 2 * count]
-    sa, sb, ka, kb = refs[2 * count :]
-    at = 0
-    for i, cut in cuts_a:
-        total = plus(view(got[i], cut), view(kept[i], cut))
-        m = total.shape[2]
-        sa[:, :, at : at + m, :] = total[:, 4:]
-        ka[:, :, at : at + m, :] = total[:, :4]
-        at += m
-    at = 0
-    for i, cut in cuts_b:
-        total = plus(view(got[i], cut), view(kept[i], cut))
-        m = total.shape[2]
-        sb[:, at : at + m, :] = total[1]
-        kb[:, at : at + m, :] = total[0]
-        at += m
-
-
-def two_kernel(ga, gb, ka, kb, sa, sb, la, lb):
-    a = plus(ga[...], ka[...])
-    sa[...] = a[1]
-    la[...] = a[0]
-    b = plus(gb[...], kb[...])
-    sb[...] = b[4:]
-    lb[...] = b[:4]
-
-
-def two_with_out_kernel(split, ga, gb, ka, kb, go, ko, sa, sb, la, lb, lx, ly):
-    ma, mb, mo = ka.shape[2], kb.shape[1], ko.shape[2]
-    two_kernel(ga, gb, ka, kb, sa.at[:, :ma, :], sb.at[:, :mb, :], la, lb)
-    total = plus(go[...], ko[...])
-    rest = mo - split
-    sb[:, mb : mb + split, :] = total[0, 4:, :split]
-    sb[:, mb + split :, :] = total[1, 4:, :split]
-    lx[...] = total[:, :4, :split]
-    sa[:, ma : ma + rest, :] = total[1, :4, split:]
-    sa[:, ma + rest :, :] = total[1, 4:, split:]
-    ly[...] = total[0, :, split:]
-
-
-def two_from_out_kernel(ga, gb, ka, kb, gx, gy, kx, ky, sa, sb, la, lb):
-    ma, mb, nx, ny = ka.shape[2], kb.shape[1], kx.shape[2], ky.shape[1]
-    two_kernel(ga, gb, ka, kb, sa.at[:, :ma, :], sb.at[:, :mb, :], la.at[:, :ma, :], lb.at[:, :mb, :])
-    x0, y0 = gx.shape[1] - 2 * nx, gy.shape[1] - 2 * ny
-    la[:, ma:, :] = plus(gx[:, x0 : x0 + nx, :], kx[0])
-    sa[:, ma:, :] = plus(gx[:, x0 + nx :, :], kx[1])
-    lb[:, mb:, :] = plus(gy[:, y0 : y0 + ny, :], ky[:4])
-    sb[:, mb:, :] = plus(gy[:, y0 + ny :, :], ky[4:])
-
-
-def three_kernel(ga, gb, ka, kb, send, keep):
-    m, mb = ka.shape[1], kb.shape[1]
-    a, b = plus(ga[:, :m, :], ka[...]), plus(gb[:, :mb, :], kb[...])
-    send[:, :m, :] = a[2:]
-    keep[:, :m, :] = a[:2]
-    send[:, m:, :] = b[2:]
-    keep[:, m:, :] = b[:2]
-
-
-def four_kernel(got, kept, send, keep):
-    total = plus(got[...], kept[...])
-    send[...] = total[1]
-    keep[...] = total[0]
+def half_of(ref, axis, side, rows, cols):
+    lead = [slice(None)] * (len(ref.shape) - 2)
+    lead[axis] = side
+    return ref[(*lead, slice(*rows), slice(*cols))]
+
+
+def split_sum_kernel(parts, n_got, n_kept, n_send, *refs):
+    got, kept, out = refs[:n_got], refs[n_got : n_got + n_kept], refs[n_got + n_kept :]
+    for axis, spans, (send, send_at), (keep, keep_at) in parts:
+        done = 0
+        for g, g_rows, g_cols, k, k_rows, k_cols in spans:
+            m = g_rows[1] - g_rows[0]
+            for side, ref, at in ((1, out[send], send_at), (0, out[n_send + keep], keep_at)):
+                lead = [slice(None)] * (len(ref.shape) - 2)
+                ref[(*lead, slice(at + done, at + done + m), slice(None))] = plus(
+                    half_of(got[g], axis, side, g_rows, g_cols), half_of(kept[k], axis, side, k_rows, k_cols)
+                )
+            done += m
 
 
 def five_kernel(got, kept, mine):
@@ -587,12 +533,12 @@
 
 
 def down_kernel(info, mine, other, out):
-    m = mine.shape[1] // 2
+    m = mine.shape[1] // 3
     cols = mine.shape[2]
     for rc, ref in ((0, mine), (1, other)):
-        for p in range(2):
+        for p in range(3):
             block = jnp.concatenate([ref[0, p * m : (p + 1) * m], ref[1, p * m : (p + 1) * m]], axis=0)
-            at = (info[8] ^ rc) * 2 * cols + p * cols
+            at = (info[8] ^ rc) * 3 * cols + p * cols
             out[:, pl.ds(pl.multiple_of(at, cols), cols)] = block.astype(F32)
 
 
@@ -619,9 +565,9 @@
             out[:, at] = jnp.concatenate(parts, axis=0).astype(F32)
 
         put(gq, (0, 0, 48), (1, 0, 48))
-        put(gk, (0, 48, 16), (1, 48, 16), (0, 160, 32), (1, 160, 32))
-        put(gv, (0, 112, 48), (1, 112, 48))
-        put(go, (0, 80, 32), (0, 192, 16), (1, 80, 32), (1, 192, 16))
+        put(gk, (0, 48, 16), (1, 48, 16), (0, 144, 32), (1, 144, 32))
+        put(gv, (0, 96, 48), (1, 96, 48))
+        put(go, (0, 80, 16), (0, 176, 32), (1, 80, 16), (1, 176, 32))
     rs = vecs[0].shape[0]
     low = [jnp.where(info[8] == 0, m[64:80].astype(F32), o[64:80].astype(F32)) for m, o in zip(mine, other)]
     for i, out in enumerate(vecs[:8]):
@@ -739,78 +685,76 @@
     def join_rows(parts):
         return parts[0] if len(parts) == 1 else jnp.concatenate(parts, axis=-2)
 
+    send_along = {"x": pp_x, "y": pp_y, "z": pp_z1, "w": pp_z2}
+
     class Sum:
-        def __init__(self, name, got, kept, cuts_a, cuts_b):
-            self.name, self.got, self.kept = name, got, kept
-            self.cuts = cuts_a, cuts_b
-
-        def run(self, kernel, outs, args, scalars=()):
-            name = self.name + kernel_name(kernel)
+        def __init__(self, name, got, kept, parts):
+            sides = lambda w: w.reshape(2, 2, 2, 2, *w.shape[2:])
+            self.name = name
+            self.got, self.kept = [sides(w) for w in got], [sides(w) for w in kept]
+            self.spans = [[(i, r, c, i, r, c) for i, r, c in spans] for spans in parts]
+            self.rows = [sum(r[1] - r[0] for _, r, _ in spans) for spans in parts]
+            self.cols = parts[0][0][2][1] - parts[0][0][2][0]
+            self.whole = sum(self.rows), self.cols
+            self.left = ["yxzw"] * len(parts)
+
+        def run(self, step, kernel, outs, args, scalars=()):
+            name = self.name + step
             return line.call(
                 kernel, [shape(o) for o in outs], args, scalars=scalars, name=name, mib=16, us=COSTS.get(name, 0.3)
             )
 
-        def one(self):
-            a, b = (sum(r1 - r0 for _, ((r0, r1), _) in cut) for cut in self.cuts)
-            c = self.cuts[0][0][1][1]
-            c = c[1] - c[0]
-            sa, sb, ka, kb = self.run(
-                functools.partial(one_kernel, *self.cuts, len(self.got)),
-                [(2, 4, a, c), (8, b, c), (2, 4, a, c), (8, b, c)],
+        def split(self, step, along):
+            ways, last = list(dict.fromkeys(along)), along[0] == "w"
+            height, kept_height, parts = dict.fromkeys(ways, 0), 0, []
+            for p, a in enumerate(along):
+                keep = (0, kept_height) if last else (p, 0)
+                parts.append((self.left[p].index(a), self.spans[p], (ways.index(a), height[a]), keep))
+                self.left[p] = self.left[p].replace(a, "")
+                height[a] += self.rows[p]
+                kept_height += self.rows[p]
+            lead = (2,) * len(self.left[0])
+            keeps = [sum(self.rows)] if last else self.rows
+            out = self.run(
+                step,
+                functools.partial(split_sum_kernel, parts, len(self.got), len(self.kept), len(ways)),
+                [(*lead, m, self.cols) for m in [*height.values(), *keeps]],
                 (*self.got, *self.kept),
             )
-            self.got, self.kept = (pp_x(sa), pp_y(sb)), (ka, kb)
-            self.dims = a, b, c
+            self.got = [send_along[a](w) for a, w in zip(ways, out[: len(ways)])]
+            self.kept = out[len(ways) :]
+            self.spans = [
+                [(i, (at, at + m), (0, self.cols), k, (k_at, k_at + m), (0, self.cols))]
+                for m, (_, _, (i, at), (k, k_at)) in zip(self.rows, parts)
+            ]
+
+        def one(self):
+            self.split("one", "xyz"[: len(self.rows)])
 
         def two(self):
-            a, b, c = self.dims
-            sa, sb, ka, kb = self.run(two_kernel, [(4, a, c), (4, b, c)] * 2, (*self.got, *self.kept))
-            self.got, self.kept = (pp_y(sa), pp_x(sb)), (ka, kb)
-
-        def two_with_out(self, got, kept, split):
-            a, b, c = self.dims
-            m = kept.shape[2]
-            rest = m - split
-            sa, sb, ka, kb, kx, ky = self.run(
-                functools.partial(two_with_out_kernel, split),
-                [(4, a + 2 * rest, c), (4, b + 2 * split, c), (4, a, c), (4, b, c), (2, 4, split, c), (8, rest, c)],
-                (*self.got, *self.kept, got, kept),
-            )
-            self.got, self.kept = (pp_y(sa), pp_x(sb)), (ka, kb)
-            return self.got[1], self.got[0], kx, ky
-
-        def two_from_out(self, gx, gy, kx, ky):
-            a, b, c = self.dims
-            a, b = a + kx.shape[2], b + ky.shape[1]
-            self.dims = a, b, c
-            sa, sb, ka, kb = self.run(
-                two_from_out_kernel, [(4, a, c), (4, b, c)] * 2, (*self.got, *self.kept, gx, gy, kx, ky)
-            )
-            self.got, self.kept = (pp_y(sa), pp_x(sb)), (ka, kb)
+            self.split("two", "yxx"[: len(self.rows)])
 
         def three(self):
-            a, b, c = self.dims
-            send, keep = self.run(three_kernel, [(2, a + b, c)] * 2, (*self.got, *self.kept))
-            self.got, self.kept = pp_z1(send), keep
+            self.split("three", "zzy"[: len(self.rows)])
 
         def four(self):
-            a, b, c = self.dims
-            send, keep = self.run(four_kernel, [(a + b, c)] * 2, (self.got, self.kept))
-            self.got, self.kept = pp_z2(send), keep
+            self.split("four", "www"[: len(self.rows)])
+
+        def mine(self):
+            (mine,) = self.run("five", five_kernel, [self.whole], (*self.got, *self.kept))
+            return mine
 
         def five(self):
-            a, b, c = self.dims
-            (mine,) = self.run(five_kernel, [(a + b, c)], (self.got, self.kept))
+            mine = self.mine()
             self.got, self.kept = pp_y(mine), mine
 
+        def six(self):
+            (both,) = self.run("six", six_kernel, [(2, *self.whole)], (info, self.kept, self.got), scalars=(0,))
+            self.got, self.kept = pp_core(both), both
+
         def five_all(self):
-            (mine,) = self.run(five_kernel, [(self.dims[0] + self.dims[1], self.dims[2])], (self.got, self.kept))
+            mine = self.mine()
             self.kept, self.got = mine, [pp_y(mine), pp_core(mine), lax.ppermute(mine, "seq", xor[3])]
-
-        def six(self):
-            a, b, c = self.dims
-            (both,) = self.run(six_kernel, [(2, a + b, c)], (info, self.kept, self.got), scalars=(0,))
-            self.got, self.kept = pp_core(both), both
 
         def end(self, kernel, outs):
             return line.call(
@@ -832,8 +776,8 @@
     )
     if fast:
         u_got = pp_core(u_send)
-        c, m = ff // 4, rs // 2
-        down = Sum("down_", [d_got], [d_keep], [(0, ((0, m), (0, c)))], [(0, ((0, m), (c, 2 * c)))])
+        c, m = ff // 6, rs // 2
+        down = Sum("down_", [d_got], [d_keep], [[(0, (0, m), (p * c, (p + 1) * c))] for p in range(3)])
         down.one()
     wire_o = shape((halves, n, rs // halves, half))
     r1, gatt, gaug, vec_c, o_send, o_keep = line.call(
@@ -846,9 +790,8 @@
         mib=14,
     )
     if fast:
-        o_got = pp_core(o_send)
-        m = half // 2
-        up = Sum("up_", [u_got], [u_keep], [(0, ((0, m // 2), (0, half)))], [(0, ((m // 2, m), (0, half)))])
+        m = half // 4
+        up = Sum("up_", [u_got], [u_keep], [[(0, (p * m, (p + 1) * m), (0, half))] for p in range(2)])
         up.one()
 
     gq, gk, gv, gqt, gkt, gvt, vec_d = line.call(
@@ -861,12 +804,12 @@
     vecs = jnp.concatenate([vec_d[:2], vec_c[:3], vec_b[:3]], axis=0)
     if fast:
         down.two()
-    rows_a, rows_b = (80, 80) if fast else (2 * width, width)
+    rows_a, rows_b = (96, 112) if fast else (2 * width, width)
     wire_a, wire_b = shape((halves, n, rows_a, half)), shape((halves, n, rows_b, half))
     qa_send, qb_send, qa_keep, qb_keep = line.call(
         functools.partial(weights_back_kernel, lay),
         [wire_a, wire_b, wire_a, wire_b],
-        (info, gqt, gkt, gvt, x, vecs, bup),
+        (info, gqt, gkt, gvt, x, vecs, bup, o_send, o_keep),
         scalars=(0,),
         name="weights_back",
         mib=16,
@@ -895,17 +838,16 @@
     if fast:
         qkv = Sum(
             "qkv_", [pp_core(qa_send), pp_core(qb_send)], [qa_keep, qb_keep],
-            [(0, ((0, 80), (0, half)))],
-            [(1, ((0, 80), (0, half)))],
+            [[(0, (0, rows_a), (0, half))], [(1, (0, rows_b), (0, half))]],
         )
         f32 = lambda *d: shape(d, F32)
-        out_sum = up.two_with_out(o_got, o_keep, 32)
+        up.two()
         down.three()
         qkv.one()
         packs = send_back()
+        down.four()
         up.three()
-        down.four()
-        qkv.two_from_out(*out_sum)
+        qkv.two()
         up.four()
         down.five()
         down.six()

time: 152 us -> 148 us (0.974); the launches traced: 152 us -> 146 us
  waiting for transfers between devices: 38.1 us -> 35.2 us
  starting transfers between devices: 39.9 us -> 38.1 us
    ppermute x12 -> x13, waiting for transfers between devices: 8.51 us -> 14.2 us  [pp_dp(): return lambda a: lax.ppermute(a, 'dp', [(i, i ^ bit) for i in range(n_dp)])]
    ppermute x9 -> x10, waiting for transfers between devices: 23.7 us -> 18.4 us  [local(): pp_y = lambda a: lax.ppermute(a, 'seq', xor[2])]
    ppermute x1, waiting for transfers between devices: 2.35 us -> 0.01 us  [five_all(): lax.ppermute(mine, 'seq', xor[3])]
    ppermute x8 -> x7, starting transfers between devices: 3.31 us -> 1.27 us  [local(): pp_core = lambda a: lax.ppermute(a, 'seq', xor[1])]
    ppermute x9 -> x10, starting transfers between devices: 9.61 us -> 10.4 us  [local(): pp_y = lambda a: lax.ppermute(a, 'seq', xor[2])]
    ppermute x12 -> x13, starting transfers between devices: 18.8 us -> 18.2 us  [pp_dp(): return lambda a: lax.ppermute(a, 'dp', [(i, i ^ bit) for i in range(n_dp)])]
  transfers between devices with their start and end apart: 39 -> 40, of which waited for: 13 -> 11; matrix products, arithmetic and copies ran while one was open for 1% -> 1% of each run, Pallas kernels for 35% -> 36%
where the time goes in v5:
time: 148 us; the launch traced here: 146 us
  Pallas kernels  69.9 us (47%)
  starting transfers between devices  38.1 us (26%)
  waiting for transfers between devices  35.2 us (24%)
  between operations  1.57 us (1%)
  other arithmetic  1.5 us (1%)
    pallas_call x32, Pallas kernels, call(): pl.pallas_call(body, out_shape=[*outs, shape((8, LANES), F32)], in_specs=...  69.9 us
    ppermute x10, waiting for transfers between devices, local(): pp_y = lambda a: lax.ppermute(a, 'seq', xor[2])  18.4 us
    ppermute x13, starting transfers between devices, pp_dp(): return lambda a: lax.ppermute(a, 'dp', [(i, i ^ bit) for i in range(n_dp)])  18.2 us
    ppermute x13, waiting for transfers between devices, pp_dp(): return lambda a: lax.ppermute(a, 'dp', [(i, i ^ bit) for i in range(n_dp)])  14.2 us
    ppermute x10, starting transfers between devices, local(): pp_y = lambda a: lax.ppermute(a, 'seq', xor[2])  10.4 us
    ppermute x6, starting transfers between devices, rel(): lax.ppermute(parts[r], 'seq', xor[r])  5.39 us
  transfers between devices with their start and end apart: 40, of which 11 were waited for; matrix products, arithmetic and copies ran while one was open for 1% of the time, Pallas kernels for 36%

profile of v5, /device:TPU:0, one launch (start us, length us, event | category | flops | bytes accessed | tf_op | source)
XLA Modules:
  0.0 146.5 jit_solution(10200259472801705053)
XLA Ops:
  0.8 1.8 %split_tokens.1 = (bf16[128,768]{1,0:T(8,128)(2,1)S(1)}, bf16[128,768]{1,0:T(8,128)(2,1)S(1)}, bf16[128,768]{1,0:T(8,128)(2,1)S(1)}, bf16[128,768]{1,0:T(8,128)(2,1)S(1)}, f32[8,128]{1,0:T(8,128)S(1)}) custom-call(s32[16]{0:T(128)S(1)} %concatenate.9.refs_0_, bf16[4,128,768]{2,1,0:T(8,128)(2,1)} %refs_1_.3), custom_call_target="tpu_custom_call" | custom-call | flops 1 | bytes 1 | tf_op jit(solution)/shard_map/split_tokens/pallas_call | solution.py:489
  2.6 0.5 collective-permute-start
  3.1 2.6 %collective-permute-start.1 = (bf16[128,768]{1,0:T(8,128)(2,1)S(1)}, bf16[128,768]{1,0:T(8,128)(2,1)S(1)}, u32[]{:S(2)}, u32[]{:S(2)}) collective-permute-start(bf16[128,768]{1,0:T(8,128)(2,1)S(1)} %get-tuple-element.176), channel_id=1, source_target_pairs={{0,2},{1,3},{2,0},{3,1},{4,6},{5,7},{6,4},{7,5},{8,10},{9,11},{10,... | collective-permute-start | bytes 589832 | tf_op jit(solution)/shard_map/ppermute | solution.py:610
  5.8 1.8 %split_grads.1 = (bf16[128,768]{1,0:T(8,128)(2,1)S(1)}, bf16[128,768]{1,0:T(8,128)(2,1)S(1)}, bf16[128,768]{1,0:T(8,128)(2,1)S(1)}, bf16[128,768]{1,0:T(8,128)(2,1)S(1)}, f32[8,128]{1,0:T(8,128)S(1)}) custom-call(s32[16]{0:T(128)S(1)} %concatenate.9.refs_0_, bf16[4,128,768]{2,1,0:T(8,128)(2,1)} %refs_1_.4, f32[8,128]{1,0:T(8,128)S(1)} %get-tuple-element.178.refs_2_), custom_call_target="tpu_custom_call" | custom-call | flops 1 | bytes 1 | tf_op jit(solution)/shard_map/split_grads/pallas_call | solution.py:489
  7.8 1.9 %collective-permute-start.4 = (bf16[128,768]{1,0:T(8,128)(2,1)S(1)}, bf16[128,768]{1,0:T(8,128)(2,1)S(1)}, u32[]{:S(2)}, u32[]{:S(2)}) collective-permute-start(bf16[128,768]{1,0:T(8,128)(2,1)S(1)} %get-tuple-element.187), channel_id=1, source_target_pairs={{0,2},{1,3},{2,0},{3,1},{4,6},{5,7},{6,4},{7,5},{8,10},{9,11},{10,... | collective-permute-start | bytes 589832 | tf_op jit(solution)/shard_map/ppermute | solution.py:610
  10.3 0.8 subtract_convert_fusion
  11.2 2.2 %fetch.1 = (bf16[768,768]{1,0:T(8,128)(2,1)S(1)}, bf16[768,768]{1,0:T(8,128)(2,1)S(1)}, bf16[768,768]{1,0:T(8,128)(2,1)S(1)}, f32[8,128]{1,0:T(8,128)S(1)}) custom-call(bf16[768,768]{1,0:T(8,128)(2,1)} %refs_4_.3, bf16[768,768]{1,0:T(8,128)(2,1)} %refs_5_.5, bf16[768,768]{1,0:T(8,128)(2,1)} %refs_6_.7, f32[8,128]{1,0:T(8,128)S(1)} %get-tuple-element.179.refs_3_), custom_call_target="tpu_custom_call" | custom-call | flops 1 | bytes 1 | tf_op jit(solution)/shard_map/fetch/pallas_call | solution.py:489
  13.6 1.6 %collective-permute-done.2.refs_3_ = bf16[128,768]{1,0:T(8,128)(2,1)S(1)} collective-permute-done((bf16[128,768]{1,0:T(8,128)(2,1)S(1)}, bf16[128,768]{1,0:T(8,128)(2,1)S(1)}, u32[]{:S(2)}, u32[]{:S(2)}) %collective-permute-start.2) | collective-permute-done | bytes 196640 | tf_op jit(solution)/shard_map/ppermute | solution.py:610
  15.3 10.8 %attend.1 = (bf16[512,768]{1,0:T(8,128)(2,1)}, bf16[512,768]{1,0:T(8,128)(2,1)}, bf16[512,768]{1,0:T(8,128)(2,1)}, bf16[512,768]{1,0:T(8,128)(2,1)}, f32[512,768...) custom-call(bf16[128,768]{1,0:T(8,128)(2,1)S(1)} %get-tuple-element., ...), custom_call_target="tpu_custom_call" | custom-call | flops 1 | bytes 1 | tf_op jit(solution)/shard_map/attend/pallas_call | solution.py:489
  26.2 13.9 %ffn.1 = (bf16[128,768]{1,0:T(8,128)(2,1)S(1)}, bf16[128,768]{1,0:T(8,128)(2,1)S(1)}, bf16[128,768]{1,0:T(8,128)(2,1)S(1)}, bf16[128,768]{1,0:T(8,128)(2,1)S(1)}...) custom-call(s32[16]{0:T(128)S(1)} %concatenate.9.refs_0_, ...), custom_call_target="tpu_custom_call" | custom-call | flops 1 | bytes 1 | tf_op jit(solution)/shard_map/ffn/pallas_call | solution.py:489
  40.2 0.4 collective-permute-start.6
  40.6 6.1 %ffn_back.1 = (bf16[2,8,192,384]{3,2,1,0:T(8,128)(2,1)S(1)}, bf16[2,8,192,384]{3,2,1,0:T(8,128)(2,1)S(1)}, f32[8,3072]{1,0:T(8,128)S(1)}, bf16[512,3072]{1,0:T(8,128)(2,1)S(1)}, f32[8,128]{1,0:T(8,128)S(1)}) custom-call(s32[16]{0:T(128)S(1)} %concatenate.9.refs_0_, f32[512,768]{1,0:T(8,128)S(1)} %get-tuple-element.197.refs_1_, ...), custom_call_target="tpu_custom_call" | custom-call | flops 1 | bytes 1 | tf_op jit(solution)/shard_map/ffn_back/pallas_call | solution.py:489
  46.9 0.6 down_one.1
  47.5 1.9 %collective-permute-start.10 = (bf16[2,2,2,48,512]{4,3,2,1,0:T(8,128)(2,1)S(1)}, bf16[2,2,2,48,512]{4,3,2,1,0:T(8,128)(2,1)S(1)}, u32[]{:S(2)}, u32[]{:S(2)}) collective-permute-start(bf16[2,2,2,48,512]{4,3,2,1,0:T(8,128)(2,1)S(1)} %get-tuple-element.230), channel_id=1, source_target_pairs={{0,8},{4,12},{8,0},{12,4},{16,24},{20,28},{24,16},{28,20},{1,9},{5... | collective-permute-start | bytes 1179656 | tf_op jit(solution)/shard_map/ppermute | solution.py:681
  49.5 1.5 %collective-permute-start.8 = (bf16[2,2,2,48,512]{4,3,2,1,0:T(8,128)(2,1)S(1)}, bf16[2,2,2,48,512]{4,3,2,1,0:T(8,128)(2,1)S(1)}, u32[]{:S(2)}, u32[]{:S(2)}) collective-permute-start(bf16[2,2,2,48,512]{4,3,2,1,0:T(8,128)(2,1)S(1)} %get-tuple-element.228), channel_id=1, source_target_pairs={{0,4},{4,0},{8,12},{12,8},{16,20},{20,16},{24,28},{28,24},{1,5},{5... | collective-permute-start | bytes 1179656 | tf_op jit(solution)/shard_map/ppermute | solution.py:681
  51.0 1.5 %collective-permute-start.9 = (bf16[2,2,2,48,512]{4,3,2,1,0:T(8,128)(2,1)S(1)}, bf16[2,2,2,48,512]{4,3,2,1,0:T(8,128)(2,1)S(1)}, u32[]{:S(2)}, u32[]{:S(2)}) collective-permute-start(bf16[2,2,2,48,512]{4,3,2,1,0:T(8,128)(2,1)S(1)} %get-tuple-element.229), channel_id=1, source_target_pairs={{0,2},{1,3},{2,0},{3,1},{4,6},{5,7},{6,4},{7,5},{8,10},{9,11},{10,... | collective-permute-start | bytes 1179656 | tf_op jit(solution)/shard_map/ppermute | solution.py:678
  52.5 7.0 %norm_back.1 = (f32[512,768]{1,0:T(8,128)S(1)}, bf16[512,768]{1,0:T(8,128)(2,1)S(1)}, bf16[512,128]{1,0:T(8,128)(2,1)S(1)}, f32[8,768]{1,0:T(8,128)S(1)}, bf16[2...) custom-call(s32[16]{0:T(128)S(1)} %concatenate.9.refs_0_, ...), custom_call_target="tpu_custom_call" | custom-call | flops 1 | bytes 1 | tf_op jit(solution)/shard_map/norm_back/pallas_call | solution.py:489
  59.5 0.6 up_one.1
  60.2 0.6 collective-permute-start.15
  60.8 0.5 collective-permute-start.16
  61.3 10.1 %attend_back.1 = (bf16[512,768]{1,0:T(8,128)(2,1)S(1)}, bf16[512,768]{1,0:T(8,128)(2,1)S(1)}, bf16[512,768]{1,0:T(8,128)(2,1)S(1)}, bf16[768,512]{1,0:T(8,128)(2...) custom-call(bf16[512,768]{1,0:T(8,128)(2,1)S(1)} %copy-done.5, ...), custom_call_target="tpu_custom_call" | custom-call | flops 1 | bytes 1 | tf_op jit(solution)/shard_map/attend_back/pallas_call | solution.py:489
  71.4 0.3 down_two.1
  71.7 1.6 %collective-permute-start.14 = (bf16[2,2,96,512]{3,2,1,0:T(8,128)(2,1)S(1)}, bf16[2,2,96,512]{3,2,1,0:T(8,128)(2,1)S(1)}, u32[]{:S(2)}, u32[]{:S(2)}) collective-permute-start(bf16[2,2,96,512]{3,2,1,0:T(8,128)(2,1)S(1)} %get-tuple-element.241), channel_id=1, source_target_pairs={{0,4},{4,0},{8,12},{12,8},{16,20},{20,16},{24,28},{28,24},{1,5},{5... | collective-permute-start | bytes 1179656 | tf_op jit(solution)/shard_map/ppermute | solution.py:681
  73.2 1.6 %collective-permute-start.13 = (bf16[2,2,48,512]{3,2,1,0:T(8,128)(2,1)S(1)}, bf16[2,2,48,512]{3,2,1,0:T(8,128)(2,1)S(1)}, u32[]{:S(2)}, u32[]{:S(2)}) collective-permute-start(bf16[2,2,48,512]{3,2,1,0:T(8,128)(2,1)S(1)} %get-tuple-element.240), channel_id=1, source_target_pairs={{0,2},{1,3},{2,0},{3,1},{4,6},{5,7},{6,4},{7,5},{8,10},{9,11},{10,... | collective-permute-start | bytes 589832 | tf_op jit(solution)/shard_map/ppermute | solution.py:678
  74.8 2.7 %weights_back.1 = (bf16[2,8,96,384]{3,2,1,0:T(8,128)(2,1)S(1)}, bf16[2,8,112,384]{3,2,1,0:T(8,128)(2,1)S(1)}, bf16[2,8,96,384]{3,2,1,0:T(8,128)(2,1)S(1)}, bf16[...) custom-call(s32[16]{0:T(128)S(1)} %concatenate.9.refs_0_, bf16[768,512]{1,0:T(8,128)(2,1)S(1)} %get-tuple-element.218.refs_1_, ...), custom_call_target="tpu_custom_call" | custom-call | flops 1 | bytes 1 | tf_op jit(solution)/shard_map/weights_back/pallas_call | solution.py:489
  77.6 0.5 collective-permute-start.11
  78.1 0.3 up_two.1
  78.5 0.6 collective-permute-start.22
  79.0 0.5 collective-permute-done.13.refs_0_
  79.6 1.5 %collective-permute-start.23 = (bf16[2,2,96,384]{3,2,1,0:T(8,128)(2,1)S(1)}, bf16[2,2,96,384]{3,2,1,0:T(8,128)(2,1)S(1)}, u32[]{:S(2)}, u32[]{:S(2)}) collective-permute-start(bf16[2,2,96,384]{3,2,1,0:T(8,128)(2,1)S(1)} %get-tuple-element.268), channel_id=1, source_target_pairs={{0,4},{4,0},{8,12},{12,8},{16,20},{20,16},{24,28},{28,24},{1,5},{5... | collective-permute-start | bytes 884744 | tf_op jit(solution)/shard_map/ppermute | solution.py:681
  81.1 3.7 %collective-permute-done.14.refs_1_ = bf16[2,2,96,512]{3,2,1,0:T(8,128)(2,1)S(1)} collective-permute-done((bf16[2,2,96,512]{3,2,1,0:T(8,128)(2,1)S(1)}, bf16[2,2,96,512]{3,2,1,0:T(8,128)(2,1)S(1)}, u32[]{:S(2)}, u32[]{:S(2)}) %collective-permute-start.14) | collective-permute-done | bytes 393248 | tf_op jit(solution)/shard_map/ppermute | solution.py:681
  84.9 0.5 collective-permute-start.24
  85.4 0.3 collective-permute-start.25
  85.7 0.6 qkv_one.1
  86.3 1.8 %collective-permute-start.21 = (bf16[2,2,2,112,384]{4,3,2,1,0:T(8,128)(2,1)S(1)}, bf16[2,2,2,112,384]{4,3,2,1,0:T(8,128)(2,1)S(1)}, u32[]{:S(2)}, u32[]{:S(2)}) collective-permute-start(bf16[2,2,2,112,384]{4,3,2,1,0:T(8,128)(2,1)S(1)} %get-tuple-element.264), channel_id=1, source_target_pairs={{0,2},{1,3},{2,0},{3,1},{4,6},{5,7},{6,4},{7,5},{8,10},{9,11},{10,... | collective-permute-start | bytes 2064392 | tf_op jit(solution)/shard_map/ppermute | solution.py:678
  88.1 3.0 %collective-permute-done.25.refs_1_ = bf16[2,48,512]{2,1,0:T(8,128)(2,1)S(1)} collective-permute-done((bf16[2,48,512]{2,1,0:T(8,128)(2,1)S(1)}, bf16[2,48,512]{2,1,0:T(8,128)(2,1)S(1)}, u32[]{:S(2)}, u32[]{:S(2)}) %collective-permute-start.25) | collective-permute-done | bytes 98336 | tf_op jit(solution)/shard_map/ppermute | solution.py:678
  91.1 0.5 collective-permute-start.20
  91.7 2.1 %input_back.1 = (bf16[128,768]{1,0:T(8,128)(2,1)S(1)}, bf16[128,768]{1,0:T(8,128)(2,1)S(1)}, bf16[128,768]{1,0:T(8,128)(2,1)S(1)}, bf16[128,768]{1,0:T(8,128)(2,1)S(1)}, f32[8,128]{1,0:T(8,128)S(1)}) custom-call(bf16[512,768]{1,0:T(8,128)(2,1)S(1)} %get-tuple-element.214.refs_0_, bf16[512,768]{1,0:T(8,128)(2,1)S(1)} %get-tuple-element.215.refs_1_, ...), custom_call_target="tpu_custom_call" | custom-call | flops 1 | bytes 1 | tf_op jit(solution)/shard_map/input_back/pallas_call | solution.py:489
  94.1 1.6 %collective-permute-start.29 = (bf16[2,192,384]{2,1,0:T(8,128)(2,1)S(1)}, bf16[2,192,384]{2,1,0:T(8,128)(2,1)S(1)}, u32[]{:S(2)}, u32[]{:S(2)}) collective-permute-start(bf16[2,192,384]{2,1,0:T(8,128)(2,1)S(1)} %get-tuple-element.285), channel_id=1, source_target_pairs={{0,8},{4,12},{8,0},{12,4},{16,24},{20,28},{24,16},{28,20},{1,9},{5... | collective-permute-start | bytes 884744 | tf_op jit(solution)/shard_map/ppermute | solution.py:681
  95.8 2.6 %collective-permute-start.28 = (bf16[144,512]{1,0:T(8,128)(2,1)S(1)}, bf16[144,512]{1,0:T(8,128)(2,1)S(1)}, u32[]{:S(2)}, u32[]{:S(2)}) collective-permute-start(bf16[144,512]{1,0:T(8,128)(2,1)S(1)} %get-tuple-element.283), channel_id=1, source_target_pairs={{0,16},{4,20},{8,24},{12,28},{16,0},{20,4},{24,8},{28,12},{1,17},{... | collective-permute-start | bytes 442376 | tf_op jit(solution)/shard_map/ppermute | solution.py:681
  98.4 5.6 %collective-permute-done.20.refs_0_ = bf16[2,2,2,96,384]{4,3,2,1,0:T(8,128)(2,1)S(1)} collective-permute-done((bf16[2,2,2,96,384]{4,3,2,1,0:T(8,128)(2,1)S(1)}, bf16[2,2,2,96,384]{4,3,2,1,0:T(8,128)(2,1)S(1)}, u32[]{:S(2)}, u32[]{:S(2)}) %collective-permute-start.20) | collective-permute-done | bytes 589856 | tf_op jit(solution)/shard_map/ppermute | solution.py:681
  103.9 0.5 collective-permute-done.21.refs_1_
  104.4 0.3 qkv_two.1
  104.7 0.6 collective-permute-start.27
  105.3 0.5 collective-permute-start.26
  105.9 1.6 %collective-permute-start.30 = (bf16[144,512]{1,0:T(8,128)(2,1)S(1)}, bf16[144,512]{1,0:T(8,128)(2,1)S(1)}, u32[]{:S(2)}, u32[]{:S(2)}) collective-permute-start(bf16[144,512]{1,0:T(8,128)(2,1)S(1)} %get-tuple-element.290.refs_1_), channel_id=1, source_target_pairs={{0,2},{1,3},{2,0},{3,1},{4,6},{5,7},{6,4},{7,5},{8,10},{9,11},{10,... | collective-permute-start | bytes 442376 | tf_op jit(solution)/shard_map/ppermute | solution.py:678
  107.5 2.6 %collective-permute-start.32 = (bf16[192,384]{1,0:T(8,128)(2,1)S(1)}, bf16[192,384]{1,0:T(8,128)(2,1)S(1)}, u32[]{:S(2)}, u32[]{:S(2)}) collective-permute-start(bf16[192,384]{1,0:T(8,128)(2,1)S(1)} %get-tuple-element.296), channel_id=1, source_target_pairs={{0,16},{4,20},{8,24},{12,28},{16,0},{20,4},{24,8},{28,12},{1,17},{... | collective-permute-start | bytes 442376 | tf_op jit(solution)/shard_map/ppermute | solution.py:681
  110.1 5.6 %collective-permute-done.30.refs_2_ = bf16[144,512]{1,0:T(8,128)(2,1)S(1)} collective-permute-done((bf16[144,512]{1,0:T(8,128)(2,1)S(1)}, bf16[144,512]{1,0:T(8,128)(2,1)S(1)}, u32[]{:S(2)}, u32[]{:S(2)}) %collective-permute-start.30) | collective-permute-done | bytes 147488 | tf_op jit(solution)/shard_map/ppermute | solution.py:678
  115.7 0.6 down_six.1
  116.6 0.3 collective-permute-start.33
  116.9 0.5 collective-permute-start.17
  117.4 1.7 %collective-permute-start.18 = (bf16[272,768]{1,0:T(8,128)(2,1)S(1)}, bf16[272,768]{1,0:T(8,128)(2,1)S(1)}, u32[]{:S(2)}, u32[]{:S(2)}) collective-permute-start(bf16[272,768]{1,0:T(8,128)(2,1)S(1)} %get-tuple-element.261), channel_id=1, source_target_pairs={{0,2},{1,3},{2,0},{3,1},{4,6},{5,7},{6,4},{7,5},{8,10},{9,11},{10,... | collective-permute-start | bytes 1253384 | tf_op jit(solution)/shard_map/ppermute | solution.py:826
  119.2 4.2 %collective-permute-done.33.refs_2_ = bf16[192,384]{1,0:T(8,128)(2,1)S(1)} collective-permute-done((bf16[192,384]{1,0:T(8,128)(2,1)S(1)}, bf16[192,384]{1,0:T(8,128)(2,1)S(1)}, u32[]{:S(2)}, u32[]{:S(2)}) %collective-permute-start.33) | collective-permute-done | bytes 147488 | tf_op jit(solution)/shard_map/ppermute | solution.py:678
  123.4 0.6 up_six.1
  124.1 2.7 %collective-permute-start.34 = (bf16[208,384]{1,0:T(8,128)(2,1)S(1)}, bf16[208,384]{1,0:T(8,128)(2,1)S(1)}, u32[]{:S(2)}, u32[]{:S(2)}) collective-permute-start(bf16[208,384]{1,0:T(8,128)(2,1)S(1)} %get-tuple-element.302), channel_id=1, source_target_pairs={{0,16},{4,20},{8,24},{12,28},{16,0},{20,4},{24,8},{28,12},{1,17},{... | collective-permute-start | bytes 479240 | tf_op jit(solution)/shard_map/ppermute | solution.py:681
  126.8 1.6 %down_end.1 = (f32[96,3072]{1,0:T(8,128)}, f32[8,128]{1,0:T(8,128)S(1)}) custom-call(s32[16]{0:T(128)S(1)} %concatenate.9.refs_0_, bf16[2,144,512]{2,1,0:T(8,128)(2,1)S(1)} %get-tuple-element.305.refs_1_, bf16[2,144,512]{2,1,0:T(8,128)(2,1)S(1)} %collective-permute-done.36.refs_2_, f32[8,128]{1,0:T(8,128)S(1)} %get-tuple-element.306.refs_3_), custom_call_target="tpu_custom_call" | custom-call | flops 1 | bytes 1 | tf_op jit(solution)/shard_map/down_end/pallas_call | solution.py:489
  128.4 1.6 %up_end.1 = (f32[768,384]{1,0:T(8,128)}, f32[8,128]{1,0:T(8,128)S(1)}) custom-call(s32[16]{0:T(128)S(1)} %concatenate.9.refs_0_, bf16[2,192,384]{2,1,0:T(8,128)(2,1)S(1)} %get-tuple-element.304.refs_1_, bf16[2,192,384]{2,1,0:T(8,128)(2,1)S(1)} %collective-permute-done.35.refs_2_, f32[8,128]{1,0:T(8,128)S(1)} %get-tuple-element.307.refs_3_), custom_call_target="tpu_custom_call" | custom-call | flops 1 | bytes 1 | tf_op jit(solution)/shard_map/up_end/pallas_call | solution.py:489
  130.1 5.0 %collective-permute-done.34.refs_0_ = bf16[208,384]{1,0:T(8,128)(2,1)S(1)} collective-permute-done((bf16[208,384]{1,0:T(8,128)(2,1)S(1)}, bf16[208,384]{1,0:T(8,128)(2,1)S(1)}, u32[]{:S(2)}, u32[]{:S(2)}) %collective-permute-start.34) | collective-permute-done | bytes 159776 | tf_op jit(solution)/shard_map/ppermute | solution.py:681
  135.1 1.7 %collective-permute-start.37 = (bf16[208,384]{1,0:T(8,128)(2,1)S(1)}, bf16[208,384]{1,0:T(8,128)(2,1)S(1)}, u32[]{:S(2)}, u32[]{:S(2)}) collective-permute-start(bf16[208,384]{1,0:T(8,128)(2,1)S(1)} %get-tuple-element.313.refs_1_), channel_id=1, source_target_pairs={{0,2},{1,3},{2,0},{3,1},{4,6},{5,7},{6,4},{7,5},{8,10},{9,11},{10,... | collective-permute-start | bytes 479240 | tf_op jit(solution)/shard_map/ppermute | solution.py:678
  136.8 0.5 collective-permute-start.39
  137.3 0.9 collective-permute-done.19.refs_5_
  138.2 1.8 %unpack.1 = (bf16[4,128,768]{2,1,0:T(8,128)(2,1)}, bf16[4,128,768]{2,1,0:T(8,128)(2,1)}, f32[4,8,768]{2,1,0:T(8,128)}, f32[8,128]{1,0:T(8,128)S(1)}) custom-call(s32[16]{0:T(128)S(1)} %concatenate.9.refs_0_, f32[4,8,128]{2,1,0:T(8,128)S(1)} %broadcast_in_dim.12.refs_1_, bf16[272,768]{1,0:T(8,128)(2,1)S(1)} %get-tuple-element.259.refs_2_, ...), custom_call_target="tpu_custom_call" | custom-call | flops 1000000000 | bytes 1 | tf_op jit(solution)/shard_map/unpack/pallas_call | solution.py:489
  140.0 4.7 %collective-permute-done.37.refs_2_ = bf16[208,384]{1,0:T(8,128)(2,1)S(1)} collective-permute-done((bf16[208,384]{1,0:T(8,128)(2,1)S(1)}, bf16[208,384]{1,0:T(8,128)(2,1)S(1)}, u32[]{:S(2)}, u32[]{:S(2)}) %collective-permute-start.37) | collective-permute-done | bytes 159776 | tf_op jit(solution)/shard_map/ppermute | solution.py:678
  144.6 1.6 %qkv_end.1 = (f32[96,768]{1,0:T(8,128)}, f32[96,768]{1,0:T(8,128)}, f32[96,768]{1,0:T(8,128)}, f32[96,768]{1,0:T(8,128)}, f32[96]{0:T(128)}, /*index=5*/f32[96]{...) custom-call(s32[16]{0:T(128)S(1)} %concatenate.9.refs_0_, ...), custom_call_target="tpu_custom_call" | custom-call | flops 1 | bytes 1 | tf_op jit(solution)/shard_map/qkv_end/pallas_call | solution.py:489
  (121 shorter events, 2.9 us)
Async XLA Ops:
  0.7 9.1 %copy-start.20 = (s32[4,8]{1,0:T(4,128)S(1)}, s32[4,8]{1,0:T(4,128)}, u32[]{:S(2)}) copy-start(s32[4,8]{1,0:T(4,128)} %param.20) | copy-start | bytes 388
  0.8 25.3 %slice-start.2 = ((s8[4718592]{0:T(1024)(128)(4,1)}), s8[524288]{0:T(1024)(128)(4,1)S(1)}, s32[]{:S(2)}) async-start(s8[4718592]{0:T(1024)(128)(4,1)} %bitcast.30), calls=%async_computation.2 | async-start | bytes 1048576
  2.6 10.9 %collective-permute-start = (bf16[128,768]{1,0:T(8,128)(2,1)S(1)}, bf16[128,768]{1,0:T(8,128)(2,1)S(1)}, u32[]{:S(2)}, u32[]{:S(2)}) collective-permute-start(bf16[128,768]{1,0:T(8,128)(2,1)S(1)} %get-tuple-element.175), channel_id=1, source_target_pairs={{0,1},{1,0},{2,3},{3,2},{4,5},{5,4},{6,7},{7,6},{8,9},{9,8},{10,11... | collective-permute-start | bytes 589832 | tf_op jit(solution)/shard_map/ppermute | solution.py:610
  3.1 10.4 %collective-permute-start.1 = (bf16[128,768]{1,0:T(8,128)(2,1)S(1)}, bf16[128,768]{1,0:T(8,128)(2,1)S(1)}, u32[]{:S(2)}, u32[]{:S(2)}) collective-permute-start(bf16[128,768]{1,0:T(8,128)(2,1)S(1)} %get-tuple-element.176), channel_id=1, source_target_pairs={{0,2},{1,3},{2,0},{3,1},{4,6},{5,7},{6,4},{7,5},{8,10},{9,11},{10,... | collective-permute-start | bytes 589832 | tf_op jit(solution)/shard_map/ppermute | solution.py:610
  5.7 9.4 %collective-permute-start.2 = (bf16[128,768]{1,0:T(8,128)(2,1)S(1)}, bf16[128,768]{1,0:T(8,128)(2,1)S(1)}, u32[]{:S(2)}, u32[]{:S(2)}) collective-permute-start(bf16[128,768]{1,0:T(8,128)(2,1)S(1)} %get-tuple-element.177), channel_id=1, source_target_pairs={{0,3},{1,2},{2,1},{3,0},{4,7},{5,6},{6,5},{7,4},{8,11},{9,10},{10,... | collective-permute-start | bytes 589832 | tf_op jit(solution)/shard_map/ppermute | solution.py:610
  7.6 18.5 %collective-permute-start.3 = (bf16[128,768]{1,0:T(8,128)(2,1)S(1)}, bf16[128,768]{1,0:T(8,128)(2,1)S(1)}, u32[]{:S(2)}, u32[]{:S(2)}) collective-permute-start(bf16[128,768]{1,0:T(8,128)(2,1)S(1)} %get-tuple-element.186), channel_id=1, source_target_pairs={{0,1},{1,0},{2,3},{3,2},{4,5},{5,4},{6,7},{7,6},{8,9},{9,8},{10,11... | collective-permute-start | bytes 589832 | tf_op jit(solution)/shard_map/ppermute | solution.py:610
  7.8 18.3 %collective-permute-start.4 = (bf16[128,768]{1,0:T(8,128)(2,1)S(1)}, bf16[128,768]{1,0:T(8,128)(2,1)S(1)}, u32[]{:S(2)}, u32[]{:S(2)}) collective-permute-start(bf16[128,768]{1,0:T(8,128)(2,1)S(1)} %get-tuple-element.187), channel_id=1, source_target_pairs={{0,2},{1,3},{2,0},{3,1},{4,6},{5,7},{6,4},{7,5},{8,10},{9,11},{10,... | collective-permute-start | bytes 589832 | tf_op jit(solution)/shard_map/ppermute | solution.py:610
  11.1 4.1 %copy-start.14 = (bf16[768]{0:T(1024)(128)(2,1)S(1)}, bf16[768]{0:T(1024)(128)(2,1)}, u32[]{:S(2)}) copy-start(bf16[768]{0:T(1024)(128)(2,1)} %refs_10_.1) | copy-start | bytes 4612
  11.1 4.1 %copy-start.15 = (bf16[768]{0:T(1024)(128)(2,1)S(1)}, bf16[768]{0:T(1024)(128)(2,1)}, u32[]{:S(2)}) copy-start(bf16[768]{0:T(1024)(128)(2,1)} %refs_11_.1) | copy-start | bytes 4612
  11.1 4.1 %copy-start.16 = (bf16[768]{0:T(1024)(128)(2,1)S(1)}, bf16[768]{0:T(1024)(128)(2,1)}, u32[]{:S(2)}) copy-start(bf16[768]{0:T(1024)(128)(2,1)} %refs_12_.1) | copy-start | bytes 4612
  11.2 15.0 %slice-start.3 = ((s8[4718592]{0:T(1024)(128)(4,1)}), s8[4194304]{0:T(1024)(128)(4,1)S(1)}, s32[]{:S(2)}) async-start(s8[4718592]{0:T(1024)(128)(4,1)} %bitcast.30), calls=%async_computation.3 | async-start | bytes 8388608
  13.5 12.6 %collective-permute-start.5 = (bf16[128,768]{1,0:T(8,128)(2,1)S(1)}, bf16[128,768]{1,0:T(8,128)(2,1)S(1)}, u32[]{:S(2)}, u32[]{:S(2)}) collective-permute-start(bf16[128,768]{1,0:T(8,128)(2,1)S(1)} %get-tuple-element.188), channel_id=1, source_target_pairs={{0,3},{1,2},{2,1},{3,0},{4,7},{5,6},{6,5},{7,4},{8,11},{9,10},{10,... | collective-permute-start | bytes 589832 | tf_op jit(solution)/shard_map/ppermute | solution.py:610
  15.2 11.0 %copy-start.11 = (bf16[768]{0:T(1024)(128)(2,1)S(1)}, bf16[768]{0:T(1024)(128)(2,1)}, u32[]{:S(2)}) copy-start(bf16[768]{0:T(1024)(128)(2,1)} %refs_6_.6) | copy-start | bytes 4612
  15.2 11.0 %copy-start.12 = (bf16[768]{0:T(1024)(128)(2,1)S(1)}, bf16[768]{0:T(1024)(128)(2,1)}, u32[]{:S(2)}) copy-start(bf16[768]{0:T(1024)(128)(2,1)} %refs_6_.5) | copy-start | bytes 4612
  15.2 11.0 %copy-start.13 = (bf16[3072]{0:T(1024)(128)(2,1)S(1)}, bf16[3072]{0:T(1024)(128)(2,1)}, u32[]{:S(2)}) copy-start(bf16[3072]{0:T(1024)(128)(2,1)} %refs_8_.1) | copy-start | bytes 18436
  15.2 10.9 %copy-start.17 = (bf16[768]{0:T(1024)(128)(2,1)S(1)}, bf16[768]{0:T(1024)(128)(2,1)}, u32[]{:S(2)}) copy-start(bf16[768]{0:T(1024)(128)(2,1)} %refs_4_.2) | copy-start | bytes 4612
  15.2 10.9 %copy-start.18 = (bf16[768]{0:T(1024)(128)(2,1)S(1)}, bf16[768]{0:T(1024)(128)(2,1)}, u32[]{:S(2)}) copy-start(bf16[768]{0:T(1024)(128)(2,1)} %refs_5_.3) | copy-start | bytes 4612
  15.3 10.9 %copy-start.19 = (bf16[768]{0:T(1024)(128)(2,1)S(1)}, bf16[768]{0:T(1024)(128)(2,1)}, u32[]{:S(2)}) copy-start(bf16[768]{0:T(1024)(128)(2,1)} %refs_6_.4) | copy-start | bytes 4612
  26.1 14.4 %slice-start = ((s8[4718592]{0:T(1024)(128)(4,1)}), s8[4194304]{0:T(1024)(128)(4,1)S(1)}, s32[]{:S(2)}) async-start(s8[4718592]{0:T(1024)(128)(4,1)} %bitcast.28), calls=%async_computation | async-start | bytes 8388608
  26.2 14.3 %slice-start.1 = ((s8[4718592]{0:T(1024)(128)(4,1)}), s8[524288]{0:T(1024)(128)(4,1)S(1)}, s32[]{:S(2)}) async-start(s8[4718592]{0:T(1024)(128)(4,1)} %bitcast.28), calls=%async_computation.1 | async-start | bytes 1048576
  40.2 6.7 %collective-permute-start.6 = (bf16[2,8,48,1536]{3,2,1,0:T(8,128)(2,1)S(1)}, bf16[2,8,48,1536]{3,2,1,0:T(8,128)(2,1)S(1)}, u32[]{:S(2)}, u32[]{:S(2)}) collective-permute-start(bf16[2,8,48,1536]{3,2,1,0:T(8,128)(2,1)S(1)} %get-tuple-element.203), channel_id=1, source_target_pairs={{0,1},{1,0},{2,3},{3,2},{4,5},{5,4},{6,7},{7,6},{8,9},{9,8},{10,11... | collective-permute-start | bytes 7077896 | tf_op jit(solution)/shard_map/ppermute | solution.py:677
  46.6 12.8 %collective-permute-start.7 = (bf16[2,8,192,384]{3,2,1,0:T(8,128)(2,1)S(1)}, bf16[2,8,192,384]{3,2,1,0:T(8,128)(2,1)S(1)}, u32[]{:S(2)}, u32[]{:S(2)}) collective-permute-start(bf16[2,8,192,384]{3,2,1,0:T(8,128)(2,1)S(1)} %get-tuple-element.210), channel_id=1, source_target_pairs={{0,1},{1,0},{2,3},{3,2},{4,5},{5,4},{6,7},{7,6},{8,9},{9,8},{10,11... | collective-permute-start | bytes 7077896 | tf_op jit(solution)/shard_map/ppermute | solution.py:677
  46.9 5.6 %copy-start.3 = (bf16[768,768]{1,0:T(8,128)(2,1)S(1)}, bf16[768,768]{1,0:T(8,128)(2,1)}, u32[]{:S(2)}) copy-start(bf16[768,768]{1,0:T(8,128)(2,1)} %refs_7_.5) | copy-start | bytes 3538948
  46.9 5.6 %copy-start.4 = (f32[512,768]{1,0:T(8,128)S(1)}, f32[512,768]{1,0:T(8,128)}, u32[]{:S(2)}) copy-start(f32[512,768]{1,0:T(8,128)} %get-tuple-element.202.refs_8_) | copy-start | bytes 4718596
  46.9 5.6 %copy-start.9 = (f32[512,128]{1,0:T(8,128)S(1)}, f32[512,128]{1,0:T(8,128)}, u32[]{:S(2)}) copy-start(f32[512,128]{1,0:T(8,128)} %get-tuple-element.201.refs_5_) | copy-start | bytes 786436
  47.5 23.8 %collective-permute-start.10 = (bf16[2,2,2,48,512]{4,3,2,1,0:T(8,128)(2,1)S(1)}, bf16[2,2,2,48,512]{4,3,2,1,0:T(8,128)(2,1)S(1)}, u32[]{:S(2)}, u32[]{:S(2)}) collective-permute-start(bf16[2,2,2,48,512]{4,3,2,1,0:T(8,128)(2,1)S(1)} %get-tuple-element.230), channel_id=1, source_target_pairs={{0,8},{4,12},{8,0},{12,4},{16,24},{20,28},{24,16},{28,20},{1,9},{5... | collective-permute-start | bytes 1179656 | tf_op jit(solution)/shard_map/ppermute | solution.py:681
  49.5 21.9 %collective-permute-start.8 = (bf16[2,2,2,48,512]{4,3,2,1,0:T(8,128)(2,1)S(1)}, bf16[2,2,2,48,512]{4,3,2,1,0:T(8,128)(2,1)S(1)}, u32[]{:S(2)}, u32[]{:S(2)}) collective-permute-start(bf16[2,2,2,48,512]{4,3,2,1,0:T(8,128)(2,1)S(1)} %get-tuple-element.228), channel_id=1, source_target_pairs={{0,4},{4,0},{8,12},{12,8},{16,20},{20,16},{24,28},{28,24},{1,5},{5... | collective-permute-start | bytes 1179656 | tf_op jit(solution)/shard_map/ppermute | solution.py:681
  51.0 20.4 %collective-permute-start.9 = (bf16[2,2,2,48,512]{4,3,2,1,0:T(8,128)(2,1)S(1)}, bf16[2,2,2,48,512]{4,3,2,1,0:T(8,128)(2,1)S(1)}, u32[]{:S(2)}, u32[]{:S(2)}) collective-permute-start(bf16[2,2,2,48,512]{4,3,2,1,0:T(8,128)(2,1)S(1)} %get-tuple-element.229), channel_id=1, source_target_pairs={{0,2},{1,3},{2,0},{3,1},{4,6},{5,7},{6,4},{7,5},{8,10},{9,11},{10,... | collective-permute-start | bytes 1179656 | tf_op jit(solution)/shard_map/ppermute | solution.py:678
  59.5 1.8 %copy-start.5 = (bf16[512,768]{1,0:T(8,128)(2,1)S(1)}, bf16[512,768]{1,0:T(8,128)(2,1)}, u32[]{:S(2)}) copy-start(bf16[512,768]{1,0:T(8,128)(2,1)} %get-tuple-element.194.refs_0_) | copy-start | bytes 2359300
  59.5 1.8 %copy-start.6 = (bf16[512,768]{1,0:T(8,128)(2,1)S(1)}, bf16[512,768]{1,0:T(8,128)(2,1)}, u32[]{:S(2)}) copy-start(bf16[512,768]{1,0:T(8,128)(2,1)} %get-tuple-element.195.refs_1_) | copy-start | bytes 2359300
  59.5 1.8 %copy-start.7 = (bf16[512,768]{1,0:T(8,128)(2,1)S(1)}, bf16[512,768]{1,0:T(8,128)(2,1)}, u32[]{:S(2)}) copy-start(bf16[512,768]{1,0:T(8,128)(2,1)} %get-tuple-element.196.refs_2_) | copy-start | bytes 2359300
  60.2 17.5 %collective-permute-start.15 = (bf16[2,2,2,96,384]{4,3,2,1,0:T(8,128)(2,1)S(1)}, bf16[2,2,2,96,384]{4,3,2,1,0:T(8,128)(2,1)S(1)}, u32[]{:S(2)}, u32[]{:S(2)}) collective-permute-start(bf16[2,2,2,96,384]{4,3,2,1,0:T(8,128)(2,1)S(1)} %get-tuple-element.245), channel_id=1, source_target_pairs={{0,4},{4,0},{8,12},{12,8},{16,20},{20,16},{24,28},{28,24},{1,5},{5... | collective-permute-start | bytes 1769480 | tf_op jit(solution)/shard_map/ppermute | solution.py:681
  60.8 17.4 %collective-permute-start.16 = (bf16[2,2,2,96,384]{4,3,2,1,0:T(8,128)(2,1)S(1)}, bf16[2,2,2,96,384]{4,3,2,1,0:T(8,128)(2,1)S(1)}, u32[]{:S(2)}, u32[]{:S(2)}) collective-permute-start(bf16[2,2,2,96,384]{4,3,2,1,0:T(8,128)(2,1)S(1)} %get-tuple-element.246), channel_id=1, source_target_pairs={{0,2},{1,3},{2,0},{3,1},{4,6},{5,7},{6,4},{7,5},{8,10},{9,11},{10,... | collective-permute-start | bytes 1769480 | tf_op jit(solution)/shard_map/ppermute | solution.py:678
  71.3 3.5 %copy-start.8 = (bf16[512,768]{1,0:T(8,128)(2,1)S(1)}, bf16[512,768]{1,0:T(8,128)(2,1)}, u32[]{:S(2)}) copy-start(bf16[512,768]{1,0:T(8,128)(2,1)} %get-tuple-element.221.refs_4_) | copy-start | bytes 2359300
  71.7 13.1 %collective-permute-start.14 = (bf16[2,2,96,512]{3,2,1,0:T(8,128)(2,1)S(1)}, bf16[2,2,96,512]{3,2,1,0:T(8,128)(2,1)S(1)}, u32[]{:S(2)}, u32[]{:S(2)}) collective-permute-start(bf16[2,2,96,512]{3,2,1,0:T(8,128)(2,1)S(1)} %get-tuple-element.241), channel_id=1, source_target_pairs={{0,4},{4,0},{8,12},{12,8},{16,20},{20,16},{24,28},{28,24},{1,5},{5... | collective-permute-start | bytes 1179656 | tf_op jit(solution)/shard_map/ppermute | solution.py:681
  73.2 6.3 %collective-permute-start.13 = (bf16[2,2,48,512]{3,2,1,0:T(8,128)(2,1)S(1)}, bf16[2,2,48,512]{3,2,1,0:T(8,128)(2,1)S(1)}, u32[]{:S(2)}, u32[]{:S(2)}) collective-permute-start(bf16[2,2,48,512]{3,2,1,0:T(8,128)(2,1)S(1)} %get-tuple-element.240), channel_id=1, source_target_pairs={{0,2},{1,3},{2,0},{3,1},{4,6},{5,7},{6,4},{7,5},{8,10},{9,11},{10,... | collective-permute-start | bytes 589832 | tf_op jit(solution)/shard_map/ppermute | solution.py:678
  77.6 8.1 %collective-permute-start.12 = (bf16[2,8,112,384]{3,2,1,0:T(8,128)(2,1)S(1)}, bf16[2,8,112,384]{3,2,1,0:T(8,128)(2,1)S(1)}, u32[]{:S(2)}, u32[]{:S(2)}) collective-permute-start(bf16[2,8,112,384]{3,2,1,0:T(8,128)(2,1)S(1)} %get-tuple-element.237), channel_id=1, source_target_pairs={{0,1},{1,0},{2,3},{3,2},{4,5},{5,4},{6,7},{7,6},{8,9},{9,8},{10,11... | collective-permute-start | bytes 4128776 | tf_op jit(solution)/shard_map/ppermute | solution.py:677
  77.6 7.7 %collective-permute-start.11 = (bf16[2,8,96,384]{3,2,1,0:T(8,128)(2,1)S(1)}, bf16[2,8,96,384]{3,2,1,0:T(8,128)(2,1)S(1)}, u32[]{:S(2)}, u32[]{:S(2)}) collective-permute-start(bf16[2,8,96,384]{3,2,1,0:T(8,128)(2,1)S(1)} %get-tuple-element.236), channel_id=1, source_target_pairs={{0,1},{1,0},{2,3},{3,2},{4,5},{5,4},{6,7},{7,6},{8,9},{9,8},{10,11... | collective-permute-start | bytes 3538952 | tf_op jit(solution)/shard_map/ppermute | solution.py:677
  78.5 15.5 %collective-permute-start.22 = (bf16[2,2,96,384]{3,2,1,0:T(8,128)(2,1)S(1)}, bf16[2,2,96,384]{3,2,1,0:T(8,128)(2,1)S(1)}, u32[]{:S(2)}, u32[]{:S(2)}) collective-permute-start(bf16[2,2,96,384]{3,2,1,0:T(8,128)(2,1)S(1)} %get-tuple-element.267), channel_id=1, source_target_pairs={{0,2},{1,3},{2,0},{3,1},{4,6},{5,7},{6,4},{7,5},{8,10},{9,11},{10,... | collective-permute-start | bytes 884744 | tf_op jit(solution)/shard_map/ppermute | solution.py:678
  79.6 14.4 %collective-permute-start.23 = (bf16[2,2,96,384]{3,2,1,0:T(8,128)(2,1)S(1)}, bf16[2,2,96,384]{3,2,1,0:T(8,128)(2,1)S(1)}, u32[]{:S(2)}, u32[]{:S(2)}) collective-permute-start(bf16[2,2,96,384]{3,2,1,0:T(8,128)(2,1)S(1)} %get-tuple-element.268), channel_id=1, source_target_pairs={{0,4},{4,0},{8,12},{12,8},{16,20},{20,16},{24,28},{28,24},{1,5},{5... | collective-permute-start | bytes 884744 | tf_op jit(solution)/shard_map/ppermute | solution.py:681
  84.9 9.0 %collective-permute-start.24 = (bf16[2,96,512]{2,1,0:T(8,128)(2,1)S(1)}, bf16[2,96,512]{2,1,0:T(8,128)(2,1)S(1)}, u32[]{:S(2)}, u32[]{:S(2)}) collective-permute-start(bf16[2,96,512]{2,1,0:T(8,128)(2,1)S(1)} %get-tuple-element.271), channel_id=1, source_target_pairs={{0,8},{4,12},{8,0},{12,4},{16,24},{20,28},{24,16},{28,20},{1,9},{5... | collective-permute-start | bytes 589832 | tf_op jit(solution)/shard_map/ppermute | solution.py:681
  85.4 5.7 %collective-permute-start.25 = (bf16[2,48,512]{2,1,0:T(8,128)(2,1)S(1)}, bf16[2,48,512]{2,1,0:T(8,128)(2,1)S(1)}, u32[]{:S(2)}, u32[]{:S(2)}) collective-permute-start(bf16[2,48,512]{2,1,0:T(8,128)(2,1)S(1)} %get-tuple-element.272), channel_id=1, source_target_pairs={{0,2},{1,3},{2,0},{3,1},{4,6},{5,7},{6,4},{7,5},{8,10},{9,11},{10,... | collective-permute-start | bytes 294920 | tf_op jit(solution)/shard_map/ppermute | solution.py:678
  85.7 6.0 %copy-start = (bf16[768,768]{1,0:T(8,128)(2,1)S(1)}, bf16[768,768]{1,0:T(8,128)(2,1)}, u32[]{:S(2)}) copy-start(bf16[768,768]{1,0:T(8,128)(2,1)} %refs_4_.3) | copy-start | bytes 3538948
  85.7 6.0 %copy-start.1 = (bf16[768,768]{1,0:T(8,128)(2,1)S(1)}, bf16[768,768]{1,0:T(8,128)(2,1)}, u32[]{:S(2)}) copy-start(bf16[768,768]{1,0:T(8,128)(2,1)} %refs_5_.5) | copy-start | bytes 3538948
  85.7 6.0 %copy-start.2 = (bf16[768,768]{1,0:T(8,128)(2,1)S(1)}, bf16[768,768]{1,0:T(8,128)(2,1)}, u32[]{:S(2)}) copy-start(bf16[768,768]{1,0:T(8,128)(2,1)} %refs_6_.7) | copy-start | bytes 3538948
  86.3 18.1 %collective-permute-start.21 = (bf16[2,2,2,112,384]{4,3,2,1,0:T(8,128)(2,1)S(1)}, bf16[2,2,2,112,384]{4,3,2,1,0:T(8,128)(2,1)S(1)}, u32[]{:S(2)}, u32[]{:S(2)}) collective-permute-start(bf16[2,2,2,112,384]{4,3,2,1,0:T(8,128)(2,1)S(1)} %get-tuple-element.264), channel_id=1, source_target_pairs={{0,2},{1,3},{2,0},{3,1},{4,6},{5,7},{6,4},{7,5},{8,10},{9,11},{10,... | collective-permute-start | bytes 2064392 | tf_op jit(solution)/shard_map/ppermute | solution.py:678
  91.1 12.8 %collective-permute-start.20 = (bf16[2,2,2,96,384]{4,3,2,1,0:T(8,128)(2,1)S(1)}, bf16[2,2,2,96,384]{4,3,2,1,0:T(8,128)(2,1)S(1)}, u32[]{:S(2)}, u32[]{:S(2)}) collective-permute-start(bf16[2,2,2,96,384]{4,3,2,1,0:T(8,128)(2,1)S(1)} %get-tuple-element.263), channel_id=1, source_target_pairs={{0,4},{4,0},{8,12},{12,8},{16,20},{20,16},{24,28},{28,24},{1,5},{5... | collective-permute-start | bytes 1769480 | tf_op jit(solution)/shard_map/ppermute | solution.py:681
  94.1 11.7 %collective-permute-start.29 = (bf16[2,192,384]{2,1,0:T(8,128)(2,1)S(1)}, bf16[2,192,384]{2,1,0:T(8,128)(2,1)S(1)}, u32[]{:S(2)}, u32[]{:S(2)}) collective-permute-start(bf16[2,192,384]{2,1,0:T(8,128)(2,1)S(1)} %get-tuple-element.285), channel_id=1, source_target_pairs={{0,8},{4,12},{8,0},{12,4},{16,24},{20,28},{24,16},{28,20},{1,9},{5... | collective-permute-start | bytes 884744 | tf_op jit(solution)/shard_map/ppermute | solution.py:681
  95.8 10.1 %collective-permute-start.28 = (bf16[144,512]{1,0:T(8,128)(2,1)S(1)}, bf16[144,512]{1,0:T(8,128)(2,1)S(1)}, u32[]{:S(2)}, u32[]{:S(2)}) collective-permute-start(bf16[144,512]{1,0:T(8,128)(2,1)S(1)} %get-tuple-element.283), channel_id=1, source_target_pairs={{0,16},{4,20},{8,24},{12,28},{16,0},{20,4},{24,8},{28,12},{1,17},{... | collective-permute-start | bytes 442376 | tf_op jit(solution)/shard_map/ppermute | solution.py:681
  104.7 11.6 %collective-permute-start.27 = (bf16[2,2,112,384]{3,2,1,0:T(8,128)(2,1)S(1)}, bf16[2,2,112,384]{3,2,1,0:T(8,128)(2,1)S(1)}, u32[]{:S(2)}, u32[]{:S(2)}) collective-permute-start(bf16[2,2,112,384]{3,2,1,0:T(8,128)(2,1)S(1)} %get-tuple-element.280), channel_id=1, source_target_pairs={{0,4},{4,0},{8,12},{12,8},{16,20},{20,16},{24,28},{28,24},{1,5},{5... | collective-permute-start | bytes 1032200 | tf_op jit(solution)/shard_map/ppermute | solution.py:681
  105.3 11.0 %collective-permute-start.26 = (bf16[2,2,96,384]{3,2,1,0:T(8,128)(2,1)S(1)}, bf16[2,2,96,384]{3,2,1,0:T(8,128)(2,1)S(1)}, u32[]{:S(2)}, u32[]{:S(2)}) collective-permute-start(bf16[2,2,96,384]{3,2,1,0:T(8,128)(2,1)S(1)} %get-tuple-element.279), channel_id=1, source_target_pairs={{0,2},{1,3},{2,0},{3,1},{4,6},{5,7},{6,4},{7,5},{8,10},{9,11},{10,... | collective-permute-start | bytes 884744 | tf_op jit(solution)/shard_map/ppermute | solution.py:678
  105.9 9.7 %collective-permute-start.30 = (bf16[144,512]{1,0:T(8,128)(2,1)S(1)}, bf16[144,512]{1,0:T(8,128)(2,1)S(1)}, u32[]{:S(2)}, u32[]{:S(2)}) collective-permute-start(bf16[144,512]{1,0:T(8,128)(2,1)S(1)} %get-tuple-element.290.refs_1_), channel_id=1, source_target_pairs={{0,2},{1,3},{2,0},{3,1},{4,6},{5,7},{6,4},{7,5},{8,10},{9,11},{10,... | collective-permute-start | bytes 442376 | tf_op jit(solution)/shard_map/ppermute | solution.py:678
  107.5 9.0 %collective-permute-start.32 = (bf16[192,384]{1,0:T(8,128)(2,1)S(1)}, bf16[192,384]{1,0:T(8,128)(2,1)S(1)}, u32[]{:S(2)}, u32[]{:S(2)}) collective-permute-start(bf16[192,384]{1,0:T(8,128)(2,1)S(1)} %get-tuple-element.296), channel_id=1, source_target_pairs={{0,16},{4,20},{8,24},{12,28},{16,0},{20,4},{24,8},{28,12},{1,17},{... | collective-permute-start | bytes 442376 | tf_op jit(solution)/shard_map/ppermute | solution.py:681
  116.4 7.5 %collective-permute-start.31 = (bf16[2,208,384]{2,1,0:T(8,128)(2,1)S(1)}, bf16[2,208,384]{2,1,0:T(8,128)(2,1)S(1)}, u32[]{:S(2)}, u32[]{:S(2)}) collective-permute-start(bf16[2,208,384]{2,1,0:T(8,128)(2,1)S(1)} %get-tuple-element.293), channel_id=1, source_target_pairs={{0,8},{4,12},{8,0},{12,4},{16,24},{20,28},{24,16},{28,20},{1,9},{5... | collective-permute-start | bytes 958472 | tf_op jit(solution)/shard_map/ppermute | solution.py:681
  116.6 6.8 %collective-permute-start.33 = (bf16[192,384]{1,0:T(8,128)(2,1)S(1)}, bf16[192,384]{1,0:T(8,128)(2,1)S(1)}, u32[]{:S(2)}, u32[]{:S(2)}) collective-permute-start(bf16[192,384]{1,0:T(8,128)(2,1)S(1)} %get-tuple-element.299.refs_1_), channel_id=1, source_target_pairs={{0,2},{1,3},{2,0},{3,1},{4,6},{5,7},{6,4},{7,5},{8,10},{9,11},{10,... | collective-permute-start | bytes 442376 | tf_op jit(solution)/shard_map/ppermute | solution.py:678
  116.9 7.2 %collective-permute-start.36 = (bf16[2,144,512]{2,1,0:T(8,128)(2,1)S(1)}, bf16[2,144,512]{2,1,0:T(8,128)(2,1)S(1)}, u32[]{:S(2)}, u32[]{:S(2)}) collective-permute-start(bf16[2,144,512]{2,1,0:T(8,128)(2,1)S(1)} %get-tuple-element.305.refs_1_), channel_id=1, source_target_pairs={{0,1},{1,0},{2,3},{3,2},{4,5},{5,4},{6,7},{7,6},{8,9},{9,8},{10,11... | collective-permute-start | bytes 884744 | tf_op jit(solution)/shard_map/ppermute | solution.py:677
  116.9 19.9 %collective-permute-start.17 = (bf16[272,768]{1,0:T(8,128)(2,1)S(1)}, bf16[272,768]{1,0:T(8,128)(2,1)S(1)}, u32[]{:S(2)}, u32[]{:S(2)}) collective-permute-start(bf16[272,768]{1,0:T(8,128)(2,1)S(1)} %get-tuple-element.260), channel_id=1, source_target_pairs={{0,1},{1,0},{2,3},{3,2},{4,5},{5,4},{6,7},{7,6},{8,9},{9,8},{10,11... | collective-permute-start | bytes 1253384 | tf_op jit(solution)/shard_map/ppermute | solution.py:826
  117.4 19.9 %collective-permute-start.18 = (bf16[272,768]{1,0:T(8,128)(2,1)S(1)}, bf16[272,768]{1,0:T(8,128)(2,1)S(1)}, u32[]{:S(2)}, u32[]{:S(2)}) collective-permute-start(bf16[272,768]{1,0:T(8,128)(2,1)S(1)} %get-tuple-element.261), channel_id=1, source_target_pairs={{0,2},{1,3},{2,0},{3,1},{4,6},{5,7},{6,4},{7,5},{8,10},{9,11},{10,... | collective-permute-start | bytes 1253384 | tf_op jit(solution)/shard_map/ppermute | solution.py:826
  123.4 14.8 %collective-permute-start.19 = (bf16[272,768]{1,0:T(8,128)(2,1)S(1)}, bf16[272,768]{1,0:T(8,128)(2,1)S(1)}, u32[]{:S(2)}, u32[]{:S(2)}) collective-permute-start(bf16[272,768]{1,0:T(8,128)(2,1)S(1)} %get-tuple-element.262), channel_id=1, source_target_pairs={{0,3},{1,2},{2,1},{3,0},{4,7},{5,6},{6,5},{7,4},{8,11},{9,10},{10,... | collective-permute-start | bytes 1253384 | tf_op jit(solution)/shard_map/ppermute | solution.py:826
  123.9 4.5 %collective-permute-start.35 = (bf16[2,192,384]{2,1,0:T(8,128)(2,1)S(1)}, bf16[2,192,384]{2,1,0:T(8,128)(2,1)S(1)}, u32[]{:S(2)}, u32[]{:S(2)}) collective-permute-start(bf16[2,192,384]{2,1,0:T(8,128)(2,1)S(1)} %get-tuple-element.304.refs_1_), channel_id=1, source_target_pairs={{0,1},{1,0},{2,3},{3,2},{4,5},{5,4},{6,7},{7,6},{8,9},{9,8},{10,11... | collective-permute-start | bytes 884744 | tf_op jit(solution)/shard_map/ppermute | solution.py:677
  124.1 10.9 %collective-permute-start.34 = (bf16[208,384]{1,0:T(8,128)(2,1)S(1)}, bf16[208,384]{1,0:T(8,128)(2,1)S(1)}, u32[]{:S(2)}, u32[]{:S(2)}) collective-permute-start(bf16[208,384]{1,0:T(8,128)(2,1)S(1)} %get-tuple-element.302), channel_id=1, source_target_pairs={{0,16},{4,20},{8,24},{12,28},{16,0},{20,4},{24,8},{28,12},{1,17},{... | collective-permute-start | bytes 479240 | tf_op jit(solution)/shard_map/ppermute | solution.py:681
  135.1 9.6 %collective-permute-start.37 = (bf16[208,384]{1,0:T(8,128)(2,1)S(1)}, bf16[208,384]{1,0:T(8,128)(2,1)S(1)}, u32[]{:S(2)}, u32[]{:S(2)}) collective-permute-start(bf16[208,384]{1,0:T(8,128)(2,1)S(1)} %get-tuple-element.313.refs_1_), channel_id=1, source_target_pairs={{0,2},{1,3},{2,0},{3,1},{4,6},{5,7},{6,4},{7,5},{8,10},{9,11},{10,... | collective-permute-start | bytes 479240 | tf_op jit(solution)/shard_map/ppermute | solution.py:678
  136.8 7.9 %collective-permute-start.38 = (bf16[208,384]{1,0:T(8,128)(2,1)S(1)}, bf16[208,384]{1,0:T(8,128)(2,1)S(1)}, u32[]{:S(2)}, u32[]{:S(2)}) collective-permute-start(bf16[208,384]{1,0:T(8,128)(2,1)S(1)} %get-tuple-element.313.refs_1_), channel_id=1, source_target_pairs={{0,1},{1,0},{2,3},{3,2},{4,5},{5,4},{6,7},{7,6},{8,9},{9,8},{10,11... | collective-permute-start | bytes 479240 | tf_op jit(solution)/shard_map/ppermute | solution.py:677
  136.8 7.9 %collective-permute-start.39 = (bf16[208,384]{1,0:T(8,128)(2,1)S(1)}, bf16[208,384]{1,0:T(8,128)(2,1)S(1)}, u32[]{:S(2)}, u32[]{:S(2)}) collective-permute-start(bf16[208,384]{1,0:T(8,128)(2,1)S(1)} %get-tuple-element.313.refs_1_), channel_id=1, source_target_pairs={{0,3},{1,2},{2,1},{3,0},{4,7},{5,6},{6,5},{7,4},{8,11},{9,10},{10,... | collective-permute-start | bytes 479240 | tf_op jit(solution)/shard_map/ppermute | solution.py:757
  (1 other events, 1.7 us)

commit v6 on v5

--- a/solution.py
+++ b/solution.py
@@ -384,7 +384,7 @@
         gvt[sl, :] = gvb.T
         return carry
 
-    lax.fori_loop(0, width // LANES, pair, 0, unroll=2)
+    lax.fori_loop(0, width // LANES, pair, 0, unroll=3)
     bq = jnp.sum(gq[...].astype(F32), axis=0, keepdims=True)
     bv = jnp.sum(gv[...].astype(F32), axis=0, keepdims=True)
     vec_out[...] = jnp.concatenate([bq, bv, jnp.zeros((6, width), F32)], axis=0)

time: 148 us -> 147 us (level)
  no operation moved by 1% of the time
where the time goes in v6:
time: 147 us; the launch traced here: 146 us
  Pallas kernels  69.7 us (47%)
  starting transfers between devices  37.8 us (26%)
  waiting for transfers between devices  35.4 us (24%)
  between operations  1.57 us (1%)
  other arithmetic  1.5 us (1%)
    pallas_call x32, Pallas kernels, call(): pl.pallas_call(body, out_shape=[*outs, shape((8, LANES), F32)], in_specs=...  69.7 us
    ppermute x10, waiting for transfers between devices, local(): pp_y = lambda a: lax.ppermute(a, 'seq', xor[2])  18.5 us
    ppermute x13, starting transfers between devices, pp_dp(): return lambda a: lax.ppermute(a, 'dp', [(i, i ^ bit) for i in range(n_dp)])  17.9 us
    ppermute x13, waiting for transfers between devices, pp_dp(): return lambda a: lax.ppermute(a, 'dp', [(i, i ^ bit) for i in range(n_dp)])  14.4 us
    ppermute x10, starting transfers between devices, local(): pp_y = lambda a: lax.ppermute(a, 'seq', xor[2])  10.4 us
    ppermute x6, starting transfers between devices, rel(): lax.ppermute(parts[r], 'seq', xor[r])  5.39 us
  transfers between devices with their start and end apart: 40, of which 11 were waited for; matrix products, arithmetic and copies ran while one was open for 1% of the time, Pallas kernels for 36%

profile of v6, /device:TPU:0, one launch (start us, length us, event | category | flops | bytes accessed | tf_op | source)
XLA Modules:
  0.0 146.2 jit_solution(14329347898021364715)
XLA Ops:
  0.8 1.8 %split_tokens.1 = (bf16[128,768]{1,0:T(8,128)(2,1)S(1)}, bf16[128,768]{1,0:T(8,128)(2,1)S(1)}, bf16[128,768]{1,0:T(8,128)(2,1)S(1)}, bf16[128,768]{1,0:T(8,128)(2,1)S(1)}, f32[8,128]{1,0:T(8,128)S(1)}) custom-call(s32[16]{0:T(128)S(1)} %concatenate.9.refs_0_, bf16[4,128,768]{2,1,0:T(8,128)(2,1)} %refs_1_.3), custom_call_target="tpu_custom_call" | custom-call | flops 1 | bytes 1 | tf_op jit(solution)/shard_map/split_tokens/pallas_call | solution.py:489
  2.6 0.5 collective-permute-start
  3.1 2.6 %collective-permute-start.1 = (bf16[128,768]{1,0:T(8,128)(2,1)S(1)}, bf16[128,768]{1,0:T(8,128)(2,1)S(1)}, u32[]{:S(2)}, u32[]{:S(2)}) collective-permute-start(bf16[128,768]{1,0:T(8,128)(2,1)S(1)} %get-tuple-element.176), channel_id=1, source_target_pairs={{0,2},{1,3},{2,0},{3,1},{4,6},{5,7},{6,4},{7,5},{8,10},{9,11},{10,... | collective-permute-start | bytes 589832 | tf_op jit(solution)/shard_map/ppermute | solution.py:610
  5.8 1.8 %split_grads.1 = (bf16[128,768]{1,0:T(8,128)(2,1)S(1)}, bf16[128,768]{1,0:T(8,128)(2,1)S(1)}, bf16[128,768]{1,0:T(8,128)(2,1)S(1)}, bf16[128,768]{1,0:T(8,128)(2,1)S(1)}, f32[8,128]{1,0:T(8,128)S(1)}) custom-call(s32[16]{0:T(128)S(1)} %concatenate.9.refs_0_, bf16[4,128,768]{2,1,0:T(8,128)(2,1)} %refs_1_.4, f32[8,128]{1,0:T(8,128)S(1)} %get-tuple-element.178.refs_2_), custom_call_target="tpu_custom_call" | custom-call | flops 1 | bytes 1 | tf_op jit(solution)/shard_map/split_grads/pallas_call | solution.py:489
  7.8 1.9 %collective-permute-start.4 = (bf16[128,768]{1,0:T(8,128)(2,1)S(1)}, bf16[128,768]{1,0:T(8,128)(2,1)S(1)}, u32[]{:S(2)}, u32[]{:S(2)}) collective-permute-start(bf16[128,768]{1,0:T(8,128)(2,1)S(1)} %get-tuple-element.187), channel_id=1, source_target_pairs={{0,2},{1,3},{2,0},{3,1},{4,6},{5,7},{6,4},{7,5},{8,10},{9,11},{10,... | collective-permute-start | bytes 589832 | tf_op jit(solution)/shard_map/ppermute | solution.py:610
  10.3 0.8 subtract_convert_fusion
  11.2 2.2 %fetch.1 = (bf16[768,768]{1,0:T(8,128)(2,1)S(1)}, bf16[768,768]{1,0:T(8,128)(2,1)S(1)}, bf16[768,768]{1,0:T(8,128)(2,1)S(1)}, f32[8,128]{1,0:T(8,128)S(1)}) custom-call(bf16[768,768]{1,0:T(8,128)(2,1)} %refs_4_.3, bf16[768,768]{1,0:T(8,128)(2,1)} %refs_5_.5, bf16[768,768]{1,0:T(8,128)(2,1)} %refs_6_.7, f32[8,128]{1,0:T(8,128)S(1)} %get-tuple-element.179.refs_3_), custom_call_target="tpu_custom_call" | custom-call | flops 1 | bytes 1 | tf_op jit(solution)/shard_map/fetch/pallas_call | solution.py:489
  13.6 1.6 %collective-permute-done.2.refs_3_ = bf16[128,768]{1,0:T(8,128)(2,1)S(1)} collective-permute-done((bf16[128,768]{1,0:T(8,128)(2,1)S(1)}, bf16[128,768]{1,0:T(8,128)(2,1)S(1)}, u32[]{:S(2)}, u32[]{:S(2)}) %collective-permute-start.2) | collective-permute-done | bytes 196640 | tf_op jit(solution)/shard_map/ppermute | solution.py:610
  15.3 10.8 %attend.1 = (bf16[512,768]{1,0:T(8,128)(2,1)}, bf16[512,768]{1,0:T(8,128)(2,1)}, bf16[512,768]{1,0:T(8,128)(2,1)}, bf16[512,768]{1,0:T(8,128)(2,1)}, f32[512,768...) custom-call(bf16[128,768]{1,0:T(8,128)(2,1)S(1)} %get-tuple-element., ...), custom_call_target="tpu_custom_call" | custom-call | flops 1 | bytes 1 | tf_op jit(solution)/shard_map/attend/pallas_call | solution.py:489
  26.2 13.9 %ffn.1 = (bf16[128,768]{1,0:T(8,128)(2,1)S(1)}, bf16[128,768]{1,0:T(8,128)(2,1)S(1)}, bf16[128,768]{1,0:T(8,128)(2,1)S(1)}, bf16[128,768]{1,0:T(8,128)(2,1)S(1)}...) custom-call(s32[16]{0:T(128)S(1)} %concatenate.9.refs_0_, ...), custom_call_target="tpu_custom_call" | custom-call | flops 1 | bytes 1 | tf_op jit(solution)/shard_map/ffn/pallas_call | solution.py:489
  40.2 0.4 collective-permute-start.6
  40.6 6.1 %ffn_back.1 = (bf16[2,8,192,384]{3,2,1,0:T(8,128)(2,1)S(1)}, bf16[2,8,192,384]{3,2,1,0:T(8,128)(2,1)S(1)}, f32[8,3072]{1,0:T(8,128)S(1)}, bf16[512,3072]{1,0:T(8,128)(2,1)S(1)}, f32[8,128]{1,0:T(8,128)S(1)}) custom-call(s32[16]{0:T(128)S(1)} %concatenate.9.refs_0_, f32[512,768]{1,0:T(8,128)S(1)} %get-tuple-element.197.refs_1_, ...), custom_call_target="tpu_custom_call" | custom-call | flops 1 | bytes 1 | tf_op jit(solution)/shard_map/ffn_back/pallas_call | solution.py:489
  46.6 0.3 collective-permute-start.7
  46.9 0.6 down_one.1
  47.5 1.9 %collective-permute-start.10 = (bf16[2,2,2,48,512]{4,3,2,1,0:T(8,128)(2,1)S(1)}, bf16[2,2,2,48,512]{4,3,2,1,0:T(8,128)(2,1)S(1)}, u32[]{:S(2)}, u32[]{:S(2)}) collective-permute-start(bf16[2,2,2,48,512]{4,3,2,1,0:T(8,128)(2,1)S(1)} %get-tuple-element.230), channel_id=1, source_target_pairs={{0,8},{4,12},{8,0},{12,4},{16,24},{20,28},{24,16},{28,20},{1,9},{5... | collective-permute-start | bytes 1179656 | tf_op jit(solution)/shard_map/ppermute | solution.py:681
  49.5 1.5 %collective-permute-start.8 = (bf16[2,2,2,48,512]{4,3,2,1,0:T(8,128)(2,1)S(1)}, bf16[2,2,2,48,512]{4,3,2,1,0:T(8,128)(2,1)S(1)}, u32[]{:S(2)}, u32[]{:S(2)}) collective-permute-start(bf16[2,2,2,48,512]{4,3,2,1,0:T(8,128)(2,1)S(1)} %get-tuple-element.228), channel_id=1, source_target_pairs={{0,4},{4,0},{8,12},{12,8},{16,20},{20,16},{24,28},{28,24},{1,5},{5... | collective-permute-start | bytes 1179656 | tf_op jit(solution)/shard_map/ppermute | solution.py:681
  51.0 1.5 %collective-permute-start.9 = (bf16[2,2,2,48,512]{4,3,2,1,0:T(8,128)(2,1)S(1)}, bf16[2,2,2,48,512]{4,3,2,1,0:T(8,128)(2,1)S(1)}, u32[]{:S(2)}, u32[]{:S(2)}) collective-permute-start(bf16[2,2,2,48,512]{4,3,2,1,0:T(8,128)(2,1)S(1)} %get-tuple-element.229), channel_id=1, source_target_pairs={{0,2},{1,3},{2,0},{3,1},{4,6},{5,7},{6,4},{7,5},{8,10},{9,11},{10,... | collective-permute-start | bytes 1179656 | tf_op jit(solution)/shard_map/ppermute | solution.py:678
  52.5 7.0 %norm_back.1 = (f32[512,768]{1,0:T(8,128)S(1)}, bf16[512,768]{1,0:T(8,128)(2,1)S(1)}, bf16[512,128]{1,0:T(8,128)(2,1)S(1)}, f32[8,768]{1,0:T(8,128)S(1)}, bf16[2...) custom-call(s32[16]{0:T(128)S(1)} %concatenate.9.refs_0_, ...), custom_call_target="tpu_custom_call" | custom-call | flops 1 | bytes 1 | tf_op jit(solution)/shard_map/norm_back/pallas_call | solution.py:489
  59.5 0.6 up_one.1
  60.2 0.6 collective-permute-start.15
  60.8 0.5 collective-permute-start.16
  61.3 9.9 %attend_back.1 = (bf16[512,768]{1,0:T(8,128)(2,1)S(1)}, bf16[512,768]{1,0:T(8,128)(2,1)S(1)}, bf16[512,768]{1,0:T(8,128)(2,1)S(1)}, bf16[768,512]{1,0:T(8,128)(2...) custom-call(bf16[512,768]{1,0:T(8,128)(2,1)S(1)} %copy-done.5, ...), custom_call_target="tpu_custom_call" | custom-call | flops 1 | bytes 1 | tf_op jit(solution)/shard_map/attend_back/pallas_call | solution.py:489
  71.2 0.3 down_two.1
  71.5 1.6 %collective-permute-start.14 = (bf16[2,2,96,512]{3,2,1,0:T(8,128)(2,1)S(1)}, bf16[2,2,96,512]{3,2,1,0:T(8,128)(2,1)S(1)}, u32[]{:S(2)}, u32[]{:S(2)}) collective-permute-start(bf16[2,2,96,512]{3,2,1,0:T(8,128)(2,1)S(1)} %get-tuple-element.241), channel_id=1, source_target_pairs={{0,4},{4,0},{8,12},{12,8},{16,20},{20,16},{24,28},{28,24},{1,5},{5... | collective-permute-start | bytes 1179656 | tf_op jit(solution)/shard_map/ppermute | solution.py:681
  73.0 1.6 %collective-permute-start.13 = (bf16[2,2,48,512]{3,2,1,0:T(8,128)(2,1)S(1)}, bf16[2,2,48,512]{3,2,1,0:T(8,128)(2,1)S(1)}, u32[]{:S(2)}, u32[]{:S(2)}) collective-permute-start(bf16[2,2,48,512]{3,2,1,0:T(8,128)(2,1)S(1)} %get-tuple-element.240), channel_id=1, source_target_pairs={{0,2},{1,3},{2,0},{3,1},{4,6},{5,7},{6,4},{7,5},{8,10},{9,11},{10,... | collective-permute-start | bytes 589832 | tf_op jit(solution)/shard_map/ppermute | solution.py:678
  74.6 2.7 %weights_back.1 = (bf16[2,8,96,384]{3,2,1,0:T(8,128)(2,1)S(1)}, bf16[2,8,112,384]{3,2,1,0:T(8,128)(2,1)S(1)}, bf16[2,8,96,384]{3,2,1,0:T(8,128)(2,1)S(1)}, bf16[...) custom-call(s32[16]{0:T(128)S(1)} %concatenate.9.refs_0_, bf16[768,512]{1,0:T(8,128)(2,1)S(1)} %get-tuple-element.218.refs_1_, ...), custom_call_target="tpu_custom_call" | custom-call | flops 1 | bytes 1 | tf_op jit(solution)/shard_map/weights_back/pallas_call | solution.py:489
  77.4 0.5 collective-permute-start.11
  77.9 0.3 up_two.1
  78.3 0.6 collective-permute-start.22
  78.8 0.7 collective-permute-done.13.refs_0_
  79.6 1.5 %collective-permute-start.23 = (bf16[2,2,96,384]{3,2,1,0:T(8,128)(2,1)S(1)}, bf16[2,2,96,384]{3,2,1,0:T(8,128)(2,1)S(1)}, u32[]{:S(2)}, u32[]{:S(2)}) collective-permute-start(bf16[2,2,96,384]{3,2,1,0:T(8,128)(2,1)S(1)} %get-tuple-element.268), channel_id=1, source_target_pairs={{0,4},{4,0},{8,12},{12,8},{16,20},{20,16},{24,28},{28,24},{1,5},{5... | collective-permute-start | bytes 884744 | tf_op jit(solution)/shard_map/ppermute | solution.py:681
  81.1 3.8 %collective-permute-done.14.refs_1_ = bf16[2,2,96,512]{3,2,1,0:T(8,128)(2,1)S(1)} collective-permute-done((bf16[2,2,96,512]{3,2,1,0:T(8,128)(2,1)S(1)}, bf16[2,2,96,512]{3,2,1,0:T(8,128)(2,1)S(1)}, u32[]{:S(2)}, u32[]{:S(2)}) %collective-permute-start.14) | collective-permute-done | bytes 393248 | tf_op jit(solution)/shard_map/ppermute | solution.py:681
  85.0 0.5 collective-permute-start.24
  85.6 0.2 collective-permute-start.25
  85.8 0.6 qkv_one.1
  86.4 1.9 %collective-permute-start.21 = (bf16[2,2,2,112,384]{4,3,2,1,0:T(8,128)(2,1)S(1)}, bf16[2,2,2,112,384]{4,3,2,1,0:T(8,128)(2,1)S(1)}, u32[]{:S(2)}, u32[]{:S(2)}) collective-permute-start(bf16[2,2,2,112,384]{4,3,2,1,0:T(8,128)(2,1)S(1)} %get-tuple-element.264), channel_id=1, source_target_pairs={{0,2},{1,3},{2,0},{3,1},{4,6},{5,7},{6,4},{7,5},{8,10},{9,11},{10,... | collective-permute-start | bytes 2064392 | tf_op jit(solution)/shard_map/ppermute | solution.py:678
  88.3 3.0 %collective-permute-done.25.refs_1_ = bf16[2,48,512]{2,1,0:T(8,128)(2,1)S(1)} collective-permute-done((bf16[2,48,512]{2,1,0:T(8,128)(2,1)S(1)}, bf16[2,48,512]{2,1,0:T(8,128)(2,1)S(1)}, u32[]{:S(2)}, u32[]{:S(2)}) %collective-permute-start.25) | collective-permute-done | bytes 98336 | tf_op jit(solution)/shard_map/ppermute | solution.py:678
  91.5 2.1 %input_back.1 = (bf16[128,768]{1,0:T(8,128)(2,1)S(1)}, bf16[128,768]{1,0:T(8,128)(2,1)S(1)}, bf16[128,768]{1,0:T(8,128)(2,1)S(1)}, bf16[128,768]{1,0:T(8,128)(2,1)S(1)}, f32[8,128]{1,0:T(8,128)S(1)}) custom-call(bf16[512,768]{1,0:T(8,128)(2,1)S(1)} %get-tuple-element.214.refs_0_, bf16[512,768]{1,0:T(8,128)(2,1)S(1)} %get-tuple-element.215.refs_1_, ...), custom_call_target="tpu_custom_call" | custom-call | flops 1 | bytes 1 | tf_op jit(solution)/shard_map/input_back/pallas_call | solution.py:489
  93.9 1.6 %collective-permute-start.29 = (bf16[2,192,384]{2,1,0:T(8,128)(2,1)S(1)}, bf16[2,192,384]{2,1,0:T(8,128)(2,1)S(1)}, u32[]{:S(2)}, u32[]{:S(2)}) collective-permute-start(bf16[2,192,384]{2,1,0:T(8,128)(2,1)S(1)} %get-tuple-element.285), channel_id=1, source_target_pairs={{0,8},{4,12},{8,0},{12,4},{16,24},{20,28},{24,16},{28,20},{1,9},{5... | collective-permute-start | bytes 884744 | tf_op jit(solution)/shard_map/ppermute | solution.py:681
  95.6 2.6 %collective-permute-start.28 = (bf16[144,512]{1,0:T(8,128)(2,1)S(1)}, bf16[144,512]{1,0:T(8,128)(2,1)S(1)}, u32[]{:S(2)}, u32[]{:S(2)}) collective-permute-start(bf16[144,512]{1,0:T(8,128)(2,1)S(1)} %get-tuple-element.283), channel_id=1, source_target_pairs={{0,16},{4,20},{8,24},{12,28},{16,0},{20,4},{24,8},{28,12},{1,17},{... | collective-permute-start | bytes 442376 | tf_op jit(solution)/shard_map/ppermute | solution.py:681
  98.2 5.5 %collective-permute-done.20.refs_0_ = bf16[2,2,2,96,384]{4,3,2,1,0:T(8,128)(2,1)S(1)} collective-permute-done((bf16[2,2,2,96,384]{4,3,2,1,0:T(8,128)(2,1)S(1)}, bf16[2,2,2,96,384]{4,3,2,1,0:T(8,128)(2,1)S(1)}, u32[]{:S(2)}, u32[]{:S(2)}) %collective-permute-start.20) | collective-permute-done | bytes 589856 | tf_op jit(solution)/shard_map/ppermute | solution.py:681
  103.7 0.5 collective-permute-done.21.refs_1_
  104.2 0.3 qkv_two.1
  104.5 0.6 collective-permute-start.27
  105.1 0.5 collective-permute-start.26
  105.7 1.6 %collective-permute-start.30 = (bf16[144,512]{1,0:T(8,128)(2,1)S(1)}, bf16[144,512]{1,0:T(8,128)(2,1)S(1)}, u32[]{:S(2)}, u32[]{:S(2)}) collective-permute-start(bf16[144,512]{1,0:T(8,128)(2,1)S(1)} %get-tuple-element.290.refs_1_), channel_id=1, source_target_pairs={{0,2},{1,3},{2,0},{3,1},{4,6},{5,7},{6,4},{7,5},{8,10},{9,11},{10,... | collective-permute-start | bytes 442376 | tf_op jit(solution)/shard_map/ppermute | solution.py:678
  107.3 2.6 %collective-permute-start.32 = (bf16[192,384]{1,0:T(8,128)(2,1)S(1)}, bf16[192,384]{1,0:T(8,128)(2,1)S(1)}, u32[]{:S(2)}, u32[]{:S(2)}) collective-permute-start(bf16[192,384]{1,0:T(8,128)(2,1)S(1)} %get-tuple-element.296), channel_id=1, source_target_pairs={{0,16},{4,20},{8,24},{12,28},{16,0},{20,4},{24,8},{28,12},{1,17},{... | collective-permute-start | bytes 442376 | tf_op jit(solution)/shard_map/ppermute | solution.py:681
  109.9 5.5 %collective-permute-done.30.refs_2_ = bf16[144,512]{1,0:T(8,128)(2,1)S(1)} collective-permute-done((bf16[144,512]{1,0:T(8,128)(2,1)S(1)}, bf16[144,512]{1,0:T(8,128)(2,1)S(1)}, u32[]{:S(2)}, u32[]{:S(2)}) %collective-permute-start.30) | collective-permute-done | bytes 147488 | tf_op jit(solution)/shard_map/ppermute | solution.py:678
  115.4 0.6 down_six.1
  116.3 0.3 collective-permute-start.33
  116.6 0.5 collective-permute-start.17
  117.1 1.7 %collective-permute-start.18 = (bf16[272,768]{1,0:T(8,128)(2,1)S(1)}, bf16[272,768]{1,0:T(8,128)(2,1)S(1)}, u32[]{:S(2)}, u32[]{:S(2)}) collective-permute-start(bf16[272,768]{1,0:T(8,128)(2,1)S(1)} %get-tuple-element.261), channel_id=1, source_target_pairs={{0,2},{1,3},{2,0},{3,1},{4,6},{5,7},{6,4},{7,5},{8,10},{9,11},{10,... | collective-permute-start | bytes 1253384 | tf_op jit(solution)/shard_map/ppermute | solution.py:826
  118.9 4.2 %collective-permute-done.33.refs_2_ = bf16[192,384]{1,0:T(8,128)(2,1)S(1)} collective-permute-done((bf16[192,384]{1,0:T(8,128)(2,1)S(1)}, bf16[192,384]{1,0:T(8,128)(2,1)S(1)}, u32[]{:S(2)}, u32[]{:S(2)}) %collective-permute-start.33) | collective-permute-done | bytes 147488 | tf_op jit(solution)/shard_map/ppermute | solution.py:678
  123.1 0.6 up_six.1
  123.8 2.7 %collective-permute-start.34 = (bf16[208,384]{1,0:T(8,128)(2,1)S(1)}, bf16[208,384]{1,0:T(8,128)(2,1)S(1)}, u32[]{:S(2)}, u32[]{:S(2)}) collective-permute-start(bf16[208,384]{1,0:T(8,128)(2,1)S(1)} %get-tuple-element.302), channel_id=1, source_target_pairs={{0,16},{4,20},{8,24},{12,28},{16,0},{20,4},{24,8},{28,12},{1,17},{... | collective-permute-start | bytes 479240 | tf_op jit(solution)/shard_map/ppermute | solution.py:681
  126.5 1.6 %down_end.1 = (f32[96,3072]{1,0:T(8,128)}, f32[8,128]{1,0:T(8,128)S(1)}) custom-call(s32[16]{0:T(128)S(1)} %concatenate.9.refs_0_, bf16[2,144,512]{2,1,0:T(8,128)(2,1)S(1)} %get-tuple-element.305.refs_1_, bf16[2,144,512]{2,1,0:T(8,128)(2,1)S(1)} %collective-permute-done.36.refs_2_, f32[8,128]{1,0:T(8,128)S(1)} %get-tuple-element.306.refs_3_), custom_call_target="tpu_custom_call" | custom-call | flops 1 | bytes 1 | tf_op jit(solution)/shard_map/down_end/pallas_call | solution.py:489
  128.1 1.6 %up_end.1 = (f32[768,384]{1,0:T(8,128)}, f32[8,128]{1,0:T(8,128)S(1)}) custom-call(s32[16]{0:T(128)S(1)} %concatenate.9.refs_0_, bf16[2,192,384]{2,1,0:T(8,128)(2,1)S(1)} %get-tuple-element.304.refs_1_, bf16[2,192,384]{2,1,0:T(8,128)(2,1)S(1)} %collective-permute-done.35.refs_2_, f32[8,128]{1,0:T(8,128)S(1)} %get-tuple-element.307.refs_3_), custom_call_target="tpu_custom_call" | custom-call | flops 1 | bytes 1 | tf_op jit(solution)/shard_map/up_end/pallas_call | solution.py:489
  129.8 5.0 %collective-permute-done.34.refs_0_ = bf16[208,384]{1,0:T(8,128)(2,1)S(1)} collective-permute-done((bf16[208,384]{1,0:T(8,128)(2,1)S(1)}, bf16[208,384]{1,0:T(8,128)(2,1)S(1)}, u32[]{:S(2)}, u32[]{:S(2)}) %collective-permute-start.34) | collective-permute-done | bytes 159776 | tf_op jit(solution)/shard_map/ppermute | solution.py:681
  134.8 1.7 %collective-permute-start.37 = (bf16[208,384]{1,0:T(8,128)(2,1)S(1)}, bf16[208,384]{1,0:T(8,128)(2,1)S(1)}, u32[]{:S(2)}, u32[]{:S(2)}) collective-permute-start(bf16[208,384]{1,0:T(8,128)(2,1)S(1)} %get-tuple-element.313.refs_1_), channel_id=1, source_target_pairs={{0,2},{1,3},{2,0},{3,1},{4,6},{5,7},{6,4},{7,5},{8,10},{9,11},{10,... | collective-permute-start | bytes 479240 | tf_op jit(solution)/shard_map/ppermute | solution.py:678
  136.5 0.5 collective-permute-start.39
  137.0 0.9 collective-permute-done.19.refs_5_
  137.9 1.8 %unpack.1 = (bf16[4,128,768]{2,1,0:T(8,128)(2,1)}, bf16[4,128,768]{2,1,0:T(8,128)(2,1)}, f32[4,8,768]{2,1,0:T(8,128)}, f32[8,128]{1,0:T(8,128)S(1)}) custom-call(s32[16]{0:T(128)S(1)} %concatenate.9.refs_0_, f32[4,8,128]{2,1,0:T(8,128)S(1)} %broadcast_in_dim.12.refs_1_, bf16[272,768]{1,0:T(8,128)(2,1)S(1)} %get-tuple-element.259.refs_2_, ...), custom_call_target="tpu_custom_call" | custom-call | flops 1000000000 | bytes 1 | tf_op jit(solution)/shard_map/unpack/pallas_call | solution.py:489
  139.7 4.7 %collective-permute-done.37.refs_2_ = bf16[208,384]{1,0:T(8,128)(2,1)S(1)} collective-permute-done((bf16[208,384]{1,0:T(8,128)(2,1)S(1)}, bf16[208,384]{1,0:T(8,128)(2,1)S(1)}, u32[]{:S(2)}, u32[]{:S(2)}) %collective-permute-start.37) | collective-permute-done | bytes 159776 | tf_op jit(solution)/shard_map/ppermute | solution.py:678
  144.4 1.6 %qkv_end.1 = (f32[96,768]{1,0:T(8,128)}, f32[96,768]{1,0:T(8,128)}, f32[96,768]{1,0:T(8,128)}, f32[96,768]{1,0:T(8,128)}, f32[96]{0:T(128)}, /*index=5*/f32[96]{...) custom-call(s32[16]{0:T(128)S(1)} %concatenate.9.refs_0_, ...), custom_call_target="tpu_custom_call" | custom-call | flops 1 | bytes 1 | tf_op jit(solution)/shard_map/qkv_end/pallas_call | solution.py:489
  (121 shorter events, 2.8 us)
Async XLA Ops:
  0.7 9.1 %copy-start.20 = (s32[4,8]{1,0:T(4,128)S(1)}, s32[4,8]{1,0:T(4,128)}, u32[]{:S(2)}) copy-start(s32[4,8]{1,0:T(4,128)} %param.20) | copy-start | bytes 388
  0.8 25.3 %slice-start.2 = ((s8[4718592]{0:T(1024)(128)(4,1)}), s8[524288]{0:T(1024)(128)(4,1)S(1)}, s32[]{:S(2)}) async-start(s8[4718592]{0:T(1024)(128)(4,1)} %bitcast.30), calls=%async_computation.2 | async-start | bytes 1048576
  2.6 10.9 %collective-permute-start = (bf16[128,768]{1,0:T(8,128)(2,1)S(1)}, bf16[128,768]{1,0:T(8,128)(2,1)S(1)}, u32[]{:S(2)}, u32[]{:S(2)}) collective-permute-start(bf16[128,768]{1,0:T(8,128)(2,1)S(1)} %get-tuple-element.175), channel_id=1, source_target_pairs={{0,1},{1,0},{2,3},{3,2},{4,5},{5,4},{6,7},{7,6},{8,9},{9,8},{10,11... | collective-permute-start | bytes 589832 | tf_op jit(solution)/shard_map/ppermute | solution.py:610
  3.1 10.4 %collective-permute-start.1 = (bf16[128,768]{1,0:T(8,128)(2,1)S(1)}, bf16[128,768]{1,0:T(8,128)(2,1)S(1)}, u32[]{:S(2)}, u32[]{:S(2)}) collective-permute-start(bf16[128,768]{1,0:T(8,128)(2,1)S(1)} %get-tuple-element.176), channel_id=1, source_target_pairs={{0,2},{1,3},{2,0},{3,1},{4,6},{5,7},{6,4},{7,5},{8,10},{9,11},{10,... | collective-permute-start | bytes 589832 | tf_op jit(solution)/shard_map/ppermute | solution.py:610
  5.7 9.4 %collective-permute-start.2 = (bf16[128,768]{1,0:T(8,128)(2,1)S(1)}, bf16[128,768]{1,0:T(8,128)(2,1)S(1)}, u32[]{:S(2)}, u32[]{:S(2)}) collective-permute-start(bf16[128,768]{1,0:T(8,128)(2,1)S(1)} %get-tuple-element.177), channel_id=1, source_target_pairs={{0,3},{1,2},{2,1},{3,0},{4,7},{5,6},{6,5},{7,4},{8,11},{9,10},{10,... | collective-permute-start | bytes 589832 | tf_op jit(solution)/shard_map/ppermute | solution.py:610
  7.6 18.5 %collective-permute-start.3 = (bf16[128,768]{1,0:T(8,128)(2,1)S(1)}, bf16[128,768]{1,0:T(8,128)(2,1)S(1)}, u32[]{:S(2)}, u32[]{:S(2)}) collective-permute-start(bf16[128,768]{1,0:T(8,128)(2,1)S(1)} %get-tuple-element.186), channel_id=1, source_target_pairs={{0,1},{1,0},{2,3},{3,2},{4,5},{5,4},{6,7},{7,6},{8,9},{9,8},{10,11... | collective-permute-start | bytes 589832 | tf_op jit(solution)/shard_map/ppermute | solution.py:610
  7.8 18.3 %collective-permute-start.4 = (bf16[128,768]{1,0:T(8,128)(2,1)S(1)}, bf16[128,768]{1,0:T(8,128)(2,1)S(1)}, u32[]{:S(2)}, u32[]{:S(2)}) collective-permute-start(bf16[128,768]{1,0:T(8,128)(2,1)S(1)} %get-tuple-element.187), channel_id=1, source_target_pairs={{0,2},{1,3},{2,0},{3,1},{4,6},{5,7},{6,4},{7,5},{8,10},{9,11},{10,... | collective-permute-start | bytes 589832 | tf_op jit(solution)/shard_map/ppermute | solution.py:610
  11.1 4.1 %copy-start.14 = (bf16[768]{0:T(1024)(128)(2,1)S(1)}, bf16[768]{0:T(1024)(128)(2,1)}, u32[]{:S(2)}) copy-start(bf16[768]{0:T(1024)(128)(2,1)} %refs_10_.1) | copy-start | bytes 4612
  11.1 4.1 %copy-start.15 = (bf16[768]{0:T(1024)(128)(2,1)S(1)}, bf16[768]{0:T(1024)(128)(2,1)}, u32[]{:S(2)}) copy-start(bf16[768]{0:T(1024)(128)(2,1)} %refs_11_.1) | copy-start | bytes 4612
  11.1 4.1 %copy-start.16 = (bf16[768]{0:T(1024)(128)(2,1)S(1)}, bf16[768]{0:T(1024)(128)(2,1)}, u32[]{:S(2)}) copy-start(bf16[768]{0:T(1024)(128)(2,1)} %refs_12_.1) | copy-start | bytes 4612
  11.2 15.0 %slice-start.3 = ((s8[4718592]{0:T(1024)(128)(4,1)}), s8[4194304]{0:T(1024)(128)(4,1)S(1)}, s32[]{:S(2)}) async-start(s8[4718592]{0:T(1024)(128)(4,1)} %bitcast.30), calls=%async_computation.3 | async-start | bytes 8388608
  13.5 12.6 %collective-permute-start.5 = (bf16[128,768]{1,0:T(8,128)(2,1)S(1)}, bf16[128,768]{1,0:T(8,128)(2,1)S(1)}, u32[]{:S(2)}, u32[]{:S(2)}) collective-permute-start(bf16[128,768]{1,0:T(8,128)(2,1)S(1)} %get-tuple-element.188), channel_id=1, source_target_pairs={{0,3},{1,2},{2,1},{3,0},{4,7},{5,6},{6,5},{7,4},{8,11},{9,10},{10,... | collective-permute-start | bytes 589832 | tf_op jit(solution)/shard_map/ppermute | solution.py:610
  15.2 11.0 %copy-start.11 = (bf16[768]{0:T(1024)(128)(2,1)S(1)}, bf16[768]{0:T(1024)(128)(2,1)}, u32[]{:S(2)}) copy-start(bf16[768]{0:T(1024)(128)(2,1)} %refs_6_.6) | copy-start | bytes 4612
  15.2 11.0 %copy-start.12 = (bf16[768]{0:T(1024)(128)(2,1)S(1)}, bf16[768]{0:T(1024)(128)(2,1)}, u32[]{:S(2)}) copy-start(bf16[768]{0:T(1024)(128)(2,1)} %refs_6_.5) | copy-start | bytes 4612
  15.2 11.0 %copy-start.13 = (bf16[3072]{0:T(1024)(128)(2,1)S(1)}, bf16[3072]{0:T(1024)(128)(2,1)}, u32[]{:S(2)}) copy-start(bf16[3072]{0:T(1024)(128)(2,1)} %refs_8_.1) | copy-start | bytes 18436
  15.2 10.9 %copy-start.17 = (bf16[768]{0:T(1024)(128)(2,1)S(1)}, bf16[768]{0:T(1024)(128)(2,1)}, u32[]{:S(2)}) copy-start(bf16[768]{0:T(1024)(128)(2,1)} %refs_4_.2) | copy-start | bytes 4612
  15.2 10.9 %copy-start.18 = (bf16[768]{0:T(1024)(128)(2,1)S(1)}, bf16[768]{0:T(1024)(128)(2,1)}, u32[]{:S(2)}) copy-start(bf16[768]{0:T(1024)(128)(2,1)} %refs_5_.3) | copy-start | bytes 4612
  15.3 10.9 %copy-start.19 = (bf16[768]{0:T(1024)(128)(2,1)S(1)}, bf16[768]{0:T(1024)(128)(2,1)}, u32[]{:S(2)}) copy-start(bf16[768]{0:T(1024)(128)(2,1)} %refs_6_.4) | copy-start | bytes 4612
  26.1 14.4 %slice-start = ((s8[4718592]{0:T(1024)(128)(4,1)}), s8[4194304]{0:T(1024)(128)(4,1)S(1)}, s32[]{:S(2)}) async-start(s8[4718592]{0:T(1024)(128)(4,1)} %bitcast.28), calls=%async_computation | async-start | bytes 8388608
  26.2 14.3 %slice-start.1 = ((s8[4718592]{0:T(1024)(128)(4,1)}), s8[524288]{0:T(1024)(128)(4,1)S(1)}, s32[]{:S(2)}) async-start(s8[4718592]{0:T(1024)(128)(4,1)} %bitcast.28), calls=%async_computation.1 | async-start | bytes 1048576
  40.2 6.7 %collective-permute-start.6 = (bf16[2,8,48,1536]{3,2,1,0:T(8,128)(2,1)S(1)}, bf16[2,8,48,1536]{3,2,1,0:T(8,128)(2,1)S(1)}, u32[]{:S(2)}, u32[]{:S(2)}) collective-permute-start(bf16[2,8,48,1536]{3,2,1,0:T(8,128)(2,1)S(1)} %get-tuple-element.203), channel_id=1, source_target_pairs={{0,1},{1,0},{2,3},{3,2},{4,5},{5,4},{6,7},{7,6},{8,9},{9,8},{10,11... | collective-permute-start | bytes 7077896 | tf_op jit(solution)/shard_map/ppermute | solution.py:677
  46.6 12.8 %collective-permute-start.7 = (bf16[2,8,192,384]{3,2,1,0:T(8,128)(2,1)S(1)}, bf16[2,8,192,384]{3,2,1,0:T(8,128)(2,1)S(1)}, u32[]{:S(2)}, u32[]{:S(2)}) collective-permute-start(bf16[2,8,192,384]{3,2,1,0:T(8,128)(2,1)S(1)} %get-tuple-element.210), channel_id=1, source_target_pairs={{0,1},{1,0},{2,3},{3,2},{4,5},{5,4},{6,7},{7,6},{8,9},{9,8},{10,11... | collective-permute-start | bytes 7077896 | tf_op jit(solution)/shard_map/ppermute | solution.py:677
  46.9 5.6 %copy-start.3 = (bf16[768,768]{1,0:T(8,128)(2,1)S(1)}, bf16[768,768]{1,0:T(8,128)(2,1)}, u32[]{:S(2)}) copy-start(bf16[768,768]{1,0:T(8,128)(2,1)} %refs_7_.5) | copy-start | bytes 3538948
  46.9 5.6 %copy-start.4 = (f32[512,768]{1,0:T(8,128)S(1)}, f32[512,768]{1,0:T(8,128)}, u32[]{:S(2)}) copy-start(f32[512,768]{1,0:T(8,128)} %get-tuple-element.202.refs_8_) | copy-start | bytes 4718596
  46.9 5.6 %copy-start.9 = (f32[512,128]{1,0:T(8,128)S(1)}, f32[512,128]{1,0:T(8,128)}, u32[]{:S(2)}) copy-start(f32[512,128]{1,0:T(8,128)} %get-tuple-element.201.refs_5_) | copy-start | bytes 786436
  47.5 23.6 %collective-permute-start.10 = (bf16[2,2,2,48,512]{4,3,2,1,0:T(8,128)(2,1)S(1)}, bf16[2,2,2,48,512]{4,3,2,1,0:T(8,128)(2,1)S(1)}, u32[]{:S(2)}, u32[]{:S(2)}) collective-permute-start(bf16[2,2,2,48,512]{4,3,2,1,0:T(8,128)(2,1)S(1)} %get-tuple-element.230), channel_id=1, source_target_pairs={{0,8},{4,12},{8,0},{12,4},{16,24},{20,28},{24,16},{28,20},{1,9},{5... | collective-permute-start | bytes 1179656 | tf_op jit(solution)/shard_map/ppermute | solution.py:681
  49.5 21.7 %collective-permute-start.8 = (bf16[2,2,2,48,512]{4,3,2,1,0:T(8,128)(2,1)S(1)}, bf16[2,2,2,48,512]{4,3,2,1,0:T(8,128)(2,1)S(1)}, u32[]{:S(2)}, u32[]{:S(2)}) collective-permute-start(bf16[2,2,2,48,512]{4,3,2,1,0:T(8,128)(2,1)S(1)} %get-tuple-element.228), channel_id=1, source_target_pairs={{0,4},{4,0},{8,12},{12,8},{16,20},{20,16},{24,28},{28,24},{1,5},{5... | collective-permute-start | bytes 1179656 | tf_op jit(solution)/shard_map/ppermute | solution.py:681
  51.0 20.2 %collective-permute-start.9 = (bf16[2,2,2,48,512]{4,3,2,1,0:T(8,128)(2,1)S(1)}, bf16[2,2,2,48,512]{4,3,2,1,0:T(8,128)(2,1)S(1)}, u32[]{:S(2)}, u32[]{:S(2)}) collective-permute-start(bf16[2,2,2,48,512]{4,3,2,1,0:T(8,128)(2,1)S(1)} %get-tuple-element.229), channel_id=1, source_target_pairs={{0,2},{1,3},{2,0},{3,1},{4,6},{5,7},{6,4},{7,5},{8,10},{9,11},{10,... | collective-permute-start | bytes 1179656 | tf_op jit(solution)/shard_map/ppermute | solution.py:678
  59.5 1.8 %copy-start.5 = (bf16[512,768]{1,0:T(8,128)(2,1)S(1)}, bf16[512,768]{1,0:T(8,128)(2,1)}, u32[]{:S(2)}) copy-start(bf16[512,768]{1,0:T(8,128)(2,1)} %get-tuple-element.194.refs_0_) | copy-start | bytes 2359300
  59.5 1.8 %copy-start.6 = (bf16[512,768]{1,0:T(8,128)(2,1)S(1)}, bf16[512,768]{1,0:T(8,128)(2,1)}, u32[]{:S(2)}) copy-start(bf16[512,768]{1,0:T(8,128)(2,1)} %get-tuple-element.195.refs_1_) | copy-start | bytes 2359300
  59.5 1.8 %copy-start.7 = (bf16[512,768]{1,0:T(8,128)(2,1)S(1)}, bf16[512,768]{1,0:T(8,128)(2,1)}, u32[]{:S(2)}) copy-start(bf16[512,768]{1,0:T(8,128)(2,1)} %get-tuple-element.196.refs_2_) | copy-start | bytes 2359300
  60.2 17.3 %collective-permute-start.15 = (bf16[2,2,2,96,384]{4,3,2,1,0:T(8,128)(2,1)S(1)}, bf16[2,2,2,96,384]{4,3,2,1,0:T(8,128)(2,1)S(1)}, u32[]{:S(2)}, u32[]{:S(2)}) collective-permute-start(bf16[2,2,2,96,384]{4,3,2,1,0:T(8,128)(2,1)S(1)} %get-tuple-element.245), channel_id=1, source_target_pairs={{0,4},{4,0},{8,12},{12,8},{16,20},{20,16},{24,28},{28,24},{1,5},{5... | collective-permute-start | bytes 1769480 | tf_op jit(solution)/shard_map/ppermute | solution.py:681
  60.8 17.2 %collective-permute-start.16 = (bf16[2,2,2,96,384]{4,3,2,1,0:T(8,128)(2,1)S(1)}, bf16[2,2,2,96,384]{4,3,2,1,0:T(8,128)(2,1)S(1)}, u32[]{:S(2)}, u32[]{:S(2)}) collective-permute-start(bf16[2,2,2,96,384]{4,3,2,1,0:T(8,128)(2,1)S(1)} %get-tuple-element.246), channel_id=1, source_target_pairs={{0,2},{1,3},{2,0},{3,1},{4,6},{5,7},{6,4},{7,5},{8,10},{9,11},{10,... | collective-permute-start | bytes 1769480 | tf_op jit(solution)/shard_map/ppermute | solution.py:678
  71.1 3.5 %copy-start.8 = (bf16[512,768]{1,0:T(8,128)(2,1)S(1)}, bf16[512,768]{1,0:T(8,128)(2,1)}, u32[]{:S(2)}) copy-start(bf16[512,768]{1,0:T(8,128)(2,1)} %get-tuple-element.221.refs_4_) | copy-start | bytes 2359300
  71.5 13.4 %collective-permute-start.14 = (bf16[2,2,96,512]{3,2,1,0:T(8,128)(2,1)S(1)}, bf16[2,2,96,512]{3,2,1,0:T(8,128)(2,1)S(1)}, u32[]{:S(2)}, u32[]{:S(2)}) collective-permute-start(bf16[2,2,96,512]{3,2,1,0:T(8,128)(2,1)S(1)} %get-tuple-element.241), channel_id=1, source_target_pairs={{0,4},{4,0},{8,12},{12,8},{16,20},{20,16},{24,28},{28,24},{1,5},{5... | collective-permute-start | bytes 1179656 | tf_op jit(solution)/shard_map/ppermute | solution.py:681
  73.0 6.5 %collective-permute-start.13 = (bf16[2,2,48,512]{3,2,1,0:T(8,128)(2,1)S(1)}, bf16[2,2,48,512]{3,2,1,0:T(8,128)(2,1)S(1)}, u32[]{:S(2)}, u32[]{:S(2)}) collective-permute-start(bf16[2,2,48,512]{3,2,1,0:T(8,128)(2,1)S(1)} %get-tuple-element.240), channel_id=1, source_target_pairs={{0,2},{1,3},{2,0},{3,1},{4,6},{5,7},{6,4},{7,5},{8,10},{9,11},{10,... | collective-permute-start | bytes 589832 | tf_op jit(solution)/shard_map/ppermute | solution.py:678
  77.4 8.4 %collective-permute-start.12 = (bf16[2,8,112,384]{3,2,1,0:T(8,128)(2,1)S(1)}, bf16[2,8,112,384]{3,2,1,0:T(8,128)(2,1)S(1)}, u32[]{:S(2)}, u32[]{:S(2)}) collective-permute-start(bf16[2,8,112,384]{3,2,1,0:T(8,128)(2,1)S(1)} %get-tuple-element.237), channel_id=1, source_target_pairs={{0,1},{1,0},{2,3},{3,2},{4,5},{5,4},{6,7},{7,6},{8,9},{9,8},{10,11... | collective-permute-start | bytes 4128776 | tf_op jit(solution)/shard_map/ppermute | solution.py:677
  77.4 8.1 %collective-permute-start.11 = (bf16[2,8,96,384]{3,2,1,0:T(8,128)(2,1)S(1)}, bf16[2,8,96,384]{3,2,1,0:T(8,128)(2,1)S(1)}, u32[]{:S(2)}, u32[]{:S(2)}) collective-permute-start(bf16[2,8,96,384]{3,2,1,0:T(8,128)(2,1)S(1)} %get-tuple-element.236), channel_id=1, source_target_pairs={{0,1},{1,0},{2,3},{3,2},{4,5},{5,4},{6,7},{7,6},{8,9},{9,8},{10,11... | collective-permute-start | bytes 3538952 | tf_op jit(solution)/shard_map/ppermute | solution.py:677
  78.3 15.5 %collective-permute-start.22 = (bf16[2,2,96,384]{3,2,1,0:T(8,128)(2,1)S(1)}, bf16[2,2,96,384]{3,2,1,0:T(8,128)(2,1)S(1)}, u32[]{:S(2)}, u32[]{:S(2)}) collective-permute-start(bf16[2,2,96,384]{3,2,1,0:T(8,128)(2,1)S(1)} %get-tuple-element.267), channel_id=1, source_target_pairs={{0,2},{1,3},{2,0},{3,1},{4,6},{5,7},{6,4},{7,5},{8,10},{9,11},{10,... | collective-permute-start | bytes 884744 | tf_op jit(solution)/shard_map/ppermute | solution.py:678
  79.6 14.2 %collective-permute-start.23 = (bf16[2,2,96,384]{3,2,1,0:T(8,128)(2,1)S(1)}, bf16[2,2,96,384]{3,2,1,0:T(8,128)(2,1)S(1)}, u32[]{:S(2)}, u32[]{:S(2)}) collective-permute-start(bf16[2,2,96,384]{3,2,1,0:T(8,128)(2,1)S(1)} %get-tuple-element.268), channel_id=1, source_target_pairs={{0,4},{4,0},{8,12},{12,8},{16,20},{20,16},{24,28},{28,24},{1,5},{5... | collective-permute-start | bytes 884744 | tf_op jit(solution)/shard_map/ppermute | solution.py:681
  85.0 8.7 %collective-permute-start.24 = (bf16[2,96,512]{2,1,0:T(8,128)(2,1)S(1)}, bf16[2,96,512]{2,1,0:T(8,128)(2,1)S(1)}, u32[]{:S(2)}, u32[]{:S(2)}) collective-permute-start(bf16[2,96,512]{2,1,0:T(8,128)(2,1)S(1)} %get-tuple-element.271), channel_id=1, source_target_pairs={{0,8},{4,12},{8,0},{12,4},{16,24},{20,28},{24,16},{28,20},{1,9},{5... | collective-permute-start | bytes 589832 | tf_op jit(solution)/shard_map/ppermute | solution.py:681
  85.6 5.7 %collective-permute-start.25 = (bf16[2,48,512]{2,1,0:T(8,128)(2,1)S(1)}, bf16[2,48,512]{2,1,0:T(8,128)(2,1)S(1)}, u32[]{:S(2)}, u32[]{:S(2)}) collective-permute-start(bf16[2,48,512]{2,1,0:T(8,128)(2,1)S(1)} %get-tuple-element.272), channel_id=1, source_target_pairs={{0,2},{1,3},{2,0},{3,1},{4,6},{5,7},{6,4},{7,5},{8,10},{9,11},{10,... | collective-permute-start | bytes 294920 | tf_op jit(solution)/shard_map/ppermute | solution.py:678
  85.8 5.7 %copy-start = (bf16[768,768]{1,0:T(8,128)(2,1)S(1)}, bf16[768,768]{1,0:T(8,128)(2,1)}, u32[]{:S(2)}) copy-start(bf16[768,768]{1,0:T(8,128)(2,1)} %refs_4_.3) | copy-start | bytes 3538948
  85.8 5.7 %copy-start.1 = (bf16[768,768]{1,0:T(8,128)(2,1)S(1)}, bf16[768,768]{1,0:T(8,128)(2,1)}, u32[]{:S(2)}) copy-start(bf16[768,768]{1,0:T(8,128)(2,1)} %refs_5_.5) | copy-start | bytes 3538948
  85.8 5.7 %copy-start.2 = (bf16[768,768]{1,0:T(8,128)(2,1)S(1)}, bf16[768,768]{1,0:T(8,128)(2,1)}, u32[]{:S(2)}) copy-start(bf16[768,768]{1,0:T(8,128)(2,1)} %refs_6_.7) | copy-start | bytes 3538948
  86.4 17.8 %collective-permute-start.21 = (bf16[2,2,2,112,384]{4,3,2,1,0:T(8,128)(2,1)S(1)}, bf16[2,2,2,112,384]{4,3,2,1,0:T(8,128)(2,1)S(1)}, u32[]{:S(2)}, u32[]{:S(2)}) collective-permute-start(bf16[2,2,2,112,384]{4,3,2,1,0:T(8,128)(2,1)S(1)} %get-tuple-element.264), channel_id=1, source_target_pairs={{0,2},{1,3},{2,0},{3,1},{4,6},{5,7},{6,4},{7,5},{8,10},{9,11},{10,... | collective-permute-start | bytes 2064392 | tf_op jit(solution)/shard_map/ppermute | solution.py:678
  91.3 12.4 %collective-permute-start.20 = (bf16[2,2,2,96,384]{4,3,2,1,0:T(8,128)(2,1)S(1)}, bf16[2,2,2,96,384]{4,3,2,1,0:T(8,128)(2,1)S(1)}, u32[]{:S(2)}, u32[]{:S(2)}) collective-permute-start(bf16[2,2,2,96,384]{4,3,2,1,0:T(8,128)(2,1)S(1)} %get-tuple-element.263), channel_id=1, source_target_pairs={{0,4},{4,0},{8,12},{12,8},{16,20},{20,16},{24,28},{28,24},{1,5},{5... | collective-permute-start | bytes 1769480 | tf_op jit(solution)/shard_map/ppermute | solution.py:681
  93.9 11.7 %collective-permute-start.29 = (bf16[2,192,384]{2,1,0:T(8,128)(2,1)S(1)}, bf16[2,192,384]{2,1,0:T(8,128)(2,1)S(1)}, u32[]{:S(2)}, u32[]{:S(2)}) collective-permute-start(bf16[2,192,384]{2,1,0:T(8,128)(2,1)S(1)} %get-tuple-element.285), channel_id=1, source_target_pairs={{0,8},{4,12},{8,0},{12,4},{16,24},{20,28},{24,16},{28,20},{1,9},{5... | collective-permute-start | bytes 884744 | tf_op jit(solution)/shard_map/ppermute | solution.py:681
  95.6 10.1 %collective-permute-start.28 = (bf16[144,512]{1,0:T(8,128)(2,1)S(1)}, bf16[144,512]{1,0:T(8,128)(2,1)S(1)}, u32[]{:S(2)}, u32[]{:S(2)}) collective-permute-start(bf16[144,512]{1,0:T(8,128)(2,1)S(1)} %get-tuple-element.283), channel_id=1, source_target_pairs={{0,16},{4,20},{8,24},{12,28},{16,0},{20,4},{24,8},{28,12},{1,17},{... | collective-permute-start | bytes 442376 | tf_op jit(solution)/shard_map/ppermute | solution.py:681
  104.5 11.5 %collective-permute-start.27 = (bf16[2,2,112,384]{3,2,1,0:T(8,128)(2,1)S(1)}, bf16[2,2,112,384]{3,2,1,0:T(8,128)(2,1)S(1)}, u32[]{:S(2)}, u32[]{:S(2)}) collective-permute-start(bf16[2,2,112,384]{3,2,1,0:T(8,128)(2,1)S(1)} %get-tuple-element.280), channel_id=1, source_target_pairs={{0,4},{4,0},{8,12},{12,8},{16,20},{20,16},{24,28},{28,24},{1,5},{5... | collective-permute-start | bytes 1032200 | tf_op jit(solution)/shard_map/ppermute | solution.py:681
  105.1 10.9 %collective-permute-start.26 = (bf16[2,2,96,384]{3,2,1,0:T(8,128)(2,1)S(1)}, bf16[2,2,96,384]{3,2,1,0:T(8,128)(2,1)S(1)}, u32[]{:S(2)}, u32[]{:S(2)}) collective-permute-start(bf16[2,2,96,384]{3,2,1,0:T(8,128)(2,1)S(1)} %get-tuple-element.279), channel_id=1, source_target_pairs={{0,2},{1,3},{2,0},{3,1},{4,6},{5,7},{6,4},{7,5},{8,10},{9,11},{10,... | collective-permute-start | bytes 884744 | tf_op jit(solution)/shard_map/ppermute | solution.py:678
  105.7 9.6 %collective-permute-start.30 = (bf16[144,512]{1,0:T(8,128)(2,1)S(1)}, bf16[144,512]{1,0:T(8,128)(2,1)S(1)}, u32[]{:S(2)}, u32[]{:S(2)}) collective-permute-start(bf16[144,512]{1,0:T(8,128)(2,1)S(1)} %get-tuple-element.290.refs_1_), channel_id=1, source_target_pairs={{0,2},{1,3},{2,0},{3,1},{4,6},{5,7},{6,4},{7,5},{8,10},{9,11},{10,... | collective-permute-start | bytes 442376 | tf_op jit(solution)/shard_map/ppermute | solution.py:678
  107.3 8.9 %collective-permute-start.32 = (bf16[192,384]{1,0:T(8,128)(2,1)S(1)}, bf16[192,384]{1,0:T(8,128)(2,1)S(1)}, u32[]{:S(2)}, u32[]{:S(2)}) collective-permute-start(bf16[192,384]{1,0:T(8,128)(2,1)S(1)} %get-tuple-element.296), channel_id=1, source_target_pairs={{0,16},{4,20},{8,24},{12,28},{16,0},{20,4},{24,8},{28,12},{1,17},{... | collective-permute-start | bytes 442376 | tf_op jit(solution)/shard_map/ppermute | solution.py:681
  116.2 7.5 %collective-permute-start.31 = (bf16[2,208,384]{2,1,0:T(8,128)(2,1)S(1)}, bf16[2,208,384]{2,1,0:T(8,128)(2,1)S(1)}, u32[]{:S(2)}, u32[]{:S(2)}) collective-permute-start(bf16[2,208,384]{2,1,0:T(8,128)(2,1)S(1)} %get-tuple-element.293), channel_id=1, source_target_pairs={{0,8},{4,12},{8,0},{12,4},{16,24},{20,28},{24,16},{28,20},{1,9},{5... | collective-permute-start | bytes 958472 | tf_op jit(solution)/shard_map/ppermute | solution.py:681
  116.3 6.8 %collective-permute-start.33 = (bf16[192,384]{1,0:T(8,128)(2,1)S(1)}, bf16[192,384]{1,0:T(8,128)(2,1)S(1)}, u32[]{:S(2)}, u32[]{:S(2)}) collective-permute-start(bf16[192,384]{1,0:T(8,128)(2,1)S(1)} %get-tuple-element.299.refs_1_), channel_id=1, source_target_pairs={{0,2},{1,3},{2,0},{3,1},{4,6},{5,7},{6,4},{7,5},{8,10},{9,11},{10,... | collective-permute-start | bytes 442376 | tf_op jit(solution)/shard_map/ppermute | solution.py:678
  116.6 7.2 %collective-permute-start.36 = (bf16[2,144,512]{2,1,0:T(8,128)(2,1)S(1)}, bf16[2,144,512]{2,1,0:T(8,128)(2,1)S(1)}, u32[]{:S(2)}, u32[]{:S(2)}) collective-permute-start(bf16[2,144,512]{2,1,0:T(8,128)(2,1)S(1)} %get-tuple-element.305.refs_1_), channel_id=1, source_target_pairs={{0,1},{1,0},{2,3},{3,2},{4,5},{5,4},{6,7},{7,6},{8,9},{9,8},{10,11... | collective-permute-start | bytes 884744 | tf_op jit(solution)/shard_map/ppermute | solution.py:677
  116.6 19.9 %collective-permute-start.17 = (bf16[272,768]{1,0:T(8,128)(2,1)S(1)}, bf16[272,768]{1,0:T(8,128)(2,1)S(1)}, u32[]{:S(2)}, u32[]{:S(2)}) collective-permute-start(bf16[272,768]{1,0:T(8,128)(2,1)S(1)} %get-tuple-element.260), channel_id=1, source_target_pairs={{0,1},{1,0},{2,3},{3,2},{4,5},{5,4},{6,7},{7,6},{8,9},{9,8},{10,11... | collective-permute-start | bytes 1253384 | tf_op jit(solution)/shard_map/ppermute | solution.py:826
  117.1 19.9 %collective-permute-start.18 = (bf16[272,768]{1,0:T(8,128)(2,1)S(1)}, bf16[272,768]{1,0:T(8,128)(2,1)S(1)}, u32[]{:S(2)}, u32[]{:S(2)}) collective-permute-start(bf16[272,768]{1,0:T(8,128)(2,1)S(1)} %get-tuple-element.261), channel_id=1, source_target_pairs={{0,2},{1,3},{2,0},{3,1},{4,6},{5,7},{6,4},{7,5},{8,10},{9,11},{10,... | collective-permute-start | bytes 1253384 | tf_op jit(solution)/shard_map/ppermute | solution.py:826
  123.1 14.8 %collective-permute-start.19 = (bf16[272,768]{1,0:T(8,128)(2,1)S(1)}, bf16[272,768]{1,0:T(8,128)(2,1)S(1)}, u32[]{:S(2)}, u32[]{:S(2)}) collective-permute-start(bf16[272,768]{1,0:T(8,128)(2,1)S(1)} %get-tuple-element.262), channel_id=1, source_target_pairs={{0,3},{1,2},{2,1},{3,0},{4,7},{5,6},{6,5},{7,4},{8,11},{9,10},{10,... | collective-permute-start | bytes 1253384 | tf_op jit(solution)/shard_map/ppermute | solution.py:826
  123.7 4.5 %collective-permute-start.35 = (bf16[2,192,384]{2,1,0:T(8,128)(2,1)S(1)}, bf16[2,192,384]{2,1,0:T(8,128)(2,1)S(1)}, u32[]{:S(2)}, u32[]{:S(2)}) collective-permute-start(bf16[2,192,384]{2,1,0:T(8,128)(2,1)S(1)} %get-tuple-element.304.refs_1_), channel_id=1, source_target_pairs={{0,1},{1,0},{2,3},{3,2},{4,5},{5,4},{6,7},{7,6},{8,9},{9,8},{10,11... | collective-permute-start | bytes 884744 | tf_op jit(solution)/shard_map/ppermute | solution.py:677
  123.8 10.9 %collective-permute-start.34 = (bf16[208,384]{1,0:T(8,128)(2,1)S(1)}, bf16[208,384]{1,0:T(8,128)(2,1)S(1)}, u32[]{:S(2)}, u32[]{:S(2)}) collective-permute-start(bf16[208,384]{1,0:T(8,128)(2,1)S(1)} %get-tuple-element.302), channel_id=1, source_target_pairs={{0,16},{4,20},{8,24},{12,28},{16,0},{20,4},{24,8},{28,12},{1,17},{... | collective-permute-start | bytes 479240 | tf_op jit(solution)/shard_map/ppermute | solution.py:681
  134.8 9.6 %collective-permute-start.37 = (bf16[208,384]{1,0:T(8,128)(2,1)S(1)}, bf16[208,384]{1,0:T(8,128)(2,1)S(1)}, u32[]{:S(2)}, u32[]{:S(2)}) collective-permute-start(bf16[208,384]{1,0:T(8,128)(2,1)S(1)} %get-tuple-element.313.refs_1_), channel_id=1, source_target_pairs={{0,2},{1,3},{2,0},{3,1},{4,6},{5,7},{6,4},{7,5},{8,10},{9,11},{10,... | collective-permute-start | bytes 479240 | tf_op jit(solution)/shard_map/ppermute | solution.py:678
  136.5 7.9 %collective-permute-start.38 = (bf16[208,384]{1,0:T(8,128)(2,1)S(1)}, bf16[208,384]{1,0:T(8,128)(2,1)S(1)}, u32[]{:S(2)}, u32[]{:S(2)}) collective-permute-start(bf16[208,384]{1,0:T(8,128)(2,1)S(1)} %get-tuple-element.313.refs_1_), channel_id=1, source_target_pairs={{0,1},{1,0},{2,3},{3,2},{4,5},{5,4},{6,7},{7,6},{8,9},{9,8},{10,11... | collective-permute-start | bytes 479240 | tf_op jit(solution)/shard_map/ppermute | solution.py:677
  136.5 7.9 %collective-permute-start.39 = (bf16[208,384]{1,0:T(8,128)(2,1)S(1)}, bf16[208,384]{1,0:T(8,128)(2,1)S(1)}, u32[]{:S(2)}, u32[]{:S(2)}) collective-permute-start(bf16[208,384]{1,0:T(8,128)(2,1)S(1)} %get-tuple-element.313.refs_1_), channel_id=1, source_target_pairs={{0,3},{1,2},{2,1},{3,0},{4,7},{5,6},{6,5},{7,4},{8,11},{9,10},{10,... | collective-permute-start | bytes 479240 | tf_op jit(solution)/shard_map/ppermute | solution.py:757
  (1 other events, 1.7 us)
